TPU v7x, 1024 devices: a whole 4x8x16 slice. The times are simulated.
1024 devices in a mesh: gx: 16 (over z_hi, y), gy: 4 (over x), gz: 16 (over z_lo, core).
Axes of the slice: x: 4, y: 8, z: 16 (z_hi: 2, z_lo: 8; z = z_hi * 8 + z_lo), core: 2. Of those that a mesh axis runs over, the one named last changes fastest.
Arguments:
- orbitals: float32 [8, 128, 32, 2048], P(None, 'gx', 'gy', 'gz'), may hold values from -6 to 6
- potential: float32 [128, 32, 2048], P('gx', 'gy', 'gz'), may hold values from -3 to 0
- proj_values: float32 [4, 2097152], P(None, ('gx', 'gy', 'gz')), may hold values from -1 to 1
- point_cell: int32 [2097152], P(('gx', 'gy', 'gz')), may hold values from 0 to 8191
- point_owner: int32 [2097152], P(('gx', 'gy', 'gz')), may hold values from 0 to 1023, as said below
- point_slot: int32 [2097152], P(('gx', 'gy', 'gz')), may hold values from 0 to 4
- point_count: int32 [1024], P(('gx', 'gy', 'gz')), may hold values from 1 to 2048, 1310720 in all
- atom_energy: float32 [4, 5120], replicated, may hold values from -2 to 2
Outputs:
- filtered: float32 [8, 128, 32, 2048], P(None, 'gx', 'gy', 'gz')
Inputs may be any that keep to these rules, and one draw needn't show every extreme that they name: `point_owner`: the owner of point i's atom differs from domain i // 2048 by at most one index along each of gx, gy and gz, counted periodically. Only the first point_count[d] of domain d's 2048 point slots are live; some domain has all of them live.
All inputs are finite; a program needn't handle non-finite values. No bound on the sum of `point_count` on one device may be relied on, other than what follows from the above.
Results may differ from a plain program's by a relative error of at most 0.0001.
Values sent between devices are 32-bit elements; how exact they have to be, the bound alone decides.
No kernel may reach another device: no remote copies, remote signals or barrier semaphores. Data moves between devices by JAX's collectives and lax.ppermute only.
A program may use at most 64 MiB of HBM per device.

v0:
```python
import jax
import jax.numpy as jnp
from jax import lax
from jax.sharding import PartitionSpec as P

DEGREE = 3
ATOM_DEV = 5


stencil_terms = (
    -5369.0 / 1800.0,
    12.0 / 7.0,
    -15.0 / 56.0,
    10.0 / 189.0,
    -1.0 / 112.0,
    2.0 / 1925.0,
    -1.0 / 16632.0,
)
lowest = -3.5
cutoff = 1.5
highest = 13.0


def with_halo(cells, sides, width):
    for axis, dim in sides:
        count = lax.axis_size(axis)
        head = lax.slice_in_dim(cells, 0, width, axis=dim)
        tail = lax.slice_in_dim(cells, cells.shape[dim] - width, cells.shape[dim], axis=dim)
        cells = jnp.concatenate(
            [
                lax.ppermute(tail, axis, [(i, (i + 1) % count) for i in range(count)]),
                cells,
                lax.ppermute(head, axis, [((i + 1) % count, i) for i in range(count)]),
            ],
            axis=dim,
        )
    return cells


def shifted(value, axis, steps):
    count = lax.axis_size(axis)
    pairs = [(source, (source + steps) % count) for source in range(count)]
    return lax.ppermute(value, axis, pairs)


def second_sum(padded, along_dim, length):

    def window(first_index):
        return lax.slice_in_dim(padded, first_index, first_index + length, axis=along_dim)

    summed = stencil_terms[0] * window(6)
    for offset in range(1, 7):
        summed = summed + stencil_terms[offset] * (window(6 + offset) + window(6 - offset))
    return summed


def laplace_part(grid_field):
    padded = with_halo(grid_field, (("gx", 1), ("gy", 2), ("gz", 3)), 6)
    padded_x = padded[:, :, 6:-6, 6:-6]
    padded_y = padded[:, 6:-6, :, 6:-6]
    padded_z = padded[:, 6:-6, 6:-6, :]
    laplace = second_sum(padded_x, 1, grid_field.shape[1])
    laplace = laplace + second_sum(padded_y, 2, grid_field.shape[2])
    return laplace + second_sum(padded_z, 3, grid_field.shape[3])


def wrapped_offset(owner_coord, own_coord, axis_count):
    remain = (owner_coord - own_coord) % axis_count
    return jnp.where(remain == 0, 0, jnp.where(remain == 1, 1, -1)).astype(jnp.int32)


def body(
    orbitals, potential, proj_values, point_cell, point_owner, point_slot, point_count, atom_energy
):
    orbital_count = orbitals.shape[0]
    cell_count = orbitals.shape[1] * orbitals.shape[2] * orbitals.shape[3]
    projector_count = proj_values.shape[0]
    point_total = proj_values.shape[1]
    live_mask = (jnp.arange(point_total, dtype=jnp.int32) < point_count[0]).astype(jnp.float32)
    masked = proj_values * live_mask[None, :]
    masked_rows = masked.T
    size_x = lax.axis_size("gx")
    size_y = lax.axis_size("gy")
    size_z = lax.axis_size("gz")
    index_x = lax.axis_index("gx")
    index_y = lax.axis_index("gy")
    index_z = lax.axis_index("gz")
    owner_x = point_owner // (size_y * size_z)
    owner_y = point_owner // size_z % size_y
    owner_z = point_owner % size_z
    neighbour_code = (wrapped_offset(owner_x, index_x, size_x) + 1) * 9
    neighbour_code = neighbour_code + (wrapped_offset(owner_y, index_y, size_y) + 1) * 3
    neighbour_code = neighbour_code + wrapped_offset(owner_z, index_z, size_z) + 1
    neighbour_seg = neighbour_code * ATOM_DEV + point_slot
    domain = (index_x * size_y + index_y) * size_z + index_z
    own_energy = lax.dynamic_slice_in_dim(atom_energy, domain * ATOM_DEV, ATOM_DEV, 1).T

    def nonlocal_part(grid_field):
        flattened = grid_field.reshape(orbital_count, cell_count)
        sampled = flattened[:, point_cell]
        contributions = (
            (masked[:, None, :] * sampled[None, :, :])
            .reshape(projector_count * orbital_count, point_total)
            .T
        )
        partials = jax.ops.segment_sum(
            contributions, neighbour_seg, num_segments=27 * ATOM_DEV
        ).reshape(3, 3, 3, -1)
        plane_sum = partials[1]
        for offset, source in ((1, 2), (-1, 0)):
            plane_sum = plane_sum + shifted(partials[source], "gx", offset)
        line_sum = plane_sum[1]
        for offset, source in ((1, 2), (-1, 0)):
            line_sum = line_sum + shifted(plane_sum[source], "gy", offset)
        owned = line_sum[1]
        for offset, source in ((1, 2), (-1, 0)):
            owned = owned + shifted(line_sum[source], "gz", offset)
        coefficients = (
            owned.reshape(ATOM_DEV, projector_count, orbital_count) * own_energy[:, :, None]
        )
        neighbourhood = with_halo(
            coefficients.reshape(1, 1, 1, -1), (("gx", 0), ("gy", 1), ("gz", 2)), 1
        )
        atom_rows = neighbourhood.reshape(27 * ATOM_DEV, projector_count, orbital_count)[
            neighbour_seg
        ]
        returned = jnp.sum(masked_rows[:, :, None] * atom_rows, axis=1)
        return jnp.zeros_like(flattened).at[:, point_cell].add(returned.T).reshape(grid_field.shape)

    def hamiltonian(grid_field):
        return (
            -0.5 * laplace_part(grid_field)
            + potential[None] * grid_field
            + nonlocal_part(grid_field)
        )

    half_width = (highest - cutoff) / 2.0
    middle = (highest + cutoff) / 2.0
    sigma_first = half_width / (lowest - middle)
    previous = orbitals
    current = sigma_first / half_width * (hamiltonian(orbitals) - middle * orbitals)
    sigma_now = sigma_first
    for degree_index in range(1, DEGREE):
        sigma_next = 1.0 / (2.0 / sigma_first - sigma_now)
        following = (
            2.0 * sigma_next / half_width * (hamiltonian(current) - middle * current)
            - sigma_now * sigma_next * previous
        )
        previous = current
        current = following
        sigma_now = sigma_next
    return current


def solution(mesh):
    return jax.shard_map(
        body,
        mesh=mesh,
        in_specs=(
            P(None, "gx", "gy", "gz"),
            P("gx", "gy", "gz"),
            P(None, ("gx", "gy", "gz")),
            P(("gx", "gy", "gz")),
            P(("gx", "gy", "gz")),
            P(("gx", "gy", "gz")),
            P(("gx", "gy", "gz")),
            P(),
        ),
        out_specs=P(None, "gx", "gy", "gz"),
        check_vma=False,
    )
```

profile of v0, /device:TPU:6, one launch (start us, length us, event | category | flops | bytes accessed | tf_op | source)
XLA Modules:
  0.0 658.0 jit_solution(14022295722015019794)
XLA Ops:
  12.7 11.5 %scatter_custom_fusion = f32[135,32]{1,0:T(8,128)S(1)} fusion(s32[2048]{0:T(1024)S(1)} %get-tuple-element.8, f32[2048,32]{1,0:T(8,128)S(1)} %copy.46, f32[]{:T(128)} %constant.106.clone.1), kind=kCustom, calls=%fused_computation.347 | custom fusion | flops 65536 | bytes 17284 | tf_op jit(solution)/shard_map/scatter-add | solution.py:106
  24.3 22.3 %collective-permute-start.7 = (f32[3,3,160]{2,1,0:T(4,128)S(1)}, f32[3,3,160]{2,1,0:T(4,128)S(1)}, u32[]{:S(2)}, u32[]{:S(2)}) collective-permute-start(f32[3,3,160]{2,1,0:T(4,128)S(1)} %squeeze.87), channel_id=1, source_target_pairs={{0,960},{64,0},{128,64},{192,128},{256,192},{320,256},{384,320},{4... | collective-permute-start | bytes 17288 | tf_op jit(solution)/shard_map/ppermute | solution.py:43
  48.6 14.4 %collective-permute-done.6 = f32[3,3,160]{2,1,0:T(4,128)S(1)} collective-permute-done((f32[3,3,160]{2,1,0:T(4,128)S(1)}, f32[3,3,160]{2,1,0:T(4,128)S(1)}, u32[]{:S(2)}, u32[]{:S(2)}) %collective-permute-start.6) | collective-permute-done | bytes 5792 | tf_op jit(solution)/shard_map/ppermute | solution.py:43
  96.6 10.6 %collective-permute-done.12 = f32[1,1,1,160]{3,2,1,0:T(1,128)S(1)} collective-permute-done((f32[1,1,1,160]{3,2,1,0:T(1,128)S(1)}, f32[1,1,1,160]{3,2,1,0:T(1,128)S(1)}, u32[]{:S(2)}, u32[]{:S(2)}) %collective-permute-start.12) | collective-permute-done | bytes 672 | tf_op jit(solution)/shard_map/ppermute | solution.py:31
  132.6 15.4 %gather_fusion.1 = f32[2048,4,8]{2,1,0:T(4,128)} fusion(f32[135,4,8]{2,1,0:T(4,128)S(1)} %reshape.97, s32[2048]{0:T(1024)S(1)} %get-tuple-element.7), kind=kCustom, calls=%fused_computation.1 | custom fusion | bytes 532480 | tf_op jit(solution)/shard_map/gather | solution.py:124
  160.3 10.7 %collective-permute-start.4 = (f32[8,20,20,6]{2,0,3,1:T(8,128)}, f32[8,20,20,6]{2,0,3,1:T(8,128)}, u32[]{:S(2)}, u32[]{:S(2)}) collective-permute-start(f32[8,20,20,6]{2,0,3,1:T(8,128)} %copy.38), channel_id=1, source_target_pairs={{1,0},{2,1},{3,2},{4,3},{5,4},{6,5},{7,6},{8,7},{9,8},{10,9},{11,1... | collective-permute-start | bytes 230408 | tf_op jit(solution)/shard_map/ppermute | solution.py:33
  171.1 13.4 %multiply_reduce_fusion.2 = f32[2048,8]{1,0:T(8,128)} fusion(f32[2048,4,8]{2,1,0:T(4,128)} %gather_fusion.1, f32[2048,4]{1,0:T(8,128)S(1)} %copy.43), kind=kLoop, calls=%fused_computation.14 | loop fusion | flops 114688 | bytes 360448 | tf_op jit(solution)/shard_map/reduce_sum | solution.py:127
  184.4 14.0 %scatter_custom_fusion.1 = f32[8,8192]{0,1:T(8,128)} fusion(s32[2048]{0:T(1024)S(1)} %get-tuple-element.64, f32[2048,8]{1,0:T(8,128)} %multiply_reduce_fusion.2, f32[]{:T(128)} %constant.106.clone.1), kind=kCustom, calls=%fused_computation.29 | custom fusion | flops 16384 | bytes 262656 | tf_op jit(solution)/shard_map/scatter-add | solution.py:128
  228.7 11.8 %scatter_custom_fusion.2 = f32[135,32]{1,0:T(8,128)S(1)} fusion(s32[2048]{0:T(1024)S(1)} %get-tuple-element.8, f32[2048,32]{1,0:T(8,128)} %copy.56, f32[]{:T(128)} %constant.106.clone.1), kind=kCustom, calls=%fused_computation.345 | custom fusion | flops 65536 | bytes 17792 | tf_op jit(solution)/shard_map/scatter-add | solution.py:106
  240.6 13.1 %collective-permute-start.25 = (f32[3,3,160]{2,1,0:T(4,128)S(1)}, f32[3,3,160]{2,1,0:T(4,128)S(1)}, u32[]{:S(2)}, u32[]{:S(2)}) collective-permute-start(f32[3,3,160]{2,1,0:T(4,128)S(1)} %squeeze.96), channel_id=1, source_target_pairs={{0,960},{64,0},{128,64},{192,128},{256,192},{320,256},{384,320},{4... | collective-permute-start | bytes 17288 | tf_op jit(solution)/shard_map/ppermute | solution.py:43
  255.8 14.4 %collective-permute-done.24 = f32[3,3,160]{2,1,0:T(4,128)S(1)} collective-permute-done((f32[3,3,160]{2,1,0:T(4,128)S(1)}, f32[3,3,160]{2,1,0:T(4,128)S(1)}, u32[]{:S(2)}, u32[]{:S(2)}) %collective-permute-start.24) | collective-permute-done | bytes 5792 | tf_op jit(solution)/shard_map/ppermute | solution.py:43
  297.9 12.5 %collective-permute-done.30 = f32[1,1,1,160]{3,2,1,0:T(1,128)S(1)} collective-permute-done((f32[1,1,1,160]{3,2,1,0:T(1,128)S(1)}, f32[1,1,1,160]{3,2,1,0:T(1,128)S(1)}, u32[]{:S(2)}, u32[]{:S(2)}) %collective-permute-start.30) | collective-permute-done | bytes 672 | tf_op jit(solution)/shard_map/ppermute | solution.py:31
  319.7 14.7 %collective-permute-start.18 = (f32[8,6,8,128]{3,0,2,1:T(8,128)S(1)}, f32[8,6,8,128]{3,0,2,1:T(8,128)S(1)}, u32[]{:S(2)}, u32[]{:S(2)}) collective-permute-start(f32[8,6,8,128]{3,0,2,1:T(8,128)S(1)} %get-tuple-element.27), channel_id=1, source_target_pairs={{64,0},{128,64},{192,128},{256,192},{320,256},{384,320},{448,384},... | collective-permute-start | bytes 589832 | tf_op jit(solution)/shard_map/ppermute | solution.py:33
  348.2 15.4 %gather_fusion.3 = f32[2048,4,8]{2,1,0:T(4,128)} fusion(f32[135,4,8]{2,1,0:T(4,128)S(1)} %reshape.100, s32[2048]{0:T(1024)S(1)} %get-tuple-element.7), kind=kCustom, calls=%fused_computation.3 | custom fusion | bytes 532480 | tf_op jit(solution)/shard_map/gather | solution.py:124
  371.8 13.4 %multiply_reduce_fusion.1 = f32[2048,8]{1,0:T(8,128)} fusion(f32[2048,4,8]{2,1,0:T(4,128)} %gather_fusion.3, f32[2048,4]{1,0:T(8,128)S(1)} %copy.43), kind=kLoop, calls=%fused_computation.13 | loop fusion | flops 114688 | bytes 360448 | tf_op jit(solution)/shard_map/reduce_sum | solution.py:127
  385.1 14.0 %scatter_custom_fusion.3 = f32[8,8192]{0,1:T(8,128)} fusion(s32[2048]{0:T(1024)} %copy-done.18, f32[2048,8]{1,0:T(8,128)} %multiply_reduce_fusion.1, f32[]{:T(128)} %constant.106.clone.1), kind=kCustom, calls=%fused_computation.27 | custom fusion | flops 16384 | bytes 262656 | tf_op jit(solution)/shard_map/scatter-add | solution.py:128
  413.7 10.4 %collective-permute-start.22 = (f32[8,20,20,6]{2,0,3,1:T(8,128)}, f32[8,20,20,6]{2,0,3,1:T(8,128)}, u32[]{:S(2)}, u32[]{:S(2)}) collective-permute-start(f32[8,20,20,6]{2,0,3,1:T(8,128)} %copy.50), channel_id=1, source_target_pairs={{1,0},{2,1},{3,2},{4,3},{5,4},{6,5},{7,6},{8,7},{9,8},{10,9},{11,1... | collective-permute-start | bytes 230408 | tf_op jit(solution)/shard_map/ppermute | solution.py:33
  450.9 11.6 %scatter_custom_fusion.4 = f32[135,32]{1,0:T(8,128)S(1)} fusion(s32[2048]{0:T(1024)} %copy-done.19, f32[2048,32]{1,0:T(8,128)S(1)} %copy.65, f32[]{:T(128)} %constant.106.clone.1), kind=kCustom, calls=%fused_computation.343 | custom fusion | flops 65536 | bytes 17792 | tf_op jit(solution)/shard_map/scatter-add | solution.py:106
  468.6 12.4 %collective-permute-done.42 = f32[3,3,160]{2,1,0:T(4,128)S(1)} collective-permute-done((f32[3,3,160]{2,1,0:T(4,128)S(1)}, f32[3,3,160]{2,1,0:T(4,128)S(1)}, u32[]{:S(2)}, u32[]{:S(2)}) %collective-permute-start.42) | collective-permute-done | bytes 5792 | tf_op jit(solution)/shard_map/ppermute | solution.py:43
  514.9 12.4 %collective-permute-done.48 = f32[1,1,1,160]{3,2,1,0:T(1,128)S(1)} collective-permute-done((f32[1,1,1,160]{3,2,1,0:T(1,128)S(1)}, f32[1,1,1,160]{3,2,1,0:T(1,128)S(1)}, u32[]{:S(2)}, u32[]{:S(2)}) %collective-permute-start.48) | collective-permute-done | bytes 672 | tf_op jit(solution)/shard_map/ppermute | solution.py:31
  536.4 14.7 %collective-permute-start.36 = (f32[8,6,8,128]{3,0,2,1:T(8,128)S(1)}, f32[8,6,8,128]{3,0,2,1:T(8,128)S(1)}, u32[]{:S(2)}, u32[]{:S(2)}) collective-permute-start(f32[8,6,8,128]{3,0,2,1:T(8,128)S(1)} %get-tuple-element.25), channel_id=1, source_target_pairs={{64,0},{128,64},{192,128},{256,192},{320,256},{384,320},{448,384},... | collective-permute-start | bytes 589832 | tf_op jit(solution)/shard_map/ppermute | solution.py:33
  565.0 15.4 %gather_fusion.5 = f32[2048,4,8]{2,1,0:T(4,128)} fusion(f32[135,4,8]{2,1,0:T(4,128)S(1)} %reshape.103, s32[2048]{0:T(1024)S(1)} %get-tuple-element.7), kind=kCustom, calls=%fused_computation.5 | custom fusion | bytes 532480 | tf_op jit(solution)/shard_map/gather | solution.py:124
  588.8 13.4 %multiply_reduce_fusion = f32[2048,8]{1,0:T(8,128)} fusion(f32[2048,4,8]{2,1,0:T(4,128)} %gather_fusion.5, f32[2048,4]{1,0:T(8,128)S(1)} %copy.43), kind=kLoop, calls=%fused_computation.12 | loop fusion | flops 114688 | bytes 360448 | tf_op jit(solution)/shard_map/reduce_sum | solution.py:127
  602.1 14.0 %scatter_custom_fusion.5 = f32[8,8192]{0,1:T(8,128)} fusion(s32[2048]{0:T(1024)} %copy-done.18, f32[2048,8]{1,0:T(8,128)} %multiply_reduce_fusion, f32[]{:T(128)} %constant.106.clone.1), kind=kCustom, calls=%fused_computation.25 | custom fusion | flops 16384 | bytes 262656 | tf_op jit(solution)/shard_map/scatter-add | solution.py:128
  (240 shorter events, 330.2 us)
Async XLA Ops:
  24.3 24.3 %collective-permute-start.7 = (f32[3,3,160]{2,1,0:T(4,128)S(1)}, f32[3,3,160]{2,1,0:T(4,128)S(1)}, u32[]{:S(2)}, u32[]{:S(2)}) collective-permute-start(f32[3,3,160]{2,1,0:T(4,128)S(1)} %squeeze.87), channel_id=1, source_target_pairs={{0,960},{64,0},{128,64},{192,128},{256,192},{320,256},{384,320},{4... | collective-permute-start | bytes 17288 | tf_op jit(solution)/shard_map/ppermute | solution.py:43
  46.6 16.4 %collective-permute-start.6 = (f32[3,3,160]{2,1,0:T(4,128)S(1)}, f32[3,3,160]{2,1,0:T(4,128)S(1)}, u32[]{:S(2)}, u32[]{:S(2)}) collective-permute-start(f32[3,3,160]{2,1,0:T(4,128)S(1)} %squeeze.86), channel_id=1, source_target_pairs={{0,64},{64,128},{128,192},{192,256},{256,320},{320,384},{384,448},... | collective-permute-start | bytes 17288 | tf_op jit(solution)/shard_map/ppermute | solution.py:43
  90.6 16.5 %collective-permute-start.12 = (f32[1,1,1,160]{3,2,1,0:T(1,128)S(1)}, f32[1,1,1,160]{3,2,1,0:T(1,128)S(1)}, u32[]{:S(2)}, u32[]{:S(2)}) collective-permute-start(f32[1,1,1,160]{3,2,1,0:T(1,128)S(1)} %bitcast.79), channel_id=1, source_target_pairs={{0,64},{64,128},{128,192},{192,256},{256,320},{320,384},{384,448},... | collective-permute-start | bytes 1928 | tf_op jit(solution)/shard_map/ppermute | solution.py:31
  94.6 28.2 %collective-permute-start.1 = (f32[8,6,8,128]{3,0,2,1:T(8,128)S(1)}, f32[8,6,8,128]{3,0,2,1:T(8,128)S(1)}, u32[]{:S(2)}, u32[]{:S(2)}) collective-permute-start(f32[8,6,8,128]{3,0,2,1:T(8,128)S(1)} %copy.73), channel_id=1, source_target_pairs={{0,64},{64,128},{128,192},{192,256},{256,320},{320,384},{384,448},... | collective-permute-start | bytes 589832 | tf_op jit(solution)/shard_map/ppermute | solution.py:31
  124.9 23.1 %collective-permute-start.2 = (f32[8,20,6,128]{3,0,2,1:T(8,128)}, f32[8,20,6,128]{3,0,2,1:T(8,128)S(1)}, u32[]{:S(2)}, u32[]{:S(2)}) collective-permute-start(f32[8,20,6,128]{3,0,2,1:T(8,128)} %get-tuple-element.24), channel_id=1, source_target_pairs={{16,0},{32,16},{48,32},{0,48},{17,1},{33,17},{49,33},{1,49},{18,2}... | collective-permute-start | bytes 1474568 | tf_op jit(solution)/shard_map/ppermute | solution.py:33
  126.8 21.2 %collective-permute-start.3 = (f32[8,20,6,128]{3,0,2,1:T(8,128)}, f32[8,20,6,128]{3,0,2,1:T(8,128)}, u32[]{:S(2)}, u32[]{:S(2)}) collective-permute-start(f32[8,20,6,128]{3,0,2,1:T(8,128)} %get-tuple-element.23), channel_id=1, source_target_pairs={{0,16},{16,32},{32,48},{48,0},{1,17},{17,33},{33,49},{49,1},{2,18}... | collective-permute-start | bytes 1474568 | tf_op jit(solution)/shard_map/ppermute | solution.py:31
  155.1 46.2 %collective-permute-start.5 = (f32[8,20,20,6]{2,0,3,1:T(8,128)}, f32[8,20,20,6]{2,0,3,1:T(8,128)}, u32[]{:S(2)}, u32[]{:S(2)}) collective-permute-start(f32[8,20,20,6]{2,0,3,1:T(8,128)} %copy.40), channel_id=1, source_target_pairs={{0,1},{1,2},{2,3},{3,4},{4,5},{5,6},{6,7},{7,8},{8,9},{9,10},{10,1... | collective-permute-start | bytes 230408 | tf_op jit(solution)/shard_map/ppermute | solution.py:31
  160.3 44.2 %collective-permute-start.4 = (f32[8,20,20,6]{2,0,3,1:T(8,128)}, f32[8,20,20,6]{2,0,3,1:T(8,128)}, u32[]{:S(2)}, u32[]{:S(2)}) collective-permute-start(f32[8,20,20,6]{2,0,3,1:T(8,128)} %copy.38), channel_id=1, source_target_pairs={{1,0},{2,1},{3,2},{4,3},{5,4},{6,5},{7,6},{8,7},{9,8},{10,9},{11,1... | collective-permute-start | bytes 230408 | tf_op jit(solution)/shard_map/ppermute | solution.py:33
  310.4 24.0 %collective-permute-start.33 = (f32[3,1,1,160]{3,2,1,0:T(1,128)S(1)}, f32[3,1,1,160]{3,2,1,0:T(1,128)S(1)}, u32[]{:S(2)}, u32[]{:S(2)}) collective-permute-start(f32[3,1,1,160]{3,2,1,0:T(1,128)S(1)} %pad_maximum_fusion.46), channel_id=1, source_target_pairs={{16,0},{32,16},{48,32},{0,48},{17,1},{33,17},{49,33},{1,49},{18,2}... | collective-permute-start | bytes 5768 | tf_op jit(solution)/shard_map/ppermute | solution.py:33
  312.3 22.1 %collective-permute-start.32 = (f32[3,1,1,160]{3,2,1,0:T(1,128)S(1)}, f32[3,1,1,160]{3,2,1,0:T(1,128)S(1)}, u32[]{:S(2)}, u32[]{:S(2)}) collective-permute-start(f32[3,1,1,160]{3,2,1,0:T(1,128)S(1)} %pad_maximum_fusion.46), channel_id=1, source_target_pairs={{0,16},{16,32},{32,48},{48,0},{1,17},{17,33},{33,49},{49,1},{2,18}... | collective-permute-start | bytes 5768 | tf_op jit(solution)/shard_map/ppermute | solution.py:31
  317.7 45.8 %collective-permute-start.19 = (f32[8,6,8,128]{3,0,2,1:T(8,128)S(1)}, f32[8,6,8,128]{3,0,2,1:T(8,128)S(1)}, u32[]{:S(2)}, u32[]{:S(2)}) collective-permute-start(f32[8,6,8,128]{3,0,2,1:T(8,128)S(1)} %get-tuple-element.28), channel_id=1, source_target_pairs={{0,64},{64,128},{128,192},{192,256},{256,320},{320,384},{384,448},... | collective-permute-start | bytes 589832 | tf_op jit(solution)/shard_map/ppermute | solution.py:31
  319.7 43.9 %collective-permute-start.18 = (f32[8,6,8,128]{3,0,2,1:T(8,128)S(1)}, f32[8,6,8,128]{3,0,2,1:T(8,128)S(1)}, u32[]{:S(2)}, u32[]{:S(2)}) collective-permute-start(f32[8,6,8,128]{3,0,2,1:T(8,128)S(1)} %get-tuple-element.27), channel_id=1, source_target_pairs={{64,0},{128,64},{192,128},{256,192},{320,256},{384,320},{448,384},... | collective-permute-start | bytes 589832 | tf_op jit(solution)/shard_map/ppermute | solution.py:33
  364.7 37.9 %collective-permute-start.20 = (f32[8,20,6,128]{3,0,2,1:T(8,128)}, f32[8,20,6,128]{3,0,2,1:T(8,128)S(1)}, u32[]{:S(2)}, u32[]{:S(2)}) collective-permute-start(f32[8,20,6,128]{3,0,2,1:T(8,128)} %get-tuple-element.22), channel_id=1, source_target_pairs={{16,0},{32,16},{48,32},{0,48},{17,1},{33,17},{49,33},{1,49},{18,2}... | collective-permute-start | bytes 1474568 | tf_op jit(solution)/shard_map/ppermute | solution.py:33
  366.6 36.0 %collective-permute-start.21 = (f32[8,20,6,128]{3,0,2,1:T(8,128)}, f32[8,20,6,128]{3,0,2,1:T(8,128)S(1)}, u32[]{:S(2)}, u32[]{:S(2)}) collective-permute-start(f32[8,20,6,128]{3,0,2,1:T(8,128)} %get-tuple-element.21), channel_id=1, source_target_pairs={{0,16},{16,32},{32,48},{48,0},{1,17},{17,33},{33,49},{49,1},{2,18}... | collective-permute-start | bytes 1474568 | tf_op jit(solution)/shard_map/ppermute | solution.py:31
  408.4 18.8 %collective-permute-start.23 = (f32[8,20,20,6]{2,0,3,1:T(8,128)}, f32[8,20,20,6]{2,0,3,1:T(8,128)}, u32[]{:S(2)}, u32[]{:S(2)}) collective-permute-start(f32[8,20,20,6]{2,0,3,1:T(8,128)} %copy.52), channel_id=1, source_target_pairs={{0,1},{1,2},{2,3},{3,4},{4,5},{5,6},{6,7},{7,8},{8,9},{9,10},{10,1... | collective-permute-start | bytes 230408 | tf_op jit(solution)/shard_map/ppermute | solution.py:31
  413.7 16.9 %collective-permute-start.22 = (f32[8,20,20,6]{2,0,3,1:T(8,128)}, f32[8,20,20,6]{2,0,3,1:T(8,128)}, u32[]{:S(2)}, u32[]{:S(2)}) collective-permute-start(f32[8,20,20,6]{2,0,3,1:T(8,128)} %copy.50), channel_id=1, source_target_pairs={{1,0},{2,1},{3,2},{4,3},{5,4},{6,5},{7,6},{8,7},{9,8},{10,9},{11,1... | collective-permute-start | bytes 230408 | tf_op jit(solution)/shard_map/ppermute | solution.py:33
  527.3 23.9 %collective-permute-start.51 = (f32[3,1,1,160]{3,2,1,0:T(1,128)S(1)}, f32[3,1,1,160]{3,2,1,0:T(1,128)S(1)}, u32[]{:S(2)}, u32[]{:S(2)}) collective-permute-start(f32[3,1,1,160]{3,2,1,0:T(1,128)S(1)} %pad_maximum_fusion.47), channel_id=1, source_target_pairs={{16,0},{32,16},{48,32},{0,48},{17,1},{33,17},{49,33},{1,49},{18,2}... | collective-permute-start | bytes 5768 | tf_op jit(solution)/shard_map/ppermute | solution.py:33
  529.2 22.0 %collective-permute-start.50 = (f32[3,1,1,160]{3,2,1,0:T(1,128)S(1)}, f32[3,1,1,160]{3,2,1,0:T(1,128)S(1)}, u32[]{:S(2)}, u32[]{:S(2)}) collective-permute-start(f32[3,1,1,160]{3,2,1,0:T(1,128)S(1)} %pad_maximum_fusion.47), channel_id=1, source_target_pairs={{0,16},{16,32},{32,48},{48,0},{1,17},{17,33},{33,49},{49,1},{2,18}... | collective-permute-start | bytes 5768 | tf_op jit(solution)/shard_map/ppermute | solution.py:31
  534.5 45.8 %collective-permute-start.37 = (f32[8,6,8,128]{3,0,2,1:T(8,128)S(1)}, f32[8,6,8,128]{3,0,2,1:T(8,128)S(1)}, u32[]{:S(2)}, u32[]{:S(2)}) collective-permute-start(f32[8,6,8,128]{3,0,2,1:T(8,128)S(1)} %get-tuple-element.26), channel_id=1, source_target_pairs={{0,64},{64,128},{128,192},{192,256},{256,320},{320,384},{384,448},... | collective-permute-start | bytes 589832 | tf_op jit(solution)/shard_map/ppermute | solution.py:31
  536.4 43.9 %collective-permute-start.36 = (f32[8,6,8,128]{3,0,2,1:T(8,128)S(1)}, f32[8,6,8,128]{3,0,2,1:T(8,128)S(1)}, u32[]{:S(2)}, u32[]{:S(2)}) collective-permute-start(f32[8,6,8,128]{3,0,2,1:T(8,128)S(1)} %get-tuple-element.25), channel_id=1, source_target_pairs={{64,0},{128,64},{192,128},{256,192},{320,256},{384,320},{448,384},... | collective-permute-start | bytes 589832 | tf_op jit(solution)/shard_map/ppermute | solution.py:33
  581.4 38.2 %collective-permute-start.38 = (f32[8,20,6,128]{3,0,2,1:T(8,128)}, f32[8,20,6,128]{3,0,2,1:T(8,128)S(1)}, u32[]{:S(2)}, u32[]{:S(2)}) collective-permute-start(f32[8,20,6,128]{3,0,2,1:T(8,128)} %get-tuple-element.18), channel_id=1, source_target_pairs={{16,0},{32,16},{48,32},{0,48},{17,1},{33,17},{49,33},{1,49},{18,2}... | collective-permute-start | bytes 1474568 | tf_op jit(solution)/shard_map/ppermute | solution.py:33
  583.4 36.3 %collective-permute-start.39 = (f32[8,20,6,128]{3,0,2,1:T(8,128)}, f32[8,20,6,128]{3,0,2,1:T(8,128)S(1)}, u32[]{:S(2)}, u32[]{:S(2)}) collective-permute-start(f32[8,20,6,128]{3,0,2,1:T(8,128)} %get-tuple-element.17), channel_id=1, source_target_pairs={{0,16},{16,32},{32,48},{48,0},{1,17},{17,33},{33,49},{49,1},{2,18}... | collective-permute-start | bytes 1474568 | tf_op jit(solution)/shard_map/ppermute | solution.py:31
  626.5 17.4 %collective-permute-start.41 = (f32[8,20,20,6]{2,0,3,1:T(8,128)}, f32[8,20,20,6]{2,0,3,1:T(8,128)}, u32[]{:S(2)}, u32[]{:S(2)}) collective-permute-start(f32[8,20,20,6]{2,0,3,1:T(8,128)} %copy.61), channel_id=1, source_target_pairs={{0,1},{1,2},{2,3},{3,4},{4,5},{5,6},{6,7},{7,8},{8,9},{9,10},{10,1... | collective-permute-start | bytes 230408 | tf_op jit(solution)/shard_map/ppermute | solution.py:31
  630.3 16.9 %collective-permute-start.40 = (f32[8,20,20,6]{2,0,3,1:T(8,128)}, f32[8,20,20,6]{2,0,3,1:T(8,128)}, u32[]{:S(2)}, u32[]{:S(2)}) collective-permute-start(f32[8,20,20,6]{2,0,3,1:T(8,128)} %copy.59), channel_id=1, source_target_pairs={{1,0},{2,1},{3,2},{4,3},{5,4},{6,5},{7,6},{8,7},{9,8},{10,9},{11,1... | collective-permute-start | bytes 230408 | tf_op jit(solution)/shard_map/ppermute | solution.py:33
  (50 other events, 1233.7 us)
where the time goes:
time: 666 us; the launch traced here: 658 us
  starting transfers between devices  238 us (36%)
  local copies, waits for them, and re-layouts  146 us (22%)
  other arithmetic  141 us (21%)
  waiting for transfers between devices  130 us (20%)
    ppermute x18, starting transfers between devices, shifted(): return lax.ppermute(value, axis, pairs)  88.2 us
    ppermute x18, starting transfers between devices, with_halo(): lax.ppermute(head, axis, [((i + 1) % count, i) for i in range(count)])  88.2 us
    ppermute x18, waiting for transfers between devices, shifted(): return lax.ppermute(value, axis, pairs)  72.9 us
    ppermute x18, starting transfers between devices, with_halo(): lax.ppermute(tail, axis, [(i, (i + 1) % count) for i in range(count)])  61.9 us
    ppermute x18, waiting for transfers between devices, with_halo(): lax.ppermute(tail, axis, [(i, (i + 1) % count) for i in range(count)])  55.9 us
    gather x3, local copies, waits for them, and re-layouts, nonlocal_part(): neighbourhood.reshape(27 * ATOM_DEV, projector_count, orbital_count)  46.1 us
    scatter-add x3, other arithmetic, nonlocal_part(): jnp.zeros_like(flattened).at[:, point_cell].add(returned.T)  42.1 us
    reduce_sum x3, other arithmetic, nonlocal_part(): returned = jnp.sum(masked_rows[:, :, None] * atom_rows, axis=1)  40.1 us
  transfers between devices with their start and end apart: 54, of which 17 were waited for; matrix products, arithmetic and copies ran while one was open for 25% of the time, Pallas kernels for 0%

commit v1 on v0

v1 whole, which is shorter than its diff:
```python
import jax
import jax.numpy as jnp
from jax import lax
from jax.experimental import pallas as pl
from jax.experimental.pallas import tpu as pltpu
from jax.sharding import PartitionSpec as P

DEGREE = 3
ATOM_DEV = 5
NORB = 8
NPROJ = 4
SIDE = 8
DEPTH = 128
HALO = 6
ROWS = NORB * SIDE * SIDE
PLANES = 9
SEGS = PLANES * 8
CHUNK = 256
POS_Y = 4
VMEM_LIMIT = 56 * 1024 * 1024

stencil_terms = (
    -5369.0 / 1800.0,
    12.0 / 7.0,
    -15.0 / 56.0,
    10.0 / 189.0,
    -1.0 / 112.0,
    2.0 / 1925.0,
    -1.0 / 16632.0,
)
lowest = -3.5
cutoff = 1.5
highest = 13.0

F32 = jnp.float32
BF16 = jnp.bfloat16
LAST = (((1,), (1,)), ((), ()))
FIRST = (((0,), (0,)), ((), ()))


def iota(shape, dim):
    return lax.broadcasted_iota(jnp.int32, shape, dim)


def one_hot(index_row, rows, kind):
    hit = iota((rows, index_row.shape[1]), 0) == index_row
    return jnp.where(hit, 1.0, 0.0).astype(kind)


def split_two(value):
    upper = value.astype(BF16)
    return upper, (value - upper.astype(F32)).astype(BF16)


def sample_partials(cells, idx_ref, wts_ref):
    upper, lower = split_two(cells)
    both = jnp.concatenate([upper, lower], axis=1)
    points = idx_ref.shape[1]
    total = jnp.zeros((SEGS + 8, 128), F32)
    for first in range(0, points, CHUNK):
        span = slice(first, first + CHUNK)
        hot_z = one_hot(idx_ref[0:1, span], DEPTH, BF16)
        picked = jnp.dot(both, jnp.concatenate([hot_z, hot_z], axis=0), preferred_element_type=F32)
        mask = iota((SIDE * SIDE, CHUNK), 0) == idx_ref[1:2, span]
        picked = picked.reshape(NORB, SIDE * SIDE, CHUNK)
        sampled = jnp.sum(jnp.where(mask[None], picked, 0.0), axis=1)
        weights = wts_ref[:, span]
        parts = [weights[k : k + 1] * sampled for k in range(POS_Y * NPROJ)]
        upper_c, lower_c = split_two(jnp.concatenate(parts, axis=0))
        hot_seg = one_hot(idx_ref[2:3, span], SEGS + 8, BF16)
        total = total + lax.dot_general(hot_seg, upper_c, LAST, preferred_element_type=F32)
        total = total + lax.dot_general(hot_seg, lower_c, LAST, preferred_element_type=F32)
    return total[:SEGS]


def scatter_returned(coefs, idx_ref, wts_ref, nonlocal_ref):
    wide = jnp.concatenate([coefs, jnp.zeros((128 - SEGS, 128), F32)], axis=0)
    upper, lower = split_two(wide.T)
    both = jnp.concatenate([upper, lower], axis=1)
    points = idx_ref.shape[1]
    for first in range(0, points, CHUNK):
        span = slice(first, first + CHUNK)
        hot_seg = one_hot(idx_ref[2:3, span], 128, BF16)
        spread = jnp.dot(both, jnp.concatenate([hot_seg, hot_seg], axis=0), preferred_element_type=F32)
        weights = wts_ref[:, span]
        returned = weights[0:1] * spread[0:NORB]
        for k in range(1, POS_Y * NPROJ):
            returned = returned + weights[k : k + 1] * spread[k * NORB : (k + 1) * NORB]
        upper_r = returned.astype(BF16).astype(F32)
        lower_r = returned - upper_r
        mask = iota((SIDE * SIDE, CHUNK), 0) == idx_ref[1:2, span]
        tall = [
            jnp.where(mask, value[o : o + 1], 0.0).astype(BF16)
            for value in (upper_r, lower_r)
            for o in range(NORB)
        ]
        hot_z = one_hot(idx_ref[0:1, span], DEPTH, BF16)
        placed = lax.dot_general(
            jnp.concatenate(tall, axis=0), hot_z, LAST, preferred_element_type=F32
        )
        placed = placed[:ROWS] + placed[ROWS:]
        if first == 0:
            nonlocal_ref[...] = placed
        else:
            nonlocal_ref[...] += placed


def write_sends(coord_ref, cells_ref, xa_ref, xb_ref, za_ref, zb_ref):
    bx, bz = coord_ref[3], coord_ref[5]
    xa_ref[...] = cells_ref[:, pl.ds(2 - 2 * bx, HALO)]
    xb_ref[...] = cells_ref[:, pl.ds(2 * bx, HALO)]
    turned = cells_ref[...].reshape(ROWS, DEPTH).T
    near, far = turned[0:8], turned[DEPTH - 8 : DEPTH]
    to_a = jnp.where(bz == 1, near, far)
    to_b = jnp.where(bz == 1, far, near)
    for k in range(ROWS // 128):
        za_ref[k] = to_a[:, k * 128 : (k + 1) * 128]
        zb_ref[k] = to_b[:, k * 128 : (k + 1) * 128]


def offset_of(place, own, count):
    remain = (place - own) & (count - 1)
    return jnp.where(remain == 0, 1, jnp.where(remain == 1, 2, 0))


def first_kernel(
    sizes, coord_ref, cells_ref, proj_ref, cell_ref, owner_ref, slot_ref,
    part_ref, xa_ref, xb_ref, za_ref, zb_ref, idx_ref, wts_ref,
):
    size_x, size_y, size_z = sizes
    points = proj_ref.shape[1]
    shift_z = size_z.bit_length() - 1
    shift_x = shift_z + size_y.bit_length() - 1
    cell, owner = cell_ref[...], owner_ref[...]
    off_x = offset_of(owner >> shift_x, coord_ref[0], size_x)
    place_y = (owner >> shift_z) & (size_y - 1)
    off_z = offset_of(owner & (size_z - 1), coord_ref[2], size_z)
    idx_ref[0:1, :] = cell & (DEPTH - 1)
    idx_ref[1:2, :] = cell >> 7
    idx_ref[2:3, :] = (off_x * 3 + off_z) * 8 + slot_ref[...]
    idx_ref[3:8, :] = jnp.zeros((5, points), jnp.int32)
    live = iota((1, points), 1) < coord_ref[6]
    for position in range(POS_Y):
        here = jnp.logical_and(live, place_y == position)
        wts_ref[position * NPROJ : (position + 1) * NPROJ, :] = jnp.where(here, proj_ref[...], 0.0)
    part_ref[...] = sample_partials(cells_ref[...].reshape(ROWS, DEPTH), idx_ref, wts_ref)
    write_sends(coord_ref, cells_ref, xa_ref, xb_ref, za_ref, zb_ref)


def band(shape, distance):
    result = jnp.zeros(shape, F32)
    for k in range(1, HALO + 1):
        result = jnp.where(distance == k, stencil_terms[k], result)
    return result


def step_kernel(
    scales, last, coord_ref, cells_ref, *refs
):
    gain, middle, back = scales
    refs = list(refs)
    before_ref = refs.pop(0) if back else None
    (pot_ref, idx_ref, wts_ref, energy_ref, own_ref, px_ref, pz_ref,
     xa_in, xb_in, ya_in, yb_in, za_in, zb_in) = refs[:13]
    outs = refs[13:]
    if last:
        next_ref, nonlocal_ref, z_ref, xext, yext = outs
    else:
        (next_ref, part_ref, xa_ref, xb_ref, za_ref, zb_ref,
         nonlocal_ref, z_ref, xext, yext) = outs
    bx, by, bz = coord_ref[3], coord_ref[4], coord_ref[5]

    odd_x, odd_z = bx == 1, bz == 1
    own0, own1, other = own_ref[0], own_ref[1], px_ref[...]
    rows_x = (
        jnp.where(odd_x, other, own0),
        jnp.where(odd_x, own0, own1),
        jnp.where(odd_x, own1, other),
    )
    planes = []
    for k in range(3):
        low, high, beyond = rows_x[k][0], rows_x[k][1], pz_ref[k]
        planes += [
            jnp.where(odd_z, beyond, low),
            jnp.where(odd_z, low, high),
            jnp.where(odd_z, high, beyond),
        ]
    coefs = jnp.concatenate(planes, axis=0) * energy_ref[...]
    scatter_returned(coefs, idx_ref, wts_ref, nonlocal_ref)

    rows = cells_ref[...].reshape(ROWS, DEPTH)
    along = iota((DEPTH, DEPTH), 1) - iota((DEPTH, DEPTH), 0)
    z_part = jnp.dot(
        rows, band((DEPTH, DEPTH), jnp.abs(along)),
        precision=lax.Precision.HIGHEST, preferred_element_type=F32,
    )
    chunks = ROWS // 128
    from_a = jnp.concatenate([za_in[k] for k in range(chunks)], axis=1)
    from_b = jnp.concatenate([zb_in[k] for k in range(chunks)], axis=1)
    faces = jnp.concatenate(
        [jnp.where(odd_z, from_a, from_b), jnp.where(odd_z, from_b, from_a)], axis=0
    )
    face_row, face_col = iota((16, DEPTH), 0), iota((16, DEPTH), 1)
    distance = jnp.where(face_row < 8, face_col + 8 - face_row, DEPTH + face_row - 8 - face_col)
    z_ref[...] = z_part + jnp.dot(
        faces.T, band((16, DEPTH), distance),
        precision=lax.Precision.HIGHEST, preferred_element_type=F32,
    )

    xext[:, HALO : HALO + SIDE] = cells_ref[...]
    xext[:, pl.ds((1 - bx) * (HALO + SIDE), HALO)] = xa_in[...]
    xext[:, pl.ds(bx * (HALO + SIDE), HALO)] = xb_in[...]
    yext[1] = cells_ref[...]
    yext[2 - 2 * by] = ya_in[...]
    yext[2 * by] = yb_in[...]

    pot = pot_ref[...] - (middle + 1.5 * stencil_terms[0])
    row = iota((SIDE, SIDE, DEPTH), 1)
    for o in range(NORB):
        here = xext[o, HALO : HALO + SIDE]
        left, right = yext[0, o], yext[2, o]
        laplace = z_ref[o * 64 : (o + 1) * 64, :].reshape(SIDE, SIDE, DEPTH)
        for k in range(1, HALO + 1):
            pair = xext[o, HALO + k : HALO + k + SIDE] + xext[o, HALO - k : HALO - k + SIDE]
            up = pltpu.roll(jnp.where(row < k, right, here), SIDE - k, 1)
            down = pltpu.roll(jnp.where(row >= SIDE - k, left, here), k, 1)
            laplace = laplace + stencil_terms[k] * (pair + (up + down))
        nonlocal_part = nonlocal_ref[o * 64 : (o + 1) * 64, :].reshape(SIDE, SIDE, DEPTH)
        result = gain * (pot * here - 0.5 * laplace + nonlocal_part)
        if back:
            result = result - back * before_ref[o]
        next_ref[o] = result
    if not last:
        part_ref[...] = sample_partials(next_ref[...].reshape(ROWS, DEPTH), idx_ref, wts_ref)
        write_sends(coord_ref, next_ref, xa_ref, xb_ref, za_ref, zb_ref)


def energy_kernel(sizes, coord_ref, energy_ref, table_ref):
    size_x, size_y, size_z = sizes
    atoms = energy_ref.shape[1]
    values = jnp.concatenate(
        [jnp.broadcast_to(energy_ref[j : j + 1, :], (NORB, atoms)) for j in range(NPROJ)], axis=0
    )
    upper = values.astype(BF16)
    rest = values - upper.astype(F32)
    middle = rest.astype(BF16)
    lower = (rest - middle.astype(F32)).astype(BF16)
    row = iota((SEGS + 8, 1), 0)
    plane, slot = row >> 3, row & 7
    off_x = jnp.where(plane >= 6, 1, jnp.where(plane >= 3, 0, -1))
    off_z = plane - 3 * (off_x + 1) - 1
    place_x = (coord_ref[0] + off_x) & (size_x - 1)
    place_z = (coord_ref[2] + off_z) & (size_z - 1)
    used = jnp.logical_and(slot < ATOM_DEV, row < SEGS)
    columns = []
    for position in range(POS_Y):
        atom = ((place_x * size_y + position) * size_z + place_z) * ATOM_DEV + slot
        atom = jnp.where(used, atom, -1)
        hot = jnp.where(iota((SEGS + 8, atoms), 1) == atom, 1.0, 0.0).astype(BF16)
        column = lax.dot_general(hot, lower, LAST, preferred_element_type=F32)
        column = column + lax.dot_general(hot, middle, LAST, preferred_element_type=F32)
        columns.append(column + lax.dot_general(hot, upper, LAST, preferred_element_type=F32))
    table_ref[...] = jnp.concatenate(columns, axis=1)[:SEGS]


def in_vmem(count):
    return [pl.BlockSpec(memory_space=pltpu.VMEM)] * count


def call(kernel, shapes, scratch, cost, *operands):
    flops, traffic = cost
    return pl.pallas_call(
        kernel,
        out_shape=[jax.ShapeDtypeStruct(s, k) for s, k in shapes],
        in_specs=[pl.BlockSpec(memory_space=pltpu.SMEM)] + in_vmem(len(operands) - 1),
        out_specs=in_vmem(len(shapes)),
        scratch_shapes=scratch,
        compiler_params=pltpu.CompilerParams(vmem_limit_bytes=VMEM_LIMIT),
        cost_estimate=pl.CostEstimate(flops=flops, bytes_accessed=traffic, transcendentals=0),
    )(*operands)


def swap_inside(value, axis):
    count = lax.axis_size(axis)
    return lax.ppermute(value, axis, [(i, i ^ 1) for i in range(count)])


def swap_across(value, axis):
    count = lax.axis_size(axis)
    pairs = [(i, (i + 1 if i % 2 else i - 1) % count) for i in range(count)]
    return lax.ppermute(value, axis, pairs)


def body(
    orbitals, potential, proj_values, point_cell, point_owner, point_slot, point_count, atom_energy
):
    sizes = tuple(lax.axis_size(axis) for axis in ("gx", "gy", "gz"))
    places = [lax.axis_index(axis) for axis in ("gx", "gy", "gz")]
    points = proj_values.shape[1]
    coord = jnp.stack(
        [p.astype(jnp.int32) for p in places]
        + [(p % 2).astype(jnp.int32) for p in places]
        + [point_count[0], jnp.int32(0)]
    )
    odd_x, odd_z = places[0] % 2 == 1, places[2] % 2 == 1

    cells_shape = orbitals.shape
    x_shape = (NORB, HALO, SIDE, DEPTH)
    z_shape = (ROWS // 128, 8, 128)
    send_shapes = [
        ((SEGS, 128), F32), (x_shape, F32), (x_shape, F32), (z_shape, F32), (z_shape, F32)
    ]

    parts, xa, xb, za, zb, idx, wts = call(
        lambda *refs: first_kernel(sizes, *refs),
        send_shapes + [((8, points), jnp.int32), ((POS_Y * NPROJ, points), F32)],
        [], (600_000_000, 2_000_000),
        coord, orbitals, proj_values,
        point_cell.reshape(1, points), point_owner.reshape(1, points), point_slot.reshape(1, points),
    )
    (energy,) = call(
        lambda *refs: energy_kernel(sizes, *refs), [((SEGS, 128), F32)], [],
        (600_000_000, 200_000), coord, atom_energy,
    )

    def exchange(parts, cells, xa, xb, za, zb):
        table = parts.reshape(3, 3, 8, 128)
        come = swap_inside(jnp.where(odd_x, table[0], table[2]), "gx")
        middle = table[1] + come
        pair = jnp.where(odd_x, jnp.stack([middle, table[2]]), jnp.stack([table[0], middle]))
        pair = pair + swap_across(pair, "gx")
        xb = swap_across(xb, "gx")

        come = swap_inside(
            jnp.concatenate([jnp.where(odd_z, pair[:, 0], pair[:, 2]), za], axis=0), "gz"
        )
        za = come[2:]
        middle = pair[:, 1] + come[:2]
        own = jnp.where(
            odd_z,
            jnp.stack([middle, pair[:, 2]], axis=1),
            jnp.stack([pair[:, 0], middle], axis=1),
        )
        come = swap_across(jnp.concatenate([own.reshape(4, 8, 128), zb], axis=0), "gz")
        zb = come[4:]
        own = own + come[:4].reshape(2, 2, 8, 128)

        own = own + swap_inside(own, "gy")
        own = own + swap_across(own, "gy")
        ya, yb = swap_inside(cells, "gy"), swap_across(cells, "gy")
        xa = swap_inside(xa, "gx")

        beyond_x = swap_inside(jnp.where(odd_x, own[0], own[1]), "gx")
        rows = jnp.where(
            odd_z,
            jnp.where(odd_x, jnp.stack([beyond_x[0], own[0, 0], own[1, 0]]),
                      jnp.stack([own[0, 0], own[1, 0], beyond_x[0]])),
            jnp.where(odd_x, jnp.stack([beyond_x[1], own[0, 1], own[1, 1]]),
                      jnp.stack([own[0, 1], own[1, 1], beyond_x[1]])),
        )
        beyond_z = swap_inside(rows, "gz")
        return own, beyond_x, beyond_z, xa, xb, ya, yb, za, zb

    half_width = (highest - cutoff) / 2.0
    middle = (highest + cutoff) / 2.0
    sigma_first = half_width / (lowest - middle)
    sigma_now = sigma_first
    previous, current = None, orbitals
    scratch = [
        pltpu.VMEM((ROWS, DEPTH), F32),
        pltpu.VMEM((ROWS, DEPTH), F32),
        pltpu.VMEM((NORB, SIDE + 2 * HALO, SIDE, DEPTH), F32),
        pltpu.VMEM((3, NORB, SIDE, SIDE, DEPTH), F32),
    ]
    for degree_index in range(DEGREE):
        if degree_index == 0:
            scales = (sigma_first / half_width, middle, 0.0)
        else:
            sigma_next = 1.0 / (2.0 / sigma_first - sigma_now)
            scales = (2.0 * sigma_next / half_width, middle, sigma_now * sigma_next)
            sigma_now = sigma_next
        last = degree_index == DEGREE - 1
        came = exchange(parts, current, xa, xb, za, zb)
        before = [] if previous is None else [previous]
        results = call(
            lambda *refs, scales=scales, last=last: step_kernel(scales, last, *refs),
            [(cells_shape, F32)] + ([] if last else send_shapes),
            scratch, (1_500_000_000, 4_000_000),
            coord, current, *before, potential, idx, wts, energy, *came,
        )
        previous, current = current, results[0]
        if not last:
            parts, xa, xb, za, zb = results[1:]
    return current


def solution(mesh):
    return jax.shard_map(
        body,
        mesh=mesh,
        in_specs=(
            P(None, "gx", "gy", "gz"),
            P("gx", "gy", "gz"),
            P(None, ("gx", "gy", "gz")),
            P(("gx", "gy", "gz")),
            P(("gx", "gy", "gz")),
            P(("gx", "gy", "gz")),
            P(("gx", "gy", "gz")),
            P(),
        ),
        out_specs=P(None, "gx", "gy", "gz"),
        check_vma=False,
    )
```

time: 666 us -> 283 us (0.42)
  the two profiles are of different devices: /device:TPU:6 before, /device:TPU:1 now
where the time goes in v1:
time: 283 us; the launch traced here: 280 us
  starting transfers between devices  180 us (64%)
  waiting for transfers between devices  52.4 us (19%)
  Pallas kernels  27.8 us (10%)
  local copies, waits for them, and re-layouts  13.4 us (5%)
  other arithmetic  4.64 us (2%)
    ppermute x15, starting transfers between devices, swap_across(): return lax.ppermute(value, axis, pairs)  96.3 us
    ppermute x21, starting transfers between devices, swap_inside(): return lax.ppermute(value, axis, [(i, i ^ 1) for i in range(count)])  84.2 us
    ppermute x15, waiting for transfers between devices, swap_across(): return lax.ppermute(value, axis, pairs)  30.8 us
    pallas_call x5, Pallas kernels, call(): pl.pallas_call(kernel, out_shape=[jax.ShapeDtypeStruct(s, k) for s, k in...  27.8 us
    ppermute x21, waiting for transfers between devices, swap_inside(): return lax.ppermute(value, axis, [(i, i ^ 1) for i in range(count)])  21.6 us
    unnamed x64, local copies, waits for them, and re-layouts  8.58 us
  transfers between devices with their start and end apart: 36, of which 19 were waited for; matrix products, arithmetic and copies ran while one was open for 1% of the time, Pallas kernels for 2%

profile of v1, /device:TPU:1, one launch (start us, length us, event | category | flops | bytes accessed | tf_op | source)
XLA Modules:
  0.0 280.1 jit_solution(1995970238197615266)
XLA Ops:
  5.4 4.0 %collective-permute-start = (f32[3,8,128]{2,1,0:T(8,128)S(1)}, f32[3,8,128]{2,1,0:T(8,128)S(1)}, u32[]{:S(2)}, u32[]{:S(2)}) collective-permute-start(f32[3,8,128]{2,1,0:T(8,128)S(1)} %get-tuple-element.53), channel_id=1, source_target_pairs={{0,64},{64,0},{128,192},{192,128},{256,320},{320,256},{384,448},{4... | collective-permute-start | bytes 36872 | tf_op jit(solution)/shard_map/ppermute | solution.py:285
  11.2 22.1 %collective-permute-start.1 = (f32[2,3,8,128]{3,2,0,1:T(8,128)S(1)}, f32[2,3,8,128]{3,2,0,1:T(8,128)S(1)}, u32[]{:S(2)}, u32[]{:S(2)}) collective-permute-start(f32[2,3,8,128]{3,2,0,1:T(8,128)S(1)} %maximum_select_fusion), channel_id=1, source_target_pairs={{0,960},{64,128},{128,64},{192,256},{256,192},{320,384},{384,320},... | collective-permute-start | bytes 73736 | tf_op jit(solution)/shard_map/ppermute | solution.py:291
  35.3 9.7 %collective-permute-start.2 = (f32[6,8,128]{2,1,0:T(8,128)S(1)}, f32[6,8,128]{2,1,0:T(8,128)S(1)}, u32[]{:S(2)}, u32[]{:S(2)}) collective-permute-start(f32[6,8,128]{2,1,0:T(8,128)S(1)} %pad_maximum_fusion.3), channel_id=1, source_target_pairs={{0,1},{1,0},{2,3},{3,2},{4,5},{5,4},{6,7},{7,6},{8,9},{9,8},{10,11... | collective-permute-start | bytes 73736 | tf_op jit(solution)/shard_map/ppermute | solution.py:285
  59.1 4.6 %collective-permute-start.11 = (f32[8,8,8,128]{3,2,1,0:T(8,128)S(1)}, f32[8,8,8,128]{3,2,1,0:T(8,128)S(1)}, u32[]{:S(2)}, u32[]{:S(2)}) collective-permute-start(f32[8,8,8,128]{3,2,1,0:T(8,128)S(1)} %copy-done.11), channel_id=1, source_target_pairs={{0,48},{16,32},{32,16},{48,0},{1,49},{17,33},{33,17},{49,1},{2,50}... | collective-permute-start | bytes 786440 | tf_op jit(solution)/shard_map/ppermute | solution.py:291
  67.5 9.4 %collective-permute-start.9 = (f32[8,6,8,128]{3,2,1,0:T(8,128)S(1)}, f32[8,6,8,128]{3,2,1,0:T(8,128)S(1)}, u32[]{:S(2)}, u32[]{:S(2)}) collective-permute-start(f32[8,6,8,128]{3,2,1,0:T(8,128)S(1)} %copy-done.22), channel_id=1, source_target_pairs={{0,960},{64,128},{128,64},{192,256},{256,192},{320,384},{384,320},... | collective-permute-start | bytes 589832 | tf_op jit(solution)/shard_map/ppermute | solution.py:291
  82.0 12.0 %collective-permute-start.7 = (f32[3,8,128]{2,1,0:T(8,128)S(1)}, f32[3,8,128]{2,1,0:T(8,128)S(1)}, u32[]{:S(2)}, u32[]{:S(2)}) collective-permute-start(f32[3,8,128]{2,1,0:T(8,128)S(1)} %fusion), channel_id=1, source_target_pairs={{0,1},{1,0},{2,3},{3,2},{4,5},{5,4},{6,7},{7,6},{8,9},{9,8},{10,11... | collective-permute-start | bytes 36872 | tf_op jit(solution)/shard_map/ppermute | solution.py:285
  93.9 4.3 %shard_map.83.refs_5_.refs_6_ = f32[72,128]{1,0:T(8,128)} custom-call(s32[8]{0:T(128)} %stack.123.refs_0_, f32[4,5120]{1,0:T(4,128)} %refs_1_.4), custom_call_target="tpu_custom_call" | custom-call | flops 600000000 | bytes 200000 | tf_op jit(solution)/shard_map/pallas_call | solution.py:272
  99.7 7.5 %shard_map.84 = (f32[8,8,8,128]{3,2,1,0:T(8,128)}, f32[72,128]{1,0:T(8,128)}, f32[8,6,8,128]{3,2,1,0:T(8,128)}, f32[8,6,8,128]{3,2,1,0:T(8,128)}, f32[4,8,128]{2,1,0:T(8,128)}, /*index=5*/f32[4,8,128]{2,1,0:T(8,128)}) custom-call(s32[8]{0:T(128)} %stack.123.refs_0_, f32[8,8,8,128]{3,2,1,0:T(8,128)} %refs_2_.5, f32[8,8,128]{2,1,0:T(8,128)} %refs_3_.3, ...), custom_call_target="tpu_custom_call" | custom-call | flops 1500000000 | bytes 4000000 | tf_op jit(solution)/shard_map/pallas_call | solution.py:272
  113.2 8.5 %collective-permute-start.13 = (f32[2,3,8,128]{3,2,1,0:T(8,128)S(1)}, f32[2,3,8,128]{3,2,1,0:T(8,128)S(1)}, u32[]{:S(2)}, u32[]{:S(2)}) collective-permute-start(f32[2,3,8,128]{3,2,1,0:T(8,128)S(1)} %maximum_select_fusion.1), channel_id=1, source_target_pairs={{0,960},{64,128},{128,64},{192,256},{256,192},{320,384},{384,320},... | collective-permute-start | bytes 73736 | tf_op jit(solution)/shard_map/ppermute | solution.py:291
  121.7 6.9 %collective-permute-done.13 = f32[2,3,8,128]{3,2,1,0:T(8,128)S(1)} collective-permute-done((f32[2,3,8,128]{3,2,1,0:T(8,128)S(1)}, f32[2,3,8,128]{3,2,1,0:T(8,128)S(1)}, u32[]{:S(2)}, u32[]{:S(2)}) %collective-permute-start.13) | collective-permute-done | bytes 24608 | tf_op jit(solution)/shard_map/ppermute | solution.py:291
  129.3 4.5 %collective-permute-start.14 = (f32[6,8,128]{2,1,0:T(8,128)S(1)}, f32[6,8,128]{2,1,0:T(8,128)S(1)}, u32[]{:S(2)}, u32[]{:S(2)}) collective-permute-start(f32[6,8,128]{2,1,0:T(8,128)S(1)} %pad_maximum_fusion.4), channel_id=1, source_target_pairs={{0,1},{1,0},{2,3},{3,2},{4,5},{5,4},{6,7},{7,6},{8,9},{9,8},{10,11... | collective-permute-start | bytes 73736 | tf_op jit(solution)/shard_map/ppermute | solution.py:285
  145.9 4.1 %collective-permute-start.17 = (f32[2,2,8,128]{3,2,1,0:T(8,128)S(1)}, f32[2,2,8,128]{3,2,1,0:T(8,128)S(1)}, u32[]{:S(2)}, u32[]{:S(2)}) collective-permute-start(f32[2,2,8,128]{3,2,1,0:T(8,128)S(1)} %fusion.28), channel_id=1, source_target_pairs={{0,48},{16,32},{32,16},{48,0},{1,49},{17,33},{33,17},{49,1},{2,50}... | collective-permute-start | bytes 49160 | tf_op jit(solution)/shard_map/ppermute | solution.py:291
  156.7 10.8 %collective-permute-start.21 = (f32[8,6,8,128]{3,2,1,0:T(8,128)S(1)}, f32[8,6,8,128]{3,2,1,0:T(8,128)S(1)}, u32[]{:S(2)}, u32[]{:S(2)}) collective-permute-start(f32[8,6,8,128]{3,2,1,0:T(8,128)S(1)} %copy-done.21), channel_id=1, source_target_pairs={{0,960},{64,128},{128,64},{192,256},{256,192},{320,384},{384,320},... | collective-permute-start | bytes 589832 | tf_op jit(solution)/shard_map/ppermute | solution.py:291
  172.6 10.7 %collective-permute-start.19 = (f32[3,8,128]{2,1,0:T(8,128)S(1)}, f32[3,8,128]{2,1,0:T(8,128)S(1)}, u32[]{:S(2)}, u32[]{:S(2)}) collective-permute-start(f32[3,8,128]{2,1,0:T(8,128)S(1)} %fusion.1), channel_id=1, source_target_pairs={{0,1},{1,0},{2,3},{3,2},{4,5},{5,4},{6,7},{7,6},{8,9},{9,8},{10,11... | collective-permute-start | bytes 36872 | tf_op jit(solution)/shard_map/ppermute | solution.py:285
  184.8 7.6 %shard_map.85 = (f32[8,8,8,128]{3,2,1,0:T(8,128)}, f32[72,128]{1,0:T(8,128)}, f32[8,6,8,128]{3,2,1,0:T(8,128)}, f32[8,6,8,128]{3,2,1,0:T(8,128)}, f32[4,8,128]{2,1,0:T(8,128)}, /*index=5*/f32[4,8,128]{2,1,0:T(8,128)}) custom-call(s32[8]{0:T(128)} %stack.123.refs_0_, f32[8,8,8,128]{3,2,1,0:T(8,128)} %get-tuple-element.31.refs_1_.refs_2_, ...), custom_call_target="tpu_custom_call" | custom-call | flops 1500000000 | bytes 4000000 | tf_op jit(solution)/shard_map/pallas_call | solution.py:272
  198.3 7.4 %collective-permute-start.25 = (f32[2,3,8,128]{3,2,1,0:T(8,128)S(1)}, f32[2,3,8,128]{3,2,1,0:T(8,128)S(1)}, u32[]{:S(2)}, u32[]{:S(2)}) collective-permute-start(f32[2,3,8,128]{3,2,1,0:T(8,128)S(1)} %maximum_select_fusion.2), channel_id=1, source_target_pairs={{0,960},{64,128},{128,64},{192,256},{256,192},{320,384},{384,320},... | collective-permute-start | bytes 73736 | tf_op jit(solution)/shard_map/ppermute | solution.py:291
  205.8 7.9 %collective-permute-done.25 = f32[2,3,8,128]{3,2,1,0:T(8,128)S(1)} collective-permute-done((f32[2,3,8,128]{3,2,1,0:T(8,128)S(1)}, f32[2,3,8,128]{3,2,1,0:T(8,128)S(1)}, u32[]{:S(2)}, u32[]{:S(2)}) %collective-permute-start.25) | collective-permute-done | bytes 24608 | tf_op jit(solution)/shard_map/ppermute | solution.py:291
  214.4 6.4 %collective-permute-start.26 = (f32[6,8,128]{2,1,0:T(8,128)S(1)}, f32[6,8,128]{2,1,0:T(8,128)S(1)}, u32[]{:S(2)}, u32[]{:S(2)}) collective-permute-start(f32[6,8,128]{2,1,0:T(8,128)S(1)} %pad_maximum_fusion.5), channel_id=1, source_target_pairs={{0,1},{1,0},{2,3},{3,2},{4,5},{5,4},{6,7},{7,6},{8,9},{9,8},{10,11... | collective-permute-start | bytes 73736 | tf_op jit(solution)/shard_map/ppermute | solution.py:285
  228.2 4.4 %collective-permute-start.28 = (f32[2,2,8,128]{3,2,0,1:T(8,128)S(1)}, f32[2,2,8,128]{3,2,0,1:T(8,128)S(1)}, u32[]{:S(2)}, u32[]{:S(2)}) collective-permute-start(f32[2,2,8,128]{3,2,0,1:T(8,128)S(1)} %copy_add_fusion), channel_id=1, source_target_pairs={{0,16},{16,0},{32,48},{48,32},{1,17},{17,1},{33,49},{49,33},{2,18}... | collective-permute-start | bytes 49160 | tf_op jit(solution)/shard_map/ppermute | solution.py:285
  234.0 4.8 %collective-permute-start.29 = (f32[2,2,8,128]{3,2,0,1:T(8,128)S(1)}, f32[2,2,8,128]{3,2,0,1:T(8,128)S(1)}, u32[]{:S(2)}, u32[]{:S(2)}) collective-permute-start(f32[2,2,8,128]{3,2,0,1:T(8,128)S(1)} %add.85), channel_id=1, source_target_pairs={{0,48},{16,32},{32,16},{48,0},{1,49},{17,33},{33,17},{49,1},{2,50}... | collective-permute-start | bytes 49160 | tf_op jit(solution)/shard_map/ppermute | solution.py:291
  244.6 12.1 %collective-permute-start.33 = (f32[8,6,8,128]{3,2,1,0:T(8,128)S(1)}, f32[8,6,8,128]{3,2,1,0:T(8,128)S(1)}, u32[]{:S(2)}, u32[]{:S(2)}) collective-permute-start(f32[8,6,8,128]{3,2,1,0:T(8,128)S(1)} %copy-done.20), channel_id=1, source_target_pairs={{0,960},{64,128},{128,64},{192,256},{256,192},{320,384},{384,320},... | collective-permute-start | bytes 589832 | tf_op jit(solution)/shard_map/ppermute | solution.py:291
  261.8 5.8 %collective-permute-start.31 = (f32[3,8,128]{2,1,0:T(8,128)S(1)}, f32[3,8,128]{2,1,0:T(8,128)S(1)}, u32[]{:S(2)}, u32[]{:S(2)}) collective-permute-start(f32[3,8,128]{2,1,0:T(8,128)S(1)} %fusion.2), channel_id=1, source_target_pairs={{0,1},{1,0},{2,3},{3,2},{4,5},{5,4},{6,7},{7,6},{8,9},{9,8},{10,11... | collective-permute-start | bytes 36872 | tf_op jit(solution)/shard_map/ppermute | solution.py:285
  268.8 5.3 %collective-permute-done.33.refs_11_ = f32[8,6,8,128]{3,2,1,0:T(8,128)S(1)} collective-permute-done((f32[8,6,8,128]{3,2,1,0:T(8,128)S(1)}, f32[8,6,8,128]{3,2,1,0:T(8,128)S(1)}, u32[]{:S(2)}, u32[]{:S(2)}) %collective-permute-start.33) | collective-permute-done | bytes 196640 | tf_op jit(solution)/shard_map/ppermute | solution.py:291
  275.0 5.1 %shard_map.86 = f32[8,8,8,128]{3,2,1,0:T(8,128)} custom-call(s32[8]{0:T(128)} %stack.123.refs_0_, f32[8,8,8,128]{3,2,1,0:T(8,128)} %get-tuple-element.37.refs_1_, f32[8,8,8,128]{3,2,1,0:T(8,128)} %get-tuple-element.31.refs_1_.refs_2_, f32[8,8,128]{2,1,0:T(8,128)} %refs_3_.3, s32[8,2048]{1,0:T(8,128)} %get-tuple-element.24.refs_3_.refs_4_, ...), custom_call_target="tpu_custom_call" | custom-call | flops 1500000000 | bytes 4000000 | tf_op jit(solution)/shard_map/pallas_call | solution.py:272
  (176 shorter events, 92.9 us)
Async XLA Ops:
  11.2 23.4 %collective-permute-start.1 = (f32[2,3,8,128]{3,2,0,1:T(8,128)S(1)}, f32[2,3,8,128]{3,2,0,1:T(8,128)S(1)}, u32[]{:S(2)}, u32[]{:S(2)}) collective-permute-start(f32[2,3,8,128]{3,2,0,1:T(8,128)S(1)} %maximum_select_fusion), channel_id=1, source_target_pairs={{0,960},{64,128},{128,64},{192,256},{256,192},{320,384},{384,320},... | collective-permute-start | bytes 73736 | tf_op jit(solution)/shard_map/ppermute | solution.py:291
  35.3 10.5 %collective-permute-start.2 = (f32[6,8,128]{2,1,0:T(8,128)S(1)}, f32[6,8,128]{2,1,0:T(8,128)S(1)}, u32[]{:S(2)}, u32[]{:S(2)}) collective-permute-start(f32[6,8,128]{2,1,0:T(8,128)S(1)} %pad_maximum_fusion.3), channel_id=1, source_target_pairs={{0,1},{1,0},{2,3},{3,2},{4,5},{5,4},{6,7},{7,6},{8,9},{9,8},{10,11... | collective-permute-start | bytes 73736 | tf_op jit(solution)/shard_map/ppermute | solution.py:285
  57.2 19.7 %collective-permute-start.5 = (f32[2,2,8,128]{3,2,1,0:T(8,128)S(1)}, f32[2,2,8,128]{3,2,1,0:T(8,128)S(1)}, u32[]{:S(2)}, u32[]{:S(2)}) collective-permute-start(f32[2,2,8,128]{3,2,1,0:T(8,128)S(1)} %fusion.29), channel_id=1, source_target_pairs={{0,48},{16,32},{32,16},{48,0},{1,49},{17,33},{33,17},{49,1},{2,50}... | collective-permute-start | bytes 49160 | tf_op jit(solution)/shard_map/ppermute | solution.py:291
  59.1 39.8 %collective-permute-start.11 = (f32[8,8,8,128]{3,2,1,0:T(8,128)S(1)}, f32[8,8,8,128]{3,2,1,0:T(8,128)S(1)}, u32[]{:S(2)}, u32[]{:S(2)}) collective-permute-start(f32[8,8,8,128]{3,2,1,0:T(8,128)S(1)} %copy-done.11), channel_id=1, source_target_pairs={{0,48},{16,32},{32,16},{48,0},{1,49},{17,33},{33,17},{49,1},{2,50}... | collective-permute-start | bytes 786440 | tf_op jit(solution)/shard_map/ppermute | solution.py:291
  63.7 35.2 %collective-permute-start.10 = (f32[8,8,8,128]{3,2,1,0:T(8,128)S(1)}, f32[8,8,8,128]{3,2,1,0:T(8,128)S(1)}, u32[]{:S(2)}, u32[]{:S(2)}) collective-permute-start(f32[8,8,8,128]{3,2,1,0:T(8,128)S(1)} %copy-done.11), channel_id=1, source_target_pairs={{0,16},{16,0},{32,48},{48,32},{1,17},{17,1},{33,49},{49,33},{2,18}... | collective-permute-start | bytes 786440 | tf_op jit(solution)/shard_map/ppermute | solution.py:285
  65.6 33.2 %collective-permute-start.8 = (f32[8,6,8,128]{3,2,1,0:T(8,128)}, f32[8,6,8,128]{3,2,1,0:T(8,128)S(1)}, u32[]{:S(2)}, u32[]{:S(2)}) collective-permute-start(f32[8,6,8,128]{3,2,1,0:T(8,128)} %get-tuple-element.29), channel_id=1, source_target_pairs={{0,64},{64,0},{128,192},{192,128},{256,320},{320,256},{384,448},{4... | collective-permute-start | bytes 589832 | tf_op jit(solution)/shard_map/ppermute | solution.py:285
  67.5 31.3 %collective-permute-start.9 = (f32[8,6,8,128]{3,2,1,0:T(8,128)S(1)}, f32[8,6,8,128]{3,2,1,0:T(8,128)S(1)}, u32[]{:S(2)}, u32[]{:S(2)}) collective-permute-start(f32[8,6,8,128]{3,2,1,0:T(8,128)S(1)} %copy-done.22), channel_id=1, source_target_pairs={{0,960},{64,128},{128,64},{192,256},{256,192},{320,384},{384,320},... | collective-permute-start | bytes 589832 | tf_op jit(solution)/shard_map/ppermute | solution.py:291
  82.0 16.9 %collective-permute-start.7 = (f32[3,8,128]{2,1,0:T(8,128)S(1)}, f32[3,8,128]{2,1,0:T(8,128)S(1)}, u32[]{:S(2)}, u32[]{:S(2)}) collective-permute-start(f32[3,8,128]{2,1,0:T(8,128)S(1)} %fusion), channel_id=1, source_target_pairs={{0,1},{1,0},{2,3},{3,2},{4,5},{5,4},{6,7},{7,6},{8,9},{9,8},{10,11... | collective-permute-start | bytes 36872 | tf_op jit(solution)/shard_map/ppermute | solution.py:285
  113.2 15.4 %collective-permute-start.13 = (f32[2,3,8,128]{3,2,1,0:T(8,128)S(1)}, f32[2,3,8,128]{3,2,1,0:T(8,128)S(1)}, u32[]{:S(2)}, u32[]{:S(2)}) collective-permute-start(f32[2,3,8,128]{3,2,1,0:T(8,128)S(1)} %maximum_select_fusion.1), channel_id=1, source_target_pairs={{0,960},{64,128},{128,64},{192,256},{256,192},{320,384},{384,320},... | collective-permute-start | bytes 73736 | tf_op jit(solution)/shard_map/ppermute | solution.py:291
  145.9 21.6 %collective-permute-start.17 = (f32[2,2,8,128]{3,2,1,0:T(8,128)S(1)}, f32[2,2,8,128]{3,2,1,0:T(8,128)S(1)}, u32[]{:S(2)}, u32[]{:S(2)}) collective-permute-start(f32[2,2,8,128]{3,2,1,0:T(8,128)S(1)} %fusion.28), channel_id=1, source_target_pairs={{0,48},{16,32},{32,16},{48,0},{1,49},{17,33},{33,17},{49,1},{2,50}... | collective-permute-start | bytes 49160 | tf_op jit(solution)/shard_map/ppermute | solution.py:291
  150.1 33.9 %collective-permute-start.23 = (f32[8,8,8,128]{3,2,1,0:T(8,128)S(1)}, f32[8,8,8,128]{3,2,1,0:T(8,128)S(1)}, u32[]{:S(2)}, u32[]{:S(2)}) collective-permute-start(f32[8,8,8,128]{3,2,1,0:T(8,128)S(1)} %copy-done.12), channel_id=1, source_target_pairs={{0,48},{16,32},{32,16},{48,0},{1,49},{17,33},{33,17},{49,1},{2,50}... | collective-permute-start | bytes 786440 | tf_op jit(solution)/shard_map/ppermute | solution.py:291
  152.4 31.5 %collective-permute-start.22 = (f32[8,8,8,128]{3,2,1,0:T(8,128)S(1)}, f32[8,8,8,128]{3,2,1,0:T(8,128)S(1)}, u32[]{:S(2)}, u32[]{:S(2)}) collective-permute-start(f32[8,8,8,128]{3,2,1,0:T(8,128)S(1)} %copy-done.12), channel_id=1, source_target_pairs={{0,16},{16,0},{32,48},{48,32},{1,17},{17,1},{33,49},{49,33},{2,18}... | collective-permute-start | bytes 786440 | tf_op jit(solution)/shard_map/ppermute | solution.py:285
  154.8 29.1 %collective-permute-start.20 = (f32[8,6,8,128]{3,2,1,0:T(8,128)}, f32[8,6,8,128]{3,2,1,0:T(8,128)S(1)}, u32[]{:S(2)}, u32[]{:S(2)}) collective-permute-start(f32[8,6,8,128]{3,2,1,0:T(8,128)} %get-tuple-element.35), channel_id=1, source_target_pairs={{0,64},{64,0},{128,192},{192,128},{256,320},{320,256},{384,448},{4... | collective-permute-start | bytes 589832 | tf_op jit(solution)/shard_map/ppermute | solution.py:285
  156.7 27.2 %collective-permute-start.21 = (f32[8,6,8,128]{3,2,1,0:T(8,128)S(1)}, f32[8,6,8,128]{3,2,1,0:T(8,128)S(1)}, u32[]{:S(2)}, u32[]{:S(2)}) collective-permute-start(f32[8,6,8,128]{3,2,1,0:T(8,128)S(1)} %copy-done.21), channel_id=1, source_target_pairs={{0,960},{64,128},{128,64},{192,256},{256,192},{320,384},{384,320},... | collective-permute-start | bytes 589832 | tf_op jit(solution)/shard_map/ppermute | solution.py:291
  172.6 11.3 %collective-permute-start.19 = (f32[3,8,128]{2,1,0:T(8,128)S(1)}, f32[3,8,128]{2,1,0:T(8,128)S(1)}, u32[]{:S(2)}, u32[]{:S(2)}) collective-permute-start(f32[3,8,128]{2,1,0:T(8,128)S(1)} %fusion.1), channel_id=1, source_target_pairs={{0,1},{1,0},{2,3},{3,2},{4,5},{5,4},{6,7},{7,6},{8,9},{9,8},{10,11... | collective-permute-start | bytes 36872 | tf_op jit(solution)/shard_map/ppermute | solution.py:285
  198.3 15.4 %collective-permute-start.25 = (f32[2,3,8,128]{3,2,1,0:T(8,128)S(1)}, f32[2,3,8,128]{3,2,1,0:T(8,128)S(1)}, u32[]{:S(2)}, u32[]{:S(2)}) collective-permute-start(f32[2,3,8,128]{3,2,1,0:T(8,128)S(1)} %maximum_select_fusion.2), channel_id=1, source_target_pairs={{0,960},{64,128},{128,64},{192,256},{256,192},{320,384},{384,320},... | collective-permute-start | bytes 73736 | tf_op jit(solution)/shard_map/ppermute | solution.py:291
  214.4 7.2 %collective-permute-start.26 = (f32[6,8,128]{2,1,0:T(8,128)S(1)}, f32[6,8,128]{2,1,0:T(8,128)S(1)}, u32[]{:S(2)}, u32[]{:S(2)}) collective-permute-start(f32[6,8,128]{2,1,0:T(8,128)S(1)} %pad_maximum_fusion.5), channel_id=1, source_target_pairs={{0,1},{1,0},{2,3},{3,2},{4,5},{5,4},{6,7},{7,6},{8,9},{9,8},{10,11... | collective-permute-start | bytes 73736 | tf_op jit(solution)/shard_map/ppermute | solution.py:285
  228.2 5.8 %collective-permute-start.28 = (f32[2,2,8,128]{3,2,0,1:T(8,128)S(1)}, f32[2,2,8,128]{3,2,0,1:T(8,128)S(1)}, u32[]{:S(2)}, u32[]{:S(2)}) collective-permute-start(f32[2,2,8,128]{3,2,0,1:T(8,128)S(1)} %copy_add_fusion), channel_id=1, source_target_pairs={{0,16},{16,0},{32,48},{48,32},{1,17},{17,1},{33,49},{49,33},{2,18}... | collective-permute-start | bytes 49160 | tf_op jit(solution)/shard_map/ppermute | solution.py:285
  234.0 22.7 %collective-permute-start.29 = (f32[2,2,8,128]{3,2,0,1:T(8,128)S(1)}, f32[2,2,8,128]{3,2,0,1:T(8,128)S(1)}, u32[]{:S(2)}, u32[]{:S(2)}) collective-permute-start(f32[2,2,8,128]{3,2,0,1:T(8,128)S(1)} %add.85), channel_id=1, source_target_pairs={{0,48},{16,32},{32,16},{48,0},{1,49},{17,33},{33,17},{49,1},{2,50}... | collective-permute-start | bytes 49160 | tf_op jit(solution)/shard_map/ppermute | solution.py:291
  238.8 35.3 %collective-permute-start.35 = (f32[8,8,8,128]{3,2,1,0:T(8,128)S(1)}, f32[8,8,8,128]{3,2,1,0:T(8,128)S(1)}, u32[]{:S(2)}, u32[]{:S(2)}) collective-permute-start(f32[8,8,8,128]{3,2,1,0:T(8,128)S(1)} %copy-done.13), channel_id=1, source_target_pairs={{0,48},{16,32},{32,16},{48,0},{1,49},{17,33},{33,17},{49,1},{2,50}... | collective-permute-start | bytes 786440 | tf_op jit(solution)/shard_map/ppermute | solution.py:291
  240.7 33.4 %collective-permute-start.34 = (f32[8,8,8,128]{3,2,1,0:T(8,128)S(1)}, f32[8,8,8,128]{3,2,1,0:T(8,128)S(1)}, u32[]{:S(2)}, u32[]{:S(2)}) collective-permute-start(f32[8,8,8,128]{3,2,1,0:T(8,128)S(1)} %copy-done.13), channel_id=1, source_target_pairs={{0,16},{16,0},{32,48},{48,32},{1,17},{17,1},{33,49},{49,33},{2,18}... | collective-permute-start | bytes 786440 | tf_op jit(solution)/shard_map/ppermute | solution.py:285
  242.7 26.1 %collective-permute-start.32 = (f32[8,6,8,128]{3,2,1,0:T(8,128)}, f32[8,6,8,128]{3,2,1,0:T(8,128)S(1)}, u32[]{:S(2)}, u32[]{:S(2)}) collective-permute-start(f32[8,6,8,128]{3,2,1,0:T(8,128)} %get-tuple-element.41), channel_id=1, source_target_pairs={{0,64},{64,0},{128,192},{192,128},{256,320},{320,256},{384,448},{4... | collective-permute-start | bytes 589832 | tf_op jit(solution)/shard_map/ppermute | solution.py:285
  244.6 29.5 %collective-permute-start.33 = (f32[8,6,8,128]{3,2,1,0:T(8,128)S(1)}, f32[8,6,8,128]{3,2,1,0:T(8,128)S(1)}, u32[]{:S(2)}, u32[]{:S(2)}) collective-permute-start(f32[8,6,8,128]{3,2,1,0:T(8,128)S(1)} %copy-done.20), channel_id=1, source_target_pairs={{0,960},{64,128},{128,64},{192,256},{256,192},{320,384},{384,320},... | collective-permute-start | bytes 589832 | tf_op jit(solution)/shard_map/ppermute | solution.py:291
  261.8 7.1 %collective-permute-start.31 = (f32[3,8,128]{2,1,0:T(8,128)S(1)}, f32[3,8,128]{2,1,0:T(8,128)S(1)}, u32[]{:S(2)}, u32[]{:S(2)}) collective-permute-start(f32[3,8,128]{2,1,0:T(8,128)S(1)} %fusion.2), channel_id=1, source_target_pairs={{0,1},{1,0},{2,3},{3,2},{4,5},{5,4},{6,7},{7,6},{8,9},{9,8},{10,11... | collective-permute-start | bytes 36872 | tf_op jit(solution)/shard_map/ppermute | solution.py:285
  (44 other events, 298.5 us)

commit v2 on v1

--- a/solution.py
+++ b/solution.py
@@ -12,12 +12,13 @@
 SIDE = 8
 DEPTH = 128
 HALO = 6
+FACE = NORB * HALO
 ROWS = NORB * SIDE * SIDE
 PLANES = 9
 SEGS = PLANES * 8
 CHUNK = 256
 POS_Y = 4
-VMEM_LIMIT = 56 * 1024 * 1024
+VMEM_LIMIT = 20 * 1024 * 1024
 
 stencil_terms = (
     -5369.0 / 1800.0,
@@ -105,10 +106,19 @@
             nonlocal_ref[...] += placed
 
 
+def write_parts(coord_ref, table, send_ref, xb_ref):
+    rows = SEGS // 3
+    odd_x = coord_ref[3] == 1
+    below, same, above = table[:rows], table[rows : 2 * rows], table[2 * rows :]
+    send_ref[...] = jnp.where(odd_x, below, above)
+    kept = [jnp.where(odd_x, same, below), jnp.where(odd_x, above, same)]
+    xb_ref[FACE:] = jnp.concatenate(kept, axis=0).reshape(6, SIDE, DEPTH)
+
+
 def write_sends(coord_ref, cells_ref, xa_ref, xb_ref, za_ref, zb_ref):
     bx, bz = coord_ref[3], coord_ref[5]
     xa_ref[...] = cells_ref[:, pl.ds(2 - 2 * bx, HALO)]
-    xb_ref[...] = cells_ref[:, pl.ds(2 * bx, HALO)]
+    xb_ref[:FACE] = cells_ref[:, pl.ds(2 * bx, HALO)].reshape(FACE, SIDE, DEPTH)
     turned = cells_ref[...].reshape(ROWS, DEPTH).T
     near, far = turned[0:8], turned[DEPTH - 8 : DEPTH]
     to_a = jnp.where(bz == 1, near, far)
@@ -125,7 +135,7 @@
 
 def first_kernel(
     sizes, coord_ref, cells_ref, proj_ref, cell_ref, owner_ref, slot_ref,
-    part_ref, xa_ref, xb_ref, za_ref, zb_ref, idx_ref, wts_ref,
+    give_ref, xa_ref, xb_ref, za_ref, zb_ref, idx_ref, wts_ref,
 ):
     size_x, size_y, size_z = sizes
     points = proj_ref.shape[1]
@@ -143,7 +153,8 @@
     for position in range(POS_Y):
         here = jnp.logical_and(live, place_y == position)
         wts_ref[position * NPROJ : (position + 1) * NPROJ, :] = jnp.where(here, proj_ref[...], 0.0)
-    part_ref[...] = sample_partials(cells_ref[...].reshape(ROWS, DEPTH), idx_ref, wts_ref)
+    table = sample_partials(cells_ref[...].reshape(ROWS, DEPTH), idx_ref, wts_ref)
+    write_parts(coord_ref, table, give_ref, xb_ref)
     write_sends(coord_ref, cells_ref, xa_ref, xb_ref, za_ref, zb_ref)
 
 
@@ -166,7 +177,7 @@
     if last:
         next_ref, nonlocal_ref, z_ref, xext, yext = outs
     else:
-        (next_ref, part_ref, xa_ref, xb_ref, za_ref, zb_ref,
+        (next_ref, give_ref, xa_ref, xb_ref, za_ref, zb_ref,
          nonlocal_ref, z_ref, xext, yext) = outs
     bx, by, bz = coord_ref[3], coord_ref[4], coord_ref[5]
 
@@ -209,7 +220,7 @@
 
     xext[:, HALO : HALO + SIDE] = cells_ref[...]
     xext[:, pl.ds((1 - bx) * (HALO + SIDE), HALO)] = xa_in[...]
-    xext[:, pl.ds(bx * (HALO + SIDE), HALO)] = xb_in[...]
+    xext[:, pl.ds(bx * (HALO + SIDE), HALO)] = xb_in[:FACE].reshape(NORB, HALO, SIDE, DEPTH)
     yext[1] = cells_ref[...]
     yext[2 - 2 * by] = ya_in[...]
     yext[2 * by] = yb_in[...]
@@ -231,7 +242,8 @@
             result = result - back * before_ref[o]
         next_ref[o] = result
     if not last:
-        part_ref[...] = sample_partials(next_ref[...].reshape(ROWS, DEPTH), idx_ref, wts_ref)
+        table = sample_partials(next_ref[...].reshape(ROWS, DEPTH), idx_ref, wts_ref)
+        write_parts(coord_ref, table, give_ref, xb_ref)
         write_sends(coord_ref, next_ref, xa_ref, xb_ref, za_ref, zb_ref)
 
 
@@ -308,10 +320,10 @@
     x_shape = (NORB, HALO, SIDE, DEPTH)
     z_shape = (ROWS // 128, 8, 128)
     send_shapes = [
-        ((SEGS, 128), F32), (x_shape, F32), (x_shape, F32), (z_shape, F32), (z_shape, F32)
+        ((SEGS // 3, 128), F32), (x_shape, F32), ((FACE + 6, SIDE, DEPTH), F32), (z_shape, F32), (z_shape, F32)
     ]
 
-    parts, xa, xb, za, zb, idx, wts = call(
+    *sends, idx, wts = call(
         lambda *refs: first_kernel(sizes, *refs),
         send_shapes + [((8, points), jnp.int32), ((POS_Y * NPROJ, points), F32)],
         [], (600_000_000, 2_000_000),
@@ -323,13 +335,20 @@
         (600_000_000, 200_000), coord, atom_energy,
     )
 
-    def exchange(parts, cells, xa, xb, za, zb):
-        table = parts.reshape(3, 3, 8, 128)
-        come = swap_inside(jnp.where(odd_x, table[0], table[2]), "gx")
-        middle = table[1] + come
-        pair = jnp.where(odd_x, jnp.stack([middle, table[2]]), jnp.stack([table[0], middle]))
-        pair = pair + swap_across(pair, "gx")
-        xb = swap_across(xb, "gx")
+    def exchange(cells, give, xa, xb, za, zb, energy):
+        come = swap_inside(give, "gx").reshape(1, 3, 8, 128)
+        place = jnp.arange(2, dtype=jnp.int32)[:, None, None, None]
+        pair = xb[FACE:].reshape(2, 3, 8, 128)
+        pair = pair + jnp.where(place == 1 - places[0] % 2, come, 0.0)
+        xb = lax.dynamic_update_slice(xb, pair.reshape(6, 8, 128), (FACE, 0, 0))
+        xb, xa, cells = lax.optimization_barrier((xb, xa, cells))
+        across = swap_across(xb, "gx")
+        ya, yb = swap_inside(cells, "gy"), swap_across(cells, "gy")
+        xa = swap_inside(xa, "gx")
+        pair = (xb[FACE:] + across[FACE:]).reshape(2, 3, 8, 128)
+        xb = across
+        pair, energy, xa, ya, yb = lax.optimization_barrier((pair, energy, xa, ya, yb))
+        pair = lax.psum(pair, "gy")
 
         come = swap_inside(
             jnp.concatenate([jnp.where(odd_z, pair[:, 0], pair[:, 2]), za], axis=0), "gz"
@@ -345,11 +364,6 @@
         zb = come[4:]
         own = own + come[:4].reshape(2, 2, 8, 128)
 
-        own = own + swap_inside(own, "gy")
-        own = own + swap_across(own, "gy")
-        ya, yb = swap_inside(cells, "gy"), swap_across(cells, "gy")
-        xa = swap_inside(xa, "gx")
-
         beyond_x = swap_inside(jnp.where(odd_x, own[0], own[1]), "gx")
         rows = jnp.where(
             odd_z,
@@ -359,7 +373,7 @@
                       jnp.stack([own[0, 1], own[1, 1], beyond_x[1]])),
         )
         beyond_z = swap_inside(rows, "gz")
-        return own, beyond_x, beyond_z, xa, xb, ya, yb, za, zb
+        return energy, own, beyond_x, beyond_z, xa, xb, ya, yb, za, zb
 
     half_width = (highest - cutoff) / 2.0
     middle = (highest + cutoff) / 2.0
@@ -380,17 +394,17 @@
             scales = (2.0 * sigma_next / half_width, middle, sigma_now * sigma_next)
             sigma_now = sigma_next
         last = degree_index == DEGREE - 1
-        came = exchange(parts, current, xa, xb, za, zb)
+        came = exchange(current, *sends, energy)
         before = [] if previous is None else [previous]
         results = call(
             lambda *refs, scales=scales, last=last: step_kernel(scales, last, *refs),
             [(cells_shape, F32)] + ([] if last else send_shapes),
             scratch, (1_500_000_000, 4_000_000),
-            coord, current, *before, potential, idx, wts, energy, *came,
+            coord, current, *before, potential, idx, wts, *came,
         )
         previous, current = current, results[0]
         if not last:
-            parts, xa, xb, za, zb = results[1:]
+            sends = results[1:]
     return current
 
 

time: 283 us -> 256 us (0.905)
  starting transfers between devices: 180 us -> 137 us
  blocking collectives: 0 us -> 36.8 us
  local copies, waits for them, and re-layouts: 13.4 us -> 1.88 us
  Pallas kernels: 27.8 us -> 21.4 us
  other arithmetic: 4.64 us -> 0.41 us
  waiting for transfers between devices: 52.4 us -> 55.8 us
    psum x0 -> x3, blocking collectives: none -> 36.8 us  [exchange(): pair = lax.psum(pair, 'gy')]
    ppermute x15 -> x9, starting transfers between devices: 96.3 us -> 63.2 us  [swap_across(): return lax.ppermute(value, axis, pairs)]
    ppermute x21 -> x18, starting transfers between devices: 84.2 us -> 74.2 us  [swap_inside(): return lax.ppermute(value, axis, [(i, i ^ 1) for i in range(count)])]
    unnamed x64 -> x16, local copies, waits for them, and re-layouts: 8.58 us -> 1.58 us
    pallas_call x5, Pallas kernels: 27.8 us -> 21.4 us  [call(): pl.pallas_call(kernel, out_shape=[jax.ShapeDtypeStruct(s, k) for s, k in...]
    ppermute x15 -> x9, waiting for transfers between devices: 30.8 us -> 36.9 us  [swap_across(): return lax.ppermute(value, axis, pairs)]
    ppermute x21 -> x18, waiting for transfers between devices: 21.6 us -> 18.9 us  [swap_inside(): return lax.ppermute(value, axis, [(i, i ^ 1) for i in range(count)])]
  transfers between devices with their start and end apart: 36 -> 27, of which waited for: 19 -> 18; matrix products, arithmetic and copies ran while one was open for 1% -> 0% of each run, Pallas kernels for 2% -> 1%
where the time goes in v2:
time: 256 us; the launch traced here: 255 us
  starting transfers between devices  137 us (54%)
  waiting for transfers between devices  55.8 us (22%)
  blocking collectives  36.8 us (14%)
  Pallas kernels  21.4 us (8%)
    ppermute x18, starting transfers between devices, swap_inside(): return lax.ppermute(value, axis, [(i, i ^ 1) for i in range(count)])  74.2 us
    ppermute x9, starting transfers between devices, swap_across(): return lax.ppermute(value, axis, pairs)  63.2 us
    ppermute x9, waiting for transfers between devices, swap_across(): return lax.ppermute(value, axis, pairs)  36.9 us
    psum x3, blocking collectives, exchange(): pair = lax.psum(pair, 'gy')  36.8 us
    pallas_call x5, Pallas kernels, call(): pl.pallas_call(kernel, out_shape=[jax.ShapeDtypeStruct(s, k) for s, k in...  21.4 us
    ppermute x18, waiting for transfers between devices, swap_inside(): return lax.ppermute(value, axis, [(i, i ^ 1) for i in range(count)])  18.9 us
  transfers between devices with their start and end apart: 27, of which 18 were waited for; matrix products, arithmetic and copies ran while one was open for 0% of the time, Pallas kernels for 1%

profile of v2, /device:TPU:1, one launch (start us, length us, event | category | flops | bytes accessed | tf_op | source)
XLA Modules:
  0.0 255.0 jit_solution(2930150077715454690)
XLA Ops:
  4.5 4.0 %collective-permute-start = (f32[24,128]{1,0:T(8,128)S(1)}, f32[24,128]{1,0:T(8,128)S(1)}, u32[]{:S(2)}, u32[]{:S(2)}) collective-permute-start(f32[24,128]{1,0:T(8,128)S(1)} %get-tuple-element.51), channel_id=1, source_target_pairs={{0,64},{64,0},{128,192},{192,128},{256,320},{320,256},{384,448},{4... | collective-permute-start | bytes 36872 | tf_op jit(solution)/shard_map/ppermute | solution.py:297
  9.7 22.1 %collective-permute-start.1 = (f32[54,8,128]{2,1,0:T(8,128)S(1)}, f32[54,8,128]{2,1,0:T(8,128)S(1)}, u32[]{:S(2)}, u32[]{:S(2)}) collective-permute-start(f32[54,8,128]{2,1,0:T(8,128)S(1)} %constant_dynamic-update-slice_fusion.2), channel_id=1, source_target_pairs={{0,960},{64,128},{128,64},{192,256},{256,192},{320,384},{384,320},... | collective-permute-start | bytes 663560 | tf_op jit(solution)/shard_map/ppermute | solution.py:303
  31.9 4.4 %collective-permute-start.4 = (f32[8,8,8,128]{3,2,1,0:T(8,128)S(1)}, f32[8,8,8,128]{3,2,1,0:T(8,128)S(1)}, u32[]{:S(2)}, u32[]{:S(2)}) collective-permute-start(f32[8,8,8,128]{3,2,1,0:T(8,128)S(1)} %copy-done.1), channel_id=1, source_target_pairs={{0,48},{16,32},{32,16},{48,0},{1,49},{17,33},{33,17},{49,1},{2,50}... | collective-permute-start | bytes 786440 | tf_op jit(solution)/shard_map/ppermute | solution.py:303
  38.2 3.3 %shard_map.83.refs_5_.refs_6_ = f32[72,128]{1,0:T(8,128)S(1)} custom-call(s32[8]{0:T(128)S(1)} %stack.93.refs_0_, f32[4,5120]{1,0:T(4,128)S(1)} %copy-done.2), custom_call_target="tpu_custom_call" | custom-call | flops 600000000 | bytes 200000 | tf_op jit(solution)/shard_map/pallas_call | solution.py:284
  43.5 4.9 %collective-permute-done.1.refs_10_ = f32[54,8,128]{2,1,0:T(8,128)S(1)} collective-permute-done((f32[54,8,128]{2,1,0:T(8,128)S(1)}, f32[54,8,128]{2,1,0:T(8,128)S(1)}, u32[]{:S(2)}, u32[]{:S(2)}) %collective-permute-start.1) | collective-permute-done | bytes 221216 | tf_op jit(solution)/shard_map/ppermute | solution.py:303
  48.4 13.3 %psum.21 = f32[2,3,8,128]{3,2,0,1:T(8,128)S(1)} all-reduce(f32[2,3,8,128]{3,2,0,1:T(8,128)S(1)} %copy.24), channel_id=1, replica_groups=mesh['gx'=16,'gy'=4,'gz'=16] {'gy'}, use_global_device_ids=true, to_apply=%region_0.1 | all-reduce | flops 6144 | bytes 49152 | tf_op jit(solution)/shard_map/psum | solution.py:351
  61.7 8.2 %collective-permute-start.5 = (f32[6,8,128]{2,1,0:T(8,128)S(1)}, f32[6,8,128]{2,1,0:T(8,128)S(1)}, u32[]{:S(2)}, u32[]{:S(2)}) collective-permute-start(f32[6,8,128]{2,1,0:T(8,128)S(1)} %pad_maximum_fusion.3), channel_id=1, source_target_pairs={{0,1},{1,0},{2,3},{3,2},{4,5},{5,4},{6,7},{7,6},{8,9},{9,8},{10,11... | collective-permute-start | bytes 73736 | tf_op jit(solution)/shard_map/ppermute | solution.py:297
  70.8 4.9 %collective-permute-start.6 = (f32[8,8,128]{2,1,0:T(8,128)S(1)}, f32[8,8,128]{2,1,0:T(8,128)S(1)}, u32[]{:S(2)}, u32[]{:S(2)}) collective-permute-start(f32[8,8,128]{2,1,0:T(8,128)S(1)} %pad_maximum_fusion), channel_id=1, source_target_pairs={{0,15},{1,2},{2,1},{3,4},{4,3},{5,6},{6,5},{7,8},{8,7},{9,10},{10,... | collective-permute-start | bytes 98312 | tf_op jit(solution)/shard_map/ppermute | solution.py:303
  82.1 8.4 %collective-permute-start.8 = (f32[3,8,128]{2,1,0:T(8,128)S(1)}, f32[3,8,128]{2,1,0:T(8,128)S(1)}, u32[]{:S(2)}, u32[]{:S(2)}) collective-permute-start(f32[3,8,128]{2,1,0:T(8,128)S(1)} %fusion.3), channel_id=1, source_target_pairs={{0,1},{1,0},{2,3},{3,2},{4,5},{5,4},{6,7},{7,6},{8,9},{9,8},{10,11... | collective-permute-start | bytes 36872 | tf_op jit(solution)/shard_map/ppermute | solution.py:297
  91.3 5.9 %shard_map.84 = (f32[8,8,8,128]{3,2,1,0:T(8,128)S(1)}, f32[24,128]{1,0:T(8,128)S(1)}, f32[8,6,8,128]{3,2,1,0:T(8,128)S(1)}, f32[54,8,128]{2,1,0:T(8,128)S(1)}, f...) custom-call(s32[8]{0:T(128)S(1)} %stack.93.refs_0_, f32[8,8,8,128]{3,2,1,0:T(8,128)S(1)} %copy-done.1, ...), custom_call_target="tpu_custom_call" | custom-call | flops 1500000000 | bytes 4000000 | tf_op jit(solution)/shard_map/pallas_call | solution.py:284
  101.7 15.1 %collective-permute-start.10 = (f32[54,8,128]{2,1,0:T(8,128)S(1)}, f32[54,8,128]{2,1,0:T(8,128)S(1)}, u32[]{:S(2)}, u32[]{:S(2)}) collective-permute-start(f32[54,8,128]{2,1,0:T(8,128)S(1)} %constant_dynamic-update-slice_fusion.1), channel_id=1, source_target_pairs={{0,960},{64,128},{128,64},{192,256},{256,192},{320,384},{384,320},... | collective-permute-start | bytes 663560 | tf_op jit(solution)/shard_map/ppermute | solution.py:303
  123.4 13.4 %collective-permute-done.10.refs_11_ = f32[54,8,128]{2,1,0:T(8,128)S(1)} collective-permute-done((f32[54,8,128]{2,1,0:T(8,128)S(1)}, f32[54,8,128]{2,1,0:T(8,128)S(1)}, u32[]{:S(2)}, u32[]{:S(2)}) %collective-permute-start.10) | collective-permute-done | bytes 221216 | tf_op jit(solution)/shard_map/ppermute | solution.py:303
  136.9 11.1 %psum.22 = f32[2,3,8,128]{3,2,1,0:T(8,128)S(1)} all-reduce(f32[2,3,8,128]{3,2,1,0:T(8,128)S(1)} %bitcast.108), channel_id=1, replica_groups=mesh['gx'=16,'gy'=4,'gz'=16] {'gy'}, use_global_device_ids=true, to_apply=%region_1.2 | all-reduce | flops 6144 | bytes 49152 | tf_op jit(solution)/shard_map/psum | solution.py:351
  148.0 5.8 %collective-permute-start.14 = (f32[6,8,128]{2,1,0:T(8,128)S(1)}, f32[6,8,128]{2,1,0:T(8,128)S(1)}, u32[]{:S(2)}, u32[]{:S(2)}) collective-permute-start(f32[6,8,128]{2,1,0:T(8,128)S(1)} %pad_maximum_fusion.4), channel_id=1, source_target_pairs={{0,1},{1,0},{2,3},{3,2},{4,5},{5,4},{6,7},{7,6},{8,9},{9,8},{10,11... | collective-permute-start | bytes 73736 | tf_op jit(solution)/shard_map/ppermute | solution.py:297
  156.6 3.3 %collective-permute-done.15 = f32[8,8,128]{2,1,0:T(8,128)S(1)} collective-permute-done((f32[8,8,128]{2,1,0:T(8,128)S(1)}, f32[8,8,128]{2,1,0:T(8,128)S(1)}, u32[]{:S(2)}, u32[]{:S(2)}) %collective-permute-start.15) | collective-permute-done | bytes 32800 | tf_op jit(solution)/shard_map/ppermute | solution.py:303
  164.6 9.9 %collective-permute-start.17 = (f32[3,8,128]{2,1,0:T(8,128)S(1)}, f32[3,8,128]{2,1,0:T(8,128)S(1)}, u32[]{:S(2)}, u32[]{:S(2)}) collective-permute-start(f32[3,8,128]{2,1,0:T(8,128)S(1)} %fusion.4), channel_id=1, source_target_pairs={{0,1},{1,0},{2,3},{3,2},{4,5},{5,4},{6,7},{7,6},{8,9},{9,8},{10,11... | collective-permute-start | bytes 36872 | tf_op jit(solution)/shard_map/ppermute | solution.py:297
  175.1 5.9 %shard_map.85 = (f32[8,8,8,128]{3,2,1,0:T(8,128)S(1)}, f32[24,128]{1,0:T(8,128)S(1)}, f32[8,6,8,128]{3,2,1,0:T(8,128)S(1)}, f32[54,8,128]{2,1,0:T(8,128)S(1)}, f...) custom-call(s32[8]{0:T(128)S(1)} %stack.93.refs_0_, f32[8,8,8,128]{3,2,1,0:T(8,128)S(1)} %get-tuple-element.69.refs_1_.refs_2_, ...), custom_call_target="tpu_custom_call" | custom-call | flops 1500000000 | bytes 4000000 | tf_op jit(solution)/shard_map/pallas_call | solution.py:284
  185.6 7.4 %collective-permute-start.19 = (f32[54,8,128]{2,1,0:T(8,128)S(1)}, f32[54,8,128]{2,1,0:T(8,128)S(1)}, u32[]{:S(2)}, u32[]{:S(2)}) collective-permute-start(f32[54,8,128]{2,1,0:T(8,128)S(1)} %constant_dynamic-update-slice_fusion), channel_id=1, source_target_pairs={{0,960},{64,128},{128,64},{192,256},{256,192},{320,384},{384,320},... | collective-permute-start | bytes 663560 | tf_op jit(solution)/shard_map/ppermute | solution.py:303
  193.0 3.5 %collective-permute-start.22 = (f32[8,8,8,128]{3,2,1,0:T(8,128)S(1)}, f32[8,8,8,128]{3,2,1,0:T(8,128)S(1)}, u32[]{:S(2)}, u32[]{:S(2)}) collective-permute-start(f32[8,8,8,128]{3,2,1,0:T(8,128)S(1)} %get-tuple-element.83.refs_1_), channel_id=1, source_target_pairs={{0,48},{16,32},{32,16},{48,0},{1,49},{17,33},{33,17},{49,1},{2,50}... | collective-permute-start | bytes 786440 | tf_op jit(solution)/shard_map/ppermute | solution.py:303
  200.4 10.5 %collective-permute-done.19.refs_11_ = f32[54,8,128]{2,1,0:T(8,128)S(1)} collective-permute-done((f32[54,8,128]{2,1,0:T(8,128)S(1)}, f32[54,8,128]{2,1,0:T(8,128)S(1)}, u32[]{:S(2)}, u32[]{:S(2)}) %collective-permute-start.19) | collective-permute-done | bytes 221216 | tf_op jit(solution)/shard_map/ppermute | solution.py:303
  210.9 12.4 %psum.23 = f32[2,3,8,128]{3,2,1,0:T(8,128)S(1)} all-reduce(f32[2,3,8,128]{3,2,1,0:T(8,128)S(1)} %bitcast.109), channel_id=1, replica_groups=mesh['gx'=16,'gy'=4,'gz'=16] {'gy'}, use_global_device_ids=true, to_apply=%region_2.3 | all-reduce | flops 6144 | bytes 49152 | tf_op jit(solution)/shard_map/psum | solution.py:351
  223.3 6.2 %collective-permute-start.23 = (f32[6,8,128]{2,1,0:T(8,128)S(1)}, f32[6,8,128]{2,1,0:T(8,128)S(1)}, u32[]{:S(2)}, u32[]{:S(2)}) collective-permute-start(f32[6,8,128]{2,1,0:T(8,128)S(1)} %pad_maximum_fusion.5), channel_id=1, source_target_pairs={{0,1},{1,0},{2,3},{3,2},{4,5},{5,4},{6,7},{7,6},{8,9},{9,8},{10,11... | collective-permute-start | bytes 73736 | tf_op jit(solution)/shard_map/ppermute | solution.py:297
  240.3 9.7 %collective-permute-start.26 = (f32[3,8,128]{2,1,0:T(8,128)S(1)}, f32[3,8,128]{2,1,0:T(8,128)S(1)}, u32[]{:S(2)}, u32[]{:S(2)}) collective-permute-start(f32[3,8,128]{2,1,0:T(8,128)S(1)} %fusion.5), channel_id=1, source_target_pairs={{0,1},{1,0},{2,3},{3,2},{4,5},{5,4},{6,7},{7,6},{8,9},{9,8},{10,11... | collective-permute-start | bytes 36872 | tf_op jit(solution)/shard_map/ppermute | solution.py:297
  250.8 4.2 %shard_map.86 = f32[8,8,8,128]{3,2,1,0:T(8,128)} custom-call(s32[8]{0:T(128)S(1)} %stack.93.refs_0_, f32[8,8,8,128]{3,2,1,0:T(8,128)S(1)} %get-tuple-element.83.refs_1_, f32[8,8,8,128]{3,2,1,0:T(8,128)S(1)} %get-tuple-element.69.refs_1_.refs_2_, f32[8,8,128]{2,1,0:T(8,128)S(1)} %copy-done.4, s32[8,2048]{1,0:T(8,128)S(1)} %get-tuple-element.48.refs_3_.refs_4_, ...), custom_call_target="tpu_custom_call" | custom-call | flops 1500000000 | bytes 4000000 | tf_op jit(solution)/shard_map/pallas_call | solution.py:284
  (105 shorter events, 55.9 us)
Async XLA Ops:
  4.5 5.1 %collective-permute-start = (f32[24,128]{1,0:T(8,128)S(1)}, f32[24,128]{1,0:T(8,128)S(1)}, u32[]{:S(2)}, u32[]{:S(2)}) collective-permute-start(f32[24,128]{1,0:T(8,128)S(1)} %get-tuple-element.51), channel_id=1, source_target_pairs={{0,64},{64,0},{128,192},{192,128},{256,320},{320,256},{384,448},{4... | collective-permute-start | bytes 36872 | tf_op jit(solution)/shard_map/ppermute | solution.py:297
  9.7 38.6 %collective-permute-start.1 = (f32[54,8,128]{2,1,0:T(8,128)S(1)}, f32[54,8,128]{2,1,0:T(8,128)S(1)}, u32[]{:S(2)}, u32[]{:S(2)}) collective-permute-start(f32[54,8,128]{2,1,0:T(8,128)S(1)} %constant_dynamic-update-slice_fusion.2), channel_id=1, source_target_pairs={{0,960},{64,128},{128,64},{192,256},{256,192},{320,384},{384,320},... | collective-permute-start | bytes 663560 | tf_op jit(solution)/shard_map/ppermute | solution.py:303
  31.9 16.5 %collective-permute-start.4 = (f32[8,8,8,128]{3,2,1,0:T(8,128)S(1)}, f32[8,8,8,128]{3,2,1,0:T(8,128)S(1)}, u32[]{:S(2)}, u32[]{:S(2)}) collective-permute-start(f32[8,8,8,128]{3,2,1,0:T(8,128)S(1)} %copy-done.1), channel_id=1, source_target_pairs={{0,48},{16,32},{32,16},{48,0},{1,49},{17,33},{33,17},{49,1},{2,50}... | collective-permute-start | bytes 786440 | tf_op jit(solution)/shard_map/ppermute | solution.py:303
  36.3 12.1 %collective-permute-start.3 = (f32[8,8,8,128]{3,2,1,0:T(8,128)S(1)}, f32[8,8,8,128]{3,2,1,0:T(8,128)S(1)}, u32[]{:S(2)}, u32[]{:S(2)}) collective-permute-start(f32[8,8,8,128]{3,2,1,0:T(8,128)S(1)} %copy-done.1), channel_id=1, source_target_pairs={{0,16},{16,0},{32,48},{48,32},{1,17},{17,1},{33,49},{49,33},{2,18}... | collective-permute-start | bytes 786440 | tf_op jit(solution)/shard_map/ppermute | solution.py:297
  41.6 6.8 %collective-permute-start.2 = (f32[8,6,8,128]{3,2,1,0:T(8,128)S(1)}, f32[8,6,8,128]{3,2,1,0:T(8,128)S(1)}, u32[]{:S(2)}, u32[]{:S(2)}) collective-permute-start(f32[8,6,8,128]{3,2,1,0:T(8,128)S(1)} %get-tuple-element.54), channel_id=1, source_target_pairs={{0,64},{64,0},{128,192},{192,128},{256,320},{320,256},{384,448},{4... | collective-permute-start | bytes 589832 | tf_op jit(solution)/shard_map/ppermute | solution.py:297
  61.7 9.1 %collective-permute-start.5 = (f32[6,8,128]{2,1,0:T(8,128)S(1)}, f32[6,8,128]{2,1,0:T(8,128)S(1)}, u32[]{:S(2)}, u32[]{:S(2)}) collective-permute-start(f32[6,8,128]{2,1,0:T(8,128)S(1)} %pad_maximum_fusion.3), channel_id=1, source_target_pairs={{0,1},{1,0},{2,3},{3,2},{4,5},{5,4},{6,7},{7,6},{8,9},{9,8},{10,11... | collective-permute-start | bytes 73736 | tf_op jit(solution)/shard_map/ppermute | solution.py:297
  70.8 6.5 %collective-permute-start.6 = (f32[8,8,128]{2,1,0:T(8,128)S(1)}, f32[8,8,128]{2,1,0:T(8,128)S(1)}, u32[]{:S(2)}, u32[]{:S(2)}) collective-permute-start(f32[8,8,128]{2,1,0:T(8,128)S(1)} %pad_maximum_fusion), channel_id=1, source_target_pairs={{0,15},{1,2},{2,1},{3,4},{4,3},{5,6},{6,5},{7,8},{8,7},{9,10},{10,... | collective-permute-start | bytes 98312 | tf_op jit(solution)/shard_map/ppermute | solution.py:303
  77.4 4.7 %collective-permute-start.7 = (f32[2,8,128]{2,1,0:T(8,128)S(1)}, f32[2,8,128]{2,1,0:T(8,128)S(1)}, u32[]{:S(2)}, u32[]{:S(2)}) collective-permute-start(f32[2,8,128]{2,1,0:T(8,128)S(1)} %fusion.9), channel_id=1, source_target_pairs={{0,64},{64,0},{128,192},{192,128},{256,320},{320,256},{384,448},{4... | collective-permute-start | bytes 24584 | tf_op jit(solution)/shard_map/ppermute | solution.py:297
  82.1 9.2 %collective-permute-start.8 = (f32[3,8,128]{2,1,0:T(8,128)S(1)}, f32[3,8,128]{2,1,0:T(8,128)S(1)}, u32[]{:S(2)}, u32[]{:S(2)}) collective-permute-start(f32[3,8,128]{2,1,0:T(8,128)S(1)} %fusion.3), channel_id=1, source_target_pairs={{0,1},{1,0},{2,3},{3,2},{4,5},{5,4},{6,7},{7,6},{8,9},{9,8},{10,11... | collective-permute-start | bytes 36872 | tf_op jit(solution)/shard_map/ppermute | solution.py:297
  101.7 35.1 %collective-permute-start.10 = (f32[54,8,128]{2,1,0:T(8,128)S(1)}, f32[54,8,128]{2,1,0:T(8,128)S(1)}, u32[]{:S(2)}, u32[]{:S(2)}) collective-permute-start(f32[54,8,128]{2,1,0:T(8,128)S(1)} %constant_dynamic-update-slice_fusion.1), channel_id=1, source_target_pairs={{0,960},{64,128},{128,64},{192,256},{256,192},{320,384},{384,320},... | collective-permute-start | bytes 663560 | tf_op jit(solution)/shard_map/ppermute | solution.py:303
  116.8 20.0 %collective-permute-start.13 = (f32[8,8,8,128]{3,2,1,0:T(8,128)S(1)}, f32[8,8,8,128]{3,2,1,0:T(8,128)S(1)}, u32[]{:S(2)}, u32[]{:S(2)}) collective-permute-start(f32[8,8,8,128]{3,2,1,0:T(8,128)S(1)} %get-tuple-element.69.refs_1_.refs_2_), channel_id=1, source_target_pairs={{0,48},{16,32},{32,16},{48,0},{1,49},{17,33},{33,17},{49,1},{2,50}... | collective-permute-start | bytes 786440 | tf_op jit(solution)/shard_map/ppermute | solution.py:303
  118.7 18.1 %collective-permute-start.12 = (f32[8,8,8,128]{3,2,1,0:T(8,128)S(1)}, f32[8,8,8,128]{3,2,1,0:T(8,128)S(1)}, u32[]{:S(2)}, u32[]{:S(2)}) collective-permute-start(f32[8,8,8,128]{3,2,1,0:T(8,128)S(1)} %get-tuple-element.69.refs_1_.refs_2_), channel_id=1, source_target_pairs={{0,16},{16,0},{32,48},{48,32},{1,17},{17,1},{33,49},{49,33},{2,18}... | collective-permute-start | bytes 786440 | tf_op jit(solution)/shard_map/ppermute | solution.py:297
  121.5 15.3 %collective-permute-start.11 = (f32[8,6,8,128]{3,2,1,0:T(8,128)S(1)}, f32[8,6,8,128]{3,2,1,0:T(8,128)S(1)}, u32[]{:S(2)}, u32[]{:S(2)}) collective-permute-start(f32[8,6,8,128]{3,2,1,0:T(8,128)S(1)} %get-tuple-element.68), channel_id=1, source_target_pairs={{0,64},{64,0},{128,192},{192,128},{256,320},{320,256},{384,448},{4... | collective-permute-start | bytes 589832 | tf_op jit(solution)/shard_map/ppermute | solution.py:297
  148.0 6.6 %collective-permute-start.14 = (f32[6,8,128]{2,1,0:T(8,128)S(1)}, f32[6,8,128]{2,1,0:T(8,128)S(1)}, u32[]{:S(2)}, u32[]{:S(2)}) collective-permute-start(f32[6,8,128]{2,1,0:T(8,128)S(1)} %pad_maximum_fusion.4), channel_id=1, source_target_pairs={{0,1},{1,0},{2,3},{3,2},{4,5},{5,4},{6,7},{7,6},{8,9},{9,8},{10,11... | collective-permute-start | bytes 73736 | tf_op jit(solution)/shard_map/ppermute | solution.py:297
  154.6 5.2 %collective-permute-start.15 = (f32[8,8,128]{2,1,0:T(8,128)S(1)}, f32[8,8,128]{2,1,0:T(8,128)S(1)}, u32[]{:S(2)}, u32[]{:S(2)}) collective-permute-start(f32[8,8,128]{2,1,0:T(8,128)S(1)} %pad_maximum_fusion.1), channel_id=1, source_target_pairs={{0,15},{1,2},{2,1},{3,4},{4,3},{5,6},{6,5},{7,8},{8,7},{9,10},{10,... | collective-permute-start | bytes 98312 | tf_op jit(solution)/shard_map/ppermute | solution.py:303
  159.9 4.7 %collective-permute-start.16 = (f32[2,8,128]{2,1,0:T(8,128)S(1)}, f32[2,8,128]{2,1,0:T(8,128)S(1)}, u32[]{:S(2)}, u32[]{:S(2)}) collective-permute-start(f32[2,8,128]{2,1,0:T(8,128)S(1)} %fusion.7), channel_id=1, source_target_pairs={{0,64},{64,0},{128,192},{192,128},{256,320},{320,256},{384,448},{4... | collective-permute-start | bytes 24584 | tf_op jit(solution)/shard_map/ppermute | solution.py:297
  164.6 10.5 %collective-permute-start.17 = (f32[3,8,128]{2,1,0:T(8,128)S(1)}, f32[3,8,128]{2,1,0:T(8,128)S(1)}, u32[]{:S(2)}, u32[]{:S(2)}) collective-permute-start(f32[3,8,128]{2,1,0:T(8,128)S(1)} %fusion.4), channel_id=1, source_target_pairs={{0,1},{1,0},{2,3},{3,2},{4,5},{5,4},{6,7},{7,6},{8,9},{9,8},{10,11... | collective-permute-start | bytes 36872 | tf_op jit(solution)/shard_map/ppermute | solution.py:297
  185.6 25.3 %collective-permute-start.19 = (f32[54,8,128]{2,1,0:T(8,128)S(1)}, f32[54,8,128]{2,1,0:T(8,128)S(1)}, u32[]{:S(2)}, u32[]{:S(2)}) collective-permute-start(f32[54,8,128]{2,1,0:T(8,128)S(1)} %constant_dynamic-update-slice_fusion), channel_id=1, source_target_pairs={{0,960},{64,128},{128,64},{192,256},{256,192},{320,384},{384,320},... | collective-permute-start | bytes 663560 | tf_op jit(solution)/shard_map/ppermute | solution.py:303
  193.0 17.9 %collective-permute-start.22 = (f32[8,8,8,128]{3,2,1,0:T(8,128)S(1)}, f32[8,8,8,128]{3,2,1,0:T(8,128)S(1)}, u32[]{:S(2)}, u32[]{:S(2)}) collective-permute-start(f32[8,8,8,128]{3,2,1,0:T(8,128)S(1)} %get-tuple-element.83.refs_1_), channel_id=1, source_target_pairs={{0,48},{16,32},{32,16},{48,0},{1,49},{17,33},{33,17},{49,1},{2,50}... | collective-permute-start | bytes 786440 | tf_op jit(solution)/shard_map/ppermute | solution.py:303
  196.5 14.4 %collective-permute-start.21 = (f32[8,8,8,128]{3,2,1,0:T(8,128)S(1)}, f32[8,8,8,128]{3,2,1,0:T(8,128)S(1)}, u32[]{:S(2)}, u32[]{:S(2)}) collective-permute-start(f32[8,8,8,128]{3,2,1,0:T(8,128)S(1)} %get-tuple-element.83.refs_1_), channel_id=1, source_target_pairs={{0,16},{16,0},{32,48},{48,32},{1,17},{17,1},{33,49},{49,33},{2,18}... | collective-permute-start | bytes 786440 | tf_op jit(solution)/shard_map/ppermute | solution.py:297
  198.4 12.4 %collective-permute-start.20 = (f32[8,6,8,128]{3,2,1,0:T(8,128)S(1)}, f32[8,6,8,128]{3,2,1,0:T(8,128)S(1)}, u32[]{:S(2)}, u32[]{:S(2)}) collective-permute-start(f32[8,6,8,128]{3,2,1,0:T(8,128)S(1)} %get-tuple-element.82), channel_id=1, source_target_pairs={{0,64},{64,0},{128,192},{192,128},{256,320},{320,256},{384,448},{4... | collective-permute-start | bytes 589832 | tf_op jit(solution)/shard_map/ppermute | solution.py:297
  223.3 7.0 %collective-permute-start.23 = (f32[6,8,128]{2,1,0:T(8,128)S(1)}, f32[6,8,128]{2,1,0:T(8,128)S(1)}, u32[]{:S(2)}, u32[]{:S(2)}) collective-permute-start(f32[6,8,128]{2,1,0:T(8,128)S(1)} %pad_maximum_fusion.5), channel_id=1, source_target_pairs={{0,1},{1,0},{2,3},{3,2},{4,5},{5,4},{6,7},{7,6},{8,9},{9,8},{10,11... | collective-permute-start | bytes 73736 | tf_op jit(solution)/shard_map/ppermute | solution.py:297
  230.3 5.2 %collective-permute-start.24 = (f32[8,8,128]{2,1,0:T(8,128)S(1)}, f32[8,8,128]{2,1,0:T(8,128)S(1)}, u32[]{:S(2)}, u32[]{:S(2)}) collective-permute-start(f32[8,8,128]{2,1,0:T(8,128)S(1)} %pad_maximum_fusion.2), channel_id=1, source_target_pairs={{0,15},{1,2},{2,1},{3,4},{4,3},{5,6},{6,5},{7,8},{8,7},{9,10},{10,... | collective-permute-start | bytes 98312 | tf_op jit(solution)/shard_map/ppermute | solution.py:303
  240.3 10.5 %collective-permute-start.26 = (f32[3,8,128]{2,1,0:T(8,128)S(1)}, f32[3,8,128]{2,1,0:T(8,128)S(1)}, u32[]{:S(2)}, u32[]{:S(2)}) collective-permute-start(f32[3,8,128]{2,1,0:T(8,128)S(1)} %fusion.5), channel_id=1, source_target_pairs={{0,1},{1,0},{2,3},{3,2},{4,5},{5,4},{6,7},{7,6},{8,9},{9,8},{10,11... | collective-permute-start | bytes 36872 | tf_op jit(solution)/shard_map/ppermute | solution.py:297
  (11 other events, 92.1 us)

commit v3 on v2

--- a/solution.py
+++ b/solution.py
@@ -12,7 +12,6 @@
 SIDE = 8
 DEPTH = 128
 HALO = 6
-FACE = NORB * HALO
 ROWS = NORB * SIDE * SIDE
 PLANES = 9
 SEGS = PLANES * 8
@@ -106,19 +105,19 @@
             nonlocal_ref[...] += placed
 
 
-def write_parts(coord_ref, table, send_ref, xb_ref):
+def write_parts(coord_ref, table, send_ref, keep_ref):
     rows = SEGS // 3
     odd_x = coord_ref[3] == 1
     below, same, above = table[:rows], table[rows : 2 * rows], table[2 * rows :]
     send_ref[...] = jnp.where(odd_x, below, above)
     kept = [jnp.where(odd_x, same, below), jnp.where(odd_x, above, same)]
-    xb_ref[FACE:] = jnp.concatenate(kept, axis=0).reshape(6, SIDE, DEPTH)
+    keep_ref[...] = jnp.concatenate(kept, axis=0)
 
 
 def write_sends(coord_ref, cells_ref, xa_ref, xb_ref, za_ref, zb_ref):
     bx, bz = coord_ref[3], coord_ref[5]
     xa_ref[...] = cells_ref[:, pl.ds(2 - 2 * bx, HALO)]
-    xb_ref[:FACE] = cells_ref[:, pl.ds(2 * bx, HALO)].reshape(FACE, SIDE, DEPTH)
+    xb_ref[...] = cells_ref[:, pl.ds(2 * bx, HALO)]
     turned = cells_ref[...].reshape(ROWS, DEPTH).T
     near, far = turned[0:8], turned[DEPTH - 8 : DEPTH]
     to_a = jnp.where(bz == 1, near, far)
@@ -135,7 +134,7 @@
 
 def first_kernel(
     sizes, coord_ref, cells_ref, proj_ref, cell_ref, owner_ref, slot_ref,
-    give_ref, xa_ref, xb_ref, za_ref, zb_ref, idx_ref, wts_ref,
+    give_ref, keep_ref, xa_ref, xb_ref, za_ref, zb_ref, idx_ref, wts_ref,
 ):
     size_x, size_y, size_z = sizes
     points = proj_ref.shape[1]
@@ -154,7 +153,7 @@
         here = jnp.logical_and(live, place_y == position)
         wts_ref[position * NPROJ : (position + 1) * NPROJ, :] = jnp.where(here, proj_ref[...], 0.0)
     table = sample_partials(cells_ref[...].reshape(ROWS, DEPTH), idx_ref, wts_ref)
-    write_parts(coord_ref, table, give_ref, xb_ref)
+    write_parts(coord_ref, table, give_ref, keep_ref)
     write_sends(coord_ref, cells_ref, xa_ref, xb_ref, za_ref, zb_ref)
 
 
@@ -177,7 +176,7 @@
     if last:
         next_ref, nonlocal_ref, z_ref, xext, yext = outs
     else:
-        (next_ref, give_ref, xa_ref, xb_ref, za_ref, zb_ref,
+        (next_ref, give_ref, keep_ref, xa_ref, xb_ref, za_ref, zb_ref,
          nonlocal_ref, z_ref, xext, yext) = outs
     bx, by, bz = coord_ref[3], coord_ref[4], coord_ref[5]
 
@@ -220,7 +219,7 @@
 
     xext[:, HALO : HALO + SIDE] = cells_ref[...]
     xext[:, pl.ds((1 - bx) * (HALO + SIDE), HALO)] = xa_in[...]
-    xext[:, pl.ds(bx * (HALO + SIDE), HALO)] = xb_in[:FACE].reshape(NORB, HALO, SIDE, DEPTH)
+    xext[:, pl.ds(bx * (HALO + SIDE), HALO)] = xb_in[...]
     yext[1] = cells_ref[...]
     yext[2 - 2 * by] = ya_in[...]
     yext[2 * by] = yb_in[...]
@@ -243,7 +242,7 @@
         next_ref[o] = result
     if not last:
         table = sample_partials(next_ref[...].reshape(ROWS, DEPTH), idx_ref, wts_ref)
-        write_parts(coord_ref, table, give_ref, xb_ref)
+        write_parts(coord_ref, table, give_ref, keep_ref)
         write_sends(coord_ref, next_ref, xa_ref, xb_ref, za_ref, zb_ref)
 
 
@@ -292,6 +291,21 @@
     )(*operands)
 
 
+def add_kernel(left_ref, right_ref, sum_ref):
+    sum_ref[...] = left_ref[...] + right_ref[...]
+
+
+def total(left, right):
+    return pl.pallas_call(
+        add_kernel,
+        out_shape=jax.ShapeDtypeStruct(left.shape, F32),
+        in_specs=in_vmem(2),
+        out_specs=in_vmem(1)[0],
+        compiler_params=pltpu.CompilerParams(vmem_limit_bytes=VMEM_LIMIT),
+        cost_estimate=pl.CostEstimate(flops=4000000000, bytes_accessed=40000000, transcendentals=0),
+    )(left, right)
+
+
 def swap_inside(value, axis):
     count = lax.axis_size(axis)
     return lax.ppermute(value, axis, [(i, i ^ 1) for i in range(count)])
@@ -315,12 +329,13 @@
         + [point_count[0], jnp.int32(0)]
     )
     odd_x, odd_z = places[0] % 2 == 1, places[2] % 2 == 1
+    some = point_count[0] > 0
 
     cells_shape = orbitals.shape
     x_shape = (NORB, HALO, SIDE, DEPTH)
     z_shape = (ROWS // 128, 8, 128)
     send_shapes = [
-        ((SEGS // 3, 128), F32), (x_shape, F32), ((FACE + 6, SIDE, DEPTH), F32), (z_shape, F32), (z_shape, F32)
+        ((SEGS // 3, 128), F32), ((2 * SEGS // 3, 128), F32), (x_shape, F32), (x_shape, F32), (z_shape, F32), (z_shape, F32)
     ]
 
     *sends, idx, wts = call(
@@ -335,34 +350,43 @@
         (600_000_000, 200_000), coord, atom_energy,
     )
 
-    def exchange(cells, give, xa, xb, za, zb, energy):
+    def exchange(cells, give, keep, xa, xb, za, zb, energy):
         come = swap_inside(give, "gx").reshape(1, 3, 8, 128)
         place = jnp.arange(2, dtype=jnp.int32)[:, None, None, None]
-        pair = xb[FACE:].reshape(2, 3, 8, 128)
+        pair = keep.reshape(2, 3, 8, 128)
         pair = pair + jnp.where(place == 1 - places[0] % 2, come, 0.0)
-        xb = lax.dynamic_update_slice(xb, pair.reshape(6, 8, 128), (FACE, 0, 0))
-        xb, xa, cells = lax.optimization_barrier((xb, xa, cells))
-        across = swap_across(xb, "gx")
-        ya, yb = swap_inside(cells, "gy"), swap_across(cells, "gy")
-        xa = swap_inside(xa, "gx")
-        pair = (xb[FACE:] + across[FACE:]).reshape(2, 3, 8, 128)
-        xb = across
-        pair, energy, xa, ya, yb = lax.optimization_barrier((pair, energy, xa, ya, yb))
-        pair = lax.psum(pair, "gy")
-
-        come = swap_inside(
-            jnp.concatenate([jnp.where(odd_z, pair[:, 0], pair[:, 2]), za], axis=0), "gz"
+        across = swap_across(pair, "gx")
+        pair, xb = lax.optimization_barrier((pair, xb))
+        xb = swap_across(xb, "gx")
+        pair = total(pair, across)
+        pair, energy = lax.optimization_barrier((pair, energy))
+
+        def along_yz(pair, cells, xa, za, zb):
+            pair = pair + swap_inside(pair, "gy")
+            pair = pair + swap_across(pair, "gy")
+            come = swap_inside(
+                jnp.concatenate([jnp.where(odd_z, pair[:, 0], pair[:, 2]), za], axis=0), "gz"
+            )
+            za = come[2:]
+            middle = pair[:, 1] + come[:2]
+            own = jnp.where(
+                odd_z,
+                jnp.stack([middle, pair[:, 2]], axis=1),
+                jnp.stack([pair[:, 0], middle], axis=1),
+            )
+            own, cells, xa = lax.optimization_barrier((own, cells, xa))
+            come = swap_across(jnp.concatenate([own.reshape(4, 8, 128), zb], axis=0), "gz")
+            ya, yb = swap_inside(cells, "gy"), swap_across(cells, "gy")
+            xa = swap_inside(xa, "gx")
+            return own + come[:4].reshape(2, 2, 8, 128), xa, ya, yb, za, come[4:]
+
+        def untouched(pair, cells, xa, za, zb):
+            return pair[:, :2], xa, cells, cells, za, zb
+
+        own, xa, ya, yb, za, zb = lax.cond(
+            some, along_yz, untouched, pair, cells, xa, za, zb
         )
-        za = come[2:]
-        middle = pair[:, 1] + come[:2]
-        own = jnp.where(
-            odd_z,
-            jnp.stack([middle, pair[:, 2]], axis=1),
-            jnp.stack([pair[:, 0], middle], axis=1),
-        )
-        come = swap_across(jnp.concatenate([own.reshape(4, 8, 128), zb], axis=0), "gz")
-        zb = come[4:]
-        own = own + come[:4].reshape(2, 2, 8, 128)
+        own, xb = lax.optimization_barrier((own, xb))
 
         beyond_x = swap_inside(jnp.where(odd_x, own[0], own[1]), "gx")
         rows = jnp.where(

time: 256 us -> 247 us (0.965)
  starting transfers between devices: 137 us -> 175 us
  blocking collectives: 36.8 us -> 0 us
  waiting for transfers between devices: 55.8 us -> 43.9 us
    psum x3 -> x0, blocking collectives: 36.8 us -> none  [exchange(): pair = lax.psum(pair, 'gy')]
    ppermute x9 -> x15, waiting for transfers between devices: 36.9 us -> 7.43 us  [swap_across(): return lax.ppermute(value, axis, pairs)]
    ppermute x18 -> x21, starting transfers between devices: 74.2 us -> 96 us  [swap_inside(): return lax.ppermute(value, axis, [(i, i ^ 1) for i in range(count)])]
    ppermute x18 -> x21, waiting for transfers between devices: 18.9 us -> 36.5 us  [swap_inside(): return lax.ppermute(value, axis, [(i, i ^ 1) for i in range(count)])]
    ppermute x9 -> x15, starting transfers between devices: 63.2 us -> 79.5 us  [swap_across(): return lax.ppermute(value, axis, pairs)]
  transfers between devices with their start and end apart: 27 -> 36, of which waited for: 18 -> 21; matrix products, arithmetic and copies ran while one was open for 0% -> 0% of each run, Pallas kernels for 1% -> 1%
where the time goes in v3:
time: 247 us; the launch traced here: 246 us
  starting transfers between devices  175 us (71%)
  waiting for transfers between devices  43.9 us (18%)
  Pallas kernels  23.4 us (9%)
    ppermute x21, starting transfers between devices, swap_inside(): return lax.ppermute(value, axis, [(i, i ^ 1) for i in range(count)])  96 us
    ppermute x15, starting transfers between devices, swap_across(): return lax.ppermute(value, axis, pairs)  79.5 us
    ppermute x21, waiting for transfers between devices, swap_inside(): return lax.ppermute(value, axis, [(i, i ^ 1) for i in range(count)])  36.5 us
    pallas_call x5, Pallas kernels, call(): pl.pallas_call(kernel, out_shape=[jax.ShapeDtypeStruct(s, k) for s, k in...  23.4 us
    ppermute x15, waiting for transfers between devices, swap_across(): return lax.ppermute(value, axis, pairs)  7.43 us
  transfers between devices with their start and end apart: 36, of which 21 were waited for; matrix products, arithmetic and copies ran while one was open for 0% of the time, Pallas kernels for 1%

profile of v3, /device:TPU:1, one launch (start us, length us, event | category | flops | bytes accessed | tf_op | source)
XLA Modules:
  0.0 245.5 jit_solution(6257745643846641826)
XLA Ops:
  4.1 4.0 %collective-permute-start.21 = (f32[24,128]{1,0:T(8,128)S(1)}, f32[24,128]{1,0:T(8,128)S(1)}, u32[]{:S(2)}, u32[]{:S(2)}) collective-permute-start(f32[24,128]{1,0:T(8,128)S(1)} %get-tuple-element.174), channel_id=1, source_target_pairs={{0,64},{64,0},{128,192},{192,128},{256,320},{320,256},{384,448},{4... | collective-permute-start | bytes 36872 | tf_op jit(solution)/shard_map/ppermute | solution.py:311
  9.2 22.1 %collective-permute-start.22 = (f32[2,3,8,128]{3,2,1,0:T(8,128)S(1)}, f32[2,3,8,128]{3,2,1,0:T(8,128)S(1)}, u32[]{:S(2)}, u32[]{:S(2)}) collective-permute-start(f32[2,3,8,128]{3,2,1,0:T(8,128)S(1)} %select_add_fusion.2.left_ref), channel_id=1, source_target_pairs={{0,960},{64,128},{128,64},{192,256},{256,192},{320,384},{384,320},... | collective-permute-start | bytes 73736 | tf_op jit(solution)/shard_map/ppermute | solution.py:317
  36.8 35.3 %conditional.3 = (f32[2,2,8,128]{3,2,1,0:T(8,128)S(1)}, f32[8,6,8,128]{3,2,1,0:T(8,128)S(1)}, f32[8,8,8,128]{3,2,1,0:T(8,128)}, f32[8,8,8,128]{3,2,1,0:T(8,128)}...) conditional(s32[]{:T(128)} %bitcast.26, (f32[2,3,8,128]{3,2,1,0:T(8,128)S(1)}, ...), branch_computations={%region_0.1_spmd, %region_1.2_spmd} | conditional | flops 47104 | bytes 4333898 | solution.py:386
  41.5 4.4 %collective-permute-start.1 = (f32[2,3,8,128]{3,2,0,1:T(8,128)S(1)}, f32[2,3,8,128]{3,2,0,1:T(8,128)S(1)}, u32[]{:S(2)}, u32[]{:S(2)}) collective-permute-start(f32[2,3,8,128]{3,2,0,1:T(8,128)S(1)} %copy_add_fusion.1), channel_id=1, source_target_pairs={{0,48},{16,32},{32,16},{48,0},{1,49},{17,33},{33,17},{49,1},{2,50}... | collective-permute-start | bytes 73736 | tf_op jit(solution)/shard_map/cond/branch_1_fun/ppermute | solution.py:317
  47.2 11.4 %collective-permute-start.2 = (f32[6,8,128]{2,1,0:T(8,128)S(1)}, f32[6,8,128]{2,1,0:T(8,128)S(1)}, u32[]{:S(2)}, u32[]{:S(2)}) collective-permute-start(f32[6,8,128]{2,1,0:T(8,128)S(1)} %pad_maximum_fusion.1), channel_id=1, source_target_pairs={{0,1},{1,0},{2,3},{3,2},{4,5},{5,4},{6,7},{7,6},{8,9},{9,8},{10,11... | collective-permute-start | bytes 73736 | tf_op jit(solution)/shard_map/cond/branch_1_fun/ppermute | solution.py:311
  67.3 4.8 %collective-permute-done.4 = f32[8,6,8,128]{3,2,1,0:T(8,128)S(1)} collective-permute-done((f32[8,6,8,128]{3,2,1,0:T(8,128)S(1)}, f32[8,6,8,128]{3,2,1,0:T(8,128)S(1)}, u32[]{:S(2)}, u32[]{:S(2)}) %collective-permute-start.4) | collective-permute-done | bytes 196640 | tf_op jit(solution)/shard_map/cond/branch_1_fun/ppermute | solution.py:311
  77.1 8.1 %collective-permute-start.25 = (f32[3,8,128]{2,1,0:T(8,128)S(1)}, f32[3,8,128]{2,1,0:T(8,128)S(1)}, u32[]{:S(2)}, u32[]{:S(2)}) collective-permute-start(f32[3,8,128]{2,1,0:T(8,128)S(1)} %fusion.3), channel_id=1, source_target_pairs={{0,1},{1,0},{2,3},{3,2},{4,5},{5,4},{6,7},{7,6},{8,9},{9,8},{10,11... | collective-permute-start | bytes 36872 | tf_op jit(solution)/shard_map/ppermute | solution.py:311
  86.0 6.4 %shard_map.85 = (f32[8,8,8,128]{3,2,1,0:T(8,128)S(1)}, f32[24,128]{1,0:T(8,128)S(1)}, f32[48,128]{1,0:T(8,128)S(1)}, f32[8,6,8,128]{3,2,1,0:T(8,128)S(1)}, f32[8...) custom-call(s32[8]{0:T(128)S(1)} %stack.93.refs_0_, f32[8,8,8,128]{3,2,1,0:T(8,128)S(1)} %copy-done.6, ...), custom_call_target="tpu_custom_call" | custom-call | flops 1500000000 | bytes 4000000 | tf_op jit(solution)/shard_map/pallas_call | solution.py:283
  96.9 14.5 %collective-permute-start.27 = (f32[2,3,8,128]{3,2,1,0:T(8,128)S(1)}, f32[2,3,8,128]{3,2,1,0:T(8,128)S(1)}, u32[]{:S(2)}, u32[]{:S(2)}) collective-permute-start(f32[2,3,8,128]{3,2,1,0:T(8,128)S(1)} %select_add_fusion.1.left_ref), channel_id=1, source_target_pairs={{0,960},{64,128},{128,64},{192,256},{256,192},{320,384},{384,320},... | collective-permute-start | bytes 73736 | tf_op jit(solution)/shard_map/ppermute | solution.py:317
  113.3 30.4 %conditional.4 = (f32[2,2,8,128]{3,2,1,0:T(8,128)S(1)}, f32[8,6,8,128]{3,2,1,0:T(8,128)S(1)}, f32[8,8,8,128]{3,2,1,0:T(8,128)}, f32[8,8,8,128]{3,2,1,0:T(8,128)}...) conditional(s32[]{:T(128)} %bitcast.26, (f32[2,3,8,128]{3,2,1,0:T(8,128)S(1)}, ...), branch_computations={%region_2.3_spmd, %region_3.4_spmd} | conditional | flops 47104 | bytes 4333898 | solution.py:386
  113.3 3.5 %collective-permute-start.7 = (f32[2,3,8,128]{3,2,0,1:T(8,128)S(1)}, f32[2,3,8,128]{3,2,0,1:T(8,128)S(1)}, u32[]{:S(2)}, u32[]{:S(2)}) collective-permute-start(f32[2,3,8,128]{3,2,0,1:T(8,128)S(1)} %copy.15), channel_id=1, source_target_pairs={{0,16},{16,0},{32,48},{48,32},{1,17},{17,1},{33,49},{49,33},{2,18}... | collective-permute-start | bytes 73736 | tf_op jit(solution)/shard_map/cond/branch_1_fun/ppermute | solution.py:311
  120.3 3.6 %collective-permute-done.8 = f32[2,3,8,128]{3,2,0,1:T(8,128)S(1)} collective-permute-done((f32[2,3,8,128]{3,2,0,1:T(8,128)S(1)}, f32[2,3,8,128]{3,2,0,1:T(8,128)S(1)}, u32[]{:S(2)}, u32[]{:S(2)}) %collective-permute-start.8) | collective-permute-done | bytes 24608 | tf_op jit(solution)/shard_map/cond/branch_1_fun/ppermute | solution.py:317
  123.9 5.8 %collective-permute-start.9 = (f32[6,8,128]{2,1,0:T(8,128)S(1)}, f32[6,8,128]{2,1,0:T(8,128)S(1)}, u32[]{:S(2)}, u32[]{:S(2)}) collective-permute-start(f32[6,8,128]{2,1,0:T(8,128)S(1)} %pad_maximum_fusion.3), channel_id=1, source_target_pairs={{0,1},{1,0},{2,3},{3,2},{4,5},{5,4},{6,7},{7,6},{8,9},{9,8},{10,11... | collective-permute-start | bytes 73736 | tf_op jit(solution)/shard_map/cond/branch_1_fun/ppermute | solution.py:311
  138.8 4.8 %collective-permute-done.11 = f32[8,6,8,128]{3,2,1,0:T(8,128)S(1)} collective-permute-done((f32[8,6,8,128]{3,2,1,0:T(8,128)S(1)}, f32[8,6,8,128]{3,2,1,0:T(8,128)S(1)}, u32[]{:S(2)}, u32[]{:S(2)}) %collective-permute-start.11) | collective-permute-done | bytes 196640 | tf_op jit(solution)/shard_map/cond/branch_1_fun/ppermute | solution.py:311
  148.3 8.1 %collective-permute-start.30 = (f32[3,8,128]{2,1,0:T(8,128)S(1)}, f32[3,8,128]{2,1,0:T(8,128)S(1)}, u32[]{:S(2)}, u32[]{:S(2)}) collective-permute-start(f32[3,8,128]{2,1,0:T(8,128)S(1)} %fusion.4), channel_id=1, source_target_pairs={{0,1},{1,0},{2,3},{3,2},{4,5},{5,4},{6,7},{7,6},{8,9},{9,8},{10,11... | collective-permute-start | bytes 36872 | tf_op jit(solution)/shard_map/ppermute | solution.py:311
  157.0 6.4 %shard_map.87 = (f32[8,8,8,128]{3,2,1,0:T(8,128)S(1)}, f32[24,128]{1,0:T(8,128)S(1)}, f32[48,128]{1,0:T(8,128)S(1)}, f32[8,6,8,128]{3,2,1,0:T(8,128)S(1)}, f32[8...) custom-call(s32[8]{0:T(128)S(1)} %stack.93.refs_0_, ...), custom_call_target="tpu_custom_call" | custom-call | flops 1500000000 | bytes 4000000 | tf_op jit(solution)/shard_map/pallas_call | solution.py:283
  167.9 13.5 %collective-permute-start.32 = (f32[2,3,8,128]{3,2,1,0:T(8,128)S(1)}, f32[2,3,8,128]{3,2,1,0:T(8,128)S(1)}, u32[]{:S(2)}, u32[]{:S(2)}) collective-permute-start(f32[2,3,8,128]{3,2,1,0:T(8,128)S(1)} %select_add_fusion.left_ref), channel_id=1, source_target_pairs={{0,960},{64,128},{128,64},{192,256},{256,192},{320,384},{384,320},... | collective-permute-start | bytes 73736 | tf_op jit(solution)/shard_map/ppermute | solution.py:317
  184.1 31.2 %conditional.5 = (f32[2,2,8,128]{3,2,1,0:T(8,128)S(1)}, f32[8,6,8,128]{3,2,1,0:T(8,128)S(1)}, f32[8,8,8,128]{3,2,1,0:T(8,128)}, f32[8,8,8,128]{3,2,1,0:T(8,128)}...) conditional(s32[]{:T(128)} %bitcast.26, (f32[2,3,8,128]{3,2,1,0:T(8,128)S(1)}, ...), branch_computations={%region_4.5_spmd, %region_5.6_spmd} | conditional | flops 47104 | bytes 4333898 | solution.py:386
  184.1 3.7 %collective-permute-start.14 = (f32[2,3,8,128]{3,2,0,1:T(8,128)S(1)}, f32[2,3,8,128]{3,2,0,1:T(8,128)S(1)}, u32[]{:S(2)}, u32[]{:S(2)}) collective-permute-start(f32[2,3,8,128]{3,2,0,1:T(8,128)S(1)} %copy.20), channel_id=1, source_target_pairs={{0,16},{16,0},{32,48},{48,32},{1,17},{17,1},{33,49},{49,33},{2,18}... | collective-permute-start | bytes 73736 | tf_op jit(solution)/shard_map/cond/branch_1_fun/ppermute | solution.py:311
  189.0 3.3 %collective-permute-start.15 = (f32[2,3,8,128]{3,2,0,1:T(8,128)S(1)}, f32[2,3,8,128]{3,2,0,1:T(8,128)S(1)}, u32[]{:S(2)}, u32[]{:S(2)}) collective-permute-start(f32[2,3,8,128]{3,2,0,1:T(8,128)S(1)} %copy_add_fusion.5), channel_id=1, source_target_pairs={{0,48},{16,32},{32,16},{48,0},{1,49},{17,33},{33,17},{49,1},{2,50}... | collective-permute-start | bytes 73736 | tf_op jit(solution)/shard_map/cond/branch_1_fun/ppermute | solution.py:317
  194.8 6.3 %collective-permute-start.16 = (f32[6,8,128]{2,1,0:T(8,128)S(1)}, f32[6,8,128]{2,1,0:T(8,128)S(1)}, u32[]{:S(2)}, u32[]{:S(2)}) collective-permute-start(f32[6,8,128]{2,1,0:T(8,128)S(1)} %pad_maximum_fusion.5), channel_id=1, source_target_pairs={{0,1},{1,0},{2,3},{3,2},{4,5},{5,4},{6,7},{7,6},{8,9},{9,8},{10,11... | collective-permute-start | bytes 73736 | tf_op jit(solution)/shard_map/cond/branch_1_fun/ppermute | solution.py:311
  210.8 4.4 %collective-permute-done.18 = f32[8,6,8,128]{3,2,1,0:T(8,128)S(1)} collective-permute-done((f32[8,6,8,128]{3,2,1,0:T(8,128)S(1)}, f32[8,6,8,128]{3,2,1,0:T(8,128)S(1)}, u32[]{:S(2)}, u32[]{:S(2)}) %collective-permute-start.18) | collective-permute-done | bytes 196640 | tf_op jit(solution)/shard_map/cond/branch_1_fun/ppermute | solution.py:311
  219.9 20.2 %collective-permute-start.35 = (f32[3,8,128]{2,1,0:T(8,128)S(1)}, f32[3,8,128]{2,1,0:T(8,128)S(1)}, u32[]{:S(2)}, u32[]{:S(2)}) collective-permute-start(f32[3,8,128]{2,1,0:T(8,128)S(1)} %fusion.5), channel_id=1, source_target_pairs={{0,1},{1,0},{2,3},{3,2},{4,5},{5,4},{6,7},{7,6},{8,9},{9,8},{10,11... | collective-permute-start | bytes 36872 | tf_op jit(solution)/shard_map/ppermute | solution.py:311
  240.9 4.7 %shard_map.89 = f32[8,8,8,128]{3,2,1,0:T(8,128)} custom-call(s32[8]{0:T(128)S(1)} %stack.93.refs_0_, f32[8,8,8,128]{3,2,1,0:T(8,128)S(1)} %get-tuple-element.210.refs_1_, f32[8,8,8,128]{3,2,1,0:T(8,128)S(1)} %get-tuple-element.191.refs_1_.refs_2_, f32[8,8,128]{2,1,0:T(8,128)S(1)} %copy-done.2, s32[8,2048]{1,0:T(8,128)S(1)} %get-tuple-element.171.refs_3_.refs_4_, ...), custom_call_target="tpu_custom_call" | custom-call | flops 1500000000 | bytes 4000000 | tf_op jit(solution)/shard_map/pallas_call | solution.py:283
  (132 shorter events, 79.9 us)
Async XLA Ops:
  9.2 27.6 %collective-permute-start.22 = (f32[2,3,8,128]{3,2,1,0:T(8,128)S(1)}, f32[2,3,8,128]{3,2,1,0:T(8,128)S(1)}, u32[]{:S(2)}, u32[]{:S(2)}) collective-permute-start(f32[2,3,8,128]{3,2,1,0:T(8,128)S(1)} %select_add_fusion.2.left_ref), channel_id=1, source_target_pairs={{0,960},{64,128},{128,64},{192,256},{256,192},{320,384},{384,320},... | collective-permute-start | bytes 73736 | tf_op jit(solution)/shard_map/ppermute | solution.py:317
  34.7 37.4 %collective-permute-start.23 = (f32[8,6,8,128]{3,2,1,0:T(8,128)S(1)}, f32[8,6,8,128]{3,2,1,0:T(8,128)S(1)}, u32[]{:S(2)}, u32[]{:S(2)}) collective-permute-start(f32[8,6,8,128]{3,2,1,0:T(8,128)S(1)} %get-tuple-element.183), channel_id=1, source_target_pairs={{0,960},{64,128},{128,64},{192,256},{256,192},{320,384},{384,320},... | collective-permute-start | bytes 589832 | tf_op jit(solution)/shard_map/ppermute | solution.py:317
  47.2 12.3 %collective-permute-start.2 = (f32[6,8,128]{2,1,0:T(8,128)S(1)}, f32[6,8,128]{2,1,0:T(8,128)S(1)}, u32[]{:S(2)}, u32[]{:S(2)}) collective-permute-start(f32[6,8,128]{2,1,0:T(8,128)S(1)} %pad_maximum_fusion.1), channel_id=1, source_target_pairs={{0,1},{1,0},{2,3},{3,2},{4,5},{5,4},{6,7},{7,6},{8,9},{9,8},{10,11... | collective-permute-start | bytes 73736 | tf_op jit(solution)/shard_map/cond/branch_1_fun/ppermute | solution.py:311
  59.5 7.7 %collective-permute-start.3 = (f32[8,8,128]{2,1,0:T(8,128)S(1)}, f32[8,8,128]{2,1,0:T(8,128)S(1)}, u32[]{:S(2)}, u32[]{:S(2)}) collective-permute-start(f32[8,8,128]{2,1,0:T(8,128)S(1)} %pad_maximum_fusion), channel_id=1, source_target_pairs={{0,15},{1,2},{2,1},{3,4},{4,3},{5,6},{6,5},{7,8},{8,7},{9,10},{10,... | collective-permute-start | bytes 98312 | tf_op jit(solution)/shard_map/cond/branch_1_fun/ppermute | solution.py:317
  61.5 10.7 %collective-permute-start.6 = (f32[8,8,8,128]{3,2,1,0:T(8,128)S(1)}, f32[8,8,8,128]{3,2,1,0:T(8,128)}, u32[]{:S(2)}, u32[]{:S(2)}) collective-permute-start(f32[8,8,8,128]{3,2,1,0:T(8,128)S(1)} %get-tuple-element.84), channel_id=1, source_target_pairs={{0,48},{16,32},{32,16},{48,0},{1,49},{17,33},{33,17},{49,1},{2,50}... | collective-permute-start | bytes 786440 | tf_op jit(solution)/shard_map/cond/branch_1_fun/ppermute | solution.py:317
  63.4 8.8 %collective-permute-start.5 = (f32[8,8,8,128]{3,2,1,0:T(8,128)S(1)}, f32[8,8,8,128]{3,2,1,0:T(8,128)}, u32[]{:S(2)}, u32[]{:S(2)}) collective-permute-start(f32[8,8,8,128]{3,2,1,0:T(8,128)S(1)} %get-tuple-element.84), channel_id=1, source_target_pairs={{0,16},{16,0},{32,48},{48,32},{1,17},{17,1},{33,49},{49,33},{2,18}... | collective-permute-start | bytes 786440 | tf_op jit(solution)/shard_map/cond/branch_1_fun/ppermute | solution.py:311
  65.3 6.8 %collective-permute-start.4 = (f32[8,6,8,128]{3,2,1,0:T(8,128)S(1)}, f32[8,6,8,128]{3,2,1,0:T(8,128)S(1)}, u32[]{:S(2)}, u32[]{:S(2)}) collective-permute-start(f32[8,6,8,128]{3,2,1,0:T(8,128)S(1)} %get-tuple-element.83), channel_id=1, source_target_pairs={{0,64},{64,0},{128,192},{192,128},{256,320},{320,256},{384,448},{4... | collective-permute-start | bytes 589832 | tf_op jit(solution)/shard_map/cond/branch_1_fun/ppermute | solution.py:311
  77.1 8.9 %collective-permute-start.25 = (f32[3,8,128]{2,1,0:T(8,128)S(1)}, f32[3,8,128]{2,1,0:T(8,128)S(1)}, u32[]{:S(2)}, u32[]{:S(2)}) collective-permute-start(f32[3,8,128]{2,1,0:T(8,128)S(1)} %fusion.3), channel_id=1, source_target_pairs={{0,1},{1,0},{2,3},{3,2},{4,5},{5,4},{6,7},{7,6},{8,9},{9,8},{10,11... | collective-permute-start | bytes 36872 | tf_op jit(solution)/shard_map/ppermute | solution.py:311
  96.9 16.4 %collective-permute-start.27 = (f32[2,3,8,128]{3,2,1,0:T(8,128)S(1)}, f32[2,3,8,128]{3,2,1,0:T(8,128)S(1)}, u32[]{:S(2)}, u32[]{:S(2)}) collective-permute-start(f32[2,3,8,128]{3,2,1,0:T(8,128)S(1)} %select_add_fusion.1.left_ref), channel_id=1, source_target_pairs={{0,960},{64,128},{128,64},{192,256},{256,192},{320,384},{384,320},... | collective-permute-start | bytes 73736 | tf_op jit(solution)/shard_map/ppermute | solution.py:317
  111.4 32.4 %collective-permute-start.28 = (f32[8,6,8,128]{3,2,1,0:T(8,128)S(1)}, f32[8,6,8,128]{3,2,1,0:T(8,128)S(1)}, u32[]{:S(2)}, u32[]{:S(2)}) collective-permute-start(f32[8,6,8,128]{3,2,1,0:T(8,128)S(1)} %get-tuple-element.202), channel_id=1, source_target_pairs={{0,960},{64,128},{128,64},{192,256},{256,192},{320,384},{384,320},... | collective-permute-start | bytes 589832 | tf_op jit(solution)/shard_map/ppermute | solution.py:317
  123.9 6.6 %collective-permute-start.9 = (f32[6,8,128]{2,1,0:T(8,128)S(1)}, f32[6,8,128]{2,1,0:T(8,128)S(1)}, u32[]{:S(2)}, u32[]{:S(2)}) collective-permute-start(f32[6,8,128]{2,1,0:T(8,128)S(1)} %pad_maximum_fusion.3), channel_id=1, source_target_pairs={{0,1},{1,0},{2,3},{3,2},{4,5},{5,4},{6,7},{7,6},{8,9},{9,8},{10,11... | collective-permute-start | bytes 73736 | tf_op jit(solution)/shard_map/cond/branch_1_fun/ppermute | solution.py:311
  130.6 8.2 %collective-permute-start.10 = (f32[8,8,128]{2,1,0:T(8,128)S(1)}, f32[8,8,128]{2,1,0:T(8,128)S(1)}, u32[]{:S(2)}, u32[]{:S(2)}) collective-permute-start(f32[8,8,128]{2,1,0:T(8,128)S(1)} %pad_maximum_fusion.2), channel_id=1, source_target_pairs={{0,15},{1,2},{2,1},{3,4},{4,3},{5,6},{6,5},{7,8},{8,7},{9,10},{10,... | collective-permute-start | bytes 98312 | tf_op jit(solution)/shard_map/cond/branch_1_fun/ppermute | solution.py:317
  132.5 11.2 %collective-permute-start.13 = (f32[8,8,8,128]{3,2,1,0:T(8,128)S(1)}, f32[8,8,8,128]{3,2,1,0:T(8,128)}, u32[]{:S(2)}, u32[]{:S(2)}) collective-permute-start(f32[8,8,8,128]{3,2,1,0:T(8,128)S(1)} %get-tuple-element.98), channel_id=1, source_target_pairs={{0,48},{16,32},{32,16},{48,0},{1,49},{17,33},{33,17},{49,1},{2,50}... | collective-permute-start | bytes 786440 | tf_op jit(solution)/shard_map/cond/branch_1_fun/ppermute | solution.py:317
  134.8 8.9 %collective-permute-start.12 = (f32[8,8,8,128]{3,2,1,0:T(8,128)S(1)}, f32[8,8,8,128]{3,2,1,0:T(8,128)}, u32[]{:S(2)}, u32[]{:S(2)}) collective-permute-start(f32[8,8,8,128]{3,2,1,0:T(8,128)S(1)} %get-tuple-element.98), channel_id=1, source_target_pairs={{0,16},{16,0},{32,48},{48,32},{1,17},{17,1},{33,49},{49,33},{2,18}... | collective-permute-start | bytes 786440 | tf_op jit(solution)/shard_map/cond/branch_1_fun/ppermute | solution.py:311
  136.8 6.8 %collective-permute-start.11 = (f32[8,6,8,128]{3,2,1,0:T(8,128)S(1)}, f32[8,6,8,128]{3,2,1,0:T(8,128)S(1)}, u32[]{:S(2)}, u32[]{:S(2)}) collective-permute-start(f32[8,6,8,128]{3,2,1,0:T(8,128)S(1)} %get-tuple-element.97), channel_id=1, source_target_pairs={{0,64},{64,0},{128,192},{192,128},{256,320},{320,256},{384,448},{4... | collective-permute-start | bytes 589832 | tf_op jit(solution)/shard_map/cond/branch_1_fun/ppermute | solution.py:311
  148.3 8.7 %collective-permute-start.30 = (f32[3,8,128]{2,1,0:T(8,128)S(1)}, f32[3,8,128]{2,1,0:T(8,128)S(1)}, u32[]{:S(2)}, u32[]{:S(2)}) collective-permute-start(f32[3,8,128]{2,1,0:T(8,128)S(1)} %fusion.4), channel_id=1, source_target_pairs={{0,1},{1,0},{2,3},{3,2},{4,5},{5,4},{6,7},{7,6},{8,9},{9,8},{10,11... | collective-permute-start | bytes 36872 | tf_op jit(solution)/shard_map/ppermute | solution.py:311
  167.9 16.1 %collective-permute-start.32 = (f32[2,3,8,128]{3,2,1,0:T(8,128)S(1)}, f32[2,3,8,128]{3,2,1,0:T(8,128)S(1)}, u32[]{:S(2)}, u32[]{:S(2)}) collective-permute-start(f32[2,3,8,128]{3,2,1,0:T(8,128)S(1)} %select_add_fusion.left_ref), channel_id=1, source_target_pairs={{0,960},{64,128},{128,64},{192,256},{256,192},{320,384},{384,320},... | collective-permute-start | bytes 73736 | tf_op jit(solution)/shard_map/ppermute | solution.py:317
  181.5 33.8 %collective-permute-start.33 = (f32[8,6,8,128]{3,2,1,0:T(8,128)S(1)}, f32[8,6,8,128]{3,2,1,0:T(8,128)S(1)}, u32[]{:S(2)}, u32[]{:S(2)}) collective-permute-start(f32[8,6,8,128]{3,2,1,0:T(8,128)S(1)} %get-tuple-element.221), channel_id=1, source_target_pairs={{0,960},{64,128},{128,64},{192,256},{256,192},{320,384},{384,320},... | collective-permute-start | bytes 589832 | tf_op jit(solution)/shard_map/ppermute | solution.py:317
  194.8 7.2 %collective-permute-start.16 = (f32[6,8,128]{2,1,0:T(8,128)S(1)}, f32[6,8,128]{2,1,0:T(8,128)S(1)}, u32[]{:S(2)}, u32[]{:S(2)}) collective-permute-start(f32[6,8,128]{2,1,0:T(8,128)S(1)} %pad_maximum_fusion.5), channel_id=1, source_target_pairs={{0,1},{1,0},{2,3},{3,2},{4,5},{5,4},{6,7},{7,6},{8,9},{9,8},{10,11... | collective-permute-start | bytes 73736 | tf_op jit(solution)/shard_map/cond/branch_1_fun/ppermute | solution.py:311
  202.0 8.7 %collective-permute-start.17 = (f32[8,8,128]{2,1,0:T(8,128)S(1)}, f32[8,8,128]{2,1,0:T(8,128)S(1)}, u32[]{:S(2)}, u32[]{:S(2)}) collective-permute-start(f32[8,8,128]{2,1,0:T(8,128)S(1)} %pad_maximum_fusion.4), channel_id=1, source_target_pairs={{0,15},{1,2},{2,1},{3,4},{4,3},{5,6},{6,5},{7,8},{8,7},{9,10},{10,... | collective-permute-start | bytes 98312 | tf_op jit(solution)/shard_map/cond/branch_1_fun/ppermute | solution.py:317
  203.9 11.3 %collective-permute-start.20 = (f32[8,8,8,128]{3,2,1,0:T(8,128)S(1)}, f32[8,8,8,128]{3,2,1,0:T(8,128)}, u32[]{:S(2)}, u32[]{:S(2)}) collective-permute-start(f32[8,8,8,128]{3,2,1,0:T(8,128)S(1)} %get-tuple-element.112), channel_id=1, source_target_pairs={{0,48},{16,32},{32,16},{48,0},{1,49},{17,33},{33,17},{49,1},{2,50}... | collective-permute-start | bytes 786440 | tf_op jit(solution)/shard_map/cond/branch_1_fun/ppermute | solution.py:317
  206.8 8.4 %collective-permute-start.19 = (f32[8,8,8,128]{3,2,1,0:T(8,128)S(1)}, f32[8,8,8,128]{3,2,1,0:T(8,128)}, u32[]{:S(2)}, u32[]{:S(2)}) collective-permute-start(f32[8,8,8,128]{3,2,1,0:T(8,128)S(1)} %get-tuple-element.112), channel_id=1, source_target_pairs={{0,16},{16,0},{32,48},{48,32},{1,17},{17,1},{33,49},{49,33},{2,18}... | collective-permute-start | bytes 786440 | tf_op jit(solution)/shard_map/cond/branch_1_fun/ppermute | solution.py:311
  208.8 6.4 %collective-permute-start.18 = (f32[8,6,8,128]{3,2,1,0:T(8,128)S(1)}, f32[8,6,8,128]{3,2,1,0:T(8,128)S(1)}, u32[]{:S(2)}, u32[]{:S(2)}) collective-permute-start(f32[8,6,8,128]{3,2,1,0:T(8,128)S(1)} %get-tuple-element.111), channel_id=1, source_target_pairs={{0,64},{64,0},{128,192},{192,128},{256,320},{320,256},{384,448},{4... | collective-permute-start | bytes 589832 | tf_op jit(solution)/shard_map/cond/branch_1_fun/ppermute | solution.py:311
  219.9 21.0 %collective-permute-start.35 = (f32[3,8,128]{2,1,0:T(8,128)S(1)}, f32[3,8,128]{2,1,0:T(8,128)S(1)}, u32[]{:S(2)}, u32[]{:S(2)}) collective-permute-start(f32[3,8,128]{2,1,0:T(8,128)S(1)} %fusion.5), channel_id=1, source_target_pairs={{0,1},{1,0},{2,3},{3,2},{4,5},{5,4},{6,7},{7,6},{8,9},{9,8},{10,11... | collective-permute-start | bytes 36872 | tf_op jit(solution)/shard_map/ppermute | solution.py:311
  (19 other events, 103.5 us)

commit v4 on v3

--- a/solution.py
+++ b/solution.py
@@ -302,7 +302,7 @@
         in_specs=in_vmem(2),
         out_specs=in_vmem(1)[0],
         compiler_params=pltpu.CompilerParams(vmem_limit_bytes=VMEM_LIMIT),
-        cost_estimate=pl.CostEstimate(flops=4000000000, bytes_accessed=40000000, transcendentals=0),
+        cost_estimate=pl.CostEstimate(flops=8000000000, bytes_accessed=80000000, transcendentals=0),
     )(left, right)
 
 
@@ -345,48 +345,86 @@
         coord, orbitals, proj_values,
         point_cell.reshape(1, points), point_owner.reshape(1, points), point_slot.reshape(1, points),
     )
-    (energy,) = call(
-        lambda *refs: energy_kernel(sizes, *refs), [((SEGS, 128), F32)], [],
-        (600_000_000, 200_000), coord, atom_energy,
-    )
+    def staged(trade, share, halo_trade, halo, finish, rest, otherwise, beside=tuple):
+        come, extra = lax.optimization_barrier((trade(share), beside()))
+        share, halo = lax.optimization_barrier((share, halo))
+        arriving = halo_trade(halo)
+        after = lax.cond(some, rest, otherwise, finish(come))
+        return lax.optimization_barrier(((*after, *extra), arriving))
+
+    def zeros_like_z(pair):
+        z_face = jnp.zeros(z_shape, F32)
+        return pair[:, :2], z_face, z_face
+
+    def zeros_like_y(pair):
+        return (*zeros_like_z(pair), jnp.zeros(cells_shape, F32))
+
+    def zeros_like_x(pair):
+        return (*zeros_like_y(pair), jnp.zeros(x_shape, F32))
+
+    def zeros_like_all(pair):
+        return (*zeros_like_x(pair), jnp.zeros(x_shape, F32))
+
+    def zeros_like_first(pair):
+        *head, face = zeros_like_all(pair)
+        return (*head, jnp.zeros((SEGS, 128), F32), face)
+
+    def energies():
+        return call(
+            lambda *refs: energy_kernel(sizes, *refs), [((SEGS, 128), F32)], [],
+            (600_000_000, 200_000), coord, atom_energy,
+        )
 
     def exchange(cells, give, keep, xa, xb, za, zb, energy):
-        come = swap_inside(give, "gx").reshape(1, 3, 8, 128)
+        first = energy is None
         place = jnp.arange(2, dtype=jnp.int32)[:, None, None, None]
-        pair = keep.reshape(2, 3, 8, 128)
-        pair = pair + jnp.where(place == 1 - places[0] % 2, come, 0.0)
-        across = swap_across(pair, "gx")
-        pair, xb = lax.optimization_barrier((pair, xb))
-        xb = swap_across(xb, "gx")
-        pair = total(pair, across)
-        pair, energy = lax.optimization_barrier((pair, energy))
-
-        def along_yz(pair, cells, xa, za, zb):
-            pair = pair + swap_inside(pair, "gy")
-            pair = pair + swap_across(pair, "gy")
+
+        def along_z(pair):
             come = swap_inside(
                 jnp.concatenate([jnp.where(odd_z, pair[:, 0], pair[:, 2]), za], axis=0), "gz"
             )
-            za = come[2:]
             middle = pair[:, 1] + come[:2]
             own = jnp.where(
                 odd_z,
                 jnp.stack([middle, pair[:, 2]], axis=1),
                 jnp.stack([pair[:, 0], middle], axis=1),
             )
-            own, cells, xa = lax.optimization_barrier((own, cells, xa))
-            come = swap_across(jnp.concatenate([own.reshape(4, 8, 128), zb], axis=0), "gz")
-            ya, yb = swap_inside(cells, "gy"), swap_across(cells, "gy")
-            xa = swap_inside(xa, "gx")
-            return own + come[:4].reshape(2, 2, 8, 128), xa, ya, yb, za, come[4:]
-
-        def untouched(pair, cells, xa, za, zb):
-            return pair[:, :2], xa, cells, cells, za, zb
-
-        own, xa, ya, yb, za, zb = lax.cond(
-            some, along_yz, untouched, pair, cells, xa, za, zb
+            far = swap_across(jnp.concatenate([own.reshape(4, 8, 128), zb], axis=0), "gz")
+            return own + far[:4].reshape(2, 2, 8, 128), come[2:], far[4:]
+
+        def along_y_across(pair):
+            (own, za_in, zb_in), yb_in = staged(
+                lambda v: swap_across(v, "gy"), pair, lambda v: swap_across(v, "gy"), cells,
+                lambda come: total(pair, come), along_z, zeros_like_z,
+            )
+            return own, za_in, zb_in, yb_in
+
+        def along_y_inside(pair):
+            rest, xa_in = staged(
+                lambda v: swap_inside(v, "gy"), pair, lambda v: swap_inside(v, "gx"), xa,
+                lambda come: total(pair, come), along_y_across, zeros_like_y,
+            )
+            return (*rest, xa_in)
+
+        def along_x_across(pair):
+            rest, xb_in = staged(
+                lambda v: swap_across(v, "gx"), pair, lambda v: swap_across(v, "gx"), xb,
+                lambda come: total(pair, come), along_y_inside, zeros_like_x,
+                energies if first else tuple,
+            )
+            return (*rest, xb_in)
+
+        rest, ya_in = staged(
+            lambda v: swap_inside(v, "gx"), give, lambda v: swap_inside(v, "gy"), cells,
+            lambda come: total(
+                keep.reshape(2, 3, 8, 128),
+                jnp.where(place == 1 - places[0] % 2, come.reshape(1, 3, 8, 128), 0.0),
+            ),
+            along_x_across, zeros_like_first if first else zeros_like_all,
         )
-        own, xb = lax.optimization_barrier((own, xb))
+        own, za, zb, yb, xa, *made, xb = rest
+        energy = made[0] if first else energy
+        ya = ya_in
 
         beyond_x = swap_inside(jnp.where(odd_x, own[0], own[1]), "gx")
         rows = jnp.where(
@@ -403,7 +441,7 @@
     middle = (highest + cutoff) / 2.0
     sigma_first = half_width / (lowest - middle)
     sigma_now = sigma_first
-    previous, current = None, orbitals
+    previous, current, energy = None, orbitals, None
     scratch = [
         pltpu.VMEM((ROWS, DEPTH), F32),
         pltpu.VMEM((ROWS, DEPTH), F32),
@@ -419,6 +457,7 @@
             sigma_now = sigma_next
         last = degree_index == DEGREE - 1
         came = exchange(current, *sends, energy)
+        energy = came[0]
         before = [] if previous is None else [previous]
         results = call(
             lambda *refs, scales=scales, last=last: step_kernel(scales, last, *refs),

time: 247 us -> 230 us (0.931)
  waiting for transfers between devices: 43.9 us -> 21.3 us
  local copies, waits for them, and re-layouts: 0.84 us -> 9.21 us
  starting transfers between devices: 175 us -> 169 us
    ppermute x21, waiting for transfers between devices: 36.5 us -> 8.88 us  [swap_inside(): return lax.ppermute(value, axis, [(i, i ^ 1) for i in range(count)])]
    ppermute x21, starting transfers between devices: 96 us -> 88.3 us  [swap_inside(): return lax.ppermute(value, axis, [(i, i ^ 1) for i in range(count)])]
    ppermute x15, waiting for transfers between devices: 7.43 us -> 12.4 us  [swap_across(): return lax.ppermute(value, axis, pairs)]
    slice x6, local copies, waits for them, and re-layouts: 0.02 us -> 3.6 us  [along_z(): return (own + far[:4].reshape(2, 2, 8, 128), come[2:], far[4:])]
  transfers between devices with their start and end apart: 36 -> 36, of which waited for: 21 -> 15; matrix products, arithmetic and copies ran while one was open for 0% -> 3% of each run, Pallas kernels for 1% -> 1%
where the time goes in v4:
time: 230 us; the launch traced here: 228 us
  starting transfers between devices  169 us (73%)
  Pallas kernels  23.8 us (10%)
  waiting for transfers between devices  21.3 us (9%)
  local copies, waits for them, and re-layouts  9.21 us (4%)
  other arithmetic  2.51 us (1%)
    ppermute x21, starting transfers between devices, swap_inside(): return lax.ppermute(value, axis, [(i, i ^ 1) for i in range(count)])  88.3 us
    ppermute x15, starting transfers between devices, swap_across(): return lax.ppermute(value, axis, pairs)  81.1 us
    pallas_call x5, Pallas kernels, call(): pl.pallas_call(kernel, out_shape=[jax.ShapeDtypeStruct(s, k) for s, k in...  23.7 us
    ppermute x15, waiting for transfers between devices, swap_across(): return lax.ppermute(value, axis, pairs)  12.4 us
    ppermute x21, waiting for transfers between devices, swap_inside(): return lax.ppermute(value, axis, [(i, i ^ 1) for i in range(count)])  8.88 us
  transfers between devices with their start and end apart: 36, of which 15 were waited for; matrix products, arithmetic and copies ran while one was open for 3% of the time, Pallas kernels for 1%

profile of v4, /device:TPU:1, one launch (start us, length us, event | category | flops | bytes accessed | tf_op | source)
XLA Modules:
  0.0 227.8 jit_solution(2050031622557684853)
XLA Ops:
  12.3 54.9 %conditional.12 = (f32[2,2,8,128]{3,2,1,0:T(8,128)}, f32[4,8,128]{2,1,0:T(8,128)}, f32[4,8,128]{2,1,0:T(8,128)}, f32[8,8,8,128]{3,2,1,0:T(8,128)}, f32[8,6,8,128...) conditional(s32[]{:T(128)} %convert_element_type.32, ...), branch_computations={%region_0.1_spmd, %region_1.8_spmd} | conditional | flops 24600047616 | bytes 243788704 | solution.py:352
  12.3 21.7 %collective-permute-start.6 = (f32[2,3,8,128]{3,2,1,0:T(8,128)S(1)}, f32[2,3,8,128]{3,2,1,0:T(8,128)S(1)}, u32[]{:S(2)}, u32[]{:S(2)}) collective-permute-start(f32[2,3,8,128]{3,2,1,0:T(8,128)S(1)} %get-tuple-element.198.left_ref), channel_id=1, source_target_pairs={{0,960},{64,128},{128,64},{192,256},{256,192},{320,384},{384,320},... | collective-permute-start | bytes 73736 | tf_op jit(solution)/shard_map/cond/branch_1_fun/ppermute | solution.py:317
  39.3 27.9 %conditional.2 = (f32[2,2,8,128]{3,2,1,0:T(8,128)}, f32[4,8,128]{2,1,0:T(8,128)}, f32[4,8,128]{2,1,0:T(8,128)}, f32[8,8,8,128]{3,2,1,0:T(8,128)}, f32[8,6,8,128]{3,2,1,0:T(8,128)}) conditional(s32[]{:T(128)} %convert_element_type.24, f32[2,3,8,128]{3,2,1,0:T(8,128)S(1)} %branch_1_fun.13, (pred[]{:T(512)}, f32[2,3,8,128]{3,2,1,0:T(8,128)S(1)}, ...), branch_computations={%region_2.2_spmd, %region_3.7_spmd} | conditional | flops 16000047104 | bytes 162703776 | solution.py:352
  43.9 23.3 %conditional.1 = (f32[2,2,8,128]{3,2,1,0:T(8,128)}, f32[4,8,128]{2,1,0:T(8,128)}, f32[4,8,128]{2,1,0:T(8,128)}, f32[8,8,8,128]{3,2,1,0:T(8,128)}) conditional(s32[]{:T(128)} %convert_element_type.15, f32[2,3,8,128]{3,2,1,0:T(8,128)S(1)} %branch_1_fun.11, (pred[]{:T(512)}, f32[2,3,8,128]{3,2,1,0:T(8,128)S(1)}, pred[]{:T(512)}, ...), branch_computations={%region_4.3_spmd, %region_5.6_spmd} | conditional | flops 8000047104 | bytes 81818880 | solution.py:352
  50.4 16.8 %conditional = (f32[2,2,8,128]{3,2,1,0:T(8,128)}, f32[4,8,128]{2,1,0:T(8,128)}, f32[4,8,128]{2,1,0:T(8,128)}) conditional(s32[]{:T(128)} %convert_element_type.14, f32[2,3,8,128]{3,2,1,0:T(8,128)S(1)} %branch_1_fun.10, (pred[]{:T(512)}, f32[2,3,8,128]{3,2,1,0:T(8,128)S(1)}, f32[4,8,128]{2,1,0:T(8,128)S(1)}, f32[4,8,128]{2,1,0:T(8,128)S(1)}) %tuple.70), branch_computations={%region_6.4_spmd, %region_7.5_spmd} | conditional | flops 47104 | bytes 671851 | solution.py:352
  50.5 9.1 %collective-permute-start = (f32[6,8,128]{2,1,0:T(8,128)S(1)}, f32[6,8,128]{2,1,0:T(8,128)S(1)}, u32[]{:S(2)}, u32[]{:S(2)}) collective-permute-start(f32[6,8,128]{2,1,0:T(8,128)S(1)} %pad_maximum_fusion.1), channel_id=1, source_target_pairs={{0,1},{1,0},{2,3},{3,2},{4,5},{5,4},{6,7},{7,6},{8,9},{9,8},{10,11... | collective-permute-start | bytes 73736 | tf_op jit(solution)/shard_map/cond/branch_1_fun/cond/branch_1_fun/cond/branch_1_fun/cond/branch_1_fun/ppermute | solution.py:311
  72.3 9.7 %collective-permute-start.27 = (f32[3,8,128]{2,1,0:T(8,128)S(1)}, f32[3,8,128]{2,1,0:T(8,128)S(1)}, u32[]{:S(2)}, u32[]{:S(2)}) collective-permute-start(f32[3,8,128]{2,1,0:T(8,128)S(1)} %fusion.3), channel_id=1, source_target_pairs={{0,1},{1,0},{2,3},{3,2},{4,5},{5,4},{6,7},{7,6},{8,9},{9,8},{10,11... | collective-permute-start | bytes 36872 | tf_op jit(solution)/shard_map/ppermute | solution.py:311
  82.9 6.5 %shard_map.85 = (f32[8,8,8,128]{3,2,1,0:T(8,128)S(1)}, f32[24,128]{1,0:T(8,128)S(1)}, f32[48,128]{1,0:T(8,128)S(1)}, f32[8,6,8,128]{3,2,1,0:T(8,128)S(1)}, f32[8...) custom-call(s32[8]{0:T(128)S(1)} %stack.93.refs_0_, f32[8,8,8,128]{3,2,1,0:T(8,128)S(1)} %copy-done.5, ...), custom_call_target="tpu_custom_call" | custom-call | flops 1500000000 | bytes 4000000 | tf_op jit(solution)/shard_map/pallas_call | solution.py:283
  93.9 40.4 %conditional.13 = (f32[2,2,8,128]{3,2,1,0:T(8,128)}, f32[4,8,128]{2,1,0:T(8,128)}, f32[4,8,128]{2,1,0:T(8,128)}, f32[8,8,8,128]{3,2,1,0:T(8,128)}, f32[8,6,8,128]{3,2,1,0:T(8,128)}, /*index=5*/f32[8,6,8,128]{3,2,1,0:T(8,128)}) conditional(s32[]{:T(128)} %convert_element_type.32, f32[2,3,8,128]{3,2,1,0:T(8,128)S(1)} %shard_map.86, (pred[]{:T(512)}, ...), branch_computations={%region_8.9_spmd, %region_9.16_spmd} | conditional | flops 24000047104 | bytes 243588688 | solution.py:352
  93.9 10.5 %collective-permute-start.14 = (f32[2,3,8,128]{3,2,1,0:T(8,128)S(1)}, f32[2,3,8,128]{3,2,1,0:T(8,128)S(1)}, u32[]{:S(2)}, u32[]{:S(2)}) collective-permute-start(f32[2,3,8,128]{3,2,1,0:T(8,128)S(1)} %get-tuple-element.242.left_ref), channel_id=1, source_target_pairs={{0,960},{64,128},{128,64},{192,256},{256,192},{320,384},{384,320},... | collective-permute-start | bytes 73736 | tf_op jit(solution)/shard_map/cond/branch_1_fun/ppermute | solution.py:317
  104.4 5.6 %collective-permute-start.15 = (f32[8,6,8,128]{3,2,1,0:T(8,128)S(1)}, f32[8,6,8,128]{3,2,1,0:T(8,128)}, u32[]{:S(2)}, u32[]{:S(2)}) collective-permute-start(f32[8,6,8,128]{3,2,1,0:T(8,128)S(1)} %get-tuple-element.254), channel_id=1, source_target_pairs={{0,960},{64,128},{128,64},{192,256},{256,192},{320,384},{384,320},... | collective-permute-start | bytes 589832 | tf_op jit(solution)/shard_map/cond/branch_1_fun/ppermute | solution.py:317
  110.1 24.3 %conditional.5 = (f32[2,2,8,128]{3,2,1,0:T(8,128)}, f32[4,8,128]{2,1,0:T(8,128)}, f32[4,8,128]{2,1,0:T(8,128)}, f32[8,8,8,128]{3,2,1,0:T(8,128)}, f32[8,6,8,128]{3,2,1,0:T(8,128)}) conditional(s32[]{:T(128)} %convert_element_type.27, f32[2,3,8,128]{3,2,1,0:T(8,128)S(1)} %branch_1_fun.16, (pred[]{:T(512)}, f32[2,3,8,128]{3,2,1,0:T(8,128)S(1)}, ...), branch_computations={%region_10.10_spmd, %region_11.15_spmd} | conditional | flops 16000047104 | bytes 162703776 | solution.py:352
  115.2 19.1 %conditional.4 = (f32[2,2,8,128]{3,2,1,0:T(8,128)}, f32[4,8,128]{2,1,0:T(8,128)}, f32[4,8,128]{2,1,0:T(8,128)}, f32[8,8,8,128]{3,2,1,0:T(8,128)}) conditional(s32[]{:T(128)} %convert_element_type.26, f32[2,3,8,128]{3,2,1,0:T(8,128)S(1)} %branch_1_fun.15, (pred[]{:T(512)}, f32[2,3,8,128]{3,2,1,0:T(8,128)S(1)}, pred[]{:T(512)}, ...), branch_computations={%region_12.11_spmd, %region_13.14_spmd} | conditional | flops 8000047104 | bytes 81818880 | solution.py:352
  121.8 12.5 %conditional.3 = (f32[2,2,8,128]{3,2,1,0:T(8,128)}, f32[4,8,128]{2,1,0:T(8,128)}, f32[4,8,128]{2,1,0:T(8,128)}) conditional(s32[]{:T(128)} %convert_element_type.25, f32[2,3,8,128]{3,2,1,0:T(8,128)S(1)} %branch_1_fun.14, (pred[]{:T(512)}, f32[2,3,8,128]{3,2,1,0:T(8,128)S(1)}, f32[4,8,128]{2,1,0:T(8,128)S(1)}, f32[4,8,128]{2,1,0:T(8,128)S(1)}) %tuple.85), branch_computations={%region_14.12_spmd, %region_15.13_spmd} | conditional | flops 47104 | bytes 671851 | solution.py:352
  121.8 5.2 %collective-permute-start.8 = (f32[6,8,128]{2,1,0:T(8,128)S(1)}, f32[6,8,128]{2,1,0:T(8,128)S(1)}, u32[]{:S(2)}, u32[]{:S(2)}) collective-permute-start(f32[6,8,128]{2,1,0:T(8,128)S(1)} %pad_maximum_fusion.3), channel_id=1, source_target_pairs={{0,1},{1,0},{2,3},{3,2},{4,5},{5,4},{6,7},{7,6},{8,9},{9,8},{10,11... | collective-permute-start | bytes 73736 | tf_op jit(solution)/shard_map/cond/branch_1_fun/cond/branch_1_fun/cond/branch_1_fun/cond/branch_1_fun/ppermute | solution.py:311
  139.7 12.5 %collective-permute-start.31 = (f32[3,8,128]{2,1,0:T(8,128)S(1)}, f32[3,8,128]{2,1,0:T(8,128)S(1)}, u32[]{:S(2)}, u32[]{:S(2)}) collective-permute-start(f32[3,8,128]{2,1,0:T(8,128)S(1)} %fusion.4), channel_id=1, source_target_pairs={{0,1},{1,0},{2,3},{3,2},{4,5},{5,4},{6,7},{7,6},{8,9},{9,8},{10,11... | collective-permute-start | bytes 36872 | tf_op jit(solution)/shard_map/ppermute | solution.py:311
  152.9 6.5 %shard_map.87 = (f32[8,8,8,128]{3,2,1,0:T(8,128)S(1)}, f32[24,128]{1,0:T(8,128)S(1)}, f32[48,128]{1,0:T(8,128)S(1)}, f32[8,6,8,128]{3,2,1,0:T(8,128)S(1)}, f32[8...) custom-call(s32[8]{0:T(128)S(1)} %stack.93.refs_0_, ...), custom_call_target="tpu_custom_call" | custom-call | flops 1500000000 | bytes 4000000 | tf_op jit(solution)/shard_map/pallas_call | solution.py:283
  164.4 42.7 %conditional.14 = (f32[2,2,8,128]{3,2,1,0:T(8,128)}, f32[4,8,128]{2,1,0:T(8,128)}, f32[4,8,128]{2,1,0:T(8,128)}, f32[8,8,8,128]{3,2,1,0:T(8,128)}, f32[8,6,8,128]{3,2,1,0:T(8,128)}, /*index=5*/f32[8,6,8,128]{3,2,1,0:T(8,128)}) conditional(s32[]{:T(128)} %convert_element_type.32, f32[2,3,8,128]{3,2,1,0:T(8,128)S(1)} %shard_map.88, (pred[]{:T(512)}, ...), branch_computations={%region_16.17_spmd, %region_17.24_spmd} | conditional | flops 24000047104 | bytes 243588688 | solution.py:352
  164.4 13.1 %collective-permute-start.22 = (f32[2,3,8,128]{3,2,1,0:T(8,128)S(1)}, f32[2,3,8,128]{3,2,1,0:T(8,128)S(1)}, u32[]{:S(2)}, u32[]{:S(2)}) collective-permute-start(f32[2,3,8,128]{3,2,1,0:T(8,128)S(1)} %get-tuple-element.282.left_ref), channel_id=1, source_target_pairs={{0,960},{64,128},{128,64},{192,256},{256,192},{320,384},{384,320},... | collective-permute-start | bytes 73736 | tf_op jit(solution)/shard_map/cond/branch_1_fun/ppermute | solution.py:317
  184.5 22.6 %conditional.8 = (f32[2,2,8,128]{3,2,1,0:T(8,128)}, f32[4,8,128]{2,1,0:T(8,128)}, f32[4,8,128]{2,1,0:T(8,128)}, f32[8,8,8,128]{3,2,1,0:T(8,128)}, f32[8,6,8,128]{3,2,1,0:T(8,128)}) conditional(s32[]{:T(128)} %convert_element_type.30, f32[2,3,8,128]{3,2,1,0:T(8,128)S(1)} %branch_1_fun.19, (pred[]{:T(512)}, f32[2,3,8,128]{3,2,1,0:T(8,128)S(1)}, ...), branch_computations={%region_18.18_spmd, %region_19.23_spmd} | conditional | flops 16000047104 | bytes 162703776 | solution.py:352
  189.6 17.5 %conditional.7 = (f32[2,2,8,128]{3,2,1,0:T(8,128)}, f32[4,8,128]{2,1,0:T(8,128)}, f32[4,8,128]{2,1,0:T(8,128)}, f32[8,8,8,128]{3,2,1,0:T(8,128)}) conditional(s32[]{:T(128)} %convert_element_type.29, f32[2,3,8,128]{3,2,1,0:T(8,128)S(1)} %branch_1_fun.18, (pred[]{:T(512)}, f32[2,3,8,128]{3,2,1,0:T(8,128)S(1)}, pred[]{:T(512)}, ...), branch_computations={%region_20.19_spmd, %region_21.22_spmd} | conditional | flops 8000047104 | bytes 81818880 | solution.py:352
  196.1 10.9 %conditional.6 = (f32[2,2,8,128]{3,2,1,0:T(8,128)}, f32[4,8,128]{2,1,0:T(8,128)}, f32[4,8,128]{2,1,0:T(8,128)}) conditional(s32[]{:T(128)} %convert_element_type.28, f32[2,3,8,128]{3,2,1,0:T(8,128)S(1)} %branch_1_fun.17, (pred[]{:T(512)}, f32[2,3,8,128]{3,2,1,0:T(8,128)S(1)}, f32[4,8,128]{2,1,0:T(8,128)S(1)}, f32[4,8,128]{2,1,0:T(8,128)S(1)}) %tuple.99), branch_computations={%region_22.20_spmd, %region_23.21_spmd} | conditional | flops 47104 | bytes 671851 | solution.py:352
  212.4 9.8 %collective-permute-start.35 = (f32[3,8,128]{2,1,0:T(8,128)S(1)}, f32[3,8,128]{2,1,0:T(8,128)S(1)}, u32[]{:S(2)}, u32[]{:S(2)}) collective-permute-start(f32[3,8,128]{2,1,0:T(8,128)S(1)} %fusion.5), channel_id=1, source_target_pairs={{0,1},{1,0},{2,3},{3,2},{4,5},{5,4},{6,7},{7,6},{8,9},{9,8},{10,11... | collective-permute-start | bytes 36872 | tf_op jit(solution)/shard_map/ppermute | solution.py:311
  223.0 4.7 %shard_map.89 = f32[8,8,8,128]{3,2,1,0:T(8,128)} custom-call(s32[8]{0:T(128)S(1)} %stack.93.refs_0_, f32[8,8,8,128]{3,2,1,0:T(8,128)S(1)} %get-tuple-element.419.refs_1_, f32[8,8,8,128]{3,2,1,0:T(8,128)S(1)} %get-tuple-element.398.refs_1_.refs_2_, f32[8,8,128]{2,1,0:T(8,128)S(1)} %copy-done.1, s32[8,2048]{1,0:T(8,128)S(1)} %get-tuple-element.361.refs_3_.refs_4_, ...), custom_call_target="tpu_custom_call" | custom-call | flops 1500000000 | bytes 4000000 | tf_op jit(solution)/shard_map/pallas_call | solution.py:283
  (138 shorter events, 111.3 us)
Async XLA Ops:
  4.1 7.2 %collective-permute-start.24 = (f32[24,128]{1,0:T(8,128)S(1)}, f32[24,128]{1,0:T(8,128)S(1)}, u32[]{:S(2)}, u32[]{:S(2)}) collective-permute-start(f32[24,128]{1,0:T(8,128)S(1)} %get-tuple-element.364), channel_id=1, source_target_pairs={{0,64},{64,0},{128,192},{192,128},{256,320},{320,256},{384,448},{4... | collective-permute-start | bytes 36872 | tf_op jit(solution)/shard_map/ppermute | solution.py:311
  8.1 59.1 %collective-permute-start.25 = (f32[8,8,8,128]{3,2,1,0:T(8,128)S(1)}, f32[8,8,8,128]{3,2,1,0:T(8,128)S(1)}, u32[]{:S(2)}, u32[]{:S(2)}) collective-permute-start(f32[8,8,8,128]{3,2,1,0:T(8,128)S(1)} %copy-done.5), channel_id=1, source_target_pairs={{0,16},{16,0},{32,48},{48,32},{1,17},{17,1},{33,49},{49,33},{2,18}... | collective-permute-start | bytes 786440 | tf_op jit(solution)/shard_map/ppermute | solution.py:311
  12.3 27.0 %collective-permute-start.6 = (f32[2,3,8,128]{3,2,1,0:T(8,128)S(1)}, f32[2,3,8,128]{3,2,1,0:T(8,128)S(1)}, u32[]{:S(2)}, u32[]{:S(2)}) collective-permute-start(f32[2,3,8,128]{3,2,1,0:T(8,128)S(1)} %get-tuple-element.198.left_ref), channel_id=1, source_target_pairs={{0,960},{64,128},{128,64},{192,256},{256,192},{320,384},{384,320},... | collective-permute-start | bytes 73736 | tf_op jit(solution)/shard_map/cond/branch_1_fun/ppermute | solution.py:317
  34.0 33.2 %collective-permute-start.7 = (f32[8,6,8,128]{3,2,1,0:T(8,128)S(1)}, f32[8,6,8,128]{3,2,1,0:T(8,128)}, u32[]{:S(2)}, u32[]{:S(2)}) collective-permute-start(f32[8,6,8,128]{3,2,1,0:T(8,128)S(1)} %get-tuple-element.214), channel_id=1, source_target_pairs={{0,960},{64,128},{128,64},{192,256},{256,192},{320,384},{384,320},... | collective-permute-start | bytes 589832 | tf_op jit(solution)/shard_map/cond/branch_1_fun/ppermute | solution.py:317
  41.5 25.7 %collective-permute-start.5 = (f32[8,6,8,128]{3,2,1,0:T(8,128)S(1)}, f32[8,6,8,128]{3,2,1,0:T(8,128)}, u32[]{:S(2)}, u32[]{:S(2)}) collective-permute-start(f32[8,6,8,128]{3,2,1,0:T(8,128)S(1)} %get-tuple-element.196), channel_id=1, source_target_pairs={{0,64},{64,0},{128,192},{192,128},{256,320},{320,256},{384,448},{4... | collective-permute-start | bytes 589832 | tf_op jit(solution)/shard_map/cond/branch_1_fun/cond/branch_1_fun/ppermute | solution.py:311
  43.9 6.5 %collective-permute-start.2 = (f32[2,3,8,128]{3,2,1,0:T(8,128)S(1)}, f32[2,3,8,128]{3,2,1,0:T(8,128)S(1)}, u32[]{:S(2)}, u32[]{:S(2)}) collective-permute-start(f32[2,3,8,128]{3,2,1,0:T(8,128)S(1)} %get-tuple-element.176.left_ref), channel_id=1, source_target_pairs={{0,48},{16,32},{32,16},{48,0},{1,49},{17,33},{33,17},{49,1},{2,50}... | collective-permute-start | bytes 73736 | tf_op jit(solution)/shard_map/cond/branch_1_fun/cond/branch_1_fun/cond/branch_1_fun/ppermute | solution.py:317
  47.9 19.3 %collective-permute-start.3 = (f32[8,8,8,128]{3,2,1,0:T(8,128)S(1)}, f32[8,8,8,128]{3,2,1,0:T(8,128)}, u32[]{:S(2)}, u32[]{:S(2)}) collective-permute-start(f32[8,8,8,128]{3,2,1,0:T(8,128)S(1)} %get-tuple-element.184), channel_id=1, source_target_pairs={{0,48},{16,32},{32,16},{48,0},{1,49},{17,33},{33,17},{49,1},{2,50}... | collective-permute-start | bytes 786440 | tf_op jit(solution)/shard_map/cond/branch_1_fun/cond/branch_1_fun/cond/branch_1_fun/ppermute | solution.py:317
  50.5 10.0 %collective-permute-start = (f32[6,8,128]{2,1,0:T(8,128)S(1)}, f32[6,8,128]{2,1,0:T(8,128)S(1)}, u32[]{:S(2)}, u32[]{:S(2)}) collective-permute-start(f32[6,8,128]{2,1,0:T(8,128)S(1)} %pad_maximum_fusion.1), channel_id=1, source_target_pairs={{0,1},{1,0},{2,3},{3,2},{4,5},{5,4},{6,7},{7,6},{8,9},{9,8},{10,11... | collective-permute-start | bytes 73736 | tf_op jit(solution)/shard_map/cond/branch_1_fun/cond/branch_1_fun/cond/branch_1_fun/cond/branch_1_fun/ppermute | solution.py:311
  72.3 10.6 %collective-permute-start.27 = (f32[3,8,128]{2,1,0:T(8,128)S(1)}, f32[3,8,128]{2,1,0:T(8,128)S(1)}, u32[]{:S(2)}, u32[]{:S(2)}) collective-permute-start(f32[3,8,128]{2,1,0:T(8,128)S(1)} %fusion.3), channel_id=1, source_target_pairs={{0,1},{1,0},{2,3},{3,2},{4,5},{5,4},{6,7},{7,6},{8,9},{9,8},{10,11... | collective-permute-start | bytes 36872 | tf_op jit(solution)/shard_map/ppermute | solution.py:311
  91.7 42.7 %collective-permute-start.29 = (f32[8,8,8,128]{3,2,1,0:T(8,128)S(1)}, f32[8,8,8,128]{3,2,1,0:T(8,128)S(1)}, u32[]{:S(2)}, u32[]{:S(2)}) collective-permute-start(f32[8,8,8,128]{3,2,1,0:T(8,128)S(1)} %get-tuple-element.398.refs_1_.refs_2_), channel_id=1, source_target_pairs={{0,16},{16,0},{32,48},{48,32},{1,17},{17,1},{33,49},{49,33},{2,18}... | collective-permute-start | bytes 786440 | tf_op jit(solution)/shard_map/ppermute | solution.py:311
  93.9 16.1 %collective-permute-start.14 = (f32[2,3,8,128]{3,2,1,0:T(8,128)S(1)}, f32[2,3,8,128]{3,2,1,0:T(8,128)S(1)}, u32[]{:S(2)}, u32[]{:S(2)}) collective-permute-start(f32[2,3,8,128]{3,2,1,0:T(8,128)S(1)} %get-tuple-element.242.left_ref), channel_id=1, source_target_pairs={{0,960},{64,128},{128,64},{192,256},{256,192},{320,384},{384,320},... | collective-permute-start | bytes 73736 | tf_op jit(solution)/shard_map/cond/branch_1_fun/ppermute | solution.py:317
  104.4 29.9 %collective-permute-start.15 = (f32[8,6,8,128]{3,2,1,0:T(8,128)S(1)}, f32[8,6,8,128]{3,2,1,0:T(8,128)}, u32[]{:S(2)}, u32[]{:S(2)}) collective-permute-start(f32[8,6,8,128]{3,2,1,0:T(8,128)S(1)} %get-tuple-element.254), channel_id=1, source_target_pairs={{0,960},{64,128},{128,64},{192,256},{256,192},{320,384},{384,320},... | collective-permute-start | bytes 589832 | tf_op jit(solution)/shard_map/cond/branch_1_fun/ppermute | solution.py:317
  113.3 21.1 %collective-permute-start.13 = (f32[8,6,8,128]{3,2,1,0:T(8,128)S(1)}, f32[8,6,8,128]{3,2,1,0:T(8,128)}, u32[]{:S(2)}, u32[]{:S(2)}) collective-permute-start(f32[8,6,8,128]{3,2,1,0:T(8,128)S(1)} %get-tuple-element.240), channel_id=1, source_target_pairs={{0,64},{64,0},{128,192},{192,128},{256,320},{320,256},{384,448},{4... | collective-permute-start | bytes 589832 | tf_op jit(solution)/shard_map/cond/branch_1_fun/cond/branch_1_fun/ppermute | solution.py:311
  115.2 6.5 %collective-permute-start.10 = (f32[2,3,8,128]{3,2,1,0:T(8,128)S(1)}, f32[2,3,8,128]{3,2,1,0:T(8,128)S(1)}, u32[]{:S(2)}, u32[]{:S(2)}) collective-permute-start(f32[2,3,8,128]{3,2,1,0:T(8,128)S(1)} %get-tuple-element.220.left_ref), channel_id=1, source_target_pairs={{0,48},{16,32},{32,16},{48,0},{1,49},{17,33},{33,17},{49,1},{2,50}... | collective-permute-start | bytes 73736 | tf_op jit(solution)/shard_map/cond/branch_1_fun/cond/branch_1_fun/cond/branch_1_fun/ppermute | solution.py:317
  117.2 17.2 %collective-permute-start.11 = (f32[8,8,8,128]{3,2,1,0:T(8,128)S(1)}, f32[8,8,8,128]{3,2,1,0:T(8,128)}, u32[]{:S(2)}, u32[]{:S(2)}) collective-permute-start(f32[8,8,8,128]{3,2,1,0:T(8,128)S(1)} %get-tuple-element.228), channel_id=1, source_target_pairs={{0,48},{16,32},{32,16},{48,0},{1,49},{17,33},{33,17},{49,1},{2,50}... | collective-permute-start | bytes 786440 | tf_op jit(solution)/shard_map/cond/branch_1_fun/cond/branch_1_fun/cond/branch_1_fun/ppermute | solution.py:317
  121.8 6.0 %collective-permute-start.8 = (f32[6,8,128]{2,1,0:T(8,128)S(1)}, f32[6,8,128]{2,1,0:T(8,128)S(1)}, u32[]{:S(2)}, u32[]{:S(2)}) collective-permute-start(f32[6,8,128]{2,1,0:T(8,128)S(1)} %pad_maximum_fusion.3), channel_id=1, source_target_pairs={{0,1},{1,0},{2,3},{3,2},{4,5},{5,4},{6,7},{7,6},{8,9},{9,8},{10,11... | collective-permute-start | bytes 73736 | tf_op jit(solution)/shard_map/cond/branch_1_fun/cond/branch_1_fun/cond/branch_1_fun/cond/branch_1_fun/ppermute | solution.py:311
  139.7 13.1 %collective-permute-start.31 = (f32[3,8,128]{2,1,0:T(8,128)S(1)}, f32[3,8,128]{2,1,0:T(8,128)S(1)}, u32[]{:S(2)}, u32[]{:S(2)}) collective-permute-start(f32[3,8,128]{2,1,0:T(8,128)S(1)} %fusion.4), channel_id=1, source_target_pairs={{0,1},{1,0},{2,3},{3,2},{4,5},{5,4},{6,7},{7,6},{8,9},{9,8},{10,11... | collective-permute-start | bytes 36872 | tf_op jit(solution)/shard_map/ppermute | solution.py:311
  162.3 44.8 %collective-permute-start.33 = (f32[8,8,8,128]{3,2,1,0:T(8,128)S(1)}, f32[8,8,8,128]{3,2,1,0:T(8,128)S(1)}, u32[]{:S(2)}, u32[]{:S(2)}) collective-permute-start(f32[8,8,8,128]{3,2,1,0:T(8,128)S(1)} %get-tuple-element.419.refs_1_), channel_id=1, source_target_pairs={{0,16},{16,0},{32,48},{48,32},{1,17},{17,1},{33,49},{49,33},{2,18}... | collective-permute-start | bytes 786440 | tf_op jit(solution)/shard_map/ppermute | solution.py:311
  164.4 20.1 %collective-permute-start.22 = (f32[2,3,8,128]{3,2,1,0:T(8,128)S(1)}, f32[2,3,8,128]{3,2,1,0:T(8,128)S(1)}, u32[]{:S(2)}, u32[]{:S(2)}) collective-permute-start(f32[2,3,8,128]{3,2,1,0:T(8,128)S(1)} %get-tuple-element.282.left_ref), channel_id=1, source_target_pairs={{0,960},{64,128},{128,64},{192,256},{256,192},{320,384},{384,320},... | collective-permute-start | bytes 73736 | tf_op jit(solution)/shard_map/cond/branch_1_fun/ppermute | solution.py:317
  177.5 29.6 %collective-permute-start.23 = (f32[8,6,8,128]{3,2,1,0:T(8,128)S(1)}, f32[8,6,8,128]{3,2,1,0:T(8,128)}, u32[]{:S(2)}, u32[]{:S(2)}) collective-permute-start(f32[8,6,8,128]{3,2,1,0:T(8,128)S(1)} %get-tuple-element.294), channel_id=1, source_target_pairs={{0,960},{64,128},{128,64},{192,256},{256,192},{320,384},{384,320},... | collective-permute-start | bytes 589832 | tf_op jit(solution)/shard_map/cond/branch_1_fun/ppermute | solution.py:317
  187.6 19.5 %collective-permute-start.21 = (f32[8,6,8,128]{3,2,1,0:T(8,128)S(1)}, f32[8,6,8,128]{3,2,1,0:T(8,128)}, u32[]{:S(2)}, u32[]{:S(2)}) collective-permute-start(f32[8,6,8,128]{3,2,1,0:T(8,128)S(1)} %get-tuple-element.280), channel_id=1, source_target_pairs={{0,64},{64,0},{128,192},{192,128},{256,320},{320,256},{384,448},{4... | collective-permute-start | bytes 589832 | tf_op jit(solution)/shard_map/cond/branch_1_fun/cond/branch_1_fun/ppermute | solution.py:311
  189.6 6.5 %collective-permute-start.18 = (f32[2,3,8,128]{3,2,1,0:T(8,128)S(1)}, f32[2,3,8,128]{3,2,1,0:T(8,128)S(1)}, u32[]{:S(2)}, u32[]{:S(2)}) collective-permute-start(f32[2,3,8,128]{3,2,1,0:T(8,128)S(1)} %get-tuple-element.260.left_ref), channel_id=1, source_target_pairs={{0,48},{16,32},{32,16},{48,0},{1,49},{17,33},{33,17},{49,1},{2,50}... | collective-permute-start | bytes 73736 | tf_op jit(solution)/shard_map/cond/branch_1_fun/cond/branch_1_fun/cond/branch_1_fun/ppermute | solution.py:317
  191.8 15.3 %collective-permute-start.19 = (f32[8,8,8,128]{3,2,1,0:T(8,128)S(1)}, f32[8,8,8,128]{3,2,1,0:T(8,128)}, u32[]{:S(2)}, u32[]{:S(2)}) collective-permute-start(f32[8,8,8,128]{3,2,1,0:T(8,128)S(1)} %get-tuple-element.268), channel_id=1, source_target_pairs={{0,48},{16,32},{32,16},{48,0},{1,49},{17,33},{33,17},{49,1},{2,50}... | collective-permute-start | bytes 786440 | tf_op jit(solution)/shard_map/cond/branch_1_fun/cond/branch_1_fun/cond/branch_1_fun/ppermute | solution.py:317
  212.4 10.6 %collective-permute-start.35 = (f32[3,8,128]{2,1,0:T(8,128)S(1)}, f32[3,8,128]{2,1,0:T(8,128)S(1)}, u32[]{:S(2)}, u32[]{:S(2)}) collective-permute-start(f32[3,8,128]{2,1,0:T(8,128)S(1)} %fusion.5), channel_id=1, source_target_pairs={{0,1},{1,0},{2,3},{3,2},{4,5},{5,4},{6,7},{7,6},{8,9},{9,8},{10,11... | collective-permute-start | bytes 36872 | tf_op jit(solution)/shard_map/ppermute | solution.py:311
  (19 other events, 80.8 us)

commit v5 on v4

--- a/solution.py
+++ b/solution.py
@@ -311,10 +311,26 @@
     return lax.ppermute(value, axis, [(i, i ^ 1) for i in range(count)])
 
 
+def across(place, count):
+    return (place + 1 if place % 2 else place - 1) % count
+
+
 def swap_across(value, axis):
     count = lax.axis_size(axis)
-    pairs = [(i, (i + 1 if i % 2 else i - 1) % count) for i in range(count)]
-    return lax.ppermute(value, axis, pairs)
+    return lax.ppermute(value, axis, [(i, across(i, count)) for i in range(count)])
+
+
+def swap_corners(value):
+    count_x, count_z = lax.axis_size("gx"), lax.axis_size("gz")
+    pairs = []
+    for x in range(count_x):
+        for z in range(count_z):
+            to_x, to_z = across(x, count_x), z
+            turns = (x if x % 2 == 0 else to_x) % (count_x // 2) == 0
+            if turns and z in (0, count_z - 1):
+                to_z = across(z, count_z)
+            pairs.append((x * count_z + z, to_x * count_z + to_z))
+    return lax.ppermute(value, ("gx", "gz"), pairs)
 
 
 def body(
@@ -352,22 +368,21 @@
         after = lax.cond(some, rest, otherwise, finish(come))
         return lax.optimization_barrier(((*after, *extra), arriving))
 
-    def zeros_like_z(pair):
+    def zeros_like_z(own):
         z_face = jnp.zeros(z_shape, F32)
-        return pair[:, :2], z_face, z_face
-
-    def zeros_like_y(pair):
-        return (*zeros_like_z(pair), jnp.zeros(cells_shape, F32))
-
-    def zeros_like_x(pair):
-        return (*zeros_like_y(pair), jnp.zeros(x_shape, F32))
+        return own, jnp.zeros((2, 8, 128), F32), jnp.zeros((3, 8, 128), F32), z_face
+
+    def zeros_like_y(own):
+        return (*zeros_like_z(own), jnp.zeros(cells_shape, F32))
+
+    def zeros_like_x(own):
+        return (*zeros_like_y(own), jnp.zeros(x_shape, F32))
 
     def zeros_like_all(pair):
-        return (*zeros_like_x(pair), jnp.zeros(x_shape, F32))
+        return (*zeros_like_x(pair[:, :2]), jnp.zeros(z_shape, F32), jnp.zeros(x_shape, F32))
 
     def zeros_like_first(pair):
-        *head, face = zeros_like_all(pair)
-        return (*head, jnp.zeros((SEGS, 128), F32), face)
+        return (*zeros_like_all(pair), jnp.zeros((SEGS, 128), F32))
 
     def energies():
         return call(
@@ -379,7 +394,34 @@
         first = energy is None
         place = jnp.arange(2, dtype=jnp.int32)[:, None, None, None]
 
-        def along_z(pair):
+        def along_z_across(own):
+            far = swap_across(jnp.concatenate([own.reshape(4, 8, 128), zb], axis=0), "gz")
+            own = own + far[:4].reshape(2, 2, 8, 128)
+            beyond_x = swap_inside(jnp.where(odd_x, own[0], own[1]), "gx")
+            rows = jnp.where(
+                odd_z,
+                jnp.where(odd_x, jnp.stack([beyond_x[0], own[0, 0], own[1, 0]]),
+                          jnp.stack([own[0, 0], own[1, 0], beyond_x[0]])),
+                jnp.where(odd_x, jnp.stack([beyond_x[1], own[0, 1], own[1, 1]]),
+                          jnp.stack([own[0, 1], own[1, 1], beyond_x[1]])),
+            )
+            return own, beyond_x, swap_inside(rows, "gz"), far[4:]
+
+        def along_y_across(own):
+            rest, yb_in = staged(
+                lambda v: swap_across(v, "gy"), own, lambda v: swap_across(v, "gy"), cells,
+                lambda come: total(own, come), along_z_across, zeros_like_z,
+            )
+            return (*rest, yb_in)
+
+        def along_y_inside(own):
+            rest, xa_in = staged(
+                lambda v: swap_inside(v, "gy"), own, lambda v: swap_inside(v, "gx"), xa,
+                lambda come: total(own, come), along_y_across, zeros_like_y,
+            )
+            return (*rest, xa_in)
+
+        def along_z_inside(pair):
             come = swap_inside(
                 jnp.concatenate([jnp.where(odd_z, pair[:, 0], pair[:, 2]), za], axis=0), "gz"
             )
@@ -389,30 +431,13 @@
                 jnp.stack([middle, pair[:, 2]], axis=1),
                 jnp.stack([pair[:, 0], middle], axis=1),
             )
-            far = swap_across(jnp.concatenate([own.reshape(4, 8, 128), zb], axis=0), "gz")
-            return own + far[:4].reshape(2, 2, 8, 128), come[2:], far[4:]
-
-        def along_y_across(pair):
-            (own, za_in, zb_in), yb_in = staged(
-                lambda v: swap_across(v, "gy"), pair, lambda v: swap_across(v, "gy"), cells,
-                lambda come: total(pair, come), along_z, zeros_like_z,
-            )
-            return own, za_in, zb_in, yb_in
-
-        def along_y_inside(pair):
-            rest, xa_in = staged(
-                lambda v: swap_inside(v, "gy"), pair, lambda v: swap_inside(v, "gx"), xa,
-                lambda come: total(pair, come), along_y_across, zeros_like_y,
-            )
-            return (*rest, xa_in)
-
-        def along_x_across(pair):
             rest, xb_in = staged(
-                lambda v: swap_across(v, "gx"), pair, lambda v: swap_across(v, "gx"), xb,
-                lambda come: total(pair, come), along_y_inside, zeros_like_x,
+                swap_corners, own, lambda v: swap_across(v, "gx"), xb,
+                lambda come: total(own, come), along_y_inside, zeros_like_x,
                 energies if first else tuple,
             )
-            return (*rest, xb_in)
+            made = rest[6:]
+            return (*rest[:6], come[2:], xb_in, *made)
 
         rest, ya_in = staged(
             lambda v: swap_inside(v, "gx"), give, lambda v: swap_inside(v, "gy"), cells,
@@ -420,22 +445,11 @@
                 keep.reshape(2, 3, 8, 128),
                 jnp.where(place == 1 - places[0] % 2, come.reshape(1, 3, 8, 128), 0.0),
             ),
-            along_x_across, zeros_like_first if first else zeros_like_all,
+            along_z_inside, zeros_like_first if first else zeros_like_all,
         )
-        own, za, zb, yb, xa, *made, xb = rest
+        own, beyond_x, beyond_z, zb_in, yb_in, xa_in, za_in, xb_in, *made = rest
         energy = made[0] if first else energy
-        ya = ya_in
-
-        beyond_x = swap_inside(jnp.where(odd_x, own[0], own[1]), "gx")
-        rows = jnp.where(
-            odd_z,
-            jnp.where(odd_x, jnp.stack([beyond_x[0], own[0, 0], own[1, 0]]),
-                      jnp.stack([own[0, 0], own[1, 0], beyond_x[0]])),
-            jnp.where(odd_x, jnp.stack([beyond_x[1], own[0, 1], own[1, 1]]),
-                      jnp.stack([own[0, 1], own[1, 1], beyond_x[1]])),
-        )
-        beyond_z = swap_inside(rows, "gz")
-        return energy, own, beyond_x, beyond_z, xa, xb, ya, yb, za, zb
+        return energy, own, beyond_x, beyond_z, xa_in, xb_in, ya_in, yb_in, za_in, zb_in
 
     half_width = (highest - cutoff) / 2.0
     middle = (highest + cutoff) / 2.0

time: 230 us -> 235 us (1.022)
  starting transfers between devices: 169 us -> 153 us
  Pallas kernels: 23.8 us -> 31.4 us
  other arithmetic: 2.51 us -> 8.58 us
  local copies, waits for them, and re-layouts: 9.21 us -> 13.7 us
    ppermute x21, starting transfers between devices: 88.3 us -> 78.1 us  [swap_inside(): return lax.ppermute(value, axis, [(i, i ^ 1) for i in range(count)])]
    pallas_call x12, Pallas kernels: 0.07 us -> 7.6 us  [total(): pl.pallas_call(add_kernel, out_shape=jax.ShapeDtypeStruct(left.shape, F32...]
    ppermute x15, starting transfers between devices: 81.1 us -> 74.9 us  [the longest x12 43.4 us: swap_across(): lax.ppermute(value, axis, [(i, across(i, count)) for i in range(count)])]
    cond x0 -> x6, local copies, waits for them, and re-layouts: none -> 6.1 us
    another operation x6 -> x0, local copies, waits for them, and re-layouts: 4 us -> none  [the longest x3 2.18 us: exchange(): jnp.stack([beyond_x[1], own[0, 1], own[1, 1]])]
    add x3, other arithmetic: 0.02 us -> 3.96 us  [along_z_across(): own = own + far[:4].reshape(2, 2, 8, 128)]
    ppermute x21, waiting for transfers between devices: 8.88 us -> 12.6 us  [swap_inside(): return lax.ppermute(value, axis, [(i, i ^ 1) for i in range(count)])]
  transfers between devices with their start and end apart: 36 -> 36, of which waited for: 15 -> 17; matrix products, arithmetic and copies ran while one was open for 3% -> 9% of each run, Pallas kernels for 1% -> 5%
where the time goes in v5:
time: 235 us; the launch traced here: 231 us
  starting transfers between devices  153 us (65%)
  Pallas kernels  31.4 us (13%)
  waiting for transfers between devices  23.3 us (10%)
  local copies, waits for them, and re-layouts  13.7 us (6%)
  other arithmetic  8.58 us (4%)
    ppermute x21, starting transfers between devices, swap_inside(): return lax.ppermute(value, axis, [(i, i ^ 1) for i in range(count)])  78.1 us
    ppermute x12, starting transfers between devices, swap_across(): lax.ppermute(value, axis, [(i, across(i, count)) for i in range(count)])  43.4 us
    ppermute x3, starting transfers between devices, swap_corners(): return lax.ppermute(value, ('gx', 'gz'), pairs)  31.5 us
    pallas_call x5, Pallas kernels, call(): pl.pallas_call(kernel, out_shape=[jax.ShapeDtypeStruct(s, k) for s, k in...  23.8 us
    ppermute x21, waiting for transfers between devices, swap_inside(): return lax.ppermute(value, axis, [(i, i ^ 1) for i in range(count)])  12.6 us
    ppermute x12, waiting for transfers between devices, swap_across(): lax.ppermute(value, axis, [(i, across(i, count)) for i in range(count)])  10.6 us
    pallas_call x12, Pallas kernels, total(): pl.pallas_call(add_kernel, out_shape=jax.ShapeDtypeStruct(left.shape, F32...  7.6 us
    cond x6, local copies, waits for them, and re-layouts  6.1 us
  transfers between devices with their start and end apart: 36, of which 17 were waited for; matrix products, arithmetic and copies ran while one was open for 9% of the time, Pallas kernels for 5%

profile of v5, /device:TPU:1, one launch (start us, length us, event | category | flops | bytes accessed | tf_op | source)
XLA Modules:
  0.0 231.2 jit_solution(8210213142010174352)
XLA Ops:
  12.3 73.5 %conditional.12 = (f32[2,2,8,128]{3,2,1,0:T(8,128)}, f32[2,8,128]{2,1,0:T(8,128)}, f32[3,8,128]{2,1,0:T(8,128)}, f32[4,8,128]{2,1,0:T(8,128)}, f32[8,8,8,128]{3,...) conditional(s32[]{:T(128)} %convert_element_type.32, ...), branch_computations={%region_0.1_spmd, %region_1.8_spmd} | conditional | flops 24600070144 | bytes 243874848 | solution.py:368
  12.3 14.4 %collective-permute-start.21 = (f32[6,8,128]{2,1,0:T(8,128)S(1)}, f32[6,8,128]{2,1,0:T(8,128)S(1)}, u32[]{:S(2)}, u32[]{:S(2)}) collective-permute-start(f32[6,8,128]{2,1,0:T(8,128)S(1)} %pad_maximum_fusion.1), channel_id=1, source_target_pairs={{0,1},{1,0},{2,3},{3,2},{4,5},{5,4},{6,7},{7,6},{8,9},{9,8},{10,11... | collective-permute-start | bytes 73736 | tf_op jit(solution)/shard_map/cond/branch_1_fun/ppermute | solution.py:311
  27.6 10.5 %collective-permute-start.22 = (f32[2,2,8,128]{3,2,1,0:T(8,128)S(1)}, f32[2,2,8,128]{3,2,1,0:T(8,128)S(1)}, u32[]{:S(2)}, u32[]{:S(2)}) collective-permute-start(f32[2,2,8,128]{3,2,1,0:T(8,128)S(1)} %maximum_select_fusion.2.left_ref), channel_id=1, source_target_pairs={{0,975},{1,961},{2,962},{3,963},{4,964},{5,965},{6,966},{7,967},{8... | collective-permute-start | bytes 49160 | tf_op jit(solution)/shard_map/cond/branch_1_fun/ppermute | solution.py:333
  41.4 5.6 %collective-permute-start.23 = (f32[8,6,8,128]{3,2,1,0:T(8,128)S(1)}, f32[8,6,8,128]{3,2,1,0:T(8,128)}, u32[]{:S(2)}, u32[]{:S(2)}) collective-permute-start(f32[8,6,8,128]{3,2,1,0:T(8,128)S(1)} %get-tuple-element.224), channel_id=1, source_target_pairs={{0,960},{64,128},{128,64},{192,256},{256,192},{320,384},{384,320},... | collective-permute-start | bytes 589832 | tf_op jit(solution)/shard_map/cond/branch_1_fun/ppermute | solution.py:320
  47.6 38.2 %conditional.2 = (f32[2,2,8,128]{3,2,1,0:T(8,128)}, f32[2,8,128]{2,1,0:T(8,128)}, f32[3,8,128]{2,1,0:T(8,128)}, f32[4,8,128]{2,1,0:T(8,128)}, f32[8,8,8,128]{3,2,1,0:T(8,128)}, /*index=5*/f32[8,6,8,128]{3,2,1,0:T(8,128)}) conditional(s32[]{:T(128)} %convert_element_type.24, f32[2,2,8,128]{3,2,1,0:T(8,128)} %branch_1_fun.13, (pred[]{:T(512)}, ...), branch_computations={%region_2.2_spmd, %region_3.7_spmd} | conditional | flops 16000048128 | bytes 162535920 | solution.py:368
  54.0 30.4 %conditional.1 = (f32[2,2,8,128]{3,2,1,0:T(8,128)}, f32[2,8,128]{2,1,0:T(8,128)}, f32[3,8,128]{2,1,0:T(8,128)}, f32[4,8,128]{2,1,0:T(8,128)}, f32[8,8,8,128]{3,2,1,0:T(8,128)}) conditional(s32[]{:T(128)} %convert_element_type.15, f32[2,2,8,128]{3,2,1,0:T(8,128)} %branch_1_fun.11, (pred[]{:T(512)}, f32[2,2,8,128]{3,2,1,0:T(8,128)}, ...), branch_computations={%region_4.3_spmd, %region_5.6_spmd} | conditional | flops 8000048128 | bytes 81651000 | solution.py:368
  61.9 22.6 %conditional = (f32[2,2,8,128]{3,2,1,0:T(8,128)}, f32[2,8,128]{2,1,0:T(8,128)}, f32[3,8,128]{2,1,0:T(8,128)}, f32[4,8,128]{2,1,0:T(8,128)}) conditional(s32[]{:T(128)} %convert_element_type.14, f32[2,2,8,128]{3,2,1,0:T(8,128)} %branch_1_fun.10, (f32[2,2,8,128]{3,2,1,0:T(8,128)}, f32[4,8,128]{2,1,0:T(8,128)S(1)}, pred[]{:T(512)}, pred[]{:T(512)}) %tuple.70), branch_computations={%region_6.4_spmd, %region_7.5_spmd} | conditional | flops 48128 | bytes 503963 | solution.py:368
  64.5 4.7 %collective-permute-done = f32[8,8,128]{2,1,0:T(8,128)S(1)} collective-permute-done((f32[8,8,128]{2,1,0:T(8,128)S(1)}, f32[8,8,128]{2,1,0:T(8,128)S(1)}, u32[]{:S(2)}, u32[]{:S(2)}) %collective-permute-start) | collective-permute-done | bytes 32800 | tf_op jit(solution)/shard_map/cond/branch_1_fun/cond/branch_1_fun/cond/branch_1_fun/cond/branch_1_fun/ppermute | solution.py:320
  77.1 6.5 %collective-permute-start.2 = (f32[3,8,128]{2,1,0:T(8,128)S(1)}, f32[3,8,128]{2,1,0:T(8,128)}, u32[]{:S(2)}, u32[]{:S(2)}) collective-permute-start(f32[3,8,128]{2,1,0:T(8,128)S(1)} %fusion), channel_id=1, source_target_pairs={{0,1},{1,0},{2,3},{3,2},{4,5},{5,4},{6,7},{7,6},{8,9},{9,8},{10,11... | collective-permute-start | bytes 36872 | tf_op jit(solution)/shard_map/cond/branch_1_fun/cond/branch_1_fun/cond/branch_1_fun/cond/branch_1_fun/ppermute | solution.py:311
  85.8 6.5 %shard_map.85 = (f32[8,8,8,128]{3,2,1,0:T(8,128)S(1)}, f32[24,128]{1,0:T(8,128)S(1)}, f32[48,128]{1,0:T(8,128)S(1)}, f32[8,6,8,128]{3,2,1,0:T(8,128)S(1)}, f32[8...) custom-call(s32[8]{0:T(128)S(1)} %stack.93.refs_0_, f32[8,8,8,128]{3,2,1,0:T(8,128)S(1)} %copy-done.5, ...), custom_call_target="tpu_custom_call" | custom-call | flops 1500000000 | bytes 4000000 | tf_op jit(solution)/shard_map/pallas_call | solution.py:283
  96.8 62.2 %conditional.13 = (f32[2,2,8,128]{3,2,1,0:T(8,128)}, f32[2,8,128]{2,1,0:T(8,128)}, f32[3,8,128]{2,1,0:T(8,128)}, f32[4,8,128]{2,1,0:T(8,128)}, f32[8,8,8,128]{3,...) conditional(s32[]{:T(128)} %convert_element_type.32, ...), branch_computations={%region_8.9_spmd, %region_9.16_spmd} | conditional | flops 24000069632 | bytes 243674848 | solution.py:368
  101.1 13.5 %collective-permute-start.25 = (f32[2,2,8,128]{3,2,1,0:T(8,128)S(1)}, f32[2,2,8,128]{3,2,1,0:T(8,128)S(1)}, u32[]{:S(2)}, u32[]{:S(2)}) collective-permute-start(f32[2,2,8,128]{3,2,1,0:T(8,128)S(1)} %maximum_select_fusion.5.left_ref), channel_id=1, source_target_pairs={{0,975},{1,961},{2,962},{3,963},{4,964},{5,965},{6,966},{7,967},{8... | collective-permute-start | bytes 49160 | tf_op jit(solution)/shard_map/cond/branch_1_fun/ppermute | solution.py:333
  117.9 41.2 %conditional.5 = (f32[2,2,8,128]{3,2,1,0:T(8,128)}, f32[2,8,128]{2,1,0:T(8,128)}, f32[3,8,128]{2,1,0:T(8,128)}, f32[4,8,128]{2,1,0:T(8,128)}, f32[8,8,8,128]{3,2,1,0:T(8,128)}, /*index=5*/f32[8,6,8,128]{3,2,1,0:T(8,128)}) conditional(s32[]{:T(128)} %convert_element_type.27, f32[2,2,8,128]{3,2,1,0:T(8,128)} %branch_1_fun.16, (pred[]{:T(512)}, ...), branch_computations={%region_10.10_spmd, %region_11.15_spmd} | conditional | flops 16000048128 | bytes 162535920 | solution.py:368
  124.3 33.5 %conditional.4 = (f32[2,2,8,128]{3,2,1,0:T(8,128)}, f32[2,8,128]{2,1,0:T(8,128)}, f32[3,8,128]{2,1,0:T(8,128)}, f32[4,8,128]{2,1,0:T(8,128)}, f32[8,8,8,128]{3,2,1,0:T(8,128)}) conditional(s32[]{:T(128)} %convert_element_type.26, f32[2,2,8,128]{3,2,1,0:T(8,128)} %branch_1_fun.15, (pred[]{:T(512)}, f32[2,2,8,128]{3,2,1,0:T(8,128)}, ...), branch_computations={%region_12.11_spmd, %region_13.14_spmd} | conditional | flops 8000048128 | bytes 81651000 | solution.py:368
  132.1 25.6 %conditional.3 = (f32[2,2,8,128]{3,2,1,0:T(8,128)}, f32[2,8,128]{2,1,0:T(8,128)}, f32[3,8,128]{2,1,0:T(8,128)}, f32[4,8,128]{2,1,0:T(8,128)}) conditional(s32[]{:T(128)} %convert_element_type.25, f32[2,2,8,128]{3,2,1,0:T(8,128)} %branch_1_fun.14, (f32[2,2,8,128]{3,2,1,0:T(8,128)}, f32[4,8,128]{2,1,0:T(8,128)S(1)}, pred[]{:T(512)}, ...), branch_computations={%region_14.12_spmd, %region_15.13_spmd} | conditional | flops 48128 | bytes 503963 | solution.py:368
  146.3 10.5 %collective-permute-start.9 = (f32[3,8,128]{2,1,0:T(8,128)S(1)}, f32[3,8,128]{2,1,0:T(8,128)}, u32[]{:S(2)}, u32[]{:S(2)}) collective-permute-start(f32[3,8,128]{2,1,0:T(8,128)S(1)} %fusion.3), channel_id=1, source_target_pairs={{0,1},{1,0},{2,3},{3,2},{4,5},{5,4},{6,7},{7,6},{8,9},{9,8},{10,11... | collective-permute-start | bytes 36872 | tf_op jit(solution)/shard_map/cond/branch_1_fun/cond/branch_1_fun/cond/branch_1_fun/cond/branch_1_fun/ppermute | solution.py:311
  159.1 6.5 %shard_map.87 = (f32[8,8,8,128]{3,2,1,0:T(8,128)S(1)}, f32[24,128]{1,0:T(8,128)S(1)}, f32[48,128]{1,0:T(8,128)S(1)}, f32[8,6,8,128]{3,2,1,0:T(8,128)S(1)}, f32[8...) custom-call(s32[8]{0:T(128)S(1)} %stack.93.refs_0_, ...), custom_call_target="tpu_custom_call" | custom-call | flops 1500000000 | bytes 4000000 | tf_op jit(solution)/shard_map/pallas_call | solution.py:283
  170.1 56.3 %conditional.14 = (f32[2,2,8,128]{3,2,1,0:T(8,128)}, f32[2,8,128]{2,1,0:T(8,128)}, f32[3,8,128]{2,1,0:T(8,128)}, f32[4,8,128]{2,1,0:T(8,128)}, f32[8,8,8,128]{3,...) conditional(s32[]{:T(128)} %convert_element_type.32, ...), branch_computations={%region_16.17_spmd, %region_17.24_spmd} | conditional | flops 24000069632 | bytes 243674848 | solution.py:368
  174.4 7.5 %collective-permute-start.28 = (f32[2,2,8,128]{3,2,1,0:T(8,128)S(1)}, f32[2,2,8,128]{3,2,1,0:T(8,128)S(1)}, u32[]{:S(2)}, u32[]{:S(2)}) collective-permute-start(f32[2,2,8,128]{3,2,1,0:T(8,128)S(1)} %maximum_select_fusion.8.left_ref), channel_id=1, source_target_pairs={{0,975},{1,961},{2,962},{3,963},{4,964},{5,965},{6,966},{7,967},{8... | collective-permute-start | bytes 49160 | tf_op jit(solution)/shard_map/cond/branch_1_fun/ppermute | solution.py:333
  182.0 8.6 %collective-permute-start.29 = (f32[8,6,8,128]{3,2,1,0:T(8,128)S(1)}, f32[8,6,8,128]{3,2,1,0:T(8,128)}, u32[]{:S(2)}, u32[]{:S(2)}) collective-permute-start(f32[8,6,8,128]{3,2,1,0:T(8,128)S(1)} %get-tuple-element.327), channel_id=1, source_target_pairs={{0,960},{64,128},{128,64},{192,256},{256,192},{320,384},{384,320},... | collective-permute-start | bytes 589832 | tf_op jit(solution)/shard_map/cond/branch_1_fun/ppermute | solution.py:320
  191.2 35.2 %conditional.8 = (f32[2,2,8,128]{3,2,1,0:T(8,128)}, f32[2,8,128]{2,1,0:T(8,128)}, f32[3,8,128]{2,1,0:T(8,128)}, f32[4,8,128]{2,1,0:T(8,128)}, f32[8,8,8,128]{3,2,1,0:T(8,128)}, /*index=5*/f32[8,6,8,128]{3,2,1,0:T(8,128)}) conditional(s32[]{:T(128)} %convert_element_type.30, f32[2,2,8,128]{3,2,1,0:T(8,128)} %branch_1_fun.19, (pred[]{:T(512)}, ...), branch_computations={%region_18.18_spmd, %region_19.23_spmd} | conditional | flops 16000048128 | bytes 162535920 | solution.py:368
  197.6 27.5 %conditional.7 = (f32[2,2,8,128]{3,2,1,0:T(8,128)}, f32[2,8,128]{2,1,0:T(8,128)}, f32[3,8,128]{2,1,0:T(8,128)}, f32[4,8,128]{2,1,0:T(8,128)}, f32[8,8,8,128]{3,2,1,0:T(8,128)}) conditional(s32[]{:T(128)} %convert_element_type.29, f32[2,2,8,128]{3,2,1,0:T(8,128)} %branch_1_fun.18, (pred[]{:T(512)}, f32[2,2,8,128]{3,2,1,0:T(8,128)}, ...), branch_computations={%region_20.19_spmd, %region_21.22_spmd} | conditional | flops 8000048128 | bytes 81651000 | solution.py:368
  205.4 19.7 %conditional.6 = (f32[2,2,8,128]{3,2,1,0:T(8,128)}, f32[2,8,128]{2,1,0:T(8,128)}, f32[3,8,128]{2,1,0:T(8,128)}, f32[4,8,128]{2,1,0:T(8,128)}) conditional(s32[]{:T(128)} %convert_element_type.28, f32[2,2,8,128]{3,2,1,0:T(8,128)} %branch_1_fun.17, (f32[2,2,8,128]{3,2,1,0:T(8,128)}, f32[4,8,128]{2,1,0:T(8,128)S(1)}, pred[]{:T(512)}, ...), branch_computations={%region_22.20_spmd, %region_23.21_spmd} | conditional | flops 48128 | bytes 503963 | solution.py:368
  226.4 4.8 %shard_map.89 = f32[8,8,8,128]{3,2,1,0:T(8,128)} custom-call(s32[8]{0:T(128)S(1)} %stack.93.refs_0_, f32[8,8,8,128]{3,2,1,0:T(8,128)S(1)} %get-tuple-element.481.refs_1_, f32[8,8,8,128]{3,2,1,0:T(8,128)S(1)} %get-tuple-element.456.refs_1_.refs_2_, f32[8,8,128]{2,1,0:T(8,128)S(1)} %copy-done.1, s32[8,2048]{1,0:T(8,128)S(1)} %get-tuple-element.413.refs_3_.refs_4_, ...), custom_call_target="tpu_custom_call" | custom-call | flops 1500000000 | bytes 4000000 | tf_op jit(solution)/shard_map/pallas_call | solution.py:283
  (138 shorter events, 130.3 us)
Async XLA Ops:
  4.1 7.2 %collective-permute-start.30 = (f32[24,128]{1,0:T(8,128)S(1)}, f32[24,128]{1,0:T(8,128)S(1)}, u32[]{:S(2)}, u32[]{:S(2)}) collective-permute-start(f32[24,128]{1,0:T(8,128)S(1)} %get-tuple-element.416), channel_id=1, source_target_pairs={{0,64},{64,0},{128,192},{192,128},{256,320},{320,256},{384,448},{4... | collective-permute-start | bytes 36872 | tf_op jit(solution)/shard_map/ppermute | solution.py:311
  8.1 77.7 %collective-permute-start.31 = (f32[8,8,8,128]{3,2,1,0:T(8,128)S(1)}, f32[8,8,8,128]{3,2,1,0:T(8,128)S(1)}, u32[]{:S(2)}, u32[]{:S(2)}) collective-permute-start(f32[8,8,8,128]{3,2,1,0:T(8,128)S(1)} %copy-done.5), channel_id=1, source_target_pairs={{0,16},{16,0},{32,48},{48,32},{1,17},{17,1},{33,49},{49,33},{2,18}... | collective-permute-start | bytes 786440 | tf_op jit(solution)/shard_map/ppermute | solution.py:311
  12.3 15.3 %collective-permute-start.21 = (f32[6,8,128]{2,1,0:T(8,128)S(1)}, f32[6,8,128]{2,1,0:T(8,128)S(1)}, u32[]{:S(2)}, u32[]{:S(2)}) collective-permute-start(f32[6,8,128]{2,1,0:T(8,128)S(1)} %pad_maximum_fusion.1), channel_id=1, source_target_pairs={{0,1},{1,0},{2,3},{3,2},{4,5},{5,4},{6,7},{7,6},{8,9},{9,8},{10,11... | collective-permute-start | bytes 73736 | tf_op jit(solution)/shard_map/cond/branch_1_fun/ppermute | solution.py:311
  27.6 19.5 %collective-permute-start.22 = (f32[2,2,8,128]{3,2,1,0:T(8,128)S(1)}, f32[2,2,8,128]{3,2,1,0:T(8,128)S(1)}, u32[]{:S(2)}, u32[]{:S(2)}) collective-permute-start(f32[2,2,8,128]{3,2,1,0:T(8,128)S(1)} %maximum_select_fusion.2.left_ref), channel_id=1, source_target_pairs={{0,975},{1,961},{2,962},{3,963},{4,964},{5,965},{6,966},{7,967},{8... | collective-permute-start | bytes 49160 | tf_op jit(solution)/shard_map/cond/branch_1_fun/ppermute | solution.py:333
  41.4 44.4 %collective-permute-start.23 = (f32[8,6,8,128]{3,2,1,0:T(8,128)S(1)}, f32[8,6,8,128]{3,2,1,0:T(8,128)}, u32[]{:S(2)}, u32[]{:S(2)}) collective-permute-start(f32[8,6,8,128]{3,2,1,0:T(8,128)S(1)} %get-tuple-element.224), channel_id=1, source_target_pairs={{0,960},{64,128},{128,64},{192,256},{256,192},{320,384},{384,320},... | collective-permute-start | bytes 589832 | tf_op jit(solution)/shard_map/cond/branch_1_fun/ppermute | solution.py:320
  49.6 34.9 %collective-permute-start.6 = (f32[8,6,8,128]{3,2,1,0:T(8,128)S(1)}, f32[8,6,8,128]{3,2,1,0:T(8,128)}, u32[]{:S(2)}, u32[]{:S(2)}) collective-permute-start(f32[8,6,8,128]{3,2,1,0:T(8,128)S(1)} %get-tuple-element.204), channel_id=1, source_target_pairs={{0,64},{64,0},{128,192},{192,128},{256,320},{320,256},{384,448},{4... | collective-permute-start | bytes 589832 | tf_op jit(solution)/shard_map/cond/branch_1_fun/cond/branch_1_fun/ppermute | solution.py:311
  54.7 6.5 %collective-permute-start.3 = (f32[2,2,8,128]{3,2,1,0:T(8,128)S(1)}, f32[2,2,8,128]{3,2,1,0:T(8,128)S(1)}, u32[]{:S(2)}, u32[]{:S(2)}) collective-permute-start(f32[2,2,8,128]{3,2,1,0:T(8,128)S(1)} %copy.160.left_ref), channel_id=1, source_target_pairs={{0,48},{16,32},{32,16},{48,0},{1,49},{17,33},{33,17},{49,1},{2,50}... | collective-permute-start | bytes 49160 | tf_op jit(solution)/shard_map/cond/branch_1_fun/cond/branch_1_fun/cond/branch_1_fun/ppermute | solution.py:320
  56.7 27.8 %collective-permute-start.4 = (f32[8,8,8,128]{3,2,1,0:T(8,128)S(1)}, f32[8,8,8,128]{3,2,1,0:T(8,128)}, u32[]{:S(2)}, u32[]{:S(2)}) collective-permute-start(f32[8,8,8,128]{3,2,1,0:T(8,128)S(1)} %get-tuple-element.191), channel_id=1, source_target_pairs={{0,48},{16,32},{32,16},{48,0},{1,49},{17,33},{33,17},{49,1},{2,50}... | collective-permute-start | bytes 786440 | tf_op jit(solution)/shard_map/cond/branch_1_fun/cond/branch_1_fun/cond/branch_1_fun/ppermute | solution.py:320
  62.6 6.7 %collective-permute-start = (f32[8,8,128]{2,1,0:T(8,128)S(1)}, f32[8,8,128]{2,1,0:T(8,128)S(1)}, u32[]{:S(2)}, u32[]{:S(2)}) collective-permute-start(f32[8,8,128]{2,1,0:T(8,128)S(1)} %pad_maximum_fusion), channel_id=1, source_target_pairs={{0,15},{1,2},{2,1},{3,4},{4,3},{5,6},{6,5},{7,8},{8,7},{9,10},{10,... | collective-permute-start | bytes 98312 | tf_op jit(solution)/shard_map/cond/branch_1_fun/cond/branch_1_fun/cond/branch_1_fun/cond/branch_1_fun/ppermute | solution.py:320
  77.1 7.4 %collective-permute-start.2 = (f32[3,8,128]{2,1,0:T(8,128)S(1)}, f32[3,8,128]{2,1,0:T(8,128)}, u32[]{:S(2)}, u32[]{:S(2)}) collective-permute-start(f32[3,8,128]{2,1,0:T(8,128)S(1)} %fusion), channel_id=1, source_target_pairs={{0,1},{1,0},{2,3},{3,2},{4,5},{5,4},{6,7},{7,6},{8,9},{9,8},{10,11... | collective-permute-start | bytes 36872 | tf_op jit(solution)/shard_map/cond/branch_1_fun/cond/branch_1_fun/cond/branch_1_fun/cond/branch_1_fun/ppermute | solution.py:311
  94.5 64.6 %collective-permute-start.33 = (f32[8,8,8,128]{3,2,1,0:T(8,128)S(1)}, f32[8,8,8,128]{3,2,1,0:T(8,128)S(1)}, u32[]{:S(2)}, u32[]{:S(2)}) collective-permute-start(f32[8,8,8,128]{3,2,1,0:T(8,128)S(1)} %get-tuple-element.456.refs_1_.refs_2_), channel_id=1, source_target_pairs={{0,16},{16,0},{32,48},{48,32},{1,17},{17,1},{33,49},{49,33},{2,18}... | collective-permute-start | bytes 786440 | tf_op jit(solution)/shard_map/ppermute | solution.py:311
  101.1 16.1 %collective-permute-start.25 = (f32[2,2,8,128]{3,2,1,0:T(8,128)S(1)}, f32[2,2,8,128]{3,2,1,0:T(8,128)S(1)}, u32[]{:S(2)}, u32[]{:S(2)}) collective-permute-start(f32[2,2,8,128]{3,2,1,0:T(8,128)S(1)} %maximum_select_fusion.5.left_ref), channel_id=1, source_target_pairs={{0,975},{1,961},{2,962},{3,963},{4,964},{5,965},{6,966},{7,967},{8... | collective-permute-start | bytes 49160 | tf_op jit(solution)/shard_map/cond/branch_1_fun/ppermute | solution.py:333
  114.6 44.4 %collective-permute-start.26 = (f32[8,6,8,128]{3,2,1,0:T(8,128)S(1)}, f32[8,6,8,128]{3,2,1,0:T(8,128)}, u32[]{:S(2)}, u32[]{:S(2)}) collective-permute-start(f32[8,6,8,128]{3,2,1,0:T(8,128)S(1)} %get-tuple-element.276), channel_id=1, source_target_pairs={{0,960},{64,128},{128,64},{192,256},{256,192},{320,384},{384,320},... | collective-permute-start | bytes 589832 | tf_op jit(solution)/shard_map/cond/branch_1_fun/ppermute | solution.py:320
  120.3 37.4 %collective-permute-start.13 = (f32[8,6,8,128]{3,2,1,0:T(8,128)S(1)}, f32[8,6,8,128]{3,2,1,0:T(8,128)}, u32[]{:S(2)}, u32[]{:S(2)}) collective-permute-start(f32[8,6,8,128]{3,2,1,0:T(8,128)S(1)} %get-tuple-element.260), channel_id=1, source_target_pairs={{0,64},{64,0},{128,192},{192,128},{256,320},{320,256},{384,448},{4... | collective-permute-start | bytes 589832 | tf_op jit(solution)/shard_map/cond/branch_1_fun/cond/branch_1_fun/ppermute | solution.py:311
  125.0 6.5 %collective-permute-start.10 = (f32[2,2,8,128]{3,2,1,0:T(8,128)S(1)}, f32[2,2,8,128]{3,2,1,0:T(8,128)S(1)}, u32[]{:S(2)}, u32[]{:S(2)}) collective-permute-start(f32[2,2,8,128]{3,2,1,0:T(8,128)S(1)} %copy.161.left_ref), channel_id=1, source_target_pairs={{0,48},{16,32},{32,16},{48,0},{1,49},{17,33},{33,17},{49,1},{2,50}... | collective-permute-start | bytes 49160 | tf_op jit(solution)/shard_map/cond/branch_1_fun/cond/branch_1_fun/cond/branch_1_fun/ppermute | solution.py:320
  128.7 29.0 %collective-permute-start.11 = (f32[8,8,8,128]{3,2,1,0:T(8,128)S(1)}, f32[8,8,8,128]{3,2,1,0:T(8,128)}, u32[]{:S(2)}, u32[]{:S(2)}) collective-permute-start(f32[8,8,8,128]{3,2,1,0:T(8,128)S(1)} %get-tuple-element.247), channel_id=1, source_target_pairs={{0,48},{16,32},{32,16},{48,0},{1,49},{17,33},{33,17},{49,1},{2,50}... | collective-permute-start | bytes 786440 | tf_op jit(solution)/shard_map/cond/branch_1_fun/cond/branch_1_fun/cond/branch_1_fun/ppermute | solution.py:320
  132.8 5.6 %collective-permute-start.7 = (f32[8,8,128]{2,1,0:T(8,128)S(1)}, f32[8,8,128]{2,1,0:T(8,128)S(1)}, u32[]{:S(2)}, u32[]{:S(2)}) collective-permute-start(f32[8,8,128]{2,1,0:T(8,128)S(1)} %pad_maximum_fusion.2), channel_id=1, source_target_pairs={{0,15},{1,2},{2,1},{3,4},{4,3},{5,6},{6,5},{7,8},{8,7},{9,10},{10,... | collective-permute-start | bytes 98312 | tf_op jit(solution)/shard_map/cond/branch_1_fun/cond/branch_1_fun/cond/branch_1_fun/cond/branch_1_fun/ppermute | solution.py:320
  146.3 11.5 %collective-permute-start.9 = (f32[3,8,128]{2,1,0:T(8,128)S(1)}, f32[3,8,128]{2,1,0:T(8,128)}, u32[]{:S(2)}, u32[]{:S(2)}) collective-permute-start(f32[3,8,128]{2,1,0:T(8,128)S(1)} %fusion.3), channel_id=1, source_target_pairs={{0,1},{1,0},{2,3},{3,2},{4,5},{5,4},{6,7},{7,6},{8,9},{9,8},{10,11... | collective-permute-start | bytes 36872 | tf_op jit(solution)/shard_map/cond/branch_1_fun/cond/branch_1_fun/cond/branch_1_fun/cond/branch_1_fun/ppermute | solution.py:311
  167.8 58.6 %collective-permute-start.35 = (f32[8,8,8,128]{3,2,1,0:T(8,128)S(1)}, f32[8,8,8,128]{3,2,1,0:T(8,128)S(1)}, u32[]{:S(2)}, u32[]{:S(2)}) collective-permute-start(f32[8,8,8,128]{3,2,1,0:T(8,128)S(1)} %get-tuple-element.481.refs_1_), channel_id=1, source_target_pairs={{0,16},{16,0},{32,48},{48,32},{1,17},{17,1},{33,49},{49,33},{2,18}... | collective-permute-start | bytes 786440 | tf_op jit(solution)/shard_map/ppermute | solution.py:311
  174.4 16.1 %collective-permute-start.28 = (f32[2,2,8,128]{3,2,1,0:T(8,128)S(1)}, f32[2,2,8,128]{3,2,1,0:T(8,128)S(1)}, u32[]{:S(2)}, u32[]{:S(2)}) collective-permute-start(f32[2,2,8,128]{3,2,1,0:T(8,128)S(1)} %maximum_select_fusion.8.left_ref), channel_id=1, source_target_pairs={{0,975},{1,961},{2,962},{3,963},{4,964},{5,965},{6,966},{7,967},{8... | collective-permute-start | bytes 49160 | tf_op jit(solution)/shard_map/cond/branch_1_fun/ppermute | solution.py:333
  182.0 44.4 %collective-permute-start.29 = (f32[8,6,8,128]{3,2,1,0:T(8,128)S(1)}, f32[8,6,8,128]{3,2,1,0:T(8,128)}, u32[]{:S(2)}, u32[]{:S(2)}) collective-permute-start(f32[8,6,8,128]{3,2,1,0:T(8,128)S(1)} %get-tuple-element.327), channel_id=1, source_target_pairs={{0,960},{64,128},{128,64},{192,256},{256,192},{320,384},{384,320},... | collective-permute-start | bytes 589832 | tf_op jit(solution)/shard_map/cond/branch_1_fun/ppermute | solution.py:320
  193.6 31.5 %collective-permute-start.20 = (f32[8,6,8,128]{3,2,1,0:T(8,128)S(1)}, f32[8,6,8,128]{3,2,1,0:T(8,128)}, u32[]{:S(2)}, u32[]{:S(2)}) collective-permute-start(f32[8,6,8,128]{3,2,1,0:T(8,128)S(1)} %get-tuple-element.311), channel_id=1, source_target_pairs={{0,64},{64,0},{128,192},{192,128},{256,320},{320,256},{384,448},{4... | collective-permute-start | bytes 589832 | tf_op jit(solution)/shard_map/cond/branch_1_fun/cond/branch_1_fun/ppermute | solution.py:311
  198.3 6.5 %collective-permute-start.17 = (f32[2,2,8,128]{3,2,1,0:T(8,128)S(1)}, f32[2,2,8,128]{3,2,1,0:T(8,128)S(1)}, u32[]{:S(2)}, u32[]{:S(2)}) collective-permute-start(f32[2,2,8,128]{3,2,1,0:T(8,128)S(1)} %copy.162.left_ref), channel_id=1, source_target_pairs={{0,48},{16,32},{32,16},{48,0},{1,49},{17,33},{33,17},{49,1},{2,50}... | collective-permute-start | bytes 49160 | tf_op jit(solution)/shard_map/cond/branch_1_fun/cond/branch_1_fun/cond/branch_1_fun/ppermute | solution.py:320
  202.0 23.1 %collective-permute-start.18 = (f32[8,8,8,128]{3,2,1,0:T(8,128)S(1)}, f32[8,8,8,128]{3,2,1,0:T(8,128)}, u32[]{:S(2)}, u32[]{:S(2)}) collective-permute-start(f32[8,8,8,128]{3,2,1,0:T(8,128)S(1)} %get-tuple-element.298), channel_id=1, source_target_pairs={{0,48},{16,32},{32,16},{48,0},{1,49},{17,33},{33,17},{49,1},{2,50}... | collective-permute-start | bytes 786440 | tf_op jit(solution)/shard_map/cond/branch_1_fun/cond/branch_1_fun/cond/branch_1_fun/ppermute | solution.py:320
  (19 other events, 141.2 us)

commit v6 on v5

--- a/solution.py
+++ b/solution.py
@@ -170,32 +170,18 @@
     gain, middle, back = scales
     refs = list(refs)
     before_ref = refs.pop(0) if back else None
-    (pot_ref, idx_ref, wts_ref, energy_ref, own_ref, px_ref, pz_ref,
-     xa_in, xb_in, ya_in, yb_in, za_in, zb_in) = refs[:13]
-    outs = refs[13:]
+    (pot_ref, idx_ref, wts_ref, energy_ref, table_ref,
+     xa_in, xb_in, corner_in, ya_in, yb_in, za_in, zb_in) = refs[:12]
+    outs = refs[12:]
     if last:
         next_ref, nonlocal_ref, z_ref, xext, yext = outs
     else:
         (next_ref, give_ref, keep_ref, xa_ref, xb_ref, za_ref, zb_ref,
          nonlocal_ref, z_ref, xext, yext) = outs
     bx, by, bz = coord_ref[3], coord_ref[4], coord_ref[5]
-
-    odd_x, odd_z = bx == 1, bz == 1
-    own0, own1, other = own_ref[0], own_ref[1], px_ref[...]
-    rows_x = (
-        jnp.where(odd_x, other, own0),
-        jnp.where(odd_x, own0, own1),
-        jnp.where(odd_x, own1, other),
-    )
-    planes = []
-    for k in range(3):
-        low, high, beyond = rows_x[k][0], rows_x[k][1], pz_ref[k]
-        planes += [
-            jnp.where(odd_z, beyond, low),
-            jnp.where(odd_z, low, high),
-            jnp.where(odd_z, high, beyond),
-        ]
-    coefs = jnp.concatenate(planes, axis=0) * energy_ref[...]
+    odd_z = bz == 1
+
+    coefs = table_ref[...] * energy_ref[...]
     scatter_returned(coefs, idx_ref, wts_ref, nonlocal_ref)
 
     rows = cells_ref[...].reshape(ROWS, DEPTH)
@@ -219,7 +205,7 @@
 
     xext[:, HALO : HALO + SIDE] = cells_ref[...]
     xext[:, pl.ds((1 - bx) * (HALO + SIDE), HALO)] = xa_in[...]
-    xext[:, pl.ds(bx * (HALO + SIDE), HALO)] = xb_in[...]
+    xext[:, pl.ds(bx * (HALO + SIDE), HALO)] = xb_in[...] + corner_in[...]
     yext[1] = cells_ref[...]
     yext[2 - 2 * by] = ya_in[...]
     yext[2 * by] = yb_in[...]
@@ -246,6 +232,26 @@
         write_sends(coord_ref, next_ref, xa_ref, xb_ref, za_ref, zb_ref)
 
 
+def table_kernel(coord_ref, own_ref, px_ref, pz_ref, far_ref, table_ref, face_ref):
+    odd_x, odd_z = coord_ref[3] == 1, coord_ref[5] == 1
+    own0, own1, other = own_ref[0], own_ref[1], px_ref[...]
+    rows_x = (
+        jnp.where(odd_x, other, own0),
+        jnp.where(odd_x, own0, own1),
+        jnp.where(odd_x, own1, other),
+    )
+    planes = []
+    for k in range(3):
+        low, high, beyond = rows_x[k][0], rows_x[k][1], pz_ref[k]
+        planes += [
+            jnp.where(odd_z, beyond, low),
+            jnp.where(odd_z, low, high),
+            jnp.where(odd_z, high, beyond),
+        ]
+    table_ref[...] = jnp.concatenate(planes, axis=0)
+    face_ref[...] = far_ref[4:]
+
+
 def energy_kernel(sizes, coord_ref, energy_ref, table_ref):
     size_x, size_y, size_z = sizes
     atoms = energy_ref.shape[1]
@@ -320,16 +326,30 @@
     return lax.ppermute(value, axis, [(i, across(i, count)) for i in range(count)])
 
 
+def is_corner(x, z, count_x, count_z):
+    upper = x if x % 2 == 0 else across(x, count_x)
+    return upper % (count_x // 2) == 0 and z in (0, count_z - 1)
+
+
 def swap_corners(value):
     count_x, count_z = lax.axis_size("gx"), lax.axis_size("gz")
     pairs = []
     for x in range(count_x):
         for z in range(count_z):
-            to_x, to_z = across(x, count_x), z
-            turns = (x if x % 2 == 0 else to_x) % (count_x // 2) == 0
-            if turns and z in (0, count_z - 1):
-                to_z = across(z, count_z)
-            pairs.append((x * count_z + z, to_x * count_z + to_z))
+            corner = is_corner(x, z, count_x, count_z)
+            to_z = across(z, count_z) if corner else z
+            pairs.append((x * count_z + z, across(x, count_x) * count_z + to_z))
+    return lax.ppermute(value, ("gx", "gz"), pairs)
+
+
+def swap_far_faces(value, corners):
+    count_x, count_z = lax.axis_size("gx"), lax.axis_size("gz")
+    pairs = [
+        (x * count_z + z, across(x, count_x) * count_z + z)
+        for x in range(count_x)
+        for z in range(count_z)
+        if is_corner(x, z, count_x, count_z) == corners
+    ]
     return lax.ppermute(value, ("gx", "gz"), pairs)
 
 
@@ -368,9 +388,11 @@
         after = lax.cond(some, rest, otherwise, finish(come))
         return lax.optimization_barrier(((*after, *extra), arriving))
 
+    def zeros_like_last(sums):
+        return jnp.zeros((SEGS, 128), F32), jnp.zeros(z_shape, F32)
+
     def zeros_like_z(own):
-        z_face = jnp.zeros(z_shape, F32)
-        return own, jnp.zeros((2, 8, 128), F32), jnp.zeros((3, 8, 128), F32), z_face
+        return (*zeros_like_last(own), jnp.zeros(x_shape, F32))
 
     def zeros_like_y(own):
         return (*zeros_like_z(own), jnp.zeros(cells_shape, F32))
@@ -394,9 +416,8 @@
         first = energy is None
         place = jnp.arange(2, dtype=jnp.int32)[:, None, None, None]
 
-        def along_z_across(own):
-            far = swap_across(jnp.concatenate([own.reshape(4, 8, 128), zb], axis=0), "gz")
-            own = own + far[:4].reshape(2, 2, 8, 128)
+        def inside_again(sums):
+            own, far = sums
             beyond_x = swap_inside(jnp.where(odd_x, own[0], own[1]), "gx")
             rows = jnp.where(
                 odd_z,
@@ -405,7 +426,20 @@
                 jnp.where(odd_x, jnp.stack([beyond_x[1], own[0, 1], own[1, 1]]),
                           jnp.stack([own[0, 1], own[1, 1], beyond_x[1]])),
             )
-            return own, beyond_x, swap_inside(rows, "gz"), far[4:]
+            return tuple(call(
+                table_kernel, [((SEGS, 128), F32), (z_shape, F32)], [], (100_000, 300_000),
+                coord, own, beyond_x, swap_inside(rows, "gz"), far,
+            ))
+
+        def along_z_across(own):
+            rest, corner_in = staged(
+                lambda v: swap_across(v, "gz"),
+                jnp.concatenate([own.reshape(4, 8, 128), zb], axis=0),
+                lambda v: swap_far_faces(v, True), xb,
+                lambda far: (total(own, far[:4].reshape(2, 2, 8, 128)), far),
+                inside_again, zeros_like_last,
+            )
+            return (*rest, corner_in)
 
         def along_y_across(own):
             rest, yb_in = staged(
@@ -432,12 +466,11 @@
                 jnp.stack([pair[:, 0], middle], axis=1),
             )
             rest, xb_in = staged(
-                swap_corners, own, lambda v: swap_across(v, "gx"), xb,
+                swap_corners, own, lambda v: swap_far_faces(v, False), xb,
                 lambda come: total(own, come), along_y_inside, zeros_like_x,
                 energies if first else tuple,
             )
-            made = rest[6:]
-            return (*rest[:6], come[2:], xb_in, *made)
+            return (*rest[:5], come[2:], xb_in, *rest[5:])
 
         rest, ya_in = staged(
             lambda v: swap_inside(v, "gx"), give, lambda v: swap_inside(v, "gy"), cells,
@@ -447,9 +480,9 @@
             ),
             along_z_inside, zeros_like_first if first else zeros_like_all,
         )
-        own, beyond_x, beyond_z, zb_in, yb_in, xa_in, za_in, xb_in, *made = rest
+        table, zb_in, corner_in, yb_in, xa_in, za_in, xb_in, *made = rest
         energy = made[0] if first else energy
-        return energy, own, beyond_x, beyond_z, xa_in, xb_in, ya_in, yb_in, za_in, zb_in
+        return energy, table, xa_in, xb_in, corner_in, ya_in, yb_in, za_in, zb_in
 
     half_width = (highest - cutoff) / 2.0
     middle = (highest + cutoff) / 2.0

time: 235 us -> 238 us (1.013)
  waiting for transfers between devices: 23.3 us -> 47 us
  local copies, waits for them, and re-layouts: 13.7 us -> 1.7 us
  other arithmetic: 8.58 us -> 0.35 us
  starting transfers between devices: 153 us -> 157 us
  Pallas kernels: 31.4 us -> 28.2 us
    ppermute x0 -> x6, starting transfers between devices: none -> 28.3 us  [swap_far_faces(): return lax.ppermute(value, ('gx', 'gz'), pairs)]
    ppermute x21, waiting for transfers between devices: 12.6 us -> 40.2 us  [swap_inside(): return lax.ppermute(value, axis, [(i, i ^ 1) for i in range(count)])]
    ppermute x12 -> x9, starting transfers between devices: 43.4 us -> 31.2 us  [swap_across(): lax.ppermute(value, axis, [(i, across(i, count)) for i in range(count)])]
    ppermute x3, starting transfers between devices: 31.5 us -> 24 us  [swap_corners(): return lax.ppermute(value, ('gx', 'gz'), pairs)]
    pallas_call x12 -> x15, Pallas kernels: 7.6 us -> 0.09 us  [total(): pl.pallas_call(add_kernel, out_shape=jax.ShapeDtypeStruct(left.shape, F32...]
    cond x6 -> x0, local copies, waits for them, and re-layouts: 6.1 us -> none
    ppermute x21, starting transfers between devices: 78.1 us -> 73 us  [swap_inside(): return lax.ppermute(value, axis, [(i, i ^ 1) for i in range(count)])]
    pallas_call x5 -> x8, Pallas kernels: 23.8 us -> 28.1 us  [call(): pl.pallas_call(kernel, out_shape=[jax.ShapeDtypeStruct(s, k) for s, k in...]
  transfers between devices with their start and end apart: 36 -> 39, of which waited for: 17 -> 21; matrix products, arithmetic and copies ran while one was open for 9% -> 0% of each run, Pallas kernels for 5% -> 3%
where the time goes in v6:
time: 238 us; the launch traced here: 235 us
  starting transfers between devices  157 us (66%)
  waiting for transfers between devices  47 us (20%)
  Pallas kernels  28.2 us (12%)
    ppermute x21, starting transfers between devices, swap_inside(): return lax.ppermute(value, axis, [(i, i ^ 1) for i in range(count)])  73 us
    ppermute x21, waiting for transfers between devices, swap_inside(): return lax.ppermute(value, axis, [(i, i ^ 1) for i in range(count)])  40.2 us
    ppermute x9, starting transfers between devices, swap_across(): lax.ppermute(value, axis, [(i, across(i, count)) for i in range(count)])  31.2 us
    ppermute x6, starting transfers between devices, swap_far_faces(): return lax.ppermute(value, ('gx', 'gz'), pairs)  28.3 us
    pallas_call x8, Pallas kernels, call(): pl.pallas_call(kernel, out_shape=[jax.ShapeDtypeStruct(s, k) for s, k in...  28.1 us
    ppermute x3, starting transfers between devices, swap_corners(): return lax.ppermute(value, ('gx', 'gz'), pairs)  24 us
    ppermute x9, waiting for transfers between devices, swap_across(): lax.ppermute(value, axis, [(i, across(i, count)) for i in range(count)])  6.85 us
  transfers between devices with their start and end apart: 39, of which 21 were waited for; matrix products, arithmetic and copies ran while one was open for 0% of the time, Pallas kernels for 3%

profile of v6, /device:TPU:1, one launch (start us, length us, event | category | flops | bytes accessed | tf_op | source)
XLA Modules:
  0.0 235.4 jit_solution(8233637051057315909)
XLA Ops:
  10.8 66.9 %conditional.15 = (f32[72,128]{1,0:T(8,128)}, f32[4,8,128]{2,1,0:T(8,128)}, f32[8,6,8,128]{3,2,1,0:T(8,128)}, f32[8,8,8,128]{3,2,1,0:T(8,128)}, f32[8,6,8,128]{3...) conditional(s32[]{:T(128)} %convert_element_type.41, () %tuple.144, ...), branch_computations={%region_0.1_spmd, %region_1.10_spmd} | conditional | flops 32600166400 | bytes 324813952 | solution.py:388
  10.8 16.5 %collective-permute-start.24 = (f32[6,8,128]{2,1,0:T(8,128)S(1)}, f32[6,8,128]{2,1,0:T(8,128)S(1)}, u32[]{:S(2)}, u32[]{:S(2)}) collective-permute-start(f32[6,8,128]{2,1,0:T(8,128)S(1)} %pad_maximum_fusion.1), channel_id=1, source_target_pairs={{0,1},{1,0},{2,3},{3,2},{4,5},{5,4},{6,7},{7,6},{8,9},{9,8},{10,11... | collective-permute-start | bytes 73736 | tf_op jit(solution)/shard_map/cond/branch_1_fun/ppermute | solution.py:317
  28.1 9.3 %collective-permute-start.25 = (f32[2,2,8,128]{3,2,1,0:T(8,128)S(1)}, f32[2,2,8,128]{3,2,1,0:T(8,128)S(1)}, u32[]{:S(2)}, u32[]{:S(2)}) collective-permute-start(f32[2,2,8,128]{3,2,1,0:T(8,128)S(1)} %maximum_select_fusion.2.left_ref), channel_id=1, source_target_pairs={{0,975},{1,961},{2,962},{3,963},{4,964},{5,965},{6,966},{7,967},{8... | collective-permute-start | bytes 49160 | tf_op jit(solution)/shard_map/cond/branch_1_fun/ppermute | solution.py:342
  40.8 6.8 %collective-permute-start.26 = (f32[8,6,8,128]{3,2,1,0:T(8,128)}, f32[8,6,8,128]{3,2,1,0:T(8,128)}, u32[]{:S(2)}, u32[]{:S(2)}) collective-permute-start(f32[8,6,8,128]{3,2,1,0:T(8,128)} %get-tuple-element.300), channel_id=1, source_target_pairs={{1,961},{2,962},{3,963},{4,964},{5,965},{6,966},{7,967},{8,968},{9... | collective-permute-start | bytes 589832 | tf_op jit(solution)/shard_map/cond/branch_1_fun/ppermute | solution.py:353
  47.6 30.1 %conditional.3 = (f32[72,128]{1,0:T(8,128)}, f32[4,8,128]{2,1,0:T(8,128)}, f32[8,6,8,128]{3,2,1,0:T(8,128)}, f32[8,8,8,128]{3,2,1,0:T(8,128)}, f32[8,6,8,128]{3,2,1,0:T(8,128)}) conditional(s32[]{:T(128)} %convert_element_type.31, () %tuple.82, (pred[]{:T(512)}, f32[2,2,8,128]{3,2,1,0:T(8,128)S(1)}, f32[4,8,128]{2,1,0:T(8,128)S(1)}, pred[]{:T(512)}, ...), branch_computations={%region_2.2_spmd, %region_3.9_spmd} | conditional | flops 24000143360 | bytes 243475008 | solution.py:388
  52.1 25.5 %conditional.2 = (f32[72,128]{1,0:T(8,128)}, f32[4,8,128]{2,1,0:T(8,128)}, f32[8,6,8,128]{3,2,1,0:T(8,128)}, f32[8,8,8,128]{3,2,1,0:T(8,128)}) conditional(s32[]{:T(128)} %convert_element_type.30, () %tuple.78, (pred[]{:T(512)}, f32[2,2,8,128]{3,2,1,0:T(8,128)S(1)}, f32[4,8,128]{2,1,0:T(8,128)S(1)}, pred[]{:T(512)}, pred[]{:T(512)}, ...), branch_computations={%region_4.3_spmd, %region_5.8_spmd} | conditional | flops 16000143360 | bytes 162622848 | solution.py:388
  58.7 19.0 %conditional.1 = (f32[72,128]{1,0:T(8,128)}, f32[4,8,128]{2,1,0:T(8,128)}, f32[8,6,8,128]{3,2,1,0:T(8,128)}) conditional(s32[]{:T(128)} %convert_element_type.20, () %tuple.74, (pred[]{:T(512)}, f32[2,2,8,128]{3,2,1,0:T(8,128)S(1)}, f32[4,8,128]{2,1,0:T(8,128)S(1)}, pred[]{:T(512)}, pred[]{:T(512)}, /*index=5*/s32[8]{0:T(128)S(1)}, ...), branch_computations={%region_6.4_spmd, %region_7.7_spmd} | conditional | flops 8000143872 | bytes 81508560 | solution.py:388
  66.5 11.2 %conditional = ((f32[72,128]{1,0:T(8,128)}, f32[4,8,128]{2,1,0:T(8,128)})) conditional(s32[]{:T(128)} %convert_element_type.19, () %tuple.70, (pred[]{:T(512)}, f32[2,2,8,128]{3,2,1,0:T(8,128)S(1)}, pred[]{:T(512)}, s32[8]{0:T(128)S(1)}, f32[8,8,128]{2,1,0:T(8,128)S(1)}) %tuple.71), branch_computations={%region_8.5_spmd, %region_9.6_spmd} | conditional | flops 135840 | bytes 492603 | solution.py:388
  80.0 7.1 %collective-permute-done.34.refs_10_ = f32[8,8,8,128]{3,2,1,0:T(8,128)S(1)} collective-permute-done((f32[8,8,8,128]{3,2,1,0:T(8,128)S(1)}, f32[8,8,8,128]{3,2,1,0:T(8,128)S(1)}, u32[]{:S(2)}, u32[]{:S(2)}) %collective-permute-start.34) | collective-permute-done | bytes 262176 | tf_op jit(solution)/shard_map/ppermute | solution.py:317
  98.3 51.7 %conditional.16 = (f32[72,128]{1,0:T(8,128)}, f32[4,8,128]{2,1,0:T(8,128)}, f32[8,6,8,128]{3,2,1,0:T(8,128)}, f32[8,8,8,128]{3,2,1,0:T(8,128)}, f32[8,6,8,128]{3...) conditional(s32[]{:T(128)} %convert_element_type.41, () %tuple.148, (pred[]{:T(512)}, ...), branch_computations={%region_10.11_spmd, %region_11.20_spmd} | conditional | flops 32000165888 | bytes 324613952 | solution.py:388
  109.9 9.6 %collective-permute-start.29 = (f32[8,6,8,128]{3,2,1,0:T(8,128)}, f32[8,6,8,128]{3,2,1,0:T(8,128)}, u32[]{:S(2)}, u32[]{:S(2)}) collective-permute-start(f32[8,6,8,128]{3,2,1,0:T(8,128)} %get-tuple-element.364), channel_id=1, source_target_pairs={{1,961},{2,962},{3,963},{4,964},{5,965},{6,966},{7,967},{8,968},{9... | collective-permute-start | bytes 589832 | tf_op jit(solution)/shard_map/cond/branch_1_fun/ppermute | solution.py:353
  119.5 30.4 %conditional.7 = (f32[72,128]{1,0:T(8,128)}, f32[4,8,128]{2,1,0:T(8,128)}, f32[8,6,8,128]{3,2,1,0:T(8,128)}, f32[8,8,8,128]{3,2,1,0:T(8,128)}, f32[8,6,8,128]{3,2,1,0:T(8,128)}) conditional(s32[]{:T(128)} %convert_element_type.35, () %tuple.105, (pred[]{:T(512)}, f32[2,2,8,128]{3,2,1,0:T(8,128)S(1)}, f32[4,8,128]{2,1,0:T(8,128)S(1)}, pred[]{:T(512)}, ...), branch_computations={%region_12.12_spmd, %region_13.19_spmd} | conditional | flops 24000143360 | bytes 243475008 | solution.py:388
  124.2 25.8 %conditional.6 = (f32[72,128]{1,0:T(8,128)}, f32[4,8,128]{2,1,0:T(8,128)}, f32[8,6,8,128]{3,2,1,0:T(8,128)}, f32[8,8,8,128]{3,2,1,0:T(8,128)}) conditional(s32[]{:T(128)} %convert_element_type.34, () %tuple.101, (pred[]{:T(512)}, f32[2,2,8,128]{3,2,1,0:T(8,128)S(1)}, f32[4,8,128]{2,1,0:T(8,128)S(1)}, pred[]{:T(512)}, pred[]{:T(512)}, ...), branch_computations={%region_14.13_spmd, %region_15.18_spmd} | conditional | flops 16000143360 | bytes 162622848 | solution.py:388
  130.7 19.2 %conditional.5 = (f32[72,128]{1,0:T(8,128)}, f32[4,8,128]{2,1,0:T(8,128)}, f32[8,6,8,128]{3,2,1,0:T(8,128)}) conditional(s32[]{:T(128)} %convert_element_type.33, () %tuple.97, (pred[]{:T(512)}, f32[2,2,8,128]{3,2,1,0:T(8,128)S(1)}, f32[4,8,128]{2,1,0:T(8,128)S(1)}, pred[]{:T(512)}, pred[]{:T(512)}, /*index=5*/s32[8]{0:T(128)S(1)}, ...), branch_computations={%region_16.14_spmd, %region_17.17_spmd} | conditional | flops 8000143872 | bytes 81508560 | solution.py:388
  139.0 10.9 %conditional.4 = ((f32[72,128]{1,0:T(8,128)}, f32[4,8,128]{2,1,0:T(8,128)})) conditional(s32[]{:T(128)} %convert_element_type.32, () %tuple.93, (pred[]{:T(512)}, f32[2,2,8,128]{3,2,1,0:T(8,128)S(1)}, pred[]{:T(512)}, s32[8]{0:T(128)S(1)}, f32[8,8,128]{2,1,0:T(8,128)S(1)}) %tuple.94), branch_computations={%region_18.15_spmd, %region_19.16_spmd} | conditional | flops 135840 | bytes 492603 | solution.py:388
  152.1 6.7 %collective-permute-done.36.refs_11_ = f32[8,8,8,128]{3,2,1,0:T(8,128)S(1)} collective-permute-done((f32[8,8,8,128]{3,2,1,0:T(8,128)S(1)}, f32[8,8,8,128]{3,2,1,0:T(8,128)S(1)}, u32[]{:S(2)}, u32[]{:S(2)}) %collective-permute-start.36) | collective-permute-done | bytes 262176 | tf_op jit(solution)/shard_map/ppermute | solution.py:317
  170.0 51.4 %conditional.17 = (f32[72,128]{1,0:T(8,128)}, f32[4,8,128]{2,1,0:T(8,128)}, f32[8,6,8,128]{3,2,1,0:T(8,128)}, f32[8,8,8,128]{3,2,1,0:T(8,128)}, f32[8,6,8,128]{3...) conditional(s32[]{:T(128)} %convert_element_type.41, () %tuple.152, (pred[]{:T(512)}, ...), branch_computations={%region_20.21_spmd, %region_21.30_spmd} | conditional | flops 32000165888 | bytes 324613952 | solution.py:388
  175.7 8.1 %collective-permute-start.31 = (f32[2,2,8,128]{3,2,1,0:T(8,128)S(1)}, f32[2,2,8,128]{3,2,1,0:T(8,128)S(1)}, u32[]{:S(2)}, u32[]{:S(2)}) collective-permute-start(f32[2,2,8,128]{3,2,1,0:T(8,128)S(1)} %maximum_select_fusion.8.left_ref), channel_id=1, source_target_pairs={{0,975},{1,961},{2,962},{3,963},{4,964},{5,965},{6,966},{7,967},{8... | collective-permute-start | bytes 49160 | tf_op jit(solution)/shard_map/cond/branch_1_fun/ppermute | solution.py:342
  183.8 8.0 %collective-permute-start.32 = (f32[8,6,8,128]{3,2,1,0:T(8,128)}, f32[8,6,8,128]{3,2,1,0:T(8,128)}, u32[]{:S(2)}, u32[]{:S(2)}) collective-permute-start(f32[8,6,8,128]{3,2,1,0:T(8,128)} %get-tuple-element.427), channel_id=1, source_target_pairs={{1,961},{2,962},{3,963},{4,964},{5,965},{6,966},{7,967},{8,968},{9... | collective-permute-start | bytes 589832 | tf_op jit(solution)/shard_map/cond/branch_1_fun/ppermute | solution.py:353
  191.9 29.5 %conditional.11 = (f32[72,128]{1,0:T(8,128)}, f32[4,8,128]{2,1,0:T(8,128)}, f32[8,6,8,128]{3,2,1,0:T(8,128)}, f32[8,8,8,128]{3,2,1,0:T(8,128)}, f32[8,6,8,128]{3,2,1,0:T(8,128)}) conditional(s32[]{:T(128)} %convert_element_type.39, () %tuple.127, (pred[]{:T(512)}, f32[2,2,8,128]{3,2,1,0:T(8,128)S(1)}, f32[4,8,128]{2,1,0:T(8,128)S(1)}, pred[]{:T(512)}, ...), branch_computations={%region_22.22_spmd, %region_23.29_spmd} | conditional | flops 24000143360 | bytes 243475008 | solution.py:388
  196.5 24.8 %conditional.10 = (f32[72,128]{1,0:T(8,128)}, f32[4,8,128]{2,1,0:T(8,128)}, f32[8,6,8,128]{3,2,1,0:T(8,128)}, f32[8,8,8,128]{3,2,1,0:T(8,128)}) conditional(s32[]{:T(128)} %convert_element_type.38, () %tuple.123, (pred[]{:T(512)}, f32[2,2,8,128]{3,2,1,0:T(8,128)S(1)}, f32[4,8,128]{2,1,0:T(8,128)S(1)}, pred[]{:T(512)}, pred[]{:T(512)}, ...), branch_computations={%region_24.23_spmd, %region_25.28_spmd} | conditional | flops 16000143360 | bytes 162622848 | solution.py:388
  203.0 18.3 %conditional.9 = (f32[72,128]{1,0:T(8,128)}, f32[4,8,128]{2,1,0:T(8,128)}, f32[8,6,8,128]{3,2,1,0:T(8,128)}) conditional(s32[]{:T(128)} %convert_element_type.37, () %tuple.119, (pred[]{:T(512)}, f32[2,2,8,128]{3,2,1,0:T(8,128)S(1)}, f32[4,8,128]{2,1,0:T(8,128)S(1)}, pred[]{:T(512)}, pred[]{:T(512)}, /*index=5*/s32[8]{0:T(128)S(1)}, ...), branch_computations={%region_26.24_spmd, %region_27.27_spmd} | conditional | flops 8000143872 | bytes 81508560 | solution.py:388
  209.6 11.7 %conditional.8 = ((f32[72,128]{1,0:T(8,128)}, f32[4,8,128]{2,1,0:T(8,128)})) conditional(s32[]{:T(128)} %convert_element_type.36, () %tuple.115, (pred[]{:T(512)}, f32[2,2,8,128]{3,2,1,0:T(8,128)S(1)}, pred[]{:T(512)}, s32[8]{0:T(128)S(1)}, f32[8,8,128]{2,1,0:T(8,128)S(1)}) %tuple.116), branch_computations={%region_28.25_spmd, %region_29.26_spmd} | conditional | flops 135840 | bytes 492603 | solution.py:388
  223.5 7.0 %collective-permute-done.38.refs_11_ = f32[8,8,8,128]{3,2,1,0:T(8,128)S(1)} collective-permute-done((f32[8,8,8,128]{3,2,1,0:T(8,128)S(1)}, f32[8,8,8,128]{3,2,1,0:T(8,128)S(1)}, u32[]{:S(2)}, u32[]{:S(2)}) %collective-permute-start.38) | collective-permute-done | bytes 262176 | tf_op jit(solution)/shard_map/ppermute | solution.py:317
  (144 shorter events, 154.7 us)
Async XLA Ops:
  10.8 17.4 %collective-permute-start.24 = (f32[6,8,128]{2,1,0:T(8,128)S(1)}, f32[6,8,128]{2,1,0:T(8,128)S(1)}, u32[]{:S(2)}, u32[]{:S(2)}) collective-permute-start(f32[6,8,128]{2,1,0:T(8,128)S(1)} %pad_maximum_fusion.1), channel_id=1, source_target_pairs={{0,1},{1,0},{2,3},{3,2},{4,5},{5,4},{6,7},{7,6},{8,9},{9,8},{10,11... | collective-permute-start | bytes 73736 | tf_op jit(solution)/shard_map/cond/branch_1_fun/ppermute | solution.py:317
  28.1 19.5 %collective-permute-start.25 = (f32[2,2,8,128]{3,2,1,0:T(8,128)S(1)}, f32[2,2,8,128]{3,2,1,0:T(8,128)S(1)}, u32[]{:S(2)}, u32[]{:S(2)}) collective-permute-start(f32[2,2,8,128]{3,2,1,0:T(8,128)S(1)} %maximum_select_fusion.2.left_ref), channel_id=1, source_target_pairs={{0,975},{1,961},{2,962},{3,963},{4,964},{5,965},{6,966},{7,967},{8... | collective-permute-start | bytes 49160 | tf_op jit(solution)/shard_map/cond/branch_1_fun/ppermute | solution.py:342
  40.8 36.9 %collective-permute-start.26 = (f32[8,6,8,128]{3,2,1,0:T(8,128)}, f32[8,6,8,128]{3,2,1,0:T(8,128)}, u32[]{:S(2)}, u32[]{:S(2)}) collective-permute-start(f32[8,6,8,128]{3,2,1,0:T(8,128)} %get-tuple-element.300), channel_id=1, source_target_pairs={{1,961},{2,962},{3,963},{4,964},{5,965},{6,966},{7,967},{8,968},{9... | collective-permute-start | bytes 589832 | tf_op jit(solution)/shard_map/cond/branch_1_fun/ppermute | solution.py:353
  49.6 28.1 %collective-permute-start.7 = (f32[8,6,8,128]{3,2,1,0:T(8,128)S(1)}, f32[8,6,8,128]{3,2,1,0:T(8,128)}, u32[]{:S(2)}, u32[]{:S(2)}) collective-permute-start(f32[8,6,8,128]{3,2,1,0:T(8,128)S(1)} %get-tuple-element.281), channel_id=1, source_target_pairs={{0,64},{64,0},{128,192},{192,128},{256,320},{320,256},{384,448},{4... | collective-permute-start | bytes 589832 | tf_op jit(solution)/shard_map/cond/branch_1_fun/cond/branch_1_fun/ppermute | solution.py:317
  52.1 6.5 %collective-permute-start.4 = (f32[2,2,8,128]{3,2,1,0:T(8,128)S(1)}, f32[2,2,8,128]{3,2,1,0:T(8,128)S(1)}, u32[]{:S(2)}, u32[]{:S(2)}) collective-permute-start(f32[2,2,8,128]{3,2,1,0:T(8,128)S(1)} %get-tuple-element.257.left_ref), channel_id=1, source_target_pairs={{0,48},{16,32},{32,16},{48,0},{1,49},{17,33},{33,17},{49,1},{2,50}... | collective-permute-start | bytes 49160 | tf_op jit(solution)/shard_map/cond/branch_1_fun/cond/branch_1_fun/cond/branch_1_fun/ppermute | solution.py:326
  54.0 23.6 %collective-permute-start.5 = (f32[8,8,8,128]{3,2,1,0:T(8,128)S(1)}, f32[8,8,8,128]{3,2,1,0:T(8,128)}, u32[]{:S(2)}, u32[]{:S(2)}) collective-permute-start(f32[8,8,8,128]{3,2,1,0:T(8,128)S(1)} %get-tuple-element.267), channel_id=1, source_target_pairs={{0,48},{16,32},{32,16},{48,0},{1,49},{17,33},{33,17},{49,1},{2,50}... | collective-permute-start | bytes 786440 | tf_op jit(solution)/shard_map/cond/branch_1_fun/cond/branch_1_fun/cond/branch_1_fun/ppermute | solution.py:326
  58.7 7.8 %collective-permute-start.2 = (f32[8,8,128]{2,1,0:T(8,128)S(1)}, f32[8,8,128]{2,1,0:T(8,128)S(1)}, u32[]{:S(2)}, u32[]{:S(2)}) collective-permute-start(f32[8,8,128]{2,1,0:T(8,128)S(1)} %pad_maximum_fusion), channel_id=1, source_target_pairs={{0,15},{1,2},{2,1},{3,4},{4,3},{5,6},{6,5},{7,8},{8,7},{9,10},{10,... | collective-permute-start | bytes 98312 | tf_op jit(solution)/shard_map/cond/branch_1_fun/cond/branch_1_fun/cond/branch_1_fun/cond/branch_1_fun/ppermute | solution.py:326
  60.6 17.0 %collective-permute-start.3 = (f32[8,6,8,128]{3,2,1,0:T(8,128)}, f32[8,6,8,128]{3,2,1,0:T(8,128)}, u32[]{:S(2)}, u32[]{:S(2)}) collective-permute-start(f32[8,6,8,128]{3,2,1,0:T(8,128)} %get-tuple-element.255), channel_id=1, source_target_pairs={{0,960},{15,975},{448,512},{463,527},{512,448},{527,463},{960,0},{... | collective-permute-start | bytes 589832 | tf_op jit(solution)/shard_map/cond/branch_1_fun/cond/branch_1_fun/cond/branch_1_fun/cond/branch_1_fun/ppermute | solution.py:353
  77.7 9.4 %collective-permute-start.34 = (f32[8,8,8,128]{3,2,1,0:T(8,128)S(1)}, f32[8,8,8,128]{3,2,1,0:T(8,128)S(1)}, u32[]{:S(2)}, u32[]{:S(2)}) collective-permute-start(f32[8,8,8,128]{3,2,1,0:T(8,128)S(1)} %copy-done.5), channel_id=1, source_target_pairs={{0,16},{16,0},{32,48},{48,32},{1,17},{17,1},{33,49},{49,33},{2,18}... | collective-permute-start | bytes 786440 | tf_op jit(solution)/shard_map/ppermute | solution.py:317
  103.4 16.1 %collective-permute-start.28 = (f32[2,2,8,128]{3,2,1,0:T(8,128)S(1)}, f32[2,2,8,128]{3,2,1,0:T(8,128)S(1)}, u32[]{:S(2)}, u32[]{:S(2)}) collective-permute-start(f32[2,2,8,128]{3,2,1,0:T(8,128)S(1)} %maximum_select_fusion.5.left_ref), channel_id=1, source_target_pairs={{0,975},{1,961},{2,962},{3,963},{4,964},{5,965},{6,966},{7,967},{8... | collective-permute-start | bytes 49160 | tf_op jit(solution)/shard_map/cond/branch_1_fun/ppermute | solution.py:342
  109.9 40.1 %collective-permute-start.29 = (f32[8,6,8,128]{3,2,1,0:T(8,128)}, f32[8,6,8,128]{3,2,1,0:T(8,128)}, u32[]{:S(2)}, u32[]{:S(2)}) collective-permute-start(f32[8,6,8,128]{3,2,1,0:T(8,128)} %get-tuple-element.364), channel_id=1, source_target_pairs={{1,961},{2,962},{3,963},{4,964},{5,965},{6,966},{7,967},{8,968},{9... | collective-permute-start | bytes 589832 | tf_op jit(solution)/shard_map/cond/branch_1_fun/ppermute | solution.py:353
  121.9 28.1 %collective-permute-start.15 = (f32[8,6,8,128]{3,2,1,0:T(8,128)S(1)}, f32[8,6,8,128]{3,2,1,0:T(8,128)}, u32[]{:S(2)}, u32[]{:S(2)}) collective-permute-start(f32[8,6,8,128]{3,2,1,0:T(8,128)S(1)} %get-tuple-element.348), channel_id=1, source_target_pairs={{0,64},{64,0},{128,192},{192,128},{256,320},{320,256},{384,448},{4... | collective-permute-start | bytes 589832 | tf_op jit(solution)/shard_map/cond/branch_1_fun/cond/branch_1_fun/ppermute | solution.py:317
  124.2 6.5 %collective-permute-start.12 = (f32[2,2,8,128]{3,2,1,0:T(8,128)S(1)}, f32[2,2,8,128]{3,2,1,0:T(8,128)S(1)}, u32[]{:S(2)}, u32[]{:S(2)}) collective-permute-start(f32[2,2,8,128]{3,2,1,0:T(8,128)S(1)} %get-tuple-element.324.left_ref), channel_id=1, source_target_pairs={{0,48},{16,32},{32,16},{48,0},{1,49},{17,33},{33,17},{49,1},{2,50}... | collective-permute-start | bytes 49160 | tf_op jit(solution)/shard_map/cond/branch_1_fun/cond/branch_1_fun/cond/branch_1_fun/ppermute | solution.py:326
  128.1 21.9 %collective-permute-start.13 = (f32[8,8,8,128]{3,2,1,0:T(8,128)S(1)}, f32[8,8,8,128]{3,2,1,0:T(8,128)}, u32[]{:S(2)}, u32[]{:S(2)}) collective-permute-start(f32[8,8,8,128]{3,2,1,0:T(8,128)S(1)} %get-tuple-element.334), channel_id=1, source_target_pairs={{0,48},{16,32},{32,16},{48,0},{1,49},{17,33},{33,17},{49,1},{2,50}... | collective-permute-start | bytes 786440 | tf_op jit(solution)/shard_map/cond/branch_1_fun/cond/branch_1_fun/cond/branch_1_fun/ppermute | solution.py:326
  130.8 8.3 %collective-permute-start.10 = (f32[8,8,128]{2,1,0:T(8,128)S(1)}, f32[8,8,128]{2,1,0:T(8,128)S(1)}, u32[]{:S(2)}, u32[]{:S(2)}) collective-permute-start(f32[8,8,128]{2,1,0:T(8,128)S(1)} %pad_maximum_fusion.2), channel_id=1, source_target_pairs={{0,15},{1,2},{2,1},{3,4},{4,3},{5,6},{6,5},{7,8},{8,7},{9,10},{10,... | collective-permute-start | bytes 98312 | tf_op jit(solution)/shard_map/cond/branch_1_fun/cond/branch_1_fun/cond/branch_1_fun/cond/branch_1_fun/ppermute | solution.py:326
  136.1 13.9 %collective-permute-start.11 = (f32[8,6,8,128]{3,2,1,0:T(8,128)}, f32[8,6,8,128]{3,2,1,0:T(8,128)}, u32[]{:S(2)}, u32[]{:S(2)}) collective-permute-start(f32[8,6,8,128]{3,2,1,0:T(8,128)} %get-tuple-element.322), channel_id=1, source_target_pairs={{0,960},{15,975},{448,512},{463,527},{512,448},{527,463},{960,0},{... | collective-permute-start | bytes 589832 | tf_op jit(solution)/shard_map/cond/branch_1_fun/cond/branch_1_fun/cond/branch_1_fun/cond/branch_1_fun/ppermute | solution.py:353
  150.0 8.8 %collective-permute-start.36 = (f32[8,8,8,128]{3,2,1,0:T(8,128)S(1)}, f32[8,8,8,128]{3,2,1,0:T(8,128)S(1)}, u32[]{:S(2)}, u32[]{:S(2)}) collective-permute-start(f32[8,8,8,128]{3,2,1,0:T(8,128)S(1)} %get-tuple-element.546.refs_1_.refs_2_), channel_id=1, source_target_pairs={{0,16},{16,0},{32,48},{48,32},{1,17},{17,1},{33,49},{49,33},{2,18}... | collective-permute-start | bytes 786440 | tf_op jit(solution)/shard_map/ppermute | solution.py:317
  175.7 16.1 %collective-permute-start.31 = (f32[2,2,8,128]{3,2,1,0:T(8,128)S(1)}, f32[2,2,8,128]{3,2,1,0:T(8,128)S(1)}, u32[]{:S(2)}, u32[]{:S(2)}) collective-permute-start(f32[2,2,8,128]{3,2,1,0:T(8,128)S(1)} %maximum_select_fusion.8.left_ref), channel_id=1, source_target_pairs={{0,975},{1,961},{2,962},{3,963},{4,964},{5,965},{6,966},{7,967},{8... | collective-permute-start | bytes 49160 | tf_op jit(solution)/shard_map/cond/branch_1_fun/ppermute | solution.py:342
  183.8 37.5 %collective-permute-start.32 = (f32[8,6,8,128]{3,2,1,0:T(8,128)}, f32[8,6,8,128]{3,2,1,0:T(8,128)}, u32[]{:S(2)}, u32[]{:S(2)}) collective-permute-start(f32[8,6,8,128]{3,2,1,0:T(8,128)} %get-tuple-element.427), channel_id=1, source_target_pairs={{1,961},{2,962},{3,963},{4,964},{5,965},{6,966},{7,967},{8,968},{9... | collective-permute-start | bytes 589832 | tf_op jit(solution)/shard_map/cond/branch_1_fun/ppermute | solution.py:353
  193.8 27.5 %collective-permute-start.23 = (f32[8,6,8,128]{3,2,1,0:T(8,128)S(1)}, f32[8,6,8,128]{3,2,1,0:T(8,128)}, u32[]{:S(2)}, u32[]{:S(2)}) collective-permute-start(f32[8,6,8,128]{3,2,1,0:T(8,128)S(1)} %get-tuple-element.411), channel_id=1, source_target_pairs={{0,64},{64,0},{128,192},{192,128},{256,320},{320,256},{384,448},{4... | collective-permute-start | bytes 589832 | tf_op jit(solution)/shard_map/cond/branch_1_fun/cond/branch_1_fun/ppermute | solution.py:317
  196.5 6.5 %collective-permute-start.20 = (f32[2,2,8,128]{3,2,1,0:T(8,128)S(1)}, f32[2,2,8,128]{3,2,1,0:T(8,128)S(1)}, u32[]{:S(2)}, u32[]{:S(2)}) collective-permute-start(f32[2,2,8,128]{3,2,1,0:T(8,128)S(1)} %get-tuple-element.387.left_ref), channel_id=1, source_target_pairs={{0,48},{16,32},{32,16},{48,0},{1,49},{17,33},{33,17},{49,1},{2,50}... | collective-permute-start | bytes 49160 | tf_op jit(solution)/shard_map/cond/branch_1_fun/cond/branch_1_fun/cond/branch_1_fun/ppermute | solution.py:326
  200.5 20.8 %collective-permute-start.21 = (f32[8,8,8,128]{3,2,1,0:T(8,128)S(1)}, f32[8,8,8,128]{3,2,1,0:T(8,128)}, u32[]{:S(2)}, u32[]{:S(2)}) collective-permute-start(f32[8,8,8,128]{3,2,1,0:T(8,128)S(1)} %get-tuple-element.397), channel_id=1, source_target_pairs={{0,48},{16,32},{32,16},{48,0},{1,49},{17,33},{33,17},{49,1},{2,50}... | collective-permute-start | bytes 786440 | tf_op jit(solution)/shard_map/cond/branch_1_fun/cond/branch_1_fun/cond/branch_1_fun/ppermute | solution.py:326
  207.6 13.7 %collective-permute-start.19 = (f32[8,6,8,128]{3,2,1,0:T(8,128)}, f32[8,6,8,128]{3,2,1,0:T(8,128)}, u32[]{:S(2)}, u32[]{:S(2)}) collective-permute-start(f32[8,6,8,128]{3,2,1,0:T(8,128)} %get-tuple-element.385), channel_id=1, source_target_pairs={{0,960},{15,975},{448,512},{463,527},{512,448},{527,463},{960,0},{... | collective-permute-start | bytes 589832 | tf_op jit(solution)/shard_map/cond/branch_1_fun/cond/branch_1_fun/cond/branch_1_fun/cond/branch_1_fun/ppermute | solution.py:353
  221.3 9.2 %collective-permute-start.38 = (f32[8,8,8,128]{3,2,1,0:T(8,128)S(1)}, f32[8,8,8,128]{3,2,1,0:T(8,128)S(1)}, u32[]{:S(2)}, u32[]{:S(2)}) collective-permute-start(f32[8,8,8,128]{3,2,1,0:T(8,128)S(1)} %get-tuple-element.569.refs_1_), channel_id=1, source_target_pairs={{0,16},{16,0},{32,48},{48,32},{1,17},{17,1},{33,49},{49,33},{2,18}... | collective-permute-start | bytes 786440 | tf_op jit(solution)/shard_map/ppermute | solution.py:317
  (22 other events, 156.3 us)

commit v7 on v6

--- a/solution.py
+++ b/solution.py
@@ -400,12 +400,6 @@
     def zeros_like_x(own):
         return (*zeros_like_y(own), jnp.zeros(x_shape, F32))
 
-    def zeros_like_all(pair):
-        return (*zeros_like_x(pair[:, :2]), jnp.zeros(z_shape, F32), jnp.zeros(x_shape, F32))
-
-    def zeros_like_first(pair):
-        return (*zeros_like_all(pair), jnp.zeros((SEGS, 128), F32))
-
     def energies():
         return call(
             lambda *refs: energy_kernel(sizes, *refs), [((SEGS, 128), F32)], [],
@@ -455,32 +449,28 @@
             )
             return (*rest, xa_in)
 
-        def along_z_inside(pair):
-            come = swap_inside(
-                jnp.concatenate([jnp.where(odd_z, pair[:, 0], pair[:, 2]), za], axis=0), "gz"
-            )
-            middle = pair[:, 1] + come[:2]
-            own = jnp.where(
-                odd_z,
-                jnp.stack([middle, pair[:, 2]], axis=1),
-                jnp.stack([pair[:, 0], middle], axis=1),
-            )
-            rest, xb_in = staged(
-                swap_corners, own, lambda v: swap_far_faces(v, False), xb,
-                lambda come: total(own, come), along_y_inside, zeros_like_x,
-                energies if first else tuple,
-            )
-            return (*rest[:5], come[2:], xb_in, *rest[5:])
-
-        rest, ya_in = staged(
-            lambda v: swap_inside(v, "gx"), give, lambda v: swap_inside(v, "gy"), cells,
-            lambda come: total(
-                keep.reshape(2, 3, 8, 128),
-                jnp.where(place == 1 - places[0] % 2, come.reshape(1, 3, 8, 128), 0.0),
-            ),
-            along_z_inside, zeros_like_first if first else zeros_like_all,
-        )
-        table, zb_in, corner_in, yb_in, xa_in, za_in, xb_in, *made = rest
+        cells, give = lax.optimization_barrier((cells, give))
+        come = swap_inside(give, "gx").reshape(1, 3, 8, 128)
+        pair = total(
+            keep.reshape(2, 3, 8, 128), jnp.where(place == 1 - places[0] % 2, come, 0.0)
+        )
+        come = swap_inside(
+            jnp.concatenate([jnp.where(odd_z, pair[:, 0], pair[:, 2]), za], axis=0), "gz"
+        )
+        za_in = come[2:]
+        middle = pair[:, 1] + come[:2]
+        own = jnp.where(
+            odd_z,
+            jnp.stack([middle, pair[:, 2]], axis=1),
+            jnp.stack([pair[:, 0], middle], axis=1),
+        )
+        ya_in = swap_inside(cells, "gy")
+        rest, xb_in = staged(
+            swap_corners, own, lambda v: swap_far_faces(v, False), xb,
+            lambda come: total(own, come), along_y_inside, zeros_like_x,
+            lambda: (ya_in, *(energies() if first else ())),
+        )
+        table, zb_in, corner_in, yb_in, xa_in, ya_in, *made = rest
         energy = made[0] if first else energy
         return energy, table, xa_in, xb_in, corner_in, ya_in, yb_in, za_in, zb_in
 

time: 238 us -> 209 us (0.88)
  waiting for transfers between devices: 47 us -> 25.5 us
  starting transfers between devices: 157 us -> 151 us
    ppermute x21, waiting for transfers between devices: 40.2 us -> 16.2 us  [swap_inside(): return lax.ppermute(value, axis, [(i, i ^ 1) for i in range(count)])]
    ppermute x9, starting transfers between devices: 31.2 us -> 28.5 us  [swap_across(): lax.ppermute(value, axis, [(i, across(i, count)) for i in range(count)])]
    ppermute x9, waiting for transfers between devices: 6.85 us -> 9.28 us  [swap_across(): lax.ppermute(value, axis, [(i, across(i, count)) for i in range(count)])]
    ppermute x21, starting transfers between devices: 73 us -> 70.6 us  [swap_inside(): return lax.ppermute(value, axis, [(i, i ^ 1) for i in range(count)])]
  transfers between devices with their start and end apart: 39 -> 39, of which waited for: 21 -> 17; matrix products, arithmetic and copies ran while one was open for 0% -> 0% of each run, Pallas kernels for 3% -> 3%
where the time goes in v7:
time: 209 us; the launch traced here: 208 us
  starting transfers between devices  151 us (72%)
  Pallas kernels  27.9 us (13%)
  waiting for transfers between devices  25.5 us (12%)
    ppermute x21, starting transfers between devices, swap_inside(): return lax.ppermute(value, axis, [(i, i ^ 1) for i in range(count)])  70.6 us
    ppermute x9, starting transfers between devices, swap_across(): lax.ppermute(value, axis, [(i, across(i, count)) for i in range(count)])  28.5 us
    ppermute x6, starting transfers between devices, swap_far_faces(): return lax.ppermute(value, ('gx', 'gz'), pairs)  28.4 us
    pallas_call x8, Pallas kernels, call(): pl.pallas_call(kernel, out_shape=[jax.ShapeDtypeStruct(s, k) for s, k in...  27.8 us
    ppermute x3, starting transfers between devices, swap_corners(): return lax.ppermute(value, ('gx', 'gz'), pairs)  24 us
    ppermute x21, waiting for transfers between devices, swap_inside(): return lax.ppermute(value, axis, [(i, i ^ 1) for i in range(count)])  16.2 us
    ppermute x9, waiting for transfers between devices, swap_across(): lax.ppermute(value, axis, [(i, across(i, count)) for i in range(count)])  9.28 us
  transfers between devices with their start and end apart: 39, of which 17 were waited for; matrix products, arithmetic and copies ran while one was open for 0% of the time, Pallas kernels for 3%

profile of v7, /device:TPU:1, one launch (start us, length us, event | category | flops | bytes accessed | tf_op | source)
XLA Modules:
  0.0 207.8 jit_solution(15369491986071575223)
XLA Ops:
  12.0 14.6 %collective-permute-start.25 = (f32[6,8,128]{2,1,0:T(8,128)S(1)}, f32[6,8,128]{2,1,0:T(8,128)S(1)}, u32[]{:S(2)}, u32[]{:S(2)}) collective-permute-start(f32[6,8,128]{2,1,0:T(8,128)S(1)} %pad_maximum_fusion.3), channel_id=1, source_target_pairs={{0,1},{1,0},{2,3},{3,2},{4,5},{5,4},{6,7},{7,6},{8,9},{9,8},{10,11... | collective-permute-start | bytes 73736 | tf_op jit(solution)/shard_map/ppermute | solution.py:317
  27.4 10.5 %collective-permute-start.26 = (f32[2,2,8,128]{3,2,0,1:T(8,128)S(1)}, f32[2,2,8,128]{3,2,0,1:T(8,128)S(1)}, u32[]{:S(2)}, u32[]{:S(2)}) collective-permute-start(f32[2,2,8,128]{3,2,0,1:T(8,128)S(1)} %maximum_select_fusion.6), channel_id=1, source_target_pairs={{0,975},{1,961},{2,962},{3,963},{4,964},{5,965},{6,966},{7,967},{8... | collective-permute-start | bytes 49160 | tf_op jit(solution)/shard_map/ppermute | solution.py:342
  41.2 5.6 %collective-permute-start.28 = (f32[8,6,8,128]{3,2,1,0:T(8,128)}, f32[8,6,8,128]{3,2,1,0:T(8,128)S(1)}, u32[]{:S(2)}, u32[]{:S(2)}) collective-permute-start(f32[8,6,8,128]{3,2,1,0:T(8,128)} %get-tuple-element.395), channel_id=1, source_target_pairs={{1,961},{2,962},{3,963},{4,964},{5,965},{6,966},{7,967},{8,968},{9... | collective-permute-start | bytes 589832 | tf_op jit(solution)/shard_map/ppermute | solution.py:353
  46.9 33.4 %conditional.12 = (f32[72,128]{1,0:T(8,128)}, f32[4,8,128]{2,1,0:T(8,128)}, f32[8,6,8,128]{3,2,1,0:T(8,128)}, f32[8,8,8,128]{3,2,1,0:T(8,128)}, f32[8,6,8,128]{3,2,1,0:T(8,128)}) conditional(s32[]{:T(128)} %convert_element_type.32, () %tuple.119, (pred[]{:T(512)}, f32[2,2,8,128]{3,2,1,0:T(8,128)S(1)}, f32[4,8,128]{2,1,0:T(8,128)S(1)}, pred[]{:T(512)}, ...), branch_computations={%region_0.1_spmd, %region_1.8_spmd} | conditional | flops 24000143360 | bytes 243475008 | solution.py:388
  51.5 28.9 %conditional.2 = (f32[72,128]{1,0:T(8,128)}, f32[4,8,128]{2,1,0:T(8,128)}, f32[8,6,8,128]{3,2,1,0:T(8,128)}, f32[8,8,8,128]{3,2,1,0:T(8,128)}) conditional(s32[]{:T(128)} %convert_element_type.24, () %tuple.65, (pred[]{:T(512)}, f32[2,2,8,128]{3,2,1,0:T(8,128)S(1)}, f32[4,8,128]{2,1,0:T(8,128)S(1)}, pred[]{:T(512)}, pred[]{:T(512)}, ...), branch_computations={%region_2.2_spmd, %region_3.7_spmd} | conditional | flops 16000143360 | bytes 162622848 | solution.py:388
  58.0 22.4 %conditional.1 = (f32[72,128]{1,0:T(8,128)}, f32[4,8,128]{2,1,0:T(8,128)}, f32[8,6,8,128]{3,2,1,0:T(8,128)}) conditional(s32[]{:T(128)} %convert_element_type.15, () %tuple.61, (pred[]{:T(512)}, f32[2,2,8,128]{3,2,1,0:T(8,128)S(1)}, f32[4,8,128]{2,1,0:T(8,128)S(1)}, pred[]{:T(512)}, pred[]{:T(512)}, /*index=5*/s32[8]{0:T(128)S(1)}, ...), branch_computations={%region_4.3_spmd, %region_5.6_spmd} | conditional | flops 8000143872 | bytes 81508560 | solution.py:388
  61.3 5.8 %collective-permute-done.2 = f32[8,8,128]{2,1,0:T(8,128)S(1)} collective-permute-done((f32[8,8,128]{2,1,0:T(8,128)S(1)}, f32[8,8,128]{2,1,0:T(8,128)S(1)}, u32[]{:S(2)}, u32[]{:S(2)}) %collective-permute-start.2) | collective-permute-done | bytes 32800 | tf_op jit(solution)/shard_map/cond/branch_1_fun/cond/branch_1_fun/cond/branch_1_fun/ppermute | solution.py:326
  67.1 13.2 %conditional = ((f32[72,128]{1,0:T(8,128)}, f32[4,8,128]{2,1,0:T(8,128)})) conditional(s32[]{:T(128)} %convert_element_type.14, () %tuple.57, (pred[]{:T(512)}, f32[2,2,8,128]{3,2,1,0:T(8,128)S(1)}, pred[]{:T(512)}, s32[8]{0:T(128)S(1)}, f32[8,8,128]{2,1,0:T(8,128)S(1)}) %tuple.58), branch_computations={%region_6.4_spmd, %region_7.5_spmd} | conditional | flops 135840 | bytes 492603 | solution.py:388
  72.0 6.4 %collective-permute-start.1 = (f32[3,8,128]{2,1,0:T(8,128)S(1)}, f32[3,8,128]{2,1,0:T(8,128)S(1)}, u32[]{:S(2)}, u32[]{:S(2)}) collective-permute-start(f32[3,8,128]{2,1,0:T(8,128)S(1)} %fusion), channel_id=1, source_target_pairs={{0,1},{1,0},{2,3},{3,2},{4,5},{5,4},{6,7},{7,6},{8,9},{9,8},{10,11... | collective-permute-start | bytes 36872 | tf_op jit(solution)/shard_map/cond/branch_1_fun/cond/branch_1_fun/cond/branch_1_fun/cond/branch_1_fun/ppermute | solution.py:317
  80.4 6.5 %shard_map.86 = (f32[8,8,8,128]{3,2,1,0:T(8,128)S(1)}, f32[24,128]{1,0:T(8,128)S(1)}, f32[48,128]{1,0:T(8,128)S(1)}, f32[8,6,8,128]{3,2,1,0:T(8,128)S(1)}, f32[8...) custom-call(s32[8]{0:T(128)S(1)} %stack.93.refs_0_, f32[8,8,8,128]{3,2,1,0:T(8,128)S(1)} %copy-done.6, ...), custom_call_target="tpu_custom_call" | custom-call | flops 1500000000 | bytes 4000000 | tf_op jit(solution)/shard_map/pallas_call | solution.py:289
  95.7 5.2 %collective-permute-start.31 = (f32[2,2,8,128]{3,2,0,1:T(8,128)S(1)}, f32[2,2,8,128]{3,2,0,1:T(8,128)S(1)}, u32[]{:S(2)}, u32[]{:S(2)}) collective-permute-start(f32[2,2,8,128]{3,2,0,1:T(8,128)S(1)} %maximum_select_fusion.7), channel_id=1, source_target_pairs={{0,975},{1,961},{2,962},{3,963},{4,964},{5,965},{6,966},{7,967},{8... | collective-permute-start | bytes 49160 | tf_op jit(solution)/shard_map/ppermute | solution.py:342
  100.9 10.9 %collective-permute-start.33 = (f32[8,6,8,128]{3,2,1,0:T(8,128)}, f32[8,6,8,128]{3,2,1,0:T(8,128)S(1)}, u32[]{:S(2)}, u32[]{:S(2)}) collective-permute-start(f32[8,6,8,128]{3,2,1,0:T(8,128)} %get-tuple-element.420), channel_id=1, source_target_pairs={{1,961},{2,962},{3,963},{4,964},{5,965},{6,966},{7,967},{8,968},{9... | collective-permute-start | bytes 589832 | tf_op jit(solution)/shard_map/ppermute | solution.py:353
  111.9 29.6 %conditional.13 = (f32[72,128]{1,0:T(8,128)}, f32[4,8,128]{2,1,0:T(8,128)}, f32[8,6,8,128]{3,2,1,0:T(8,128)}, f32[8,8,8,128]{3,2,1,0:T(8,128)}, f32[8,6,8,128]{3,2,1,0:T(8,128)}) conditional(s32[]{:T(128)} %convert_element_type.32, () %tuple.125, (pred[]{:T(512)}, f32[2,2,8,128]{3,2,1,0:T(8,128)S(1)}, f32[4,8,128]{2,1,0:T(8,128)S(1)}, pred[]{:T(512)}, ...), branch_computations={%region_8.9_spmd, %region_9.16_spmd} | conditional | flops 24000143360 | bytes 243475008 | solution.py:388
  116.5 24.7 %conditional.5 = (f32[72,128]{1,0:T(8,128)}, f32[4,8,128]{2,1,0:T(8,128)}, f32[8,6,8,128]{3,2,1,0:T(8,128)}, f32[8,8,8,128]{3,2,1,0:T(8,128)}) conditional(s32[]{:T(128)} %convert_element_type.27, () %tuple.81, (pred[]{:T(512)}, f32[2,2,8,128]{3,2,1,0:T(8,128)S(1)}, f32[4,8,128]{2,1,0:T(8,128)S(1)}, pred[]{:T(512)}, pred[]{:T(512)}, ...), branch_computations={%region_10.10_spmd, %region_11.15_spmd} | conditional | flops 16000143360 | bytes 162622848 | solution.py:388
  123.0 18.2 %conditional.4 = (f32[72,128]{1,0:T(8,128)}, f32[4,8,128]{2,1,0:T(8,128)}, f32[8,6,8,128]{3,2,1,0:T(8,128)}) conditional(s32[]{:T(128)} %convert_element_type.26, () %tuple.77, (pred[]{:T(512)}, f32[2,2,8,128]{3,2,1,0:T(8,128)S(1)}, f32[4,8,128]{2,1,0:T(8,128)S(1)}, pred[]{:T(512)}, pred[]{:T(512)}, /*index=5*/s32[8]{0:T(128)S(1)}, ...), branch_computations={%region_12.11_spmd, %region_13.14_spmd} | conditional | flops 8000143872 | bytes 81508560 | solution.py:388
  128.9 12.3 %conditional.3 = ((f32[72,128]{1,0:T(8,128)}, f32[4,8,128]{2,1,0:T(8,128)})) conditional(s32[]{:T(128)} %convert_element_type.25, () %tuple.73, (pred[]{:T(512)}, f32[2,2,8,128]{3,2,1,0:T(8,128)S(1)}, pred[]{:T(512)}, s32[8]{0:T(128)S(1)}, f32[8,8,128]{2,1,0:T(8,128)S(1)}) %tuple.74), branch_computations={%region_14.12_spmd, %region_15.13_spmd} | conditional | flops 135840 | bytes 492603 | solution.py:388
  133.3 5.9 %collective-permute-start.9 = (f32[3,8,128]{2,1,0:T(8,128)S(1)}, f32[3,8,128]{2,1,0:T(8,128)S(1)}, u32[]{:S(2)}, u32[]{:S(2)}) collective-permute-start(f32[3,8,128]{2,1,0:T(8,128)S(1)} %fusion.1), channel_id=1, source_target_pairs={{0,1},{1,0},{2,3},{3,2},{4,5},{5,4},{6,7},{7,6},{8,9},{9,8},{10,11... | collective-permute-start | bytes 36872 | tf_op jit(solution)/shard_map/cond/branch_1_fun/cond/branch_1_fun/cond/branch_1_fun/cond/branch_1_fun/ppermute | solution.py:317
  141.4 6.5 %shard_map.89 = (f32[8,8,8,128]{3,2,1,0:T(8,128)S(1)}, f32[24,128]{1,0:T(8,128)S(1)}, f32[48,128]{1,0:T(8,128)S(1)}, f32[8,6,8,128]{3,2,1,0:T(8,128)S(1)}, f32[8...) custom-call(s32[8]{0:T(128)S(1)} %stack.93.refs_0_, ...), custom_call_target="tpu_custom_call" | custom-call | flops 1500000000 | bytes 4000000 | tf_op jit(solution)/shard_map/pallas_call | solution.py:289
  156.7 8.3 %collective-permute-start.36 = (f32[2,2,8,128]{3,2,0,1:T(8,128)S(1)}, f32[2,2,8,128]{3,2,0,1:T(8,128)S(1)}, u32[]{:S(2)}, u32[]{:S(2)}) collective-permute-start(f32[2,2,8,128]{3,2,0,1:T(8,128)S(1)} %maximum_select_fusion.8), channel_id=1, source_target_pairs={{0,975},{1,961},{2,962},{3,963},{4,964},{5,965},{6,966},{7,967},{8... | collective-permute-start | bytes 49160 | tf_op jit(solution)/shard_map/ppermute | solution.py:342
  165.1 7.7 %collective-permute-start.38 = (f32[8,6,8,128]{3,2,1,0:T(8,128)}, f32[8,6,8,128]{3,2,1,0:T(8,128)S(1)}, u32[]{:S(2)}, u32[]{:S(2)}) collective-permute-start(f32[8,6,8,128]{3,2,1,0:T(8,128)} %get-tuple-element.444), channel_id=1, source_target_pairs={{1,961},{2,962},{3,963},{4,964},{5,965},{6,966},{7,967},{8,968},{9... | collective-permute-start | bytes 589832 | tf_op jit(solution)/shard_map/ppermute | solution.py:353
  172.9 30.1 %conditional.14 = (f32[72,128]{1,0:T(8,128)}, f32[4,8,128]{2,1,0:T(8,128)}, f32[8,6,8,128]{3,2,1,0:T(8,128)}, f32[8,8,8,128]{3,2,1,0:T(8,128)}, f32[8,6,8,128]{3,2,1,0:T(8,128)}) conditional(s32[]{:T(128)} %convert_element_type.32, () %tuple.131, (pred[]{:T(512)}, f32[2,2,8,128]{3,2,1,0:T(8,128)S(1)}, f32[4,8,128]{2,1,0:T(8,128)S(1)}, pred[]{:T(512)}, ...), branch_computations={%region_16.17_spmd, %region_17.24_spmd} | conditional | flops 24000143360 | bytes 243475008 | solution.py:388
  177.6 25.4 %conditional.8 = (f32[72,128]{1,0:T(8,128)}, f32[4,8,128]{2,1,0:T(8,128)}, f32[8,6,8,128]{3,2,1,0:T(8,128)}, f32[8,8,8,128]{3,2,1,0:T(8,128)}) conditional(s32[]{:T(128)} %convert_element_type.30, () %tuple.97, (pred[]{:T(512)}, f32[2,2,8,128]{3,2,1,0:T(8,128)S(1)}, f32[4,8,128]{2,1,0:T(8,128)S(1)}, pred[]{:T(512)}, pred[]{:T(512)}, ...), branch_computations={%region_18.18_spmd, %region_19.23_spmd} | conditional | flops 16000143360 | bytes 162622848 | solution.py:388
  184.1 18.9 %conditional.7 = (f32[72,128]{1,0:T(8,128)}, f32[4,8,128]{2,1,0:T(8,128)}, f32[8,6,8,128]{3,2,1,0:T(8,128)}) conditional(s32[]{:T(128)} %convert_element_type.29, () %tuple.93, (pred[]{:T(512)}, f32[2,2,8,128]{3,2,1,0:T(8,128)S(1)}, f32[4,8,128]{2,1,0:T(8,128)S(1)}, pred[]{:T(512)}, pred[]{:T(512)}, /*index=5*/s32[8]{0:T(128)S(1)}, ...), branch_computations={%region_20.19_spmd, %region_21.22_spmd} | conditional | flops 8000143872 | bytes 81508560 | solution.py:388
  191.6 11.4 %conditional.6 = ((f32[72,128]{1,0:T(8,128)}, f32[4,8,128]{2,1,0:T(8,128)})) conditional(s32[]{:T(128)} %convert_element_type.28, () %tuple.89, (pred[]{:T(512)}, f32[2,2,8,128]{3,2,1,0:T(8,128)S(1)}, pred[]{:T(512)}, s32[8]{0:T(128)S(1)}, f32[8,8,128]{2,1,0:T(8,128)S(1)}) %tuple.90), branch_computations={%region_22.20_spmd, %region_23.21_spmd} | conditional | flops 135840 | bytes 492603 | solution.py:388
  (150 shorter events, 112.0 us)
Async XLA Ops:
  4.7 7.2 %collective-permute-start.24 = (f32[24,128]{1,0:T(8,128)S(1)}, f32[24,128]{1,0:T(8,128)S(1)}, u32[]{:S(2)}, u32[]{:S(2)}) collective-permute-start(f32[24,128]{1,0:T(8,128)S(1)} %get-tuple-element.381), channel_id=1, source_target_pairs={{0,64},{64,0},{128,192},{192,128},{256,320},{320,256},{384,448},{4... | collective-permute-start | bytes 36872 | tf_op jit(solution)/shard_map/ppermute | solution.py:317
  8.7 38.2 %collective-permute-start.27 = (f32[8,8,8,128]{3,2,1,0:T(8,128)S(1)}, f32[8,8,8,128]{3,2,1,0:T(8,128)S(1)}, u32[]{:S(2)}, u32[]{:S(2)}) collective-permute-start(f32[8,8,8,128]{3,2,1,0:T(8,128)S(1)} %copy-done.6), channel_id=1, source_target_pairs={{0,16},{16,0},{32,48},{48,32},{1,17},{17,1},{33,49},{49,33},{2,18}... | collective-permute-start | bytes 786440 | tf_op jit(solution)/shard_map/ppermute | solution.py:317
  12.0 15.4 %collective-permute-start.25 = (f32[6,8,128]{2,1,0:T(8,128)S(1)}, f32[6,8,128]{2,1,0:T(8,128)S(1)}, u32[]{:S(2)}, u32[]{:S(2)}) collective-permute-start(f32[6,8,128]{2,1,0:T(8,128)S(1)} %pad_maximum_fusion.3), channel_id=1, source_target_pairs={{0,1},{1,0},{2,3},{3,2},{4,5},{5,4},{6,7},{7,6},{8,9},{9,8},{10,11... | collective-permute-start | bytes 73736 | tf_op jit(solution)/shard_map/ppermute | solution.py:317
  27.4 19.5 %collective-permute-start.26 = (f32[2,2,8,128]{3,2,0,1:T(8,128)S(1)}, f32[2,2,8,128]{3,2,0,1:T(8,128)S(1)}, u32[]{:S(2)}, u32[]{:S(2)}) collective-permute-start(f32[2,2,8,128]{3,2,0,1:T(8,128)S(1)} %maximum_select_fusion.6), channel_id=1, source_target_pairs={{0,975},{1,961},{2,962},{3,963},{4,964},{5,965},{6,966},{7,967},{8... | collective-permute-start | bytes 49160 | tf_op jit(solution)/shard_map/ppermute | solution.py:342
  41.2 39.1 %collective-permute-start.28 = (f32[8,6,8,128]{3,2,1,0:T(8,128)}, f32[8,6,8,128]{3,2,1,0:T(8,128)S(1)}, u32[]{:S(2)}, u32[]{:S(2)}) collective-permute-start(f32[8,6,8,128]{3,2,1,0:T(8,128)} %get-tuple-element.395), channel_id=1, source_target_pairs={{1,961},{2,962},{3,963},{4,964},{5,965},{6,966},{7,967},{8,968},{9... | collective-permute-start | bytes 589832 | tf_op jit(solution)/shard_map/ppermute | solution.py:353
  48.9 31.4 %collective-permute-start.7 = (f32[8,6,8,128]{3,2,1,0:T(8,128)S(1)}, f32[8,6,8,128]{3,2,1,0:T(8,128)}, u32[]{:S(2)}, u32[]{:S(2)}) collective-permute-start(f32[8,6,8,128]{3,2,1,0:T(8,128)S(1)} %get-tuple-element.219), channel_id=1, source_target_pairs={{0,64},{64,0},{128,192},{192,128},{256,320},{320,256},{384,448},{4... | collective-permute-start | bytes 589832 | tf_op jit(solution)/shard_map/cond/branch_1_fun/ppermute | solution.py:317
  53.4 27.0 %collective-permute-start.5 = (f32[8,8,8,128]{3,2,1,0:T(8,128)S(1)}, f32[8,8,8,128]{3,2,1,0:T(8,128)}, u32[]{:S(2)}, u32[]{:S(2)}) collective-permute-start(f32[8,8,8,128]{3,2,1,0:T(8,128)S(1)} %get-tuple-element.205), channel_id=1, source_target_pairs={{0,48},{16,32},{32,16},{48,0},{1,49},{17,33},{33,17},{49,1},{2,50}... | collective-permute-start | bytes 786440 | tf_op jit(solution)/shard_map/cond/branch_1_fun/cond/branch_1_fun/ppermute | solution.py:326
  58.0 9.1 %collective-permute-start.2 = (f32[8,8,128]{2,1,0:T(8,128)S(1)}, f32[8,8,128]{2,1,0:T(8,128)S(1)}, u32[]{:S(2)}, u32[]{:S(2)}) collective-permute-start(f32[8,8,128]{2,1,0:T(8,128)S(1)} %pad_maximum_fusion), channel_id=1, source_target_pairs={{0,15},{1,2},{2,1},{3,4},{4,3},{5,6},{6,5},{7,8},{8,7},{9,10},{10,... | collective-permute-start | bytes 98312 | tf_op jit(solution)/shard_map/cond/branch_1_fun/cond/branch_1_fun/cond/branch_1_fun/ppermute | solution.py:326
  59.9 20.4 %collective-permute-start.3 = (f32[8,6,8,128]{3,2,1,0:T(8,128)}, f32[8,6,8,128]{3,2,1,0:T(8,128)}, u32[]{:S(2)}, u32[]{:S(2)}) collective-permute-start(f32[8,6,8,128]{3,2,1,0:T(8,128)} %get-tuple-element.193), channel_id=1, source_target_pairs={{0,960},{15,975},{448,512},{463,527},{512,448},{527,463},{960,0},{... | collective-permute-start | bytes 589832 | tf_op jit(solution)/shard_map/cond/branch_1_fun/cond/branch_1_fun/cond/branch_1_fun/ppermute | solution.py:353
  72.0 7.2 %collective-permute-start.1 = (f32[3,8,128]{2,1,0:T(8,128)S(1)}, f32[3,8,128]{2,1,0:T(8,128)S(1)}, u32[]{:S(2)}, u32[]{:S(2)}) collective-permute-start(f32[3,8,128]{2,1,0:T(8,128)S(1)} %fusion), channel_id=1, source_target_pairs={{0,1},{1,0},{2,3},{3,2},{4,5},{5,4},{6,7},{7,6},{8,9},{9,8},{10,11... | collective-permute-start | bytes 36872 | tf_op jit(solution)/shard_map/cond/branch_1_fun/cond/branch_1_fun/cond/branch_1_fun/cond/branch_1_fun/ppermute | solution.py:317
  88.8 23.0 %collective-permute-start.32 = (f32[8,8,8,128]{3,2,1,0:T(8,128)S(1)}, f32[8,8,8,128]{3,2,1,0:T(8,128)S(1)}, u32[]{:S(2)}, u32[]{:S(2)}) collective-permute-start(f32[8,8,8,128]{3,2,1,0:T(8,128)S(1)} %get-tuple-element.409.refs_1_.refs_2_), channel_id=1, source_target_pairs={{0,16},{16,0},{32,48},{48,32},{1,17},{17,1},{33,49},{49,33},{2,18}... | collective-permute-start | bytes 786440 | tf_op jit(solution)/shard_map/ppermute | solution.py:317
  95.7 16.1 %collective-permute-start.31 = (f32[2,2,8,128]{3,2,0,1:T(8,128)S(1)}, f32[2,2,8,128]{3,2,0,1:T(8,128)S(1)}, u32[]{:S(2)}, u32[]{:S(2)}) collective-permute-start(f32[2,2,8,128]{3,2,0,1:T(8,128)S(1)} %maximum_select_fusion.7), channel_id=1, source_target_pairs={{0,975},{1,961},{2,962},{3,963},{4,964},{5,965},{6,966},{7,967},{8... | collective-permute-start | bytes 49160 | tf_op jit(solution)/shard_map/ppermute | solution.py:342
  100.9 40.6 %collective-permute-start.33 = (f32[8,6,8,128]{3,2,1,0:T(8,128)}, f32[8,6,8,128]{3,2,1,0:T(8,128)S(1)}, u32[]{:S(2)}, u32[]{:S(2)}) collective-permute-start(f32[8,6,8,128]{3,2,1,0:T(8,128)} %get-tuple-element.420), channel_id=1, source_target_pairs={{1,961},{2,962},{3,963},{4,964},{5,965},{6,966},{7,967},{8,968},{9... | collective-permute-start | bytes 589832 | tf_op jit(solution)/shard_map/ppermute | solution.py:353
  113.8 27.4 %collective-permute-start.15 = (f32[8,6,8,128]{3,2,1,0:T(8,128)S(1)}, f32[8,6,8,128]{3,2,1,0:T(8,128)}, u32[]{:S(2)}, u32[]{:S(2)}) collective-permute-start(f32[8,6,8,128]{3,2,1,0:T(8,128)S(1)} %get-tuple-element.260), channel_id=1, source_target_pairs={{0,64},{64,0},{128,192},{192,128},{256,320},{320,256},{384,448},{4... | collective-permute-start | bytes 589832 | tf_op jit(solution)/shard_map/cond/branch_1_fun/ppermute | solution.py:317
  120.2 21.0 %collective-permute-start.13 = (f32[8,8,8,128]{3,2,1,0:T(8,128)S(1)}, f32[8,8,8,128]{3,2,1,0:T(8,128)}, u32[]{:S(2)}, u32[]{:S(2)}) collective-permute-start(f32[8,8,8,128]{3,2,1,0:T(8,128)S(1)} %get-tuple-element.246), channel_id=1, source_target_pairs={{0,48},{16,32},{32,16},{48,0},{1,49},{17,33},{33,17},{49,1},{2,50}... | collective-permute-start | bytes 786440 | tf_op jit(solution)/shard_map/cond/branch_1_fun/cond/branch_1_fun/ppermute | solution.py:326
  126.2 15.0 %collective-permute-start.11 = (f32[8,6,8,128]{3,2,1,0:T(8,128)}, f32[8,6,8,128]{3,2,1,0:T(8,128)}, u32[]{:S(2)}, u32[]{:S(2)}) collective-permute-start(f32[8,6,8,128]{3,2,1,0:T(8,128)} %get-tuple-element.234), channel_id=1, source_target_pairs={{0,960},{15,975},{448,512},{463,527},{512,448},{527,463},{960,0},{... | collective-permute-start | bytes 589832 | tf_op jit(solution)/shard_map/cond/branch_1_fun/cond/branch_1_fun/cond/branch_1_fun/ppermute | solution.py:353
  133.3 6.7 %collective-permute-start.9 = (f32[3,8,128]{2,1,0:T(8,128)S(1)}, f32[3,8,128]{2,1,0:T(8,128)S(1)}, u32[]{:S(2)}, u32[]{:S(2)}) collective-permute-start(f32[3,8,128]{2,1,0:T(8,128)S(1)} %fusion.1), channel_id=1, source_target_pairs={{0,1},{1,0},{2,3},{3,2},{4,5},{5,4},{6,7},{7,6},{8,9},{9,8},{10,11... | collective-permute-start | bytes 36872 | tf_op jit(solution)/shard_map/cond/branch_1_fun/cond/branch_1_fun/cond/branch_1_fun/cond/branch_1_fun/ppermute | solution.py:317
  149.9 23.0 %collective-permute-start.37 = (f32[8,8,8,128]{3,2,1,0:T(8,128)S(1)}, f32[8,8,8,128]{3,2,1,0:T(8,128)S(1)}, u32[]{:S(2)}, u32[]{:S(2)}) collective-permute-start(f32[8,8,8,128]{3,2,1,0:T(8,128)S(1)} %get-tuple-element.433.refs_1_), channel_id=1, source_target_pairs={{0,16},{16,0},{32,48},{48,32},{1,17},{17,1},{33,49},{49,33},{2,18}... | collective-permute-start | bytes 786440 | tf_op jit(solution)/shard_map/ppermute | solution.py:317
  156.7 16.1 %collective-permute-start.36 = (f32[2,2,8,128]{3,2,0,1:T(8,128)S(1)}, f32[2,2,8,128]{3,2,0,1:T(8,128)S(1)}, u32[]{:S(2)}, u32[]{:S(2)}) collective-permute-start(f32[2,2,8,128]{3,2,0,1:T(8,128)S(1)} %maximum_select_fusion.8), channel_id=1, source_target_pairs={{0,975},{1,961},{2,962},{3,963},{4,964},{5,965},{6,966},{7,967},{8... | collective-permute-start | bytes 49160 | tf_op jit(solution)/shard_map/ppermute | solution.py:342
  165.1 37.9 %collective-permute-start.38 = (f32[8,6,8,128]{3,2,1,0:T(8,128)}, f32[8,6,8,128]{3,2,1,0:T(8,128)S(1)}, u32[]{:S(2)}, u32[]{:S(2)}) collective-permute-start(f32[8,6,8,128]{3,2,1,0:T(8,128)} %get-tuple-element.444), channel_id=1, source_target_pairs={{1,961},{2,962},{3,963},{4,964},{5,965},{6,966},{7,967},{8,968},{9... | collective-permute-start | bytes 589832 | tf_op jit(solution)/shard_map/ppermute | solution.py:353
  174.9 28.1 %collective-permute-start.23 = (f32[8,6,8,128]{3,2,1,0:T(8,128)S(1)}, f32[8,6,8,128]{3,2,1,0:T(8,128)}, u32[]{:S(2)}, u32[]{:S(2)}) collective-permute-start(f32[8,6,8,128]{3,2,1,0:T(8,128)S(1)} %get-tuple-element.301), channel_id=1, source_target_pairs={{0,64},{64,0},{128,192},{192,128},{256,320},{320,256},{384,448},{4... | collective-permute-start | bytes 589832 | tf_op jit(solution)/shard_map/cond/branch_1_fun/ppermute | solution.py:317
  181.2 21.8 %collective-permute-start.21 = (f32[8,8,8,128]{3,2,1,0:T(8,128)S(1)}, f32[8,8,8,128]{3,2,1,0:T(8,128)}, u32[]{:S(2)}, u32[]{:S(2)}) collective-permute-start(f32[8,8,8,128]{3,2,1,0:T(8,128)S(1)} %get-tuple-element.287), channel_id=1, source_target_pairs={{0,48},{16,32},{32,16},{48,0},{1,49},{17,33},{33,17},{49,1},{2,50}... | collective-permute-start | bytes 786440 | tf_op jit(solution)/shard_map/cond/branch_1_fun/cond/branch_1_fun/ppermute | solution.py:326
  184.1 7.4 %collective-permute-start.18 = (f32[8,8,128]{2,1,0:T(8,128)S(1)}, f32[8,8,128]{2,1,0:T(8,128)S(1)}, u32[]{:S(2)}, u32[]{:S(2)}) collective-permute-start(f32[8,8,128]{2,1,0:T(8,128)S(1)} %pad_maximum_fusion.2), channel_id=1, source_target_pairs={{0,15},{1,2},{2,1},{3,4},{4,3},{5,6},{6,5},{7,8},{8,7},{9,10},{10,... | collective-permute-start | bytes 98312 | tf_op jit(solution)/shard_map/cond/branch_1_fun/cond/branch_1_fun/cond/branch_1_fun/ppermute | solution.py:326
  188.2 14.8 %collective-permute-start.19 = (f32[8,6,8,128]{3,2,1,0:T(8,128)}, f32[8,6,8,128]{3,2,1,0:T(8,128)}, u32[]{:S(2)}, u32[]{:S(2)}) collective-permute-start(f32[8,6,8,128]{3,2,1,0:T(8,128)} %get-tuple-element.275), channel_id=1, source_target_pairs={{0,960},{15,975},{448,512},{463,527},{512,448},{527,463},{960,0},{... | collective-permute-start | bytes 589832 | tf_op jit(solution)/shard_map/cond/branch_1_fun/cond/branch_1_fun/cond/branch_1_fun/ppermute | solution.py:353
  (22 other events, 145.4 us)

commit v8 on v7

--- a/solution.py
+++ b/solution.py
@@ -15,7 +15,7 @@
 ROWS = NORB * SIDE * SIDE
 PLANES = 9
 SEGS = PLANES * 8
-CHUNK = 256
+CHUNK = 1024
 POS_Y = 4
 VMEM_LIMIT = 20 * 1024 * 1024
 
@@ -78,6 +78,7 @@
     upper, lower = split_two(wide.T)
     both = jnp.concatenate([upper, lower], axis=1)
     points = idx_ref.shape[1]
+    sums = []
     for first in range(0, points, CHUNK):
         span = slice(first, first + CHUNK)
         hot_seg = one_hot(idx_ref[2:3, span], 128, BF16)
@@ -86,23 +87,21 @@
         returned = weights[0:1] * spread[0:NORB]
         for k in range(1, POS_Y * NPROJ):
             returned = returned + weights[k : k + 1] * spread[k * NORB : (k + 1) * NORB]
-        upper_r = returned.astype(BF16).astype(F32)
-        lower_r = returned - upper_r
-        mask = iota((SIDE * SIDE, CHUNK), 0) == idx_ref[1:2, span]
-        tall = [
-            jnp.where(mask, value[o : o + 1], 0.0).astype(BF16)
-            for value in (upper_r, lower_r)
-            for o in range(NORB)
-        ]
+        upper_r, lower_r = split_two(returned)
+        hot_xy = one_hot(idx_ref[1:2, span], SIDE * SIDE, BF16)
+        tall = jnp.concatenate(
+            [
+                jnp.concatenate([hot_xy * value[o : o + 1] for o in range(NORB)], axis=0)
+                for value in (upper_r, lower_r)
+            ],
+            axis=1,
+        )
         hot_z = one_hot(idx_ref[0:1, span], DEPTH, BF16)
         placed = lax.dot_general(
-            jnp.concatenate(tall, axis=0), hot_z, LAST, preferred_element_type=F32
-        )
-        placed = placed[:ROWS] + placed[ROWS:]
-        if first == 0:
-            nonlocal_ref[...] = placed
-        else:
-            nonlocal_ref[...] += placed
+            tall, jnp.concatenate([hot_z, hot_z], axis=1), LAST, preferred_element_type=F32
+        )
+        sums.append(placed)
+    nonlocal_ref[...] = sum(sums[1:], sums[0])
 
 
 def write_parts(coord_ref, table, send_ref, keep_ref):
@@ -297,19 +296,20 @@
     )(*operands)
 
 
-def add_kernel(left_ref, right_ref, sum_ref):
-    sum_ref[...] = left_ref[...] + right_ref[...]
-
-
-def total(left, right):
+def add_kernel(*refs):
+    *parts, sum_ref = refs
+    sum_ref[...] = sum((part[...] for part in parts[1:]), parts[0][...])
+
+
+def total(*parts):
     return pl.pallas_call(
         add_kernel,
-        out_shape=jax.ShapeDtypeStruct(left.shape, F32),
-        in_specs=in_vmem(2),
+        out_shape=jax.ShapeDtypeStruct(parts[0].shape, F32),
+        in_specs=in_vmem(len(parts)),
         out_specs=in_vmem(1)[0],
         compiler_params=pltpu.CompilerParams(vmem_limit_bytes=VMEM_LIMIT),
         cost_estimate=pl.CostEstimate(flops=8000000000, bytes_accessed=80000000, transcendentals=0),
-    )(left, right)
+    )(*parts)
 
 
 def swap_inside(value, axis):
@@ -324,6 +324,11 @@
 def swap_across(value, axis):
     count = lax.axis_size(axis)
     return lax.ppermute(value, axis, [(i, across(i, count)) for i in range(count)])
+
+
+def swap_over(value, axis):
+    count = lax.axis_size(axis)
+    return lax.ppermute(value, axis, [(i, (i + 2) % count) for i in range(count)])
 
 
 def is_corner(x, z, count_x, count_z):
@@ -396,9 +401,6 @@
 
     def zeros_like_y(own):
         return (*zeros_like_z(own), jnp.zeros(cells_shape, F32))
-
-    def zeros_like_x(own):
-        return (*zeros_like_y(own), jnp.zeros(x_shape, F32))
 
     def energies():
         return call(
@@ -435,21 +437,15 @@
             )
             return (*rest, corner_in)
 
-        def along_y_across(own):
+        def along_y(own):
             rest, yb_in = staged(
-                lambda v: swap_across(v, "gy"), own, lambda v: swap_across(v, "gy"), cells,
-                lambda come: total(own, come), along_z_across, zeros_like_z,
+                lambda v: (swap_inside(v, "gy"), swap_across(v, "gy"), swap_over(v, "gy")), own,
+                lambda v: swap_across(v, "gy"), cells,
+                lambda come: total(own, *come), along_z_across, zeros_like_z,
             )
             return (*rest, yb_in)
 
-        def along_y_inside(own):
-            rest, xa_in = staged(
-                lambda v: swap_inside(v, "gy"), own, lambda v: swap_inside(v, "gx"), xa,
-                lambda come: total(own, come), along_y_across, zeros_like_y,
-            )
-            return (*rest, xa_in)
-
-        cells, give = lax.optimization_barrier((cells, give))
+        cells, xa, give = lax.optimization_barrier((cells, xa, give))
         come = swap_inside(give, "gx").reshape(1, 3, 8, 128)
         pair = total(
             keep.reshape(2, 3, 8, 128), jnp.where(place == 1 - places[0] % 2, come, 0.0)
@@ -464,11 +460,11 @@
             jnp.stack([middle, pair[:, 2]], axis=1),
             jnp.stack([pair[:, 0], middle], axis=1),
         )
-        ya_in = swap_inside(cells, "gy")
+        ya_in, xa_in = swap_inside(cells, "gy"), swap_inside(xa, "gx")
         rest, xb_in = staged(
             swap_corners, own, lambda v: swap_far_faces(v, False), xb,
-            lambda come: total(own, come), along_y_inside, zeros_like_x,
-            lambda: (ya_in, *(energies() if first else ())),
+            lambda come: total(own, come), along_y, zeros_like_y,
+            lambda: (xa_in, ya_in, *(energies() if first else ())),
         )
         table, zb_in, corner_in, yb_in, xa_in, ya_in, *made = rest
         energy = made[0] if first else energy

time: 209 us -> 218 us (1.043)
  starting transfers between devices: 151 us -> 166 us
  waiting for transfers between devices: 25.5 us -> 20.9 us
    ppermute x0 -> x3, starting transfers between devices: none -> 8.72 us  [swap_over(): lax.ppermute(value, axis, [(i, (i + 2) % count) for i in range(count)])]
    ppermute x21, starting transfers between devices: 70.6 us -> 75.6 us  [swap_inside(): return lax.ppermute(value, axis, [(i, i ^ 1) for i in range(count)])]
    ppermute x6, starting transfers between devices: 28.4 us -> 24.7 us  [swap_far_faces(): return lax.ppermute(value, ('gx', 'gz'), pairs)]
    ppermute x3, starting transfers between devices: 24 us -> 27.7 us  [swap_corners(): return lax.ppermute(value, ('gx', 'gz'), pairs)]
    ppermute x21, waiting for transfers between devices: 16.2 us -> 13.1 us  [swap_inside(): return lax.ppermute(value, axis, [(i, i ^ 1) for i in range(count)])]
  transfers between devices with their start and end apart: 39 -> 42, of which waited for: 17 -> 12; matrix products, arithmetic and copies ran while one was open for 0% -> 0% of each run, Pallas kernels for 3% -> 3%
where the time goes in v8:
time: 218 us; the launch traced here: 216 us
  starting transfers between devices  166 us (76%)
  Pallas kernels  26 us (12%)
  waiting for transfers between devices  20.9 us (10%)
    ppermute x21, starting transfers between devices, swap_inside(): return lax.ppermute(value, axis, [(i, i ^ 1) for i in range(count)])  75.6 us
    ppermute x9, starting transfers between devices, swap_across(): lax.ppermute(value, axis, [(i, across(i, count)) for i in range(count)])  29.6 us
    ppermute x3, starting transfers between devices, swap_corners(): return lax.ppermute(value, ('gx', 'gz'), pairs)  27.7 us
    pallas_call x8, Pallas kernels, call(): pl.pallas_call(kernel, out_shape=[jax.ShapeDtypeStruct(s, k) for s, k in...  25.9 us
    ppermute x6, starting transfers between devices, swap_far_faces(): return lax.ppermute(value, ('gx', 'gz'), pairs)  24.7 us
    ppermute x21, waiting for transfers between devices, swap_inside(): return lax.ppermute(value, axis, [(i, i ^ 1) for i in range(count)])  13.1 us
    ppermute x3, starting transfers between devices, swap_over(): lax.ppermute(value, axis, [(i, (i + 2) % count) for i in range(count)])  8.72 us
    ppermute x9, waiting for transfers between devices, swap_across(): lax.ppermute(value, axis, [(i, across(i, count)) for i in range(count)])  7.81 us
  transfers between devices with their start and end apart: 42, of which 12 were waited for; matrix products, arithmetic and copies ran while one was open for 0% of the time, Pallas kernels for 3%

profile of v8, /device:TPU:1, one launch (start us, length us, event | category | flops | bytes accessed | tf_op | source)
XLA Modules:
  0.0 216.2 jit_solution(11935068137320250526)
XLA Ops:
  13.9 14.7 %collective-permute-start.25 = (f32[6,8,128]{2,1,0:T(8,128)S(1)}, f32[6,8,128]{2,1,0:T(8,128)S(1)}, u32[]{:S(2)}, u32[]{:S(2)}) collective-permute-start(f32[6,8,128]{2,1,0:T(8,128)S(1)} %pad_maximum_fusion.3), channel_id=1, source_target_pairs={{0,1},{1,0},{2,3},{3,2},{4,5},{5,4},{6,7},{7,6},{8,9},{9,8},{10,11... | collective-permute-start | bytes 73736 | tf_op jit(solution)/shard_map/ppermute | solution.py:317
  29.5 10.8 %collective-permute-start.26 = (f32[2,2,8,128]{3,2,0,1:T(8,128)S(1)}, f32[2,2,8,128]{3,2,0,1:T(8,128)S(1)}, u32[]{:S(2)}, u32[]{:S(2)}) collective-permute-start(f32[2,2,8,128]{3,2,0,1:T(8,128)S(1)} %maximum_select_fusion.6), channel_id=1, source_target_pairs={{0,975},{1,961},{2,962},{3,963},{4,964},{5,965},{6,966},{7,967},{8... | collective-permute-start | bytes 49160 | tf_op jit(solution)/shard_map/ppermute | solution.py:347
  43.7 5.3 %collective-permute-start.29 = (f32[8,6,8,128]{3,2,1,0:T(8,128)}, f32[8,6,8,128]{3,2,1,0:T(8,128)S(1)}, u32[]{:S(2)}, u32[]{:S(2)}) collective-permute-start(f32[8,6,8,128]{3,2,1,0:T(8,128)} %get-tuple-element.312), channel_id=1, source_target_pairs={{1,961},{2,962},{3,963},{4,964},{5,965},{6,966},{7,967},{8,968},{9... | collective-permute-start | bytes 589832 | tf_op jit(solution)/shard_map/ppermute | solution.py:358
  49.1 31.3 %conditional.9 = (f32[72,128]{1,0:T(8,128)}, f32[4,8,128]{2,1,0:T(8,128)}, f32[8,6,8,128]{3,2,1,0:T(8,128)}, f32[8,8,8,128]{3,2,1,0:T(8,128)}) conditional(s32[]{:T(128)} %convert_element_type.23, () %tuple.95, (pred[]{:T(512)}, f32[2,2,8,128]{3,2,1,0:T(8,128)S(1)}, f32[4,8,128]{2,1,0:T(8,128)S(1)}, pred[]{:T(512)}, pred[]{:T(512)}, ...), branch_computations={%region_0.1_spmd, %region_1.6_spmd} | conditional | flops 16000143360 | bytes 162753984 | solution.py:393
  61.2 19.2 %conditional.1 = (f32[72,128]{1,0:T(8,128)}, f32[4,8,128]{2,1,0:T(8,128)}, f32[8,6,8,128]{3,2,1,0:T(8,128)}) conditional(s32[]{:T(128)} %convert_element_type.10, () %tuple.48, (pred[]{:T(512)}, f32[2,2,8,128]{3,2,1,0:T(8,128)S(1)}, f32[4,8,128]{2,1,0:T(8,128)S(1)}, pred[]{:T(512)}, pred[]{:T(512)}, /*index=5*/s32[8]{0:T(128)S(1)}, ...), branch_computations={%region_2.2_spmd, %region_3.5_spmd} | conditional | flops 8000143872 | bytes 81508560 | solution.py:393
  65.0 4.4 %collective-permute-done.2 = f32[8,8,128]{2,1,0:T(8,128)S(1)} collective-permute-done((f32[8,8,128]{2,1,0:T(8,128)S(1)}, f32[8,8,128]{2,1,0:T(8,128)S(1)}, u32[]{:S(2)}, u32[]{:S(2)}) %collective-permute-start.2) | collective-permute-done | bytes 32800 | tf_op jit(solution)/shard_map/cond/branch_1_fun/cond/branch_1_fun/ppermute | solution.py:326
  69.4 11.0 %conditional = ((f32[72,128]{1,0:T(8,128)}, f32[4,8,128]{2,1,0:T(8,128)})) conditional(s32[]{:T(128)} %convert_element_type.6, () %tuple.44, (pred[]{:T(512)}, f32[2,2,8,128]{3,2,1,0:T(8,128)S(1)}, pred[]{:T(512)}, s32[8]{0:T(128)S(1)}, f32[8,8,128]{2,1,0:T(8,128)S(1)}) %tuple.45), branch_computations={%region_4.3_spmd, %region_5.4_spmd} | conditional | flops 135840 | bytes 492603 | solution.py:393
  74.2 4.2 %collective-permute-start.1 = (f32[3,8,128]{2,1,0:T(8,128)S(1)}, f32[3,8,128]{2,1,0:T(8,128)S(1)}, u32[]{:S(2)}, u32[]{:S(2)}) collective-permute-start(f32[3,8,128]{2,1,0:T(8,128)S(1)} %fusion), channel_id=1, source_target_pairs={{0,1},{1,0},{2,3},{3,2},{4,5},{5,4},{6,7},{7,6},{8,9},{9,8},{10,11... | collective-permute-start | bytes 36872 | tf_op jit(solution)/shard_map/cond/branch_1_fun/cond/branch_1_fun/cond/branch_1_fun/ppermute | solution.py:317
  80.4 5.8 %shard_map.86 = (f32[8,8,8,128]{3,2,1,0:T(8,128)S(1)}, f32[24,128]{1,0:T(8,128)S(1)}, f32[48,128]{1,0:T(8,128)S(1)}, f32[8,6,8,128]{3,2,1,0:T(8,128)S(1)}, f32[8...) custom-call(s32[8]{0:T(128)S(1)} %stack.93.refs_0_, f32[8,8,8,128]{3,2,1,0:T(8,128)S(1)} %copy-done.6, ...), custom_call_target="tpu_custom_call" | custom-call | flops 1500000000 | bytes 4000000 | tf_op jit(solution)/shard_map/pallas_call | solution.py:288
  97.8 8.5 %collective-permute-start.32 = (f32[2,2,8,128]{3,2,0,1:T(8,128)S(1)}, f32[2,2,8,128]{3,2,0,1:T(8,128)S(1)}, u32[]{:S(2)}, u32[]{:S(2)}) collective-permute-start(f32[2,2,8,128]{3,2,0,1:T(8,128)S(1)} %maximum_select_fusion.7), channel_id=1, source_target_pairs={{0,975},{1,961},{2,962},{3,963},{4,964},{5,965},{6,966},{7,967},{8... | collective-permute-start | bytes 49160 | tf_op jit(solution)/shard_map/ppermute | solution.py:347
  106.3 7.6 %collective-permute-start.35 = (f32[8,6,8,128]{3,2,1,0:T(8,128)}, f32[8,6,8,128]{3,2,1,0:T(8,128)S(1)}, u32[]{:S(2)}, u32[]{:S(2)}) collective-permute-start(f32[8,6,8,128]{3,2,1,0:T(8,128)} %get-tuple-element.338), channel_id=1, source_target_pairs={{1,961},{2,962},{3,963},{4,964},{5,965},{6,966},{7,967},{8,968},{9... | collective-permute-start | bytes 589832 | tf_op jit(solution)/shard_map/ppermute | solution.py:358
  113.9 33.7 %conditional.10 = (f32[72,128]{1,0:T(8,128)}, f32[4,8,128]{2,1,0:T(8,128)}, f32[8,6,8,128]{3,2,1,0:T(8,128)}, f32[8,8,8,128]{3,2,1,0:T(8,128)}) conditional(s32[]{:T(128)} %convert_element_type.23, () %tuple.101, (pred[]{:T(512)}, f32[2,2,8,128]{3,2,1,0:T(8,128)S(1)}, f32[4,8,128]{2,1,0:T(8,128)S(1)}, pred[]{:T(512)}, pred[]{:T(512)}, ...), branch_computations={%region_6.7_spmd, %region_7.12_spmd} | conditional | flops 16000143360 | bytes 162753984 | solution.py:393
  126.7 20.8 %conditional.3 = (f32[72,128]{1,0:T(8,128)}, f32[4,8,128]{2,1,0:T(8,128)}, f32[8,6,8,128]{3,2,1,0:T(8,128)}) conditional(s32[]{:T(128)} %convert_element_type.19, () %tuple.60, (pred[]{:T(512)}, f32[2,2,8,128]{3,2,1,0:T(8,128)S(1)}, f32[4,8,128]{2,1,0:T(8,128)S(1)}, pred[]{:T(512)}, pred[]{:T(512)}, /*index=5*/s32[8]{0:T(128)S(1)}, ...), branch_computations={%region_8.8_spmd, %region_9.11_spmd} | conditional | flops 8000143872 | bytes 81508560 | solution.py:393
  126.8 5.9 %collective-permute-start.10 = (f32[8,8,128]{2,1,0:T(8,128)S(1)}, f32[8,8,128]{2,1,0:T(8,128)S(1)}, u32[]{:S(2)}, u32[]{:S(2)}) collective-permute-start(f32[8,8,128]{2,1,0:T(8,128)S(1)} %pad_maximum_fusion.1), channel_id=1, source_target_pairs={{0,15},{1,2},{2,1},{3,4},{4,3},{5,6},{6,5},{7,8},{8,7},{9,10},{10,... | collective-permute-start | bytes 98312 | tf_op jit(solution)/shard_map/cond/branch_1_fun/cond/branch_1_fun/ppermute | solution.py:326
  134.6 12.9 %conditional.2 = ((f32[72,128]{1,0:T(8,128)}, f32[4,8,128]{2,1,0:T(8,128)})) conditional(s32[]{:T(128)} %convert_element_type.18, () %tuple.56, (pred[]{:T(512)}, f32[2,2,8,128]{3,2,1,0:T(8,128)S(1)}, pred[]{:T(512)}, s32[8]{0:T(128)S(1)}, f32[8,8,128]{2,1,0:T(8,128)S(1)}) %tuple.57), branch_computations={%region_10.9_spmd, %region_11.10_spmd} | conditional | flops 135840 | bytes 492603 | solution.py:393
  139.0 6.5 %collective-permute-start.9 = (f32[3,8,128]{2,1,0:T(8,128)S(1)}, f32[3,8,128]{2,1,0:T(8,128)S(1)}, u32[]{:S(2)}, u32[]{:S(2)}) collective-permute-start(f32[3,8,128]{2,1,0:T(8,128)S(1)} %fusion.1), channel_id=1, source_target_pairs={{0,1},{1,0},{2,3},{3,2},{4,5},{5,4},{6,7},{7,6},{8,9},{9,8},{10,11... | collective-permute-start | bytes 36872 | tf_op jit(solution)/shard_map/cond/branch_1_fun/cond/branch_1_fun/cond/branch_1_fun/ppermute | solution.py:317
  147.7 5.8 %shard_map.89 = (f32[8,8,8,128]{3,2,1,0:T(8,128)S(1)}, f32[24,128]{1,0:T(8,128)S(1)}, f32[48,128]{1,0:T(8,128)S(1)}, f32[8,6,8,128]{3,2,1,0:T(8,128)S(1)}, f32[8...) custom-call(s32[8]{0:T(128)S(1)} %stack.93.refs_0_, ...), custom_call_target="tpu_custom_call" | custom-call | flops 1500000000 | bytes 4000000 | tf_op jit(solution)/shard_map/pallas_call | solution.py:288
  165.4 8.3 %collective-permute-start.38 = (f32[2,2,8,128]{3,2,0,1:T(8,128)S(1)}, f32[2,2,8,128]{3,2,0,1:T(8,128)S(1)}, u32[]{:S(2)}, u32[]{:S(2)}) collective-permute-start(f32[2,2,8,128]{3,2,0,1:T(8,128)S(1)} %maximum_select_fusion.8), channel_id=1, source_target_pairs={{0,975},{1,961},{2,962},{3,963},{4,964},{5,965},{6,966},{7,967},{8... | collective-permute-start | bytes 49160 | tf_op jit(solution)/shard_map/ppermute | solution.py:347
  173.7 7.7 %collective-permute-start.41 = (f32[8,6,8,128]{3,2,1,0:T(8,128)}, f32[8,6,8,128]{3,2,1,0:T(8,128)S(1)}, u32[]{:S(2)}, u32[]{:S(2)}) collective-permute-start(f32[8,6,8,128]{3,2,1,0:T(8,128)} %get-tuple-element.363), channel_id=1, source_target_pairs={{1,961},{2,962},{3,963},{4,964},{5,965},{6,966},{7,967},{8,968},{9... | collective-permute-start | bytes 589832 | tf_op jit(solution)/shard_map/ppermute | solution.py:358
  181.6 30.2 %conditional.11 = (f32[72,128]{1,0:T(8,128)}, f32[4,8,128]{2,1,0:T(8,128)}, f32[8,6,8,128]{3,2,1,0:T(8,128)}, f32[8,8,8,128]{3,2,1,0:T(8,128)}) conditional(s32[]{:T(128)} %convert_element_type.23, () %tuple.107, (pred[]{:T(512)}, f32[2,2,8,128]{3,2,1,0:T(8,128)S(1)}, f32[4,8,128]{2,1,0:T(8,128)S(1)}, pred[]{:T(512)}, pred[]{:T(512)}, ...), branch_computations={%region_12.13_spmd, %region_13.18_spmd} | conditional | flops 16000143360 | bytes 162753984 | solution.py:393
  194.6 17.1 %conditional.5 = (f32[72,128]{1,0:T(8,128)}, f32[4,8,128]{2,1,0:T(8,128)}, f32[8,6,8,128]{3,2,1,0:T(8,128)}) conditional(s32[]{:T(128)} %convert_element_type.21, () %tuple.72, (pred[]{:T(512)}, f32[2,2,8,128]{3,2,1,0:T(8,128)S(1)}, f32[4,8,128]{2,1,0:T(8,128)S(1)}, pred[]{:T(512)}, pred[]{:T(512)}, /*index=5*/s32[8]{0:T(128)S(1)}, ...), branch_computations={%region_14.14_spmd, %region_15.17_spmd} | conditional | flops 8000143872 | bytes 81508560 | solution.py:393
  200.8 11.0 %conditional.4 = ((f32[72,128]{1,0:T(8,128)}, f32[4,8,128]{2,1,0:T(8,128)})) conditional(s32[]{:T(128)} %convert_element_type.20, () %tuple.68, (pred[]{:T(512)}, f32[2,2,8,128]{3,2,1,0:T(8,128)S(1)}, pred[]{:T(512)}, s32[8]{0:T(128)S(1)}, f32[8,8,128]{2,1,0:T(8,128)S(1)}) %tuple.69), branch_computations={%region_16.15_spmd, %region_17.16_spmd} | conditional | flops 135840 | bytes 492603 | solution.py:393
  205.6 4.2 %collective-permute-start.17 = (f32[3,8,128]{2,1,0:T(8,128)S(1)}, f32[3,8,128]{2,1,0:T(8,128)S(1)}, u32[]{:S(2)}, u32[]{:S(2)}) collective-permute-start(f32[3,8,128]{2,1,0:T(8,128)S(1)} %fusion.2), channel_id=1, source_target_pairs={{0,1},{1,0},{2,3},{3,2},{4,5},{5,4},{6,7},{7,6},{8,9},{9,8},{10,11... | collective-permute-start | bytes 36872 | tf_op jit(solution)/shard_map/cond/branch_1_fun/cond/branch_1_fun/cond/branch_1_fun/ppermute | solution.py:317
  211.8 4.4 %shard_map.92 = f32[8,8,8,128]{3,2,1,0:T(8,128)} custom-call(s32[8]{0:T(128)S(1)} %stack.93.refs_0_, f32[8,8,8,128]{3,2,1,0:T(8,128)S(1)} %get-tuple-element.353.refs_1_, f32[8,8,8,128]{3,2,1,0:T(8,128)S(1)} %get-tuple-element.328.refs_1_.refs_2_, f32[8,8,128]{2,1,0:T(8,128)S(1)} %copy-done.2, s32[8,2048]{1,0:T(8,128)S(1)} %get-tuple-element.293.refs_3_.refs_4_, ...), custom_call_target="tpu_custom_call" | custom-call | flops 1500000000 | bytes 4000000 | tf_op jit(solution)/shard_map/pallas_call | solution.py:288
  (150 shorter events, 110.1 us)
Async XLA Ops:
  8.6 40.4 %collective-permute-start.27 = (f32[8,6,8,128]{3,2,1,0:T(8,128)S(1)}, f32[8,6,8,128]{3,2,1,0:T(8,128)S(1)}, u32[]{:S(2)}, u32[]{:S(2)}) collective-permute-start(f32[8,6,8,128]{3,2,1,0:T(8,128)S(1)} %get-tuple-element.300), channel_id=1, source_target_pairs={{0,64},{64,0},{128,192},{192,128},{256,320},{320,256},{384,448},{4... | collective-permute-start | bytes 589832 | tf_op jit(solution)/shard_map/ppermute | solution.py:317
  10.5 38.5 %collective-permute-start.28 = (f32[8,8,8,128]{3,2,1,0:T(8,128)S(1)}, f32[8,8,8,128]{3,2,1,0:T(8,128)S(1)}, u32[]{:S(2)}, u32[]{:S(2)}) collective-permute-start(f32[8,8,8,128]{3,2,1,0:T(8,128)S(1)} %copy-done.6), channel_id=1, source_target_pairs={{0,16},{16,0},{32,48},{48,32},{1,17},{17,1},{33,49},{49,33},{2,18}... | collective-permute-start | bytes 786440 | tf_op jit(solution)/shard_map/ppermute | solution.py:317
  13.9 15.6 %collective-permute-start.25 = (f32[6,8,128]{2,1,0:T(8,128)S(1)}, f32[6,8,128]{2,1,0:T(8,128)S(1)}, u32[]{:S(2)}, u32[]{:S(2)}) collective-permute-start(f32[6,8,128]{2,1,0:T(8,128)S(1)} %pad_maximum_fusion.3), channel_id=1, source_target_pairs={{0,1},{1,0},{2,3},{3,2},{4,5},{5,4},{6,7},{7,6},{8,9},{9,8},{10,11... | collective-permute-start | bytes 73736 | tf_op jit(solution)/shard_map/ppermute | solution.py:317
  29.5 19.5 %collective-permute-start.26 = (f32[2,2,8,128]{3,2,0,1:T(8,128)S(1)}, f32[2,2,8,128]{3,2,0,1:T(8,128)S(1)}, u32[]{:S(2)}, u32[]{:S(2)}) collective-permute-start(f32[2,2,8,128]{3,2,0,1:T(8,128)S(1)} %maximum_select_fusion.6), channel_id=1, source_target_pairs={{0,975},{1,961},{2,962},{3,963},{4,964},{5,965},{6,966},{7,967},{8... | collective-permute-start | bytes 49160 | tf_op jit(solution)/shard_map/ppermute | solution.py:347
  43.7 36.7 %collective-permute-start.29 = (f32[8,6,8,128]{3,2,1,0:T(8,128)}, f32[8,6,8,128]{3,2,1,0:T(8,128)S(1)}, u32[]{:S(2)}, u32[]{:S(2)}) collective-permute-start(f32[8,6,8,128]{3,2,1,0:T(8,128)} %get-tuple-element.312), channel_id=1, source_target_pairs={{1,961},{2,962},{3,963},{4,964},{5,965},{6,966},{7,967},{8,968},{9... | collective-permute-start | bytes 589832 | tf_op jit(solution)/shard_map/ppermute | solution.py:358
  49.1 12.1 %collective-permute-start.4 = (f32[2,2,8,128]{3,2,1,0:T(8,128)S(1)}, f32[2,2,8,128]{3,2,1,0:T(8,128)S(1)}, u32[]{:S(2)}, u32[]{:S(2)}) collective-permute-start(f32[2,2,8,128]{3,2,1,0:T(8,128)S(1)} %get-tuple-element.141.refs_0_), channel_id=1, source_target_pairs={{0,16},{16,0},{32,48},{48,32},{1,17},{17,1},{33,49},{49,33},{2,18}... | collective-permute-start | bytes 49160 | tf_op jit(solution)/shard_map/cond/branch_1_fun/ppermute | solution.py:317
  58.4 22.0 %collective-permute-start.7 = (f32[8,8,8,128]{3,2,1,0:T(8,128)S(1)}, f32[8,8,8,128]{3,2,1,0:T(8,128)}, u32[]{:S(2)}, u32[]{:S(2)}) collective-permute-start(f32[8,8,8,128]{3,2,1,0:T(8,128)S(1)} %get-tuple-element.154), channel_id=1, source_target_pairs={{0,48},{16,32},{32,16},{48,0},{1,49},{17,33},{33,17},{49,1},{2,50}... | collective-permute-start | bytes 786440 | tf_op jit(solution)/shard_map/cond/branch_1_fun/ppermute | solution.py:326
  63.6 16.8 %collective-permute-start.3 = (f32[8,6,8,128]{3,2,1,0:T(8,128)}, f32[8,6,8,128]{3,2,1,0:T(8,128)}, u32[]{:S(2)}, u32[]{:S(2)}) collective-permute-start(f32[8,6,8,128]{3,2,1,0:T(8,128)} %get-tuple-element.139), channel_id=1, source_target_pairs={{0,960},{15,975},{448,512},{463,527},{512,448},{527,463},{960,0},{... | collective-permute-start | bytes 589832 | tf_op jit(solution)/shard_map/cond/branch_1_fun/cond/branch_1_fun/ppermute | solution.py:358
  88.1 25.8 %collective-permute-start.33 = (f32[8,6,8,128]{3,2,1,0:T(8,128)S(1)}, f32[8,6,8,128]{3,2,1,0:T(8,128)S(1)}, u32[]{:S(2)}, u32[]{:S(2)}) collective-permute-start(f32[8,6,8,128]{3,2,1,0:T(8,128)S(1)} %get-tuple-element.327), channel_id=1, source_target_pairs={{0,64},{64,0},{128,192},{192,128},{256,320},{320,256},{384,448},{4... | collective-permute-start | bytes 589832 | tf_op jit(solution)/shard_map/ppermute | solution.py:317
  91.5 22.4 %collective-permute-start.34 = (f32[8,8,8,128]{3,2,1,0:T(8,128)S(1)}, f32[8,8,8,128]{3,2,1,0:T(8,128)S(1)}, u32[]{:S(2)}, u32[]{:S(2)}) collective-permute-start(f32[8,8,8,128]{3,2,1,0:T(8,128)S(1)} %get-tuple-element.328.refs_1_.refs_2_), channel_id=1, source_target_pairs={{0,16},{16,0},{32,48},{48,32},{1,17},{17,1},{33,49},{49,33},{2,18}... | collective-permute-start | bytes 786440 | tf_op jit(solution)/shard_map/ppermute | solution.py:317
  97.8 16.1 %collective-permute-start.32 = (f32[2,2,8,128]{3,2,0,1:T(8,128)S(1)}, f32[2,2,8,128]{3,2,0,1:T(8,128)S(1)}, u32[]{:S(2)}, u32[]{:S(2)}) collective-permute-start(f32[2,2,8,128]{3,2,0,1:T(8,128)S(1)} %maximum_select_fusion.7), channel_id=1, source_target_pairs={{0,975},{1,961},{2,962},{3,963},{4,964},{5,965},{6,966},{7,967},{8... | collective-permute-start | bytes 49160 | tf_op jit(solution)/shard_map/ppermute | solution.py:347
  106.3 41.4 %collective-permute-start.35 = (f32[8,6,8,128]{3,2,1,0:T(8,128)}, f32[8,6,8,128]{3,2,1,0:T(8,128)S(1)}, u32[]{:S(2)}, u32[]{:S(2)}) collective-permute-start(f32[8,6,8,128]{3,2,1,0:T(8,128)} %get-tuple-element.338), channel_id=1, source_target_pairs={{1,961},{2,962},{3,963},{4,964},{5,965},{6,966},{7,967},{8,968},{9... | collective-permute-start | bytes 589832 | tf_op jit(solution)/shard_map/ppermute | solution.py:358
  114.0 12.7 %collective-permute-start.12 = (f32[2,2,8,128]{3,2,1,0:T(8,128)S(1)}, f32[2,2,8,128]{3,2,1,0:T(8,128)S(1)}, u32[]{:S(2)}, u32[]{:S(2)}) collective-permute-start(f32[2,2,8,128]{3,2,1,0:T(8,128)S(1)} %get-tuple-element.171.refs_0_), channel_id=1, source_target_pairs={{0,16},{16,0},{32,48},{48,32},{1,17},{17,1},{33,49},{49,33},{2,18}... | collective-permute-start | bytes 49160 | tf_op jit(solution)/shard_map/cond/branch_1_fun/ppermute | solution.py:317
  117.1 9.6 %collective-permute-start.13 = (f32[2,2,8,128]{3,2,1,0:T(8,128)S(1)}, f32[2,2,8,128]{3,2,1,0:T(8,128)S(1)}, u32[]{:S(2)}, u32[]{:S(2)}) collective-permute-start(f32[2,2,8,128]{3,2,1,0:T(8,128)S(1)} %get-tuple-element.171.refs_0_), channel_id=1, source_target_pairs={{0,48},{16,32},{32,16},{48,0},{1,49},{17,33},{33,17},{49,1},{2,50}... | collective-permute-start | bytes 49160 | tf_op jit(solution)/shard_map/cond/branch_1_fun/ppermute | solution.py:326
  123.0 24.5 %collective-permute-start.15 = (f32[8,8,8,128]{3,2,1,0:T(8,128)S(1)}, f32[8,8,8,128]{3,2,1,0:T(8,128)}, u32[]{:S(2)}, u32[]{:S(2)}) collective-permute-start(f32[8,8,8,128]{3,2,1,0:T(8,128)S(1)} %get-tuple-element.184), channel_id=1, source_target_pairs={{0,48},{16,32},{32,16},{48,0},{1,49},{17,33},{33,17},{49,1},{2,50}... | collective-permute-start | bytes 786440 | tf_op jit(solution)/shard_map/cond/branch_1_fun/ppermute | solution.py:326
  132.7 14.8 %collective-permute-start.11 = (f32[8,6,8,128]{3,2,1,0:T(8,128)}, f32[8,6,8,128]{3,2,1,0:T(8,128)}, u32[]{:S(2)}, u32[]{:S(2)}) collective-permute-start(f32[8,6,8,128]{3,2,1,0:T(8,128)} %get-tuple-element.169), channel_id=1, source_target_pairs={{0,960},{15,975},{448,512},{463,527},{512,448},{527,463},{960,0},{... | collective-permute-start | bytes 589832 | tf_op jit(solution)/shard_map/cond/branch_1_fun/cond/branch_1_fun/ppermute | solution.py:358
  155.4 26.1 %collective-permute-start.39 = (f32[8,6,8,128]{3,2,1,0:T(8,128)S(1)}, f32[8,6,8,128]{3,2,1,0:T(8,128)S(1)}, u32[]{:S(2)}, u32[]{:S(2)}) collective-permute-start(f32[8,6,8,128]{3,2,1,0:T(8,128)S(1)} %get-tuple-element.352), channel_id=1, source_target_pairs={{0,64},{64,0},{128,192},{192,128},{256,320},{320,256},{384,448},{4... | collective-permute-start | bytes 589832 | tf_op jit(solution)/shard_map/ppermute | solution.py:317
  158.8 22.7 %collective-permute-start.40 = (f32[8,8,8,128]{3,2,1,0:T(8,128)S(1)}, f32[8,8,8,128]{3,2,1,0:T(8,128)S(1)}, u32[]{:S(2)}, u32[]{:S(2)}) collective-permute-start(f32[8,8,8,128]{3,2,1,0:T(8,128)S(1)} %get-tuple-element.353.refs_1_), channel_id=1, source_target_pairs={{0,16},{16,0},{32,48},{48,32},{1,17},{17,1},{33,49},{49,33},{2,18}... | collective-permute-start | bytes 786440 | tf_op jit(solution)/shard_map/ppermute | solution.py:317
  165.4 16.1 %collective-permute-start.38 = (f32[2,2,8,128]{3,2,0,1:T(8,128)S(1)}, f32[2,2,8,128]{3,2,0,1:T(8,128)S(1)}, u32[]{:S(2)}, u32[]{:S(2)}) collective-permute-start(f32[2,2,8,128]{3,2,0,1:T(8,128)S(1)} %maximum_select_fusion.8), channel_id=1, source_target_pairs={{0,975},{1,961},{2,962},{3,963},{4,964},{5,965},{6,966},{7,967},{8... | collective-permute-start | bytes 49160 | tf_op jit(solution)/shard_map/ppermute | solution.py:347
  173.7 38.0 %collective-permute-start.41 = (f32[8,6,8,128]{3,2,1,0:T(8,128)}, f32[8,6,8,128]{3,2,1,0:T(8,128)S(1)}, u32[]{:S(2)}, u32[]{:S(2)}) collective-permute-start(f32[8,6,8,128]{3,2,1,0:T(8,128)} %get-tuple-element.363), channel_id=1, source_target_pairs={{1,961},{2,962},{3,963},{4,964},{5,965},{6,966},{7,967},{8,968},{9... | collective-permute-start | bytes 589832 | tf_op jit(solution)/shard_map/ppermute | solution.py:358
  181.6 13.0 %collective-permute-start.20 = (f32[2,2,8,128]{3,2,1,0:T(8,128)S(1)}, f32[2,2,8,128]{3,2,1,0:T(8,128)S(1)}, u32[]{:S(2)}, u32[]{:S(2)}) collective-permute-start(f32[2,2,8,128]{3,2,1,0:T(8,128)S(1)} %get-tuple-element.201.refs_0_), channel_id=1, source_target_pairs={{0,16},{16,0},{32,48},{48,32},{1,17},{17,1},{33,49},{49,33},{2,18}... | collective-permute-start | bytes 49160 | tf_op jit(solution)/shard_map/cond/branch_1_fun/ppermute | solution.py:317
  184.4 10.2 %collective-permute-start.21 = (f32[2,2,8,128]{3,2,1,0:T(8,128)S(1)}, f32[2,2,8,128]{3,2,1,0:T(8,128)S(1)}, u32[]{:S(2)}, u32[]{:S(2)}) collective-permute-start(f32[2,2,8,128]{3,2,1,0:T(8,128)S(1)} %get-tuple-element.201.refs_0_), channel_id=1, source_target_pairs={{0,48},{16,32},{32,16},{48,0},{1,49},{17,33},{33,17},{49,1},{2,50}... | collective-permute-start | bytes 49160 | tf_op jit(solution)/shard_map/cond/branch_1_fun/ppermute | solution.py:326
  190.6 21.2 %collective-permute-start.23 = (f32[8,8,8,128]{3,2,1,0:T(8,128)S(1)}, f32[8,8,8,128]{3,2,1,0:T(8,128)}, u32[]{:S(2)}, u32[]{:S(2)}) collective-permute-start(f32[8,8,8,128]{3,2,1,0:T(8,128)S(1)} %get-tuple-element.214), channel_id=1, source_target_pairs={{0,48},{16,32},{32,16},{48,0},{1,49},{17,33},{33,17},{49,1},{2,50}... | collective-permute-start | bytes 786440 | tf_op jit(solution)/shard_map/cond/branch_1_fun/ppermute | solution.py:326
  196.6 15.2 %collective-permute-start.19 = (f32[8,6,8,128]{3,2,1,0:T(8,128)}, f32[8,6,8,128]{3,2,1,0:T(8,128)}, u32[]{:S(2)}, u32[]{:S(2)}) collective-permute-start(f32[8,6,8,128]{3,2,1,0:T(8,128)} %get-tuple-element.199), channel_id=1, source_target_pairs={{0,960},{15,975},{448,512},{463,527},{512,448},{527,463},{960,0},{... | collective-permute-start | bytes 589832 | tf_op jit(solution)/shard_map/cond/branch_1_fun/cond/branch_1_fun/ppermute | solution.py:358
  (25 other events, 183.3 us)

commit v9 on v7

--- a/solution.py
+++ b/solution.py
@@ -15,7 +15,7 @@
 ROWS = NORB * SIDE * SIDE
 PLANES = 9
 SEGS = PLANES * 8
-CHUNK = 256
+CHUNK = 1024
 POS_Y = 4
 VMEM_LIMIT = 20 * 1024 * 1024
 
@@ -78,6 +78,7 @@
     upper, lower = split_two(wide.T)
     both = jnp.concatenate([upper, lower], axis=1)
     points = idx_ref.shape[1]
+    sums = []
     for first in range(0, points, CHUNK):
         span = slice(first, first + CHUNK)
         hot_seg = one_hot(idx_ref[2:3, span], 128, BF16)
@@ -86,23 +87,21 @@
         returned = weights[0:1] * spread[0:NORB]
         for k in range(1, POS_Y * NPROJ):
             returned = returned + weights[k : k + 1] * spread[k * NORB : (k + 1) * NORB]
-        upper_r = returned.astype(BF16).astype(F32)
-        lower_r = returned - upper_r
-        mask = iota((SIDE * SIDE, CHUNK), 0) == idx_ref[1:2, span]
-        tall = [
-            jnp.where(mask, value[o : o + 1], 0.0).astype(BF16)
-            for value in (upper_r, lower_r)
-            for o in range(NORB)
-        ]
+        upper_r, lower_r = split_two(returned)
+        hot_xy = one_hot(idx_ref[1:2, span], SIDE * SIDE, BF16)
+        tall = jnp.concatenate(
+            [
+                jnp.concatenate([hot_xy * value[o : o + 1] for o in range(NORB)], axis=0)
+                for value in (upper_r, lower_r)
+            ],
+            axis=1,
+        )
         hot_z = one_hot(idx_ref[0:1, span], DEPTH, BF16)
         placed = lax.dot_general(
-            jnp.concatenate(tall, axis=0), hot_z, LAST, preferred_element_type=F32
-        )
-        placed = placed[:ROWS] + placed[ROWS:]
-        if first == 0:
-            nonlocal_ref[...] = placed
-        else:
-            nonlocal_ref[...] += placed
+            tall, jnp.concatenate([hot_z, hot_z], axis=1), LAST, preferred_element_type=F32
+        )
+        sums.append(placed)
+    nonlocal_ref[...] = sum(sums[1:], sums[0])
 
 
 def write_parts(coord_ref, table, send_ref, keep_ref):
@@ -388,18 +387,6 @@
         after = lax.cond(some, rest, otherwise, finish(come))
         return lax.optimization_barrier(((*after, *extra), arriving))
 
-    def zeros_like_last(sums):
-        return jnp.zeros((SEGS, 128), F32), jnp.zeros(z_shape, F32)
-
-    def zeros_like_z(own):
-        return (*zeros_like_last(own), jnp.zeros(x_shape, F32))
-
-    def zeros_like_y(own):
-        return (*zeros_like_z(own), jnp.zeros(cells_shape, F32))
-
-    def zeros_like_x(own):
-        return (*zeros_like_y(own), jnp.zeros(x_shape, F32))
-
     def energies():
         return call(
             lambda *refs: energy_kernel(sizes, *refs), [((SEGS, 128), F32)], [],
@@ -410,9 +397,24 @@
         first = energy is None
         place = jnp.arange(2, dtype=jnp.int32)[:, None, None, None]
 
+        def zeros_like_last(sums):
+            made = (jnp.zeros((SEGS, 128), F32),) if first else ()
+            return (jnp.zeros((SEGS, 128), F32), jnp.zeros(z_shape, F32), *made)
+
+        def zeros_like_z(own):
+            return (*zeros_like_last(own), jnp.zeros(x_shape, F32))
+
+        def zeros_like_y(own):
+            return (*zeros_like_z(own), jnp.zeros(cells_shape, F32))
+
+        def zeros_like_x(own):
+            return (*zeros_like_y(own), jnp.zeros(x_shape, F32))
+
         def inside_again(sums):
             own, far = sums
             beyond_x = swap_inside(jnp.where(odd_x, own[0], own[1]), "gx")
+            made = energies() if first else ()
+            beyond_x, made = lax.optimization_barrier((beyond_x, tuple(made)))
             rows = jnp.where(
                 odd_z,
                 jnp.where(odd_x, jnp.stack([beyond_x[0], own[0, 0], own[1, 0]]),
@@ -420,10 +422,11 @@
                 jnp.where(odd_x, jnp.stack([beyond_x[1], own[0, 1], own[1, 1]]),
                           jnp.stack([own[0, 1], own[1, 1], beyond_x[1]])),
             )
-            return tuple(call(
+            laid = call(
                 table_kernel, [((SEGS, 128), F32), (z_shape, F32)], [], (100_000, 300_000),
                 coord, own, beyond_x, swap_inside(rows, "gz"), far,
-            ))
+            )
+            return (*laid, *made)
 
         def along_z_across(own):
             rest, corner_in = staged(
@@ -468,9 +471,9 @@
         rest, xb_in = staged(
             swap_corners, own, lambda v: swap_far_faces(v, False), xb,
             lambda come: total(own, come), along_y_inside, zeros_like_x,
-            lambda: (ya_in, *(energies() if first else ())),
-        )
-        table, zb_in, corner_in, yb_in, xa_in, ya_in, *made = rest
+            lambda: (ya_in,),
+        )
+        table, zb_in, *made, corner_in, yb_in, xa_in, ya_in = rest
         energy = made[0] if first else energy
         return energy, table, xa_in, xb_in, corner_in, ya_in, yb_in, za_in, zb_in
 

time: 209 us -> 205 us (0.981)
  waiting for transfers between devices: 25.5 us -> 18.9 us
    ppermute x21, waiting for transfers between devices: 16.2 us -> 10.9 us  [swap_inside(): return lax.ppermute(value, axis, [(i, i ^ 1) for i in range(count)])]
    ppermute x3, starting transfers between devices: 24 us -> 26.5 us  [swap_corners(): return lax.ppermute(value, ('gx', 'gz'), pairs)]
    ppermute x6, starting transfers between devices: 28.4 us -> 25.8 us  [swap_far_faces(): return lax.ppermute(value, ('gx', 'gz'), pairs)]
  transfers between devices with their start and end apart: 39 -> 39, of which waited for: 17 -> 14; matrix products, arithmetic and copies ran while one was open for 0% -> 0% of each run, Pallas kernels for 3% -> 4%
where the time goes in v9:
time: 205 us; the launch traced here: 203 us
  starting transfers between devices  153 us (75%)
  Pallas kernels  27 us (13%)
  waiting for transfers between devices  18.9 us (9%)
    ppermute x21, starting transfers between devices, swap_inside(): return lax.ppermute(value, axis, [(i, i ^ 1) for i in range(count)])  72.3 us
    ppermute x9, starting transfers between devices, swap_across(): lax.ppermute(value, axis, [(i, across(i, count)) for i in range(count)])  28.1 us
    pallas_call x8, Pallas kernels, call(): pl.pallas_call(kernel, out_shape=[jax.ShapeDtypeStruct(s, k) for s, k in...  26.9 us
    ppermute x3, starting transfers between devices, swap_corners(): return lax.ppermute(value, ('gx', 'gz'), pairs)  26.5 us
    ppermute x6, starting transfers between devices, swap_far_faces(): return lax.ppermute(value, ('gx', 'gz'), pairs)  25.8 us
    ppermute x21, waiting for transfers between devices, swap_inside(): return lax.ppermute(value, axis, [(i, i ^ 1) for i in range(count)])  10.9 us
    ppermute x9, waiting for transfers between devices, swap_across(): lax.ppermute(value, axis, [(i, across(i, count)) for i in range(count)])  7.97 us
  transfers between devices with their start and end apart: 39, of which 14 were waited for; matrix products, arithmetic and copies ran while one was open for 0% of the time, Pallas kernels for 4%

profile of v9, /device:TPU:1, one launch (start us, length us, event | category | flops | bytes accessed | tf_op | source)
XLA Modules:
  0.0 202.5 jit_solution(18081234323663044162)
XLA Ops:
  11.8 14.4 %collective-permute-start.25 = (f32[6,8,128]{2,1,0:T(8,128)S(1)}, f32[6,8,128]{2,1,0:T(8,128)S(1)}, u32[]{:S(2)}, u32[]{:S(2)}) collective-permute-start(f32[6,8,128]{2,1,0:T(8,128)S(1)} %pad_maximum_fusion.3), channel_id=1, source_target_pairs={{0,1},{1,0},{2,3},{3,2},{4,5},{5,4},{6,7},{7,6},{8,9},{9,8},{10,11... | collective-permute-start | bytes 73736 | tf_op jit(solution)/shard_map/ppermute | solution.py:316
  27.1 10.5 %collective-permute-start.26 = (f32[2,2,8,128]{3,2,0,1:T(8,128)S(1)}, f32[2,2,8,128]{3,2,0,1:T(8,128)S(1)}, u32[]{:S(2)}, u32[]{:S(2)}) collective-permute-start(f32[2,2,8,128]{3,2,0,1:T(8,128)S(1)} %maximum_select_fusion.6), channel_id=1, source_target_pairs={{0,975},{1,961},{2,962},{3,963},{4,964},{5,965},{6,966},{7,967},{8... | collective-permute-start | bytes 49160 | tf_op jit(solution)/shard_map/ppermute | solution.py:341
  37.6 5.6 %collective-permute-start.28 = (f32[8,6,8,128]{3,2,1,0:T(8,128)}, f32[8,6,8,128]{3,2,1,0:T(8,128)S(1)}, u32[]{:S(2)}, u32[]{:S(2)}) collective-permute-start(f32[8,6,8,128]{3,2,1,0:T(8,128)} %get-tuple-element.414), channel_id=1, source_target_pairs={{1,961},{2,962},{3,963},{4,964},{5,965},{6,966},{7,967},{8,968},{9... | collective-permute-start | bytes 589832 | tf_op jit(solution)/shard_map/ppermute | solution.py:352
  44.2 33.2 %conditional.12 = (f32[72,128]{1,0:T(8,128)}, f32[4,8,128]{2,1,0:T(8,128)}, f32[72,128]{1,0:T(8,128)}, f32[8,6,8,128]{3,2,1,0:T(8,128)}, f32[8,8,8,128]{3,2,1,0:T(8,128)}, /*index=5*/f32[8,6,8,128]{3,2,1,0:T(8,128)}) conditional(s32[]{:T(128)} %convert_element_type.32, () %tuple.121, (pred[]{:T(512)}, f32[2,2,8,128]{3,2,1,0:T(8,128)S(1)}, ...), branch_computations={%region_0.1_spmd, %region_1.8_spmd} | conditional | flops 24600143872 | bytes 243675056 | solution.py:387
  49.2 28.2 %conditional.2 = (f32[72,128]{1,0:T(8,128)}, f32[4,8,128]{2,1,0:T(8,128)}, f32[72,128]{1,0:T(8,128)}, f32[8,6,8,128]{3,2,1,0:T(8,128)}, f32[8,8,8,128]{3,2,1,0:T(8,128)}) conditional(s32[]{:T(128)} %convert_element_type.24, () %tuple.67, (pred[]{:T(512)}, f32[2,2,8,128]{3,2,1,0:T(8,128)S(1)}, f32[4,8,128]{2,1,0:T(8,128)S(1)}, pred[]{:T(512)}, ...), branch_computations={%region_2.2_spmd, %region_3.7_spmd} | conditional | flops 16600143872 | bytes 162822880 | solution.py:387
  51.1 4.6 %collective-permute-start.5 = (f32[8,8,8,128]{3,2,1,0:T(8,128)S(1)}, f32[8,8,8,128]{3,2,1,0:T(8,128)}, u32[]{:S(2)}, u32[]{:S(2)}) collective-permute-start(f32[8,8,8,128]{3,2,1,0:T(8,128)S(1)} %get-tuple-element.222), channel_id=1, source_target_pairs={{0,48},{16,32},{32,16},{48,0},{1,49},{17,33},{33,17},{49,1},{2,50}... | collective-permute-start | bytes 786440 | tf_op jit(solution)/shard_map/cond/branch_1_fun/cond/branch_1_fun/ppermute | solution.py:325
  55.7 21.7 %conditional.1 = (f32[72,128]{1,0:T(8,128)}, f32[4,8,128]{2,1,0:T(8,128)}, f32[72,128]{1,0:T(8,128)}, f32[8,6,8,128]{3,2,1,0:T(8,128)}) conditional(s32[]{:T(128)} %convert_element_type.15, () %tuple.63, (pred[]{:T(512)}, f32[2,2,8,128]{3,2,1,0:T(8,128)S(1)}, f32[4,8,128]{2,1,0:T(8,128)S(1)}, pred[]{:T(512)}, s32[8]{0:T(128)S(1)}, ...), branch_computations={%region_4.3_spmd, %region_5.6_spmd} | conditional | flops 8600143872 | bytes 81708592 | solution.py:387
  63.5 13.9 %conditional = (f32[72,128]{1,0:T(8,128)}, f32[4,8,128]{2,1,0:T(8,128)}, f32[72,128]{1,0:T(8,128)}) conditional(s32[]{:T(128)} %convert_element_type.14, () %tuple.59, (pred[]{:T(512)}, f32[2,2,8,128]{3,2,1,0:T(8,128)S(1)}, s32[8]{0:T(128)S(1)}, f32[4,5120]{1,0:T(4,128)S(1)}, pred[]{:T(512)}, /*index=5*/f32[8,8,128]{2,1,0:T(8,128)S(1)}) %tuple.60), branch_computations={%region_6.4_spmd, %region_7.5_spmd} | conditional | flops 600135808 | bytes 692619 | solution.py:387
  69.4 6.0 %collective-permute-start.1 = (f32[3,8,128]{2,1,0:T(8,128)S(1)}, f32[3,8,128]{2,1,0:T(8,128)S(1)}, u32[]{:S(2)}, u32[]{:S(2)}) collective-permute-start(f32[3,8,128]{2,1,0:T(8,128)S(1)} %fusion), channel_id=1, source_target_pairs={{0,1},{1,0},{2,3},{3,2},{4,5},{5,4},{6,7},{7,6},{8,9},{9,8},{10,11... | collective-permute-start | bytes 36872 | tf_op jit(solution)/shard_map/cond/branch_1_fun/cond/branch_1_fun/cond/branch_1_fun/cond/branch_1_fun/ppermute | solution.py:316
  77.5 5.9 %shard_map.86 = (f32[8,8,8,128]{3,2,1,0:T(8,128)S(1)}, f32[24,128]{1,0:T(8,128)S(1)}, f32[48,128]{1,0:T(8,128)S(1)}, f32[8,6,8,128]{3,2,1,0:T(8,128)S(1)}, f32[8...) custom-call(s32[8]{0:T(128)S(1)} %stack.93.refs_0_, f32[8,8,8,128]{3,2,1,0:T(8,128)S(1)} %copy-done.5, ...), custom_call_target="tpu_custom_call" | custom-call | flops 1500000000 | bytes 4000000 | tf_op jit(solution)/shard_map/pallas_call | solution.py:288
  92.6 7.7 %collective-permute-start.31 = (f32[2,2,8,128]{3,2,0,1:T(8,128)S(1)}, f32[2,2,8,128]{3,2,0,1:T(8,128)S(1)}, u32[]{:S(2)}, u32[]{:S(2)}) collective-permute-start(f32[2,2,8,128]{3,2,0,1:T(8,128)S(1)} %maximum_select_fusion.7), channel_id=1, source_target_pairs={{0,975},{1,961},{2,962},{3,963},{4,964},{5,965},{6,966},{7,967},{8... | collective-permute-start | bytes 49160 | tf_op jit(solution)/shard_map/ppermute | solution.py:341
  100.4 8.4 %collective-permute-start.33 = (f32[8,6,8,128]{3,2,1,0:T(8,128)}, f32[8,6,8,128]{3,2,1,0:T(8,128)S(1)}, u32[]{:S(2)}, u32[]{:S(2)}) collective-permute-start(f32[8,6,8,128]{3,2,1,0:T(8,128)} %get-tuple-element.439), channel_id=1, source_target_pairs={{1,961},{2,962},{3,963},{4,964},{5,965},{6,966},{7,967},{8,968},{9... | collective-permute-start | bytes 589832 | tf_op jit(solution)/shard_map/ppermute | solution.py:352
  108.8 29.3 %conditional.13 = (f32[72,128]{1,0:T(8,128)}, f32[4,8,128]{2,1,0:T(8,128)}, f32[8,6,8,128]{3,2,1,0:T(8,128)}, f32[8,8,8,128]{3,2,1,0:T(8,128)}, f32[8,6,8,128]{3,2,1,0:T(8,128)}) conditional(s32[]{:T(128)} %convert_element_type.32, () %tuple.127, (pred[]{:T(512)}, f32[2,2,8,128]{3,2,1,0:T(8,128)S(1)}, f32[4,8,128]{2,1,0:T(8,128)S(1)}, pred[]{:T(512)}, ...), branch_computations={%region_8.9_spmd, %region_9.16_spmd} | conditional | flops 24000143360 | bytes 243475008 | solution.py:387
  114.3 23.6 %conditional.5 = (f32[72,128]{1,0:T(8,128)}, f32[4,8,128]{2,1,0:T(8,128)}, f32[8,6,8,128]{3,2,1,0:T(8,128)}, f32[8,8,8,128]{3,2,1,0:T(8,128)}) conditional(s32[]{:T(128)} %convert_element_type.27, () %tuple.83, (pred[]{:T(512)}, f32[2,2,8,128]{3,2,1,0:T(8,128)S(1)}, f32[4,8,128]{2,1,0:T(8,128)S(1)}, pred[]{:T(512)}, pred[]{:T(512)}, ...), branch_computations={%region_10.10_spmd, %region_11.15_spmd} | conditional | flops 16000143360 | bytes 162622848 | solution.py:387
  120.8 17.1 %conditional.4 = (f32[72,128]{1,0:T(8,128)}, f32[4,8,128]{2,1,0:T(8,128)}, f32[8,6,8,128]{3,2,1,0:T(8,128)}) conditional(s32[]{:T(128)} %convert_element_type.26, () %tuple.79, (pred[]{:T(512)}, f32[2,2,8,128]{3,2,1,0:T(8,128)S(1)}, f32[4,8,128]{2,1,0:T(8,128)S(1)}, pred[]{:T(512)}, pred[]{:T(512)}, /*index=5*/s32[8]{0:T(128)S(1)}, ...), branch_computations={%region_12.11_spmd, %region_13.14_spmd} | conditional | flops 8000143872 | bytes 81508560 | solution.py:387
  126.4 11.5 %conditional.3 = ((f32[72,128]{1,0:T(8,128)}, f32[4,8,128]{2,1,0:T(8,128)})) conditional(s32[]{:T(128)} %convert_element_type.25, () %tuple.75, (pred[]{:T(512)}, f32[2,2,8,128]{3,2,1,0:T(8,128)S(1)}, pred[]{:T(512)}, s32[8]{0:T(128)S(1)}, f32[8,8,128]{2,1,0:T(8,128)S(1)}) %tuple.76), branch_computations={%region_14.12_spmd, %region_15.13_spmd} | conditional | flops 135840 | bytes 492603 | solution.py:387
  130.8 5.1 %collective-permute-start.9 = (f32[3,8,128]{2,1,0:T(8,128)S(1)}, f32[3,8,128]{2,1,0:T(8,128)S(1)}, u32[]{:S(2)}, u32[]{:S(2)}) collective-permute-start(f32[3,8,128]{2,1,0:T(8,128)S(1)} %fusion.1), channel_id=1, source_target_pairs={{0,1},{1,0},{2,3},{3,2},{4,5},{5,4},{6,7},{7,6},{8,9},{9,8},{10,11... | collective-permute-start | bytes 36872 | tf_op jit(solution)/shard_map/cond/branch_1_fun/cond/branch_1_fun/cond/branch_1_fun/cond/branch_1_fun/ppermute | solution.py:316
  138.1 5.9 %shard_map.89 = (f32[8,8,8,128]{3,2,1,0:T(8,128)S(1)}, f32[24,128]{1,0:T(8,128)S(1)}, f32[48,128]{1,0:T(8,128)S(1)}, f32[8,6,8,128]{3,2,1,0:T(8,128)S(1)}, f32[8...) custom-call(s32[8]{0:T(128)S(1)} %stack.93.refs_0_, ...), custom_call_target="tpu_custom_call" | custom-call | flops 1500000000 | bytes 4000000 | tf_op jit(solution)/shard_map/pallas_call | solution.py:288
  152.8 8.3 %collective-permute-start.36 = (f32[2,2,8,128]{3,2,0,1:T(8,128)S(1)}, f32[2,2,8,128]{3,2,0,1:T(8,128)S(1)}, u32[]{:S(2)}, u32[]{:S(2)}) collective-permute-start(f32[2,2,8,128]{3,2,0,1:T(8,128)S(1)} %maximum_select_fusion.8), channel_id=1, source_target_pairs={{0,975},{1,961},{2,962},{3,963},{4,964},{5,965},{6,966},{7,967},{8... | collective-permute-start | bytes 49160 | tf_op jit(solution)/shard_map/ppermute | solution.py:341
  161.2 7.7 %collective-permute-start.38 = (f32[8,6,8,128]{3,2,1,0:T(8,128)}, f32[8,6,8,128]{3,2,1,0:T(8,128)S(1)}, u32[]{:S(2)}, u32[]{:S(2)}) collective-permute-start(f32[8,6,8,128]{3,2,1,0:T(8,128)} %get-tuple-element.463), channel_id=1, source_target_pairs={{1,961},{2,962},{3,963},{4,964},{5,965},{6,966},{7,967},{8,968},{9... | collective-permute-start | bytes 589832 | tf_op jit(solution)/shard_map/ppermute | solution.py:352
  169.0 29.0 %conditional.14 = (f32[72,128]{1,0:T(8,128)}, f32[4,8,128]{2,1,0:T(8,128)}, f32[8,6,8,128]{3,2,1,0:T(8,128)}, f32[8,8,8,128]{3,2,1,0:T(8,128)}, f32[8,6,8,128]{3,2,1,0:T(8,128)}) conditional(s32[]{:T(128)} %convert_element_type.32, () %tuple.133, (pred[]{:T(512)}, f32[2,2,8,128]{3,2,1,0:T(8,128)S(1)}, f32[4,8,128]{2,1,0:T(8,128)S(1)}, pred[]{:T(512)}, ...), branch_computations={%region_16.17_spmd, %region_17.24_spmd} | conditional | flops 24000143360 | bytes 243475008 | solution.py:387
  173.7 24.3 %conditional.8 = (f32[72,128]{1,0:T(8,128)}, f32[4,8,128]{2,1,0:T(8,128)}, f32[8,6,8,128]{3,2,1,0:T(8,128)}, f32[8,8,8,128]{3,2,1,0:T(8,128)}) conditional(s32[]{:T(128)} %convert_element_type.30, () %tuple.99, (pred[]{:T(512)}, f32[2,2,8,128]{3,2,1,0:T(8,128)S(1)}, f32[4,8,128]{2,1,0:T(8,128)S(1)}, pred[]{:T(512)}, pred[]{:T(512)}, ...), branch_computations={%region_18.18_spmd, %region_19.23_spmd} | conditional | flops 16000143360 | bytes 162622848 | solution.py:387
  180.2 17.8 %conditional.7 = (f32[72,128]{1,0:T(8,128)}, f32[4,8,128]{2,1,0:T(8,128)}, f32[8,6,8,128]{3,2,1,0:T(8,128)}) conditional(s32[]{:T(128)} %convert_element_type.29, () %tuple.95, (pred[]{:T(512)}, f32[2,2,8,128]{3,2,1,0:T(8,128)S(1)}, f32[4,8,128]{2,1,0:T(8,128)S(1)}, pred[]{:T(512)}, pred[]{:T(512)}, /*index=5*/s32[8]{0:T(128)S(1)}, ...), branch_computations={%region_20.19_spmd, %region_21.22_spmd} | conditional | flops 8000143872 | bytes 81508560 | solution.py:387
  187.7 10.3 %conditional.6 = ((f32[72,128]{1,0:T(8,128)}, f32[4,8,128]{2,1,0:T(8,128)})) conditional(s32[]{:T(128)} %convert_element_type.28, () %tuple.91, (pred[]{:T(512)}, f32[2,2,8,128]{3,2,1,0:T(8,128)S(1)}, pred[]{:T(512)}, s32[8]{0:T(128)S(1)}, f32[8,8,128]{2,1,0:T(8,128)S(1)}) %tuple.92), branch_computations={%region_22.20_spmd, %region_23.21_spmd} | conditional | flops 135840 | bytes 492603 | solution.py:387
  (150 shorter events, 110.5 us)
Async XLA Ops:
  4.5 7.2 %collective-permute-start.24 = (f32[24,128]{1,0:T(8,128)S(1)}, f32[24,128]{1,0:T(8,128)S(1)}, u32[]{:S(2)}, u32[]{:S(2)}) collective-permute-start(f32[24,128]{1,0:T(8,128)S(1)} %get-tuple-element.400), channel_id=1, source_target_pairs={{0,64},{64,0},{128,192},{192,128},{256,320},{320,256},{384,448},{4... | collective-permute-start | bytes 36872 | tf_op jit(solution)/shard_map/ppermute | solution.py:316
  8.6 34.7 %collective-permute-start.27 = (f32[8,8,8,128]{3,2,1,0:T(8,128)S(1)}, f32[8,8,8,128]{3,2,1,0:T(8,128)S(1)}, u32[]{:S(2)}, u32[]{:S(2)}) collective-permute-start(f32[8,8,8,128]{3,2,1,0:T(8,128)S(1)} %copy-done.5), channel_id=1, source_target_pairs={{0,16},{16,0},{32,48},{48,32},{1,17},{17,1},{33,49},{49,33},{2,18}... | collective-permute-start | bytes 786440 | tf_op jit(solution)/shard_map/ppermute | solution.py:316
  11.8 15.3 %collective-permute-start.25 = (f32[6,8,128]{2,1,0:T(8,128)S(1)}, f32[6,8,128]{2,1,0:T(8,128)S(1)}, u32[]{:S(2)}, u32[]{:S(2)}) collective-permute-start(f32[6,8,128]{2,1,0:T(8,128)S(1)} %pad_maximum_fusion.3), channel_id=1, source_target_pairs={{0,1},{1,0},{2,3},{3,2},{4,5},{5,4},{6,7},{7,6},{8,9},{9,8},{10,11... | collective-permute-start | bytes 73736 | tf_op jit(solution)/shard_map/ppermute | solution.py:316
  27.1 16.1 %collective-permute-start.26 = (f32[2,2,8,128]{3,2,0,1:T(8,128)S(1)}, f32[2,2,8,128]{3,2,0,1:T(8,128)S(1)}, u32[]{:S(2)}, u32[]{:S(2)}) collective-permute-start(f32[2,2,8,128]{3,2,0,1:T(8,128)S(1)} %maximum_select_fusion.6), channel_id=1, source_target_pairs={{0,975},{1,961},{2,962},{3,963},{4,964},{5,965},{6,966},{7,967},{8... | collective-permute-start | bytes 49160 | tf_op jit(solution)/shard_map/ppermute | solution.py:341
  37.6 39.8 %collective-permute-start.28 = (f32[8,6,8,128]{3,2,1,0:T(8,128)}, f32[8,6,8,128]{3,2,1,0:T(8,128)S(1)}, u32[]{:S(2)}, u32[]{:S(2)}) collective-permute-start(f32[8,6,8,128]{3,2,1,0:T(8,128)} %get-tuple-element.414), channel_id=1, source_target_pairs={{1,961},{2,962},{3,963},{4,964},{5,965},{6,966},{7,967},{8,968},{9... | collective-permute-start | bytes 589832 | tf_op jit(solution)/shard_map/ppermute | solution.py:352
  46.3 31.2 %collective-permute-start.7 = (f32[8,6,8,128]{3,2,1,0:T(8,128)S(1)}, f32[8,6,8,128]{3,2,1,0:T(8,128)}, u32[]{:S(2)}, u32[]{:S(2)}) collective-permute-start(f32[8,6,8,128]{3,2,1,0:T(8,128)S(1)} %get-tuple-element.238), channel_id=1, source_target_pairs={{0,64},{64,0},{128,192},{192,128},{256,320},{320,256},{384,448},{4... | collective-permute-start | bytes 589832 | tf_op jit(solution)/shard_map/cond/branch_1_fun/ppermute | solution.py:316
  51.1 26.3 %collective-permute-start.5 = (f32[8,8,8,128]{3,2,1,0:T(8,128)S(1)}, f32[8,8,8,128]{3,2,1,0:T(8,128)}, u32[]{:S(2)}, u32[]{:S(2)}) collective-permute-start(f32[8,8,8,128]{3,2,1,0:T(8,128)S(1)} %get-tuple-element.222), channel_id=1, source_target_pairs={{0,48},{16,32},{32,16},{48,0},{1,49},{17,33},{33,17},{49,1},{2,50}... | collective-permute-start | bytes 786440 | tf_op jit(solution)/shard_map/cond/branch_1_fun/cond/branch_1_fun/ppermute | solution.py:325
  55.8 7.7 %collective-permute-start.2 = (f32[8,8,128]{2,1,0:T(8,128)S(1)}, f32[8,8,128]{2,1,0:T(8,128)S(1)}, u32[]{:S(2)}, u32[]{:S(2)}) collective-permute-start(f32[8,8,128]{2,1,0:T(8,128)S(1)} %pad_maximum_fusion), channel_id=1, source_target_pairs={{0,15},{1,2},{2,1},{3,4},{4,3},{5,6},{6,5},{7,8},{8,7},{9,10},{10,... | collective-permute-start | bytes 98312 | tf_op jit(solution)/shard_map/cond/branch_1_fun/cond/branch_1_fun/cond/branch_1_fun/ppermute | solution.py:325
  57.7 19.7 %collective-permute-start.3 = (f32[8,6,8,128]{3,2,1,0:T(8,128)}, f32[8,6,8,128]{3,2,1,0:T(8,128)}, u32[]{:S(2)}, u32[]{:S(2)}) collective-permute-start(f32[8,6,8,128]{3,2,1,0:T(8,128)} %get-tuple-element.208), channel_id=1, source_target_pairs={{0,960},{15,975},{448,512},{463,527},{512,448},{527,463},{960,0},{... | collective-permute-start | bytes 589832 | tf_op jit(solution)/shard_map/cond/branch_1_fun/cond/branch_1_fun/cond/branch_1_fun/ppermute | solution.py:352
  69.4 6.9 %collective-permute-start.1 = (f32[3,8,128]{2,1,0:T(8,128)S(1)}, f32[3,8,128]{2,1,0:T(8,128)S(1)}, u32[]{:S(2)}, u32[]{:S(2)}) collective-permute-start(f32[3,8,128]{2,1,0:T(8,128)S(1)} %fusion), channel_id=1, source_target_pairs={{0,1},{1,0},{2,3},{3,2},{4,5},{5,4},{6,7},{7,6},{8,9},{9,8},{10,11... | collective-permute-start | bytes 36872 | tf_op jit(solution)/shard_map/cond/branch_1_fun/cond/branch_1_fun/cond/branch_1_fun/cond/branch_1_fun/ppermute | solution.py:316
  87.0 21.7 %collective-permute-start.32 = (f32[8,8,8,128]{3,2,1,0:T(8,128)S(1)}, f32[8,8,8,128]{3,2,1,0:T(8,128)S(1)}, u32[]{:S(2)}, u32[]{:S(2)}) collective-permute-start(f32[8,8,8,128]{3,2,1,0:T(8,128)S(1)} %get-tuple-element.428.refs_1_.refs_2_), channel_id=1, source_target_pairs={{0,16},{16,0},{32,48},{48,32},{1,17},{17,1},{33,49},{49,33},{2,18}... | collective-permute-start | bytes 786440 | tf_op jit(solution)/shard_map/ppermute | solution.py:316
  92.6 16.1 %collective-permute-start.31 = (f32[2,2,8,128]{3,2,0,1:T(8,128)S(1)}, f32[2,2,8,128]{3,2,0,1:T(8,128)S(1)}, u32[]{:S(2)}, u32[]{:S(2)}) collective-permute-start(f32[2,2,8,128]{3,2,0,1:T(8,128)S(1)} %maximum_select_fusion.7), channel_id=1, source_target_pairs={{0,975},{1,961},{2,962},{3,963},{4,964},{5,965},{6,966},{7,967},{8... | collective-permute-start | bytes 49160 | tf_op jit(solution)/shard_map/ppermute | solution.py:341
  100.4 37.7 %collective-permute-start.33 = (f32[8,6,8,128]{3,2,1,0:T(8,128)}, f32[8,6,8,128]{3,2,1,0:T(8,128)S(1)}, u32[]{:S(2)}, u32[]{:S(2)}) collective-permute-start(f32[8,6,8,128]{3,2,1,0:T(8,128)} %get-tuple-element.439), channel_id=1, source_target_pairs={{1,961},{2,962},{3,963},{4,964},{5,965},{6,966},{7,967},{8,968},{9... | collective-permute-start | bytes 589832 | tf_op jit(solution)/shard_map/ppermute | solution.py:352
  112.3 25.6 %collective-permute-start.15 = (f32[8,6,8,128]{3,2,1,0:T(8,128)S(1)}, f32[8,6,8,128]{3,2,1,0:T(8,128)}, u32[]{:S(2)}, u32[]{:S(2)}) collective-permute-start(f32[8,6,8,128]{3,2,1,0:T(8,128)S(1)} %get-tuple-element.279), channel_id=1, source_target_pairs={{0,64},{64,0},{128,192},{192,128},{256,320},{320,256},{384,448},{4... | collective-permute-start | bytes 589832 | tf_op jit(solution)/shard_map/cond/branch_1_fun/ppermute | solution.py:316
  114.3 6.5 %collective-permute-start.12 = (f32[2,2,8,128]{3,2,1,0:T(8,128)S(1)}, f32[2,2,8,128]{3,2,1,0:T(8,128)S(1)}, u32[]{:S(2)}, u32[]{:S(2)}) collective-permute-start(f32[2,2,8,128]{3,2,1,0:T(8,128)S(1)} %get-tuple-element.255.left_ref), channel_id=1, source_target_pairs={{0,48},{16,32},{32,16},{48,0},{1,49},{17,33},{33,17},{49,1},{2,50}... | collective-permute-start | bytes 49160 | tf_op jit(solution)/shard_map/cond/branch_1_fun/cond/branch_1_fun/ppermute | solution.py:325
  118.0 19.9 %collective-permute-start.13 = (f32[8,8,8,128]{3,2,1,0:T(8,128)S(1)}, f32[8,8,8,128]{3,2,1,0:T(8,128)}, u32[]{:S(2)}, u32[]{:S(2)}) collective-permute-start(f32[8,8,8,128]{3,2,1,0:T(8,128)S(1)} %get-tuple-element.265), channel_id=1, source_target_pairs={{0,48},{16,32},{32,16},{48,0},{1,49},{17,33},{33,17},{49,1},{2,50}... | collective-permute-start | bytes 786440 | tf_op jit(solution)/shard_map/cond/branch_1_fun/cond/branch_1_fun/ppermute | solution.py:325
  123.1 14.8 %collective-permute-start.11 = (f32[8,6,8,128]{3,2,1,0:T(8,128)}, f32[8,6,8,128]{3,2,1,0:T(8,128)}, u32[]{:S(2)}, u32[]{:S(2)}) collective-permute-start(f32[8,6,8,128]{3,2,1,0:T(8,128)} %get-tuple-element.253), channel_id=1, source_target_pairs={{0,960},{15,975},{448,512},{463,527},{512,448},{527,463},{960,0},{... | collective-permute-start | bytes 589832 | tf_op jit(solution)/shard_map/cond/branch_1_fun/cond/branch_1_fun/cond/branch_1_fun/ppermute | solution.py:352
  146.0 23.0 %collective-permute-start.37 = (f32[8,8,8,128]{3,2,1,0:T(8,128)S(1)}, f32[8,8,8,128]{3,2,1,0:T(8,128)S(1)}, u32[]{:S(2)}, u32[]{:S(2)}) collective-permute-start(f32[8,8,8,128]{3,2,1,0:T(8,128)S(1)} %get-tuple-element.452.refs_1_), channel_id=1, source_target_pairs={{0,16},{16,0},{32,48},{48,32},{1,17},{17,1},{33,49},{49,33},{2,18}... | collective-permute-start | bytes 786440 | tf_op jit(solution)/shard_map/ppermute | solution.py:316
  152.8 16.1 %collective-permute-start.36 = (f32[2,2,8,128]{3,2,0,1:T(8,128)S(1)}, f32[2,2,8,128]{3,2,0,1:T(8,128)S(1)}, u32[]{:S(2)}, u32[]{:S(2)}) collective-permute-start(f32[2,2,8,128]{3,2,0,1:T(8,128)S(1)} %maximum_select_fusion.8), channel_id=1, source_target_pairs={{0,975},{1,961},{2,962},{3,963},{4,964},{5,965},{6,966},{7,967},{8... | collective-permute-start | bytes 49160 | tf_op jit(solution)/shard_map/ppermute | solution.py:341
  161.2 36.8 %collective-permute-start.38 = (f32[8,6,8,128]{3,2,1,0:T(8,128)}, f32[8,6,8,128]{3,2,1,0:T(8,128)S(1)}, u32[]{:S(2)}, u32[]{:S(2)}) collective-permute-start(f32[8,6,8,128]{3,2,1,0:T(8,128)} %get-tuple-element.463), channel_id=1, source_target_pairs={{1,961},{2,962},{3,963},{4,964},{5,965},{6,966},{7,967},{8,968},{9... | collective-permute-start | bytes 589832 | tf_op jit(solution)/shard_map/ppermute | solution.py:352
  171.0 27.0 %collective-permute-start.23 = (f32[8,6,8,128]{3,2,1,0:T(8,128)S(1)}, f32[8,6,8,128]{3,2,1,0:T(8,128)}, u32[]{:S(2)}, u32[]{:S(2)}) collective-permute-start(f32[8,6,8,128]{3,2,1,0:T(8,128)S(1)} %get-tuple-element.320), channel_id=1, source_target_pairs={{0,64},{64,0},{128,192},{192,128},{256,320},{320,256},{384,448},{4... | collective-permute-start | bytes 589832 | tf_op jit(solution)/shard_map/cond/branch_1_fun/ppermute | solution.py:316
  178.0 20.0 %collective-permute-start.21 = (f32[8,8,8,128]{3,2,1,0:T(8,128)S(1)}, f32[8,8,8,128]{3,2,1,0:T(8,128)}, u32[]{:S(2)}, u32[]{:S(2)}) collective-permute-start(f32[8,8,8,128]{3,2,1,0:T(8,128)S(1)} %get-tuple-element.306), channel_id=1, source_target_pairs={{0,48},{16,32},{32,16},{48,0},{1,49},{17,33},{33,17},{49,1},{2,50}... | collective-permute-start | bytes 786440 | tf_op jit(solution)/shard_map/cond/branch_1_fun/cond/branch_1_fun/ppermute | solution.py:325
  180.2 7.5 %collective-permute-start.18 = (f32[8,8,128]{2,1,0:T(8,128)S(1)}, f32[8,8,128]{2,1,0:T(8,128)S(1)}, u32[]{:S(2)}, u32[]{:S(2)}) collective-permute-start(f32[8,8,128]{2,1,0:T(8,128)S(1)} %pad_maximum_fusion.2), channel_id=1, source_target_pairs={{0,15},{1,2},{2,1},{3,4},{4,3},{5,6},{6,5},{7,8},{8,7},{9,10},{10,... | collective-permute-start | bytes 98312 | tf_op jit(solution)/shard_map/cond/branch_1_fun/cond/branch_1_fun/cond/branch_1_fun/ppermute | solution.py:325
  184.7 13.3 %collective-permute-start.19 = (f32[8,6,8,128]{3,2,1,0:T(8,128)}, f32[8,6,8,128]{3,2,1,0:T(8,128)}, u32[]{:S(2)}, u32[]{:S(2)}) collective-permute-start(f32[8,6,8,128]{3,2,1,0:T(8,128)} %get-tuple-element.294), channel_id=1, source_target_pairs={{0,960},{15,975},{448,512},{463,527},{512,448},{527,463},{960,0},{... | collective-permute-start | bytes 589832 | tf_op jit(solution)/shard_map/cond/branch_1_fun/cond/branch_1_fun/cond/branch_1_fun/ppermute | solution.py:352
  (22 other events, 120.9 us)
